TPU v7x, 256 devices: a whole 4x4x8 slice. The times are simulated.
256 devices in a mesh: src: 16 (over z, x_hi), dom: 16 (over y, x_lo, core).
Axes of the slice: x: 4 (x_hi: 2, x_lo: 2; x = x_hi * 2 + x_lo), y: 4, z: 8, core: 2. Of those that a mesh axis runs over, the one named last changes fastest.
Arguments:
- primary: float32 [16, 4, 32, 128, 128], P('src', None, 'dom'), may hold values from -6 to 6
- conductivity: float32 [3, 32, 128, 128], P(None, 'dom'), may hold values from 0.5 to 2
- observed: float32 [16, 4, 1024], P('src'), may hold values from -6 to 6
- receivers: int32 [16, 1024], P('src'), may hold values from 0 to 524287
Outputs:
- gradient: float32 [3, 32, 128, 128], P(None, 'dom')
- predicted: float32 [16, 4, 1024], P('src')
Inputs may be any that keep to these rules, and one draw needn't show every extreme that they name: receivers may share a cell.
All inputs are finite; a program needn't handle non-finite values.
Results may differ from a plain program's by a relative error of at most 0.0001.
Values sent between devices are 32-bit elements; how exact they have to be, the bound alone decides.
No kernel may reach another device: no remote copies, remote signals or barrier semaphores. Data moves between devices by JAX's collectives and lax.ppermute only.
A program may use at most 128 MiB of HBM per device.

v0:
```python
import jax
import jax.numpy as jnp
from jax import lax
from jax.sharding import PartitionSpec as P

ITERS = 3


def extended_2(block, sides, width):
    for axis, dim in sides:
        count = lax.axis_size(axis)
        forward = [(i, i + 1) for i in range(count - 1)]
        backward = [(target, source) for source, target in forward]
        low = lax.ppermute(
            lax.slice_in_dim(block, block.shape[dim] - width, None, axis=dim), axis, forward
        )
        high = lax.ppermute(lax.slice_in_dim(block, 0, width, axis=dim), axis, backward)
        block = jnp.concatenate([low, block, high], axis=dim)
    return block


def neighbour_upper(field, along):
    extent = field.shape[along]
    inner_part = lax.slice_in_dim(field, 1, extent, axis=along)
    zeros_part = jnp.zeros_like(lax.slice_in_dim(field, 0, 1, axis=along))
    return jnp.concatenate([inner_part, zeros_part], axis=along)


def neighbour_lower(field, along):
    extent = field.shape[along]
    inner_part = lax.slice_in_dim(field, 0, extent - 1, axis=along)
    zeros_part = jnp.zeros_like(lax.slice_in_dim(field, 0, 1, axis=along))
    return jnp.concatenate([zeros_part, inner_part], axis=along)


def face_pair(conduct, along):
    return (
        0.5 * (conduct + neighbour_upper(conduct, along)),
        0.5 * (conduct + neighbour_lower(conduct, along)),
    )


def diagonal_of(face_list):
    result = face_list[0][0] + face_list[0][1]
    for component in (1, 2):
        result = result + face_list[component][0] + face_list[component][1]
    return result


def operate(extended, face_list, diagonal):
    field = extended[:, 1:-1]
    result = diagonal * field
    upper, lower = face_list[0]
    result = result - upper * extended[:, 2:] - lower * extended[:, :-2]
    for component in (1, 2):
        upper, lower = face_list[component]
        result = (
            result
            - upper * neighbour_upper(field, component + 1)
            - lower * neighbour_lower(field, component + 1)
        )
    return result


def column(values):
    return values[:, None, None, None]


def local_inner(left, right):
    return jnp.sum(left * right, axis=(1, 2, 3))


def extend_rims(field):
    return extended_2(field, (("dom", 1),), 1)


def summed(values):
    return lax.psum(values, "dom")


def precond_solve(right_side, face_list, diagonal):
    iterate = jnp.zeros_like(right_side)
    rim_low = jnp.zeros_like(right_side[:, :1])
    rim_high = jnp.zeros_like(right_side[:, :1])
    residual = right_side
    scaled = residual / diagonal
    direction = scaled
    norm_now = summed(local_inner(residual, scaled))
    for iteration in range(ITERS):
        dir_ext = extend_rims(direction)
        image = operate(dir_ext, face_list, diagonal)
        step_len = column(norm_now / summed(local_inner(direction, image)))
        iterate = iterate + step_len * direction
        rim_low = rim_low + step_len * dir_ext[:, :1]
        rim_high = rim_high + step_len * dir_ext[:, -1:]
        residual = residual - step_len * image
        if iteration + 1 < ITERS:
            scaled = residual / diagonal
            norm_next = summed(local_inner(residual, scaled))
            direction = scaled + column(norm_next / norm_now) * direction
            norm_now = norm_next
    return (iterate, rim_low, rim_high)


def per_device(primary, conductivity, observed, receivers):
    primary_g = primary[0]
    observed_g = observed[0]
    cells_g = receivers[0]
    domains = lax.axis_size("dom")
    position = lax.axis_index("dom")
    sources, layers, extent_y, extent_z = primary_g.shape
    stacked = jnp.concatenate([primary_g, conductivity[0:1]], axis=0)
    extended = extended_2(stacked, (("dom", 1),), 1)
    primary_ext = extended[:sources]
    cond_ext = extended[sources]
    cond_first = conductivity[0]
    face_list = [(0.5 * (cond_first + cond_ext[2:]), 0.5 * (cond_first + cond_ext[:-2]))]
    face_list = face_list + [face_pair(conductivity[component], component) for component in (1, 2)]
    diagonal = diagonal_of(face_list)
    layer_pos = lax.broadcasted_iota(jnp.int32, (layers, extent_y, extent_z), 0)
    at_top = jnp.logical_and(position == domains - 1, layer_pos == layers - 1)
    at_bottom = jnp.logical_and(position == 0, layer_pos == 0)
    ones_field = jnp.ones((layers, extent_y, extent_z), jnp.float32)
    unit_faces = [
        (
            jnp.where(at_top, 0.5, 1.0).astype(jnp.float32),
            jnp.where(at_bottom, 0.5, 1.0).astype(jnp.float32),
        )
    ]
    unit_faces = unit_faces + [face_pair(ones_field, component) for component in (1, 2)]
    unit_diagonal = diagonal_of(unit_faces)
    right_side = operate(primary_ext, unit_faces, unit_diagonal) - operate(
        primary_ext, face_list, diagonal
    )
    secondary, sec_low, sec_high = precond_solve(right_side, face_list, diagonal)
    potential = primary_g + secondary
    pot_ext = jnp.concatenate(
        [primary_ext[:, :1] + sec_low, potential, primary_ext[:, -1:] + sec_high], axis=1
    )
    plane_size = extent_y * extent_z
    layer_of = cells_g // plane_size
    in_plane = cells_g - layer_of * plane_size
    local_layer = layer_of - position * layers
    inside = jnp.logical_and(local_layer >= 0, local_layer < layers)
    local_cell = jnp.clip(local_layer, 0, layers - 1) * plane_size + in_plane
    flattened = potential.reshape(sources, -1)
    picked = jnp.where(inside[None, :], jnp.take(flattened, local_cell, axis=1), 0.0)
    predicted = lax.psum(picked, "dom")
    weights = jnp.where(inside[None, :], predicted - observed_g, 0.0)
    source = jnp.zeros_like(flattened).at[:, local_cell].add(weights).reshape(potential.shape)
    adjoint, adj_low, adj_high = precond_solve(source, face_list, diagonal)
    adj_ext = jnp.concatenate([adj_low, adjoint, adj_high], axis=1)
    upper_term = (potential - pot_ext[:, 2:]) * (adjoint - adj_ext[:, 2:])
    lower_term = (potential - pot_ext[:, :-2]) * (adjoint - adj_ext[:, :-2])
    pieces = [-0.5 * jnp.sum(upper_term + lower_term, axis=0)]
    for component in (1, 2):
        along = component + 1
        upper_term = (potential - neighbour_upper(potential, along)) * (
            adjoint - neighbour_upper(adjoint, along)
        )
        lower_term = (potential - neighbour_lower(potential, along)) * (
            adjoint - neighbour_lower(adjoint, along)
        )
        pieces.append(-0.5 * jnp.sum(upper_term + lower_term, axis=0))
    local_grad = jnp.stack(pieces)
    summed_grad = lax.psum(local_grad, "src")
    return (summed_grad, predicted[None])


def solution(mesh):
    placed = (
        P("src", None, "dom", None, None),
        P(None, "dom", None, None),
        P("src", None, None),
        P("src", None),
    )
    return jax.shard_map(
        per_device,
        mesh=mesh,
        in_specs=placed,
        out_specs=(P(None, "dom", None, None), P("src", None, None)),
        check_vma=False,
    )
```

profile of v0, /device:TPU:4, one launch (start us, length us, event | category | flops | bytes accessed | tf_op | source)
XLA Modules:
  0.0 664.8 jit_solution(13524334445278450123)
XLA Ops:
  7.2 1.1 slice_bitcast_fusion
  8.3 1.1 pad_maximum_fusion.18
  9.4 1.8 collective-permute-start.1
  11.1 1.3 collective-permute-start
  12.4 1.4 fusion.103
  14.6 1.3 compare_and_fusion
  17.0 1.3 fusion.102
  18.3 1.3 fusion.71
  19.7 1.4 pad_maximum_fusion
  21.1 2.0 broadcast_divide_fusion.1
  23.4 1.3 collective-permute-start.2
  24.7 6.3 collective-permute-start.3
  31.1 1.0 collective-permute-done.3
  32.9 32.4 %all-reduce.41 = (f32[4]{0:T(128)S(1)}, f32[4]{0:T(128)S(1)}) all-reduce(f32[4]{0:T(128)S(1)} %get-tuple-element.10, f32[4]{0:T(128)S(1)} %get-tuple-element.9), channel_id=1, replica_groups=mesh['src'=16,'dom'=16] {'dom'}, use_global_device_ids=true, to_apply=%region_1.2 | all-reduce | flops 8 | bytes 64 | tf_op jit(solution)/shard_map/psum | solution.py:78
  65.6 27.5 %psum.100 = f32[4]{0:T(128)S(1)} all-reduce(f32[4]{0:T(128)S(1)} %get-tuple-element.23), channel_id=1, replica_groups=mesh['src'=16,'dom'=16] {'dom'}, use_global_device_ids=true, to_apply=%region_5.6 | all-reduce | flops 4 | bytes 32 | tf_op jit(solution)/shard_map/psum | solution.py:78
  93.4 1.3 collective-permute-start.4
  94.7 3.0 collective-permute-start.5
  99.6 32.2 %psum.101 = f32[4]{0:T(128)} all-reduce(f32[4]{0:T(128)S(1)} %get-tuple-element.21), channel_id=1, replica_groups=mesh['src'=16,'dom'=16] {'dom'}, use_global_device_ids=true, to_apply=%region_7.8 | all-reduce | flops 4 | bytes 32 | tf_op jit(solution)/shard_map/psum | solution.py:78
  133.8 27.7 %psum.102 = f32[4]{0:T(128)} all-reduce(f32[4]{0:T(128)} %multiply_reduce_fusion.4), channel_id=1, replica_groups=mesh['src'=16,'dom'=16] {'dom'}, use_global_device_ids=true, to_apply=%region_9.10 | all-reduce | flops 4 | bytes 32 | tf_op jit(solution)/shard_map/psum | solution.py:78
  162.1 1.2 multiply_add_fusion.3
  163.4 1.3 collective-permute-start.6
  164.7 3.0 collective-permute-start.7
  170.2 1.7 copy.12
  172.0 32.0 %psum.103 = f32[4]{0:T(128)S(1)} all-reduce(f32[4]{0:T(128)S(1)} %fusion.64), channel_id=1, replica_groups=mesh['src'=16,'dom'=16] {'dom'}, use_global_device_ids=true, to_apply=%region_11.12 | all-reduce | flops 4 | bytes 32 | tf_op jit(solution)/shard_map/psum | solution.py:78
  205.4 8.6 %copy.11 = f32[4,2,128,128]{0,3,2,1:T(8,128)} copy(f32[4,2,128,128]{3,2,1,0:T(8,128)S(1)} %add_add_fusion) | data formatting | bytes 1048576 | tf_op jit(solution)/shard_map/add | solution.py:136
  214.0 8.6 %gather_fusion = f32[1024,4]{1,0:T(8,128)S(1)} fusion(f32[4,32768]{0,1:T(8,128)} %bitcast.78, s32[1024]{0:T(1024)S(1)} %broadcast_clamp_fusion), kind=kCustom, calls=%fused_computation | custom fusion | bytes 36864 | tf_op jit(solution)/shard_map/jit(_take)/gather | solution.py:147
  223.6 58.3 %psum.104 = f32[4,1024]{0,1:T(8,128)S(1)} all-reduce(f32[4,1024]{0,1:T(8,128)S(1)} %select_bitcast_fusion), channel_id=1, replica_groups=mesh['src'=16,'dom'=16] {'dom'}, use_global_device_ids=true, to_apply=%region_12.13 | all-reduce | flops 4096 | bytes 32768 | tf_op jit(solution)/shard_map/psum | solution.py:148
  282.0 13.4 %scatter_custom_fusion = f32[4,32768]{0,1:T(8,128)} fusion(s32[1024]{0:T(1024)S(1)} %bitcast.82, f32[]{:T(128)} %constant.79.clone.1, f32[4,1024]{0,1:T(8,128)S(1)} %psum.104, f32[1,4,1024]{1,2,0:T(8,128)S(1)} %copy-done.8, pred[1024]{0:T(1024)(128)(4,1)S(1)} %and_reduce_fusion), kind=kCustom, calls=%fused_computation.4 | custom fusion | flops 12288 | bytes 1574912 | tf_op jit(solution)/shard_map/scatter-add | solution.py:150
  295.4 10.1 %copy.13 = f32[4,2,128,128]{3,2,1,0:T(8,128)S(1)} copy(f32[4,2,128,128]{0,3,2,1:T(8,128)} %bitcast.71) | data formatting | bytes 1048576 | tf_op jit(solution)/shard_map/reshape | solution.py:150
  305.8 15.3 %fusion = f32[4]{0:T(128)S(1)} fusion(f32[4,32768]{0,1:T(8,128)} %scatter_custom_fusion, f32[32768]{0:T(1024)S(1)} %bitcast.72), kind=kLoop, calls=%fused_computation.3 | loop fusion | flops 393212 | bytes 655376 | tf_op jit(solution)/shard_map/reduce_sum | solution.py:70
  321.2 1.3 collective-permute-start.8
  322.5 3.0 collective-permute-start.9
  327.5 29.1 %all-reduce.40 = (f32[4]{0:T(128)S(1)}, f32[4]{0:T(128)S(1)}) all-reduce(f32[4]{0:T(128)S(1)} %fusion, f32[4]{0:T(128)S(1)} %get-tuple-element.19), channel_id=1, replica_groups=mesh['src'=16,'dom'=16] {'dom'}, use_global_device_ids=true, to_apply=%region_15.16 | all-reduce | flops 8 | bytes 64 | tf_op jit(solution)/shard_map/psum | solution.py:78
  356.9 27.1 %psum.107 = f32[4]{0:T(128)S(1)} all-reduce(f32[4]{0:T(128)S(1)} %get-tuple-element.17), channel_id=1, replica_groups=mesh['src'=16,'dom'=16] {'dom'}, use_global_device_ids=true, to_apply=%region_19.20 | all-reduce | flops 4 | bytes 32 | tf_op jit(solution)/shard_map/psum | solution.py:78
  384.3 1.3 collective-permute-start.10
  385.6 3.0 collective-permute-start.11
  390.5 32.0 %psum.108 = f32[4]{0:T(128)S(1)} all-reduce(f32[4]{0:T(128)S(1)} %get-tuple-element.15), channel_id=1, replica_groups=mesh['src'=16,'dom'=16] {'dom'}, use_global_device_ids=true, to_apply=%region_21.22 | all-reduce | flops 4 | bytes 32 | tf_op jit(solution)/shard_map/psum | solution.py:78
  422.8 1.1 fusion.80
  423.9 27.6 %psum.109 = f32[4]{0:T(128)} all-reduce(f32[4]{0:T(128)S(1)} %multiply_reduce_fusion), channel_id=1, replica_groups=mesh['src'=16,'dom'=16] {'dom'}, use_global_device_ids=true, to_apply=%region_23.24 | all-reduce | flops 4 | bytes 32 | tf_op jit(solution)/shard_map/psum | solution.py:78
  452.2 1.2 multiply_add_fusion.1
  453.5 1.3 collective-permute-start.12
  454.8 3.0 collective-permute-start.13
  460.6 32.0 %psum.110 = f32[4]{0:T(128)S(1)} all-reduce(f32[4]{0:T(128)S(1)} %fusion.65), channel_id=1, replica_groups=mesh['src'=16,'dom'=16] {'dom'}, use_global_device_ids=true, to_apply=%region_25.26 | all-reduce | flops 4 | bytes 32 | tf_op jit(solution)/shard_map/psum | solution.py:78
  493.7 1.5 multiply_add_fusion.6
  495.2 2.3 fusion.6
  498.3 1.8 copy.15
  500.2 156.0 %all-reduce.44.cloned.1.call-done = f32[3,2,128,128]{3,2,1,0:T(8,128)} async-done(((f32[3,2,128,128]{3,2,1,0:T(8,128)}), f32[3,2,128,128]{3,2,1,0:T(8,128)}) %all-reduce.44.cloned.1.call-update) | async-done | bytes 393232 | tf_op jit(solution)/shard_map/psum | solution.py:166
  656.2 1.8 copy.17
  (142 shorter events, 23.2 us)
Async XLA Ops:
  7.2 649.0 %all-reduce.44.cloned.1.call-start = ((), (), s32[]{:S(2)}) async-start(), calls=%async_computation | async-start | bytes 786432 | tf_op jit(solution)/shard_map/psum | solution.py:166
  9.4 8.9 %collective-permute-start.1 = (f32[5,1,128,128]{3,2,1,0:T(8,128)S(1)}, f32[5,1,128,128]{3,2,1,0:T(8,128)S(1)}, u32[]{:S(2)}, u32[]{:S(2)}) collective-permute-start(f32[5,1,128,128]{3,2,1,0:T(8,128)S(1)} %get-tuple-element.37), channel_id=1, source_target_pairs={{0,1},{1,2},{2,3},{3,4},{4,5},{5,6},{6,7},{7,8},{8,9},{9,10},{10,1... | collective-permute-start | bytes 983048 | tf_op jit(solution)/shard_map/ppermute | solution.py:14
  11.1 7.2 %collective-permute-start = (f32[5,1,128,128]{3,2,1,0:T(8,128)S(1)}, f32[5,1,128,128]{3,2,1,0:T(8,128)S(1)}, u32[]{:S(2)}, u32[]{:S(2)}) collective-permute-start(f32[5,1,128,128]{3,2,1,0:T(8,128)S(1)} %get-tuple-element.38), channel_id=1, source_target_pairs={{1,0},{2,1},{3,2},{4,3},{5,4},{6,5},{7,6},{8,7},{9,8},{10,9},{11,1... | collective-permute-start | bytes 983048 | tf_op jit(solution)/shard_map/ppermute | solution.py:17
  18.3 47.1 %copy-start.4 = (f32[5,1,128,128]{3,2,1,0:T(8,128)}, f32[5,1,128,128]{3,2,1,0:T(8,128)S(1)}, u32[]{:S(2)}) copy-start(f32[5,1,128,128]{3,2,1,0:T(8,128)S(1)} %collective-permute-done.1) | copy-start | bytes 983044
  18.3 2.8 copy-start.6
  19.7 114.1 %copy-start.27 = (s32[1,1024]{1,0:T(1,128)S(1)}, s32[1,1024]{1,0:T(1,128)}, u32[]{:S(2)}) copy-start(s32[1,1024]{1,0:T(1,128)} %param.7) | copy-start | bytes 12292
  23.4 7.7 %collective-permute-start.2 = (f32[4,1,128,128]{3,2,1,0:T(8,128)S(1)}, f32[4,1,128,128]{3,2,1,0:T(8,128)S(1)}, u32[]{:S(2)}, u32[]{:S(2)}) collective-permute-start(f32[4,1,128,128]{3,2,1,0:T(8,128)S(1)} %get-tuple-element.77), channel_id=1, source_target_pairs={{1,0},{2,1},{3,2},{4,3},{5,4},{6,5},{7,6},{8,7},{9,8},{10,9},{11,1... | collective-permute-start | bytes 786440 | tf_op jit(solution)/shard_map/ppermute | solution.py:17
  24.7 179.9 %copy-start = (f32[1,4,2,128,128]{4,3,2,1,0:T(8,128)S(1)}, f32[1,4,2,128,128]{4,3,2,1,0:T(8,128)}, u32[]{:S(2)}) copy-start(f32[1,4,2,128,128]{4,3,2,1,0:T(8,128)} %param.4) | copy-start | bytes 1572868
  24.7 7.5 %collective-permute-start.3 = (f32[4,1,128,128]{3,2,1,0:T(8,128)S(1)}, f32[4,1,128,128]{3,2,1,0:T(8,128)S(1)}, u32[]{:S(2)}, u32[]{:S(2)}) collective-permute-start(f32[4,1,128,128]{3,2,1,0:T(8,128)S(1)} %get-tuple-element.78), channel_id=1, source_target_pairs={{0,1},{1,2},{2,3},{3,4},{4,5},{5,6},{6,7},{7,8},{8,9},{9,10},{10,1... | collective-permute-start | bytes 786440 | tf_op jit(solution)/shard_map/ppermute | solution.py:14
  31.1 1.8 copy-start.15
  32.2 0.7 copy-start.17
  65.4 33.5 %copy-start.30 = (f32[4]{0:T(128)}, f32[4]{0:T(128)S(1)}, u32[]{:S(2)}) copy-start(f32[4]{0:T(128)S(1)} %div.98) | copy-start | bytes 52
  93.1 5.8 copy-start.32
  93.4 4.6 collective-permute-start.4
  94.7 4.2 collective-permute-start.5
  97.9 1.5 copy-start.19
  98.8 0.7 copy-start.21
  99.6 61.9 %copy-start.3 = (f32[4,2,128,128]{3,2,1,0:T(8,128)}, f32[4,2,128,128]{3,2,1,0:T(8,128)S(1)}, u32[]{:S(2)}) copy-start(f32[4,2,128,128]{3,2,1,0:T(8,128)S(1)} %get-tuple-element.22) | copy-start | bytes 1572868
  132.5 0.5 copy-start.28
  163.4 4.6 collective-permute-start.6
  164.7 4.2 collective-permute-start.7
  168.0 0.9 copy-start.23
  168.9 0.7 copy-start.25
  205.4 76.5 %copy-start.8 = (f32[1,4,1024]{1,2,0:T(8,128)S(1)}, f32[1,4,1024]{1,2,0:T(8,128)}, u32[]{:S(2)}) copy-start(f32[1,4,1024]{1,2,0:T(8,128)} %copy.12) | copy-start | bytes 49156
  281.9 13.4 %copy-start.1 = (f32[4,1024]{0,1:T(8,128)}, f32[4,1024]{0,1:T(8,128)S(1)}, u32[]{:S(2)}) copy-start(f32[4,1024]{0,1:T(8,128)S(1)} %psum.104) | copy-start | bytes 49156
  295.3 30.2 %copy-start.5 = (f32[5,1,128,128]{3,2,1,0:T(8,128)S(1)}, f32[5,1,128,128]{3,2,1,0:T(8,128)}, u32[]{:S(2)}) copy-start(f32[5,1,128,128]{3,2,1,0:T(8,128)} %copy-done.4) | copy-start | bytes 983044
  295.3 30.2 %copy-start.7 = (f32[5,1,128,128]{3,2,1,0:T(8,128)S(1)}, f32[5,1,128,128]{3,2,1,0:T(8,128)}, u32[]{:S(2)}) copy-start(f32[5,1,128,128]{3,2,1,0:T(8,128)} %copy-done.6) | copy-start | bytes 983044
  295.3 30.2 %copy-start.16 = (f32[4,1,128,128]{3,2,1,0:T(8,128)S(1)}, f32[4,1,128,128]{3,2,1,0:T(8,128)}, u32[]{:S(2)}) copy-start(f32[4,1,128,128]{3,2,1,0:T(8,128)} %copy-done.15) | copy-start | bytes 786436
  295.3 30.2 %copy-start.18 = (f32[4,1,128,128]{3,2,1,0:T(8,128)S(1)}, f32[4,1,128,128]{3,2,1,0:T(8,128)}, u32[]{:S(2)}) copy-start(f32[4,1,128,128]{3,2,1,0:T(8,128)} %copy-done.17) | copy-start | bytes 786436
  295.4 30.2 %copy-start.20 = (f32[4,1,128,128]{3,2,1,0:T(8,128)S(1)}, f32[4,1,128,128]{3,2,1,0:T(8,128)}, u32[]{:S(2)}) copy-start(f32[4,1,128,128]{3,2,1,0:T(8,128)} %copy-done.19) | copy-start | bytes 786436
  295.4 30.2 %copy-start.29 = (f32[4]{0:T(128)S(1)}, f32[4]{0:T(128)}, u32[]{:S(2)}) copy-start(f32[4]{0:T(128)} %copy-done.28) | copy-start | bytes 52
  295.4 30.2 %copy-start.31 = (f32[4]{0:T(128)S(1)}, f32[4]{0:T(128)}, u32[]{:S(2)}) copy-start(f32[4]{0:T(128)} %copy-done.30) | copy-start | bytes 52
  305.5 20.1 %copy-start.22 = (f32[4,1,128,128]{3,2,1,0:T(8,128)S(1)}, f32[4,1,128,128]{3,2,1,0:T(8,128)}, u32[]{:S(2)}) copy-start(f32[4,1,128,128]{3,2,1,0:T(8,128)} %copy-done.21) | copy-start | bytes 786436
  305.5 20.1 %copy-start.24 = (f32[4,1,128,128]{3,2,1,0:T(8,128)S(1)}, f32[4,1,128,128]{3,2,1,0:T(8,128)}, u32[]{:S(2)}) copy-start(f32[4,1,128,128]{3,2,1,0:T(8,128)} %copy-done.23) | copy-start | bytes 786436
  305.5 20.1 %copy-start.26 = (f32[4,1,128,128]{3,2,1,0:T(8,128)S(1)}, f32[4,1,128,128]{3,2,1,0:T(8,128)}, u32[]{:S(2)}) copy-start(f32[4,1,128,128]{3,2,1,0:T(8,128)} %copy-done.25) | copy-start | bytes 786436
  321.2 5.5 collective-permute-start.8
  322.5 4.3 collective-permute-start.9
  326.7 0.7 copy-start.9
  326.7 0.8 copy-start.10
  384.3 4.6 collective-permute-start.10
  385.6 4.2 collective-permute-start.11
  388.9 1.5 copy-start.11
  389.8 0.7 copy-start.12
  390.5 61.0 %copy-start.2 = (f32[4,2,128,128]{3,2,1,0:T(8,128)}, f32[4,2,128,128]{3,2,1,0:T(8,128)S(1)}, u32[]{:S(2)}) copy-start(f32[4,2,128,128]{3,2,1,0:T(8,128)S(1)} %get-tuple-element.16) | copy-start | bytes 1572868
  453.5 4.6 collective-permute-start.12
  454.8 4.2 collective-permute-start.13
  458.1 1.5 copy-start.13
  459.0 0.7 copy-start.14
Sparse Core Ops, SparseCore 0:
  498.4 157.6 all-reduce.43
where the time goes:
time: 666 us; the launch traced here: 665 us
  blocking collectives  358 us (54%)
  waiting for transfers between devices  161 us (24%)
  other arithmetic  56.5 us (8%)
  local copies, waits for them, and re-layouts  42.5 us (6%)
  starting transfers between devices  32.4 us (5%)
  between operations  14.8 us (2%)
    psum x10, blocking collectives, summed(): return lax.psum(values, 'dom')  300 us
    psum x1, waiting for transfers between devices, per_device(): summed_grad = lax.psum(local_grad, 'src')  156 us
    psum x1, blocking collectives, per_device(): predicted = lax.psum(picked, 'dom')  58.3 us
    ppermute x7, starting transfers between devices, extended_2(): lax.ppermute(lax.slice_in_dim(block, block.shape[dim] - width, None, axis...  23.3 us
    reduce_sum x11, other arithmetic, local_inner(): return jnp.sum(left * right, axis=(1, 2, 3))  20.7 us
    scatter-add x1, other arithmetic, per_device(): jnp.zeros_like(flattened).at[:, local_cell].add(weights)  13.4 us
  transfers between devices with their start and end apart: 15, of which 6 were waited for; matrix products, arithmetic and copies ran while one was open for 1% of the time, Pallas kernels for 0%

commit v1 on v0

v1 whole, which is shorter than its diff:
```python
import functools
import jax
import jax.numpy as jnp
from jax import lax
from jax.experimental import pallas as pl
from jax.experimental.pallas import tpu as pltpu
from jax.sharding import Mesh, PartitionSpec as P

F32 = jnp.float32
BF16 = jnp.bfloat16
LIMIT = 48 * 1024 * 1024
DEEP = 12
KEPT = 4
CHIPS = 8


def pieces_of(values):
    first = values.astype(BF16)
    rest = values - first.astype(F32)
    second = rest.astype(BF16)
    third = (rest - second.astype(F32)).astype(BF16)
    return first, second, third


def fold(plane):
    return jnp.sum(plane.reshape(plane.shape[0] // 8, 8, plane.shape[1]), axis=0)


def ahead(plane, axis):
    return pltpu.roll(plane, plane.shape[axis] - 1, axis)


def behind(plane, axis):
    return pltpu.roll(plane, 1, axis)


def neighbours(field, s, i, kx, ky, kz):
    mid = field[s, i]
    total = kx[i] * field[s, i + 1] + kx[i - 1] * field[s, i - 1]
    total = total + ky[i] * ahead(mid, 0) + behind(ky[i] * mid, 0)
    return total + kz[i] * ahead(mid, 1) + behind(kz[i] * mid, 1)


def krylov(t0, t1, t2, kx, ky, kz, dinv, dg):
    sources = t0.shape[0]

    def apply_planes(source, target, first, last):
        def body(i, carry):
            for s in range(sources):
                target[s, i] = source[s, i] - dinv[i] * neighbours(source, s, i, kx, ky, kz)
            return carry

        lax.fori_loop(first, last + 1, body, 0)

    apply_planes(t0, t1, 2, 9)
    apply_planes(t1, t2, 3, 8)

    def body(i, sums):
        sums = list(sums)
        for s in range(sources):
            a0, a1, a2 = t0[s, i], t1[s, i], t2[s, i]
            a3 = a2 - dinv[i] * neighbours(t2, s, i, kx, ky, kz)
            d = dg[i]
            b1 = a0 - a1
            b2 = b1 - (a1 - a2)
            b3 = b2 - ((a1 - a2) - (a2 - a3))
            d0, d1, d2, e1, e2 = d * a0, d * a1, d * a2, d * b1, d * b2
            terms = [
                d0 * a0, d0 * a1, d1 * a1, d1 * a2, d2 * a2, d2 * a3,
                d0 * b1, e1 * b1, e1 * b2, e2 * b2, e2 * b3,
            ]
            for k, term in enumerate(terms):
                sums[k * sources + s] = sums[k * sources + s] + fold(term)
        return tuple(sums)

    zero = jnp.zeros((8, t0.shape[3]), F32)
    sums = lax.fori_loop(4, 8, body, (zero,) * (11 * sources))
    rows = [jnp.sum(x) * jnp.ones((1, 128), F32) for x in sums]
    rows = rows + [jnp.zeros((1, 128), F32)] * (24 - len(rows))
    return jnp.concatenate(rows, axis=0)


def weights_of(moments):
    t = [moments[2 * k : 2 * k + 2] for k in range(6)]
    m = [t[0]] + [moments[2 * k : 2 * k + 2] for k in range(6, 11)]
    near = t[1] < 0.5 * t[0]
    g = [jnp.where(near, t[k + 1], m[k] - m[k + 1]) for k in range(5)]
    h = [jnp.where(near, t[k], m[k]) for k in range(3)]
    l1 = g[1] / g[0]
    l2 = g[2] / g[0]
    d1 = g[2] - l1 * g[1]
    e2 = g[3] - l2 * g[1]
    l21 = e2 / d1
    d2 = g[4] - l2 * g[2] - l21 * e2
    y1 = h[1] - l1 * h[0]
    y2 = h[2] - l2 * h[0] - l21 * y1
    c2 = y2 / d2
    c1 = y1 / d1 - l21 * c2
    c0 = h[0] / g[0] - l1 * c1 - l2 * c2
    w0 = jnp.where(near, c0, c0 + c1 + c2)
    w1 = jnp.where(near, c1, -(c1 + 2.0 * c2))
    return w0, w1, c2


def one_hot(count, first, picked):
    place = lax.broadcasted_iota(jnp.int32, (count, picked.shape[1]), 0) + first
    return place == picked


def forward_kernel(
    p_own, p_pair, p_low, p_low_pair, p_high, p_high_pair,
    c_own, c_pair, c_low, c_low_pair, c_high, c_high_pair, cells,
    kx, ky, kz, dinv, dg, prim, t0, t1, t2, sent, cond, hot,
):
    block = 2 * lax.axis_index("y") + lax.axis_index("xl")
    core = lax.axis_index("c")
    here = pl.ds(2 * core, 2)
    other = pl.ds(2 - 2 * core, 2)
    for base, first, second in ((0, p_low, p_low_pair), (4, p_own, p_pair), (8, p_high, p_high_pair)):
        prim[:, pl.ds(base + 2 * core, 2)] = first[...]
        prim[:, pl.ds(base + 2 - 2 * core, 2)] = second[...]
    for base, first, second in ((0, c_low, c_low_pair), (4, c_own, c_pair), (8, c_high, c_high_pair)):
        cond[:, pl.ds(base + 2 * core, 2)] = first[...]
        cond[:, pl.ds(base + 2 - 2 * core, 2)] = second[...]
    rows, lanes = prim.shape[2], prim.shape[3]
    shape = (rows, lanes)
    row_at = lax.broadcasted_iota(jnp.int32, shape, 0)
    lane_at = lax.broadcasted_iota(jnp.int32, shape, 1)
    mask_y = jnp.where(row_at < rows - 1, 1.0, 0.0).astype(F32)
    mask_z = jnp.where(lane_at < lanes - 1, 1.0, 0.0).astype(F32)
    edge = jnp.where(row_at == 0, 0.5, 0.0) + jnp.where(row_at == rows - 1, 0.5, 0.0)
    edge = edge + jnp.where(lane_at == 0, 0.5, 0.0) + jnp.where(lane_at == lanes - 1, 0.5, 0.0)
    unit = (6.0 - edge).astype(F32)
    layers = 4 * CHIPS

    kx[0] = 0.5 * (cond[0, 0] + cond[0, 1])

    def coefficients(i, carry):
        layer = 4 * block - 4 + i
        inside = jnp.where(jnp.logical_and(layer >= 0, layer < layers), 1.0, 0.0).astype(F32)
        first = 0.5 * (cond[0, i] + cond[0, i + 1])
        kx[i] = first
        along_y = cond[1, i]
        along_z = cond[2, i]
        up_y = 0.5 * (along_y + ahead(along_y, 0)) * mask_y
        up_z = 0.5 * (along_z + ahead(along_z, 1)) * mask_z
        ky[i] = up_y
        kz[i] = up_z
        low_y = behind(up_y, 0)
        low_z = behind(up_z, 1)
        up_y = jnp.where(row_at == rows - 1, 0.5 * along_y, up_y)
        up_z = jnp.where(lane_at == lanes - 1, 0.5 * along_z, up_z)
        low_y = jnp.where(row_at == 0, 0.5 * along_y, low_y)
        low_z = jnp.where(lane_at == 0, 0.5 * along_z, low_z)
        diagonal = first + kx[i - 1] + up_y + low_y + up_z + low_z
        inverse = jnp.where(inside > 0.5, 1.0 / diagonal, 0.0)
        dg[i] = diagonal
        dinv[i] = inverse
        return carry

    lax.fori_loop(1, 11, coefficients, 0)

    def right_side(i, carry):
        layer = 4 * block - 4 + i
        outer = jnp.where(jnp.logical_or(layer == 0, layer == layers - 1), 0.5, 0.0).astype(F32)
        diagonal = (unit - outer) - dg[i]
        upper, lower = 1.0 - kx[i], 1.0 - kx[i - 1]
        diff_y = mask_y - ky[i]
        diff_z = mask_z - kz[i]
        inverse = dinv[i]
        for s in range(2):
            mid = prim[s, i]
            total = diagonal * mid - upper * prim[s, i + 1] - lower * prim[s, i - 1]
            total = total - diff_y * ahead(mid, 0) - behind(diff_y * mid, 0)
            total = total - diff_z * ahead(mid, 1) - behind(diff_z * mid, 1)
            t0[s, i] = inverse * total
        return carry

    lax.fori_loop(1, 11, right_side, 0)
    moments = krylov(t0, t1, t2, kx, ky, kz, dinv, dg)

    picked = cells[...]
    row_of = picked // lanes
    lane_of = picked - row_of * lanes
    count = picked.shape[1]
    for j in range(4):
        rows_hot = one_hot(rows, (4 * block + j) * rows, row_of)
        rows_hot = jnp.where(rows_hot, 1.0, 0.0).astype(BF16)
        for piece in range(3):
            hot[pl.ds((piece * 4 + j) * rows, rows)] = rows_hot
    lane_hot = one_hot(lanes, 0, lane_of)
    samples = []
    for field in (prim, t0, t1, t2):
        for s in range(2):
            turned = [jnp.transpose(field[s, 4 + j]) for j in range(4)]
            parts = [pieces_of(x) for x in turned]
            left = jnp.concatenate([parts[j][k] for k in range(3) for j in range(4)], axis=1)
            spread = jnp.dot(left, hot[...], preferred_element_type=F32)
            samples.append(jnp.sum(jnp.where(lane_hot, spread, 0.0), axis=0, keepdims=True))
    sample = jnp.concatenate(samples, axis=0)
    for k in range(CHIPS):
        sent[k, :, :count] = sample
        for j in range(3):
            sent[k, :, count + 128 * j : count + 128 * (j + 1)] = moments[8 * j : 8 * j + 8]


def adjoint_kernel(
    got, observed, cells, kx, ky, kz, dinv, dg, prim, f0, f1, f2,
    a0, a1, a2, pot, predicted, sent, heavy,
):
    block = 2 * lax.axis_index("y") + lax.axis_index("xl")
    core = lax.axis_index("c")
    rows, lanes = prim.shape[2], prim.shape[3]
    count = cells.shape[1]
    total = got[0]
    for k in range(1, CHIPS):
        total = total + got[k]
    moments = jnp.concatenate([total[:, count + 128 * j : count + 128 * (j + 1)] for j in range(3)], axis=0)
    weights = weights_of(moments)
    sample = total[:, :count]
    value = sample[0:2]
    for k in range(3):
        value = value + weights[k][:, 0:1] * sample[2 * k + 2 : 2 * k + 4]
    predicted[...] = value
    seen = jnp.where(core == 0, observed[0:2], observed[2:4])
    misfit = value - seen
    for i in range(6):
        for s in range(2):
            w = [weights[k][s : s + 1, :] for k in range(3)]
            pot[s, i] = prim[s, i + 3] + w[0] * f0[s, i + 3] + w[1] * f1[s, i + 3] + w[2] * f2[s, i + 3]

    picked = cells[...]
    row_of = picked // lanes
    lane_of = picked - row_of * lanes
    lane_hot = one_hot(lanes, 0, lane_of)
    for s in range(2):
        spread = jnp.where(lane_hot, misfit[s : s + 1], 0.0)
        for k, piece in enumerate(pieces_of(spread)):
            heavy[pl.ds(s * lanes, lanes), count * k : count * (k + 1)] = piece

    def scatter(i, carry):
        rows_hot = one_hot(rows, (4 * block - 4 + i) * rows, row_of)
        rows_hot = jnp.where(rows_hot, 1.0, 0.0).astype(BF16)
        left = jnp.concatenate([rows_hot] * 3, axis=1)
        source = lax.dot_general(
            left, heavy[...], (((1,), (1,)), ((), ())), preferred_element_type=F32
        )
        inverse = dinv[i]
        for s in range(2):
            a0[s, i] = inverse * source[:, s * lanes : (s + 1) * lanes]
        return carry

    lax.fori_loop(1, 11, scatter, 0)
    moments = krylov(a0, a1, a2, kx, ky, kz, dinv, dg)
    for k in range(CHIPS):
        sent[k] = moments


def gradient_kernel(got, a0, a1, a2, pot, pred, pred_pair, kept, given, predicted, adj):
    core = lax.axis_index("c")
    moments = got[0]
    for k in range(1, CHIPS):
        moments = moments + got[k]
    weights = weights_of(moments)
    rows, lanes = pot.shape[2], pot.shape[3]
    row_at = lax.broadcasted_iota(jnp.int32, (rows, lanes), 0)
    lane_at = lax.broadcasted_iota(jnp.int32, (rows, lanes), 1)
    predicted[pl.ds(core, 1)] = pred[...][None]
    predicted[pl.ds(1 - core, 1)] = pred_pair[...][None]
    for i in range(6):
        for s in range(2):
            w = [weights[k][s : s + 1, :] for k in range(3)]
            adj[s, i] = w[0] * a0[s, i + 3] + w[1] * a1[s, i + 3] + w[2] * a2[s, i + 3]

    def along(mid_p, mid_a, axis, at):
        last = mid_p.shape[axis] - 1
        next_p = jnp.where(at == last, 0.0, ahead(mid_p, axis))
        next_a = jnp.where(at == last, 0.0, ahead(mid_a, axis))
        upper = (mid_p - next_p) * (mid_a - next_a)
        lower = jnp.where(at == 0, mid_p * mid_a, behind(upper, axis))
        return upper + lower

    for target, first in ((given, 1 + 2 * (1 - core)), (kept, 1 + 2 * core)):
        for j in range(2):
            i = first + j
            sums = [0.0, 0.0, 0.0]
            for s in range(2):
                mid_p, mid_a = pot[s, i], adj[s, i]
                upper = (mid_p - pot[s, i + 1]) * (mid_a - adj[s, i + 1])
                lower = (mid_p - pot[s, i - 1]) * (mid_a - adj[s, i - 1])
                sums[0] = sums[0] + upper + lower
                sums[1] = sums[1] + along(mid_p, mid_a, 0, row_at)
                sums[2] = sums[2] + along(mid_p, mid_a, 1, lane_at)
            for k in range(3):
                target[:, 2 * k + j] = (-0.5 * sums[k]).reshape(rows // 8, 8, lanes)


def call(kernel, outs, scratch=()):
    vmem = pl.BlockSpec(memory_space=pltpu.VMEM)

    def run(*args):
        return pl.pallas_call(
            kernel,
            out_shape=tuple(jax.ShapeDtypeStruct(x, F32) for x in outs),
            in_specs=[vmem] * len(args),
            out_specs=tuple([vmem] * len(outs)),
            scratch_shapes=list(scratch),
            compiler_params=pltpu.CompilerParams(vmem_limit_bytes=LIMIT),
        )(*args)

    return run


NAMES = ("xh", "y", "xl", "c")


def routes(sizes, move):
    pairs = []
    nx, ny = sizes
    index = lambda h, y, l, c: ((h * ny + y) * 2 + l) * 2 + c
    for h in range(nx):
        for y in range(ny):
            for l in range(2):
                for c in range(2):
                    target = move(h, y, l, c)
                    if target is not None:
                        pairs.append((index(h, y, l, c), index(*target)))
    return pairs


def per_device(high_count, primary, conductivity, observed, receivers):
    chain = CHIPS // 2
    sizes = (high_count, chain)
    core = lax.axis_index("c")

    def step(by, flip, around):
        def move(h, y, l, c):
            block = 2 * y + l + by
            if block < 0 or block >= CHIPS:
                return None
            c = 1 - c if flip else c
            side = 2 * h + l
            if around:
                wrap = 1 if (l == 1) else -1
                side = (side + wrap) % (2 * high_count)
                return (side // 2, block // 2, side % 2, c)
            return (h, block // 2, block % 2, c)

        return routes(sizes, move)

    def send(x, pairs):
        return lax.ppermute(x, NAMES, pairs)

    fields = primary[0]
    same = lax.dynamic_slice_in_dim(fields, 2 * core, 2, axis=0)
    cross = lax.dynamic_slice_in_dim(fields, 2 - 2 * core, 2, axis=0)
    swap = routes(sizes, lambda h, y, l, c: (h, y, l, 1 - c))
    c_low = send(conductivity, step(1, False, True))
    c_high = send(conductivity, step(-1, False, True))
    p_low = send(same, step(1, False, False))
    p_high = send(same, step(-1, False, False))
    p_low_pair = send(cross, step(1, True, False))
    p_high_pair = send(cross, step(-1, True, False))
    p_pair = send(cross, swap)
    c_pair = send(conductivity, swap)
    c_low_pair = send(c_low, swap)
    c_high_pair = send(c_high, swap)

    rows, lanes = primary.shape[3], primary.shape[4]
    count = receivers.shape[1]
    deep = (DEEP, rows, lanes)
    pairs = (2, DEEP, rows, lanes)
    payload = (CHIPS, 8, count + 384)
    kx, ky, kz, dinv, dg, prim, f0, f1, f2, sent = call(
        forward_kernel,
        [deep] * 5 + [pairs] * 4 + [payload],
        [pltpu.VMEM((3,) + deep, F32), pltpu.VMEM((12 * rows, count), BF16)],
    )(
        same, p_pair, p_low, p_low_pair, p_high, p_high_pair,
        conductivity, c_pair, c_low, c_low_pair, c_high, c_high_pair, receivers,
    )
    got = lax.all_to_all(sent, ("y", "xl"), 0, 0, tiled=True)
    six = (2, 6, rows, lanes)
    a0, a1, a2, pot, pred, sent = call(
        adjoint_kernel,
        [pairs] * 3 + [six, (2, count), (CHIPS, 24, 128)],
        [pltpu.VMEM((2 * lanes, 3 * count), BF16)],
    )(got, observed[0], receivers, kx, ky, kz, dinv, dg, prim, f0, f1, f2)
    pred_pair = send(pred, swap)
    got = lax.all_to_all(sent, ("y", "xl"), 0, 0, tiled=True)
    chunks = (rows // 8, 6, 8, lanes)
    kept, given, predicted = call(
        gradient_kernel, [chunks, chunks, (2, 2, count)], [pltpu.VMEM(six, F32)]
    )(got, a0, a1, a2, pot, pred, pred_pair)
    total = kept + send(given, swap)
    parts = lax.all_to_all(total, ("z", "xh"), 0, 0, tiled=True)
    share = jnp.sum(parts, axis=0, keepdims=True)
    spread = jnp.broadcast_to(share, chunks)
    whole = lax.all_to_all(spread, ("z", "xh"), 0, 0, tiled=True)
    grad = jnp.transpose(whole, (1, 0, 2, 3)).reshape(3, 2, rows, lanes)
    return grad, predicted.reshape(1, 4, count)


def solution(mesh):
    groups = mesh.shape["src"]
    high = 2 if groups > 1 else 1
    devices = mesh.devices.reshape(groups // high, high, CHIPS // 2, 2, 2)
    inner = Mesh(devices, ("z", "xh", "y", "xl", "c"))
    src, dom = ("z", "xh"), ("y", "xl", "c")
    return jax.shard_map(
        functools.partial(per_device, high),
        mesh=inner,
        in_specs=(P(src, None, dom, None, None), P(None, dom, None, None), P(src, None, None), P(src, None)),
        out_specs=(P(None, dom, None, None), P(src, None, None)),
        check_vma=False,
    )
```

time: 666 us -> 155 us (0.23)
  blocking collectives: 358 us -> 42.4 us
  waiting for transfers between devices: 161 us -> 32.7 us
  other arithmetic: 56.5 us -> 0.07 us
  local copies, waits for them, and re-layouts: 42.5 us -> 11.1 us
  Pallas kernels: 0 us -> 30.8 us
  between operations: 14.8 us -> 0.76 us
    psum x11 -> x0, blocking collectives: 358 us -> none  [the longest x10 300 us: summed(): return lax.psum(values, 'dom')]
    psum x1 -> x0, waiting for transfers between devices: 156 us -> none  [per_device(): summed_grad = lax.psum(local_grad, 'src')]
    all_to_all x0 -> x2, blocking collectives: none -> 42.4 us  [the longest x1 24.4 us: per_device(): parts = lax.all_to_all(total, ('z', 'xh'), 0, 0, tiled=True)]
    pallas_call x0 -> x3, Pallas kernels: none -> 30.8 us  [run(): pl.pallas_call(kernel, out_shape=tuple((jax.ShapeDtypeStruct(x, F32) for...]
    reduce_sum x12 -> x1, other arithmetic: 23 us -> 0.03 us  [per_device(): share = jnp.sum(parts, axis=0, keepdims=True)]
    all_to_all x0 -> x2, waiting for transfers between devices: none -> 17.2 us  [the longest x1 12 us: per_device(): whole = lax.all_to_all(spread, ('z', 'xh'), 0, 0, tiled=True)]
    scatter-add x1 -> x0, other arithmetic: 13.4 us -> none  [per_device(): jnp.zeros_like(flattened).at[:, local_cell].add(weights)]
    ppermute x14 -> x12, waiting for transfers between devices: 4.68 us -> 15.5 us  [send(): return lax.ppermute(x, NAMES, pairs)]
  transfers between devices with their start and end apart: 15 -> 14, of which waited for: 6 -> 8; matrix products, arithmetic and copies ran while one was open for 1% -> 1% of each run, Pallas kernels for 0% -> 0%
where the time goes in v1:
time: 155 us; the launch traced here: 153 us
  blocking collectives  42.4 us (27%)
  starting transfers between devices  35.3 us (23%)
  waiting for transfers between devices  32.7 us (21%)
  Pallas kernels  30.8 us (20%)
  local copies, waits for them, and re-layouts  11.1 us (7%)
    pallas_call x3, Pallas kernels, run(): pl.pallas_call(kernel, out_shape=tuple((jax.ShapeDtypeStruct(x, F32) for...  30.8 us
    ppermute x12, starting transfers between devices, send(): return lax.ppermute(x, NAMES, pairs)  25.2 us
    all_to_all x1, blocking collectives, per_device(): parts = lax.all_to_all(total, ('z', 'xh'), 0, 0, tiled=True)  24.4 us
    all_to_all x1, blocking collectives, per_device(): got = lax.all_to_all(sent, ('y', 'xl'), 0, 0, tiled=True)  18 us
    ppermute x12, waiting for transfers between devices, send(): return lax.ppermute(x, NAMES, pairs)  15.5 us
    all_to_all x1, waiting for transfers between devices, per_device(): whole = lax.all_to_all(spread, ('z', 'xh'), 0, 0, tiled=True)  12 us
    unnamed x18, local copies, waits for them, and re-layouts  7.9 us
    all_to_all x1, starting transfers between devices, per_device(): whole = lax.all_to_all(spread, ('z', 'xh'), 0, 0, tiled=True)  6.74 us
  transfers between devices with their start and end apart: 14, of which 8 were waited for; matrix products, arithmetic and copies ran while one was open for 1% of the time, Pallas kernels for 0%

profile of v1, /device:TPU:4, one launch (start us, length us, event | category | flops | bytes accessed | tf_op | source)
XLA Modules:
  0.0 153.1 jit_solution(14402189309203112653)
XLA Ops:
  0.6 2.5 %collective-permute-start.6 = (f32[3,2,128,128]{3,2,1,0:T(8,128)}, f32[3,2,128,128]{3,2,1,0:T(8,128)S(1)}, u32[]{:S(2)}, u32[]{:S(2)}) collective-permute-start(f32[3,2,128,128]{3,2,1,0:T(8,128)} %c_own.1), channel_id=1, source_target_pairs={{0,18},{1,19},{2,20},{3,21},{4,22},{5,23},{6,24},{7,25},{8,26},{9,... | collective-permute-start | bytes 1179656 | tf_op jit(solution)/shard_map/ppermute | solution.py:352
  3.1 1.3 collective-permute-start.8
  4.4 1.1 dynamic-slice_bitcast_fusion
  5.5 1.3 collective-permute-start.4
  6.8 5.9 %collective-permute-start.2 = (f32[2,2,128,128]{3,2,1,0:T(8,128)S(1)}, f32[2,2,128,128]{3,2,1,0:T(8,128)S(1)}, u32[]{:S(2)}, u32[]{:S(2)}) collective-permute-start(f32[2,2,128,128]{3,2,1,0:T(8,128)S(1)} %get-tuple-element.40), channel_id=1, source_target_pairs={{0,3},{1,2},{2,5},{3,4},{4,7},{5,6},{6,9},{7,8},{8,11},{9,10},{10,... | collective-permute-start | bytes 786440 | tf_op jit(solution)/shard_map/ppermute | solution.py:352
  12.7 1.3 collective-permute-start
  14.1 2.1 %collective-permute-done.4.p_high_pair = f32[2,2,128,128]{3,2,1,0:T(8,128)S(1)} collective-permute-done((f32[2,2,128,128]{3,2,1,0:T(8,128)S(1)}, f32[2,2,128,128]{3,2,1,0:T(8,128)S(1)}, u32[]{:S(2)}, u32[]{:S(2)}) %collective-permute-start.4) | collective-permute-done | bytes 262176 | tf_op jit(solution)/shard_map/ppermute | solution.py:352
  16.2 2.6 %collective-permute-start.5 = (f32[3,2,128,128]{3,2,1,0:T(8,128)}, f32[3,2,128,128]{3,2,1,0:T(8,128)S(1)}, u32[]{:S(2)}, u32[]{:S(2)}) collective-permute-start(f32[3,2,128,128]{3,2,1,0:T(8,128)} %c_own.1), channel_id=1, source_target_pairs={{0,1},{1,0},{2,3},{3,2},{4,5},{5,4},{6,7},{7,6},{8,9},{9,8},{10,11... | collective-permute-start | bytes 1179656 | tf_op jit(solution)/shard_map/ppermute | solution.py:352
  18.8 0.0 collective-permute-done.6.c_low
  18.8 0.0 collective-permute-start.7
  18.8 4.3 %collective-permute-done.8.c_high = f32[3,2,128,128]{3,2,1,0:T(8,128)S(1)} collective-permute-done((f32[3,2,128,128]{3,2,1,0:T(8,128)}, f32[3,2,128,128]{3,2,1,0:T(8,128)S(1)}, u32[]{:S(2)}, u32[]{:S(2)}) %collective-permute-start.8) | collective-permute-done | bytes 393248 | tf_op jit(solution)/shard_map/ppermute | solution.py:352
  23.0 0.0 collective-permute-start.9
  23.0 0.0 collective-permute-done.2.p_low_pair
  23.0 1.3 collective-permute-start.3
  24.3 0.0 collective-permute-done.p_pair
  24.3 8.8 %collective-permute-start.1 = (f32[2,2,128,128]{3,2,1,0:T(8,128)S(1)}, f32[2,2,128,128]{3,2,1,0:T(8,128)S(1)}, u32[]{:S(2)}, u32[]{:S(2)}) collective-permute-start(f32[2,2,128,128]{3,2,1,0:T(8,128)S(1)} %get-tuple-element.41.p_own), channel_id=1, source_target_pairs={{0,2},{1,3},{2,4},{3,5},{4,6},{5,7},{6,8},{7,9},{8,10},{9,11},{10,... | collective-permute-start | bytes 786440 | tf_op jit(solution)/shard_map/ppermute | solution.py:352
  33.1 5.2 %collective-permute-done.3.p_high = f32[2,2,128,128]{3,2,1,0:T(8,128)S(1)} collective-permute-done((f32[2,2,128,128]{3,2,1,0:T(8,128)S(1)}, f32[2,2,128,128]{3,2,1,0:T(8,128)S(1)}, u32[]{:S(2)}, u32[]{:S(2)}) %collective-permute-start.3) | collective-permute-done | bytes 262176 | tf_op jit(solution)/shard_map/ppermute | solution.py:352
  38.3 1.0 collective-permute-done.1.p_low
  39.3 0.0 collective-permute-done.5.c_pair
  39.3 0.0 collective-permute-done.7.c_low_pair
  39.4 0.0 collective-permute-done.9.c_high_pair
  39.4 0.0 copy-start.5
  39.4 1.0 copy-done.5
  40.4 0.0 copy-start.6
  40.4 0.7 copy-done.6
  41.0 13.3 %shard_map.59 = (f32[12,128,128]{2,1,0:T(8,128)S(1)}, f32[12,128,128]{2,1,0:T(8,128)S(1)}, f32[12,128,128]{2,1,0:T(8,128)}, f32[12,128,128]{2,1,0:T(8,128)}, f32...) custom-call(f32[2,2,128,128]{3,2,1,0:T(8,128)S(1)} %get-tuple-elemen, ...), custom_call_target="tpu_custom_call" | custom-call | tf_op jit(solution)/shard_map/pallas_call | solution.py:302
  54.4 18.0 %all_to_all.20.got = f32[8,8,1408]{2,1,0:T(8,128)S(1)} all-to-all(f32[8,8,1408]{2,1,0:T(8,128)S(1)} %get-tuple-element.21), channel_id=1, replica_groups=mesh['z'=8,'xh'=2,'y'=4,'xl'=2,'c'=2] {'y','xl'}, dimensions={0} | all-to-all | bytes 720896 | tf_op jit(solution)/shard_map/all_to_all | solution.py:382
  72.4 0.0 copy-done.7
  72.4 0.0 copy-done.8
  72.4 1.1 copy-done.2
  73.5 1.1 copy-done.3
  74.6 1.1 copy-done.4
  75.8 15.0 %shard_map.60 = (f32[2,12,128,128]{3,2,1,0:T(8,128)}, f32[2,12,128,128]{3,2,1,0:T(8,128)}, f32[2,12,128,128]{3,2,1,0:T(8,128)}, f32[2,6,128,128]{3,2,1,0:T(8,128...) custom-call(f32[8,8,1408]{2,1,0:T(8,128)S(1)} %all_to_all.20.got, f32[4,1024]{1,0:T(4,128)S(1)} %bitcast.8, ...), custom_call_target="tpu_custom_call" | custom-call | tf_op jit(solution)/shard_map/pallas_call | solution.py:302
  90.8 3.4 %all-to-all-start.1 = ((f32[8,24,128]{2,1,0:T(8,128)}), f32[8,24,128]{2,1,0:T(8,128)S(1)}, u32[]{:S(2)}, u32[]{:S(2)}) async-start(f32[8,24,128]{2,1,0:T(8,128)} %get-tuple-element.31), calls=%async_computation.1 | async-start | bytes 196608 | tf_op jit(solution)/shard_map/all_to_all | solution.py:390
  94.2 0.1 collective-permute-start.10
  94.3 1.2 collective-permute-done.10.pred_pair
  95.4 5.2 %all-to-all-done.1.got = f32[8,24,128]{2,1,0:T(8,128)S(1)} async-done(((f32[8,24,128]{2,1,0:T(8,128)}), f32[8,24,128]{2,1,0:T(8,128)S(1)}, u32[]{:S(2)}, u32[]{:S(2)}) %all-to-all-start.1) | async-done | bytes 98336 | tf_op jit(solution)/shard_map/all_to_all | solution.py:390
  100.7 1.4 copy-done
  102.1 1.4 copy-done.1
  103.5 2.5 %shard_map.61 = (f32[16,6,8,128]{3,2,1,0:T(8,128)S(1)}, f32[16,6,8,128]{3,2,1,0:T(8,128)S(1)}, f32[2,2,1024]{2,1,0:T(2,128)S(1)}) custom-call(f32[8,24,128]{2,1,0:T(8,128)S(1)} %all-to-all-done.1.got, f32[2,12,128,128]{3,2,1,0:T(8,128)S(1)} %copy-done, f32[2,12,128,128]{3,2,1,0:T(8,128)S(1)} %copy-done.1, f32[2,12,128,128]{3,2,1,0:T(8,128)} %get-tuple-element.34.a2, ...), custom_call_target="tpu_custom_call" | custom-call | tf_op jit(solution)/shard_map/pallas_call | solution.py:302
  105.9 0.1 collective-permute-start.11
  106.0 1.7 %collective-permute-done.11 = f32[16,6,8,128]{3,2,1,0:T(8,128)S(1)} collective-permute-done((f32[16,6,8,128]{3,2,1,0:T(8,128)S(1)}, f32[16,6,8,128]{3,2,1,0:T(8,128)S(1)}, u32[]{:S(2)}, u32[]{:S(2)}) %collective-permute-start.11) | collective-permute-done | bytes 393248 | tf_op jit(solution)/shard_map/ppermute | solution.py:352
  107.8 24.4 %all_to_all.21 = f32[16,6,8,128]{3,2,1,0:T(8,128)S(1)} all-to-all(f32[16,6,8,128]{3,2,1,0:T(8,128)S(1)} %add.12), channel_id=1, replica_groups=mesh['z'=8,'xh'=2,'y'=4,'xl'=2,'c'=2] {'z','xh'}, dimensions={0} | all-to-all | bytes 786432 | tf_op jit(solution)/shard_map/all_to_all | solution.py:396
  132.2 0.8 broadcast_in_dim.2
  133.0 6.7 %all-to-all-start.3 = ((f32[16,6,8,128]{3,2,1,0:T(8,128)}), f32[16,6,8,128]{3,2,1,0:T(8,128)S(1)}, u32[]{:S(2)}, u32[]{:S(2)}) async-start(f32[16,6,8,128]{3,2,1,0:T(8,128)} %broadcast_in_dim.2), calls=%async_computation.3 | async-start | bytes 786432 | tf_op jit(solution)/shard_map/all_to_all | solution.py:399
  139.7 0.6 reshape.14
  140.3 12.0 %all-to-all-done.3 = f32[16,6,8,128]{3,2,1,0:T(8,128)S(1)} async-done(((f32[16,6,8,128]{3,2,1,0:T(8,128)}), f32[16,6,8,128]{3,2,1,0:T(8,128)S(1)}, u32[]{:S(2)}, u32[]{:S(2)}) %all-to-all-start.3) | async-done | bytes 393248 | tf_op jit(solution)/shard_map/all_to_all | solution.py:399
  152.3 0.8 copy.6
  (9 shorter events, 0.1 us)
Async XLA Ops:
  0.6 18.1 %collective-permute-start.6 = (f32[3,2,128,128]{3,2,1,0:T(8,128)}, f32[3,2,128,128]{3,2,1,0:T(8,128)S(1)}, u32[]{:S(2)}, u32[]{:S(2)}) collective-permute-start(f32[3,2,128,128]{3,2,1,0:T(8,128)} %c_own.1), channel_id=1, source_target_pairs={{0,18},{1,19},{2,20},{3,21},{4,22},{5,23},{6,24},{7,25},{8,26},{9,... | collective-permute-start | bytes 1179656 | tf_op jit(solution)/shard_map/ppermute | solution.py:352
  3.1 19.9 %collective-permute-start.8 = (f32[3,2,128,128]{3,2,1,0:T(8,128)}, f32[3,2,128,128]{3,2,1,0:T(8,128)S(1)}, u32[]{:S(2)}, u32[]{:S(2)}) collective-permute-start(f32[3,2,128,128]{3,2,1,0:T(8,128)} %c_own.1), channel_id=1, source_target_pairs={{2,16},{3,17},{4,18},{5,19},{6,20},{7,21},{8,22},{9,23},{10,24},{1... | collective-permute-start | bytes 1179656 | tf_op jit(solution)/shard_map/ppermute | solution.py:352
  5.5 10.7 %collective-permute-start.4 = (f32[2,2,128,128]{3,2,1,0:T(8,128)S(1)}, f32[2,2,128,128]{3,2,1,0:T(8,128)S(1)}, u32[]{:S(2)}, u32[]{:S(2)}) collective-permute-start(f32[2,2,128,128]{3,2,1,0:T(8,128)S(1)} %get-tuple-element.40), channel_id=1, source_target_pairs={{2,1},{3,0},{4,3},{5,2},{6,5},{7,4},{8,7},{9,6},{10,9},{11,8},{12,... | collective-permute-start | bytes 786440 | tf_op jit(solution)/shard_map/ppermute | solution.py:352
  6.8 16.3 %collective-permute-start.2 = (f32[2,2,128,128]{3,2,1,0:T(8,128)S(1)}, f32[2,2,128,128]{3,2,1,0:T(8,128)S(1)}, u32[]{:S(2)}, u32[]{:S(2)}) collective-permute-start(f32[2,2,128,128]{3,2,1,0:T(8,128)S(1)} %get-tuple-element.40), channel_id=1, source_target_pairs={{0,3},{1,2},{2,5},{3,4},{4,7},{5,6},{6,9},{7,8},{8,11},{9,10},{10,... | collective-permute-start | bytes 786440 | tf_op jit(solution)/shard_map/ppermute | solution.py:352
  12.7 11.6 %collective-permute-start = (f32[2,2,128,128]{3,2,1,0:T(8,128)S(1)}, f32[2,2,128,128]{3,2,1,0:T(8,128)S(1)}, u32[]{:S(2)}, u32[]{:S(2)}) collective-permute-start(f32[2,2,128,128]{3,2,1,0:T(8,128)S(1)} %get-tuple-element.40), channel_id=1, source_target_pairs={{0,1},{1,0},{2,3},{3,2},{4,5},{5,4},{6,7},{7,6},{8,9},{9,8},{10,11... | collective-permute-start | bytes 786440 | tf_op jit(solution)/shard_map/ppermute | solution.py:352
  16.2 23.2 %collective-permute-start.5 = (f32[3,2,128,128]{3,2,1,0:T(8,128)}, f32[3,2,128,128]{3,2,1,0:T(8,128)S(1)}, u32[]{:S(2)}, u32[]{:S(2)}) collective-permute-start(f32[3,2,128,128]{3,2,1,0:T(8,128)} %c_own.1), channel_id=1, source_target_pairs={{0,1},{1,0},{2,3},{3,2},{4,5},{5,4},{6,7},{7,6},{8,9},{9,8},{10,11... | collective-permute-start | bytes 1179656 | tf_op jit(solution)/shard_map/ppermute | solution.py:352
  18.8 20.6 %collective-permute-start.7 = (f32[3,2,128,128]{3,2,1,0:T(8,128)S(1)}, f32[3,2,128,128]{3,2,1,0:T(8,128)S(1)}, u32[]{:S(2)}, u32[]{:S(2)}) collective-permute-start(f32[3,2,128,128]{3,2,1,0:T(8,128)S(1)} %collective-permute-done.6.c_low), channel_id=1, source_target_pairs={{0,1},{1,0},{2,3},{3,2},{4,5},{5,4},{6,7},{7,6},{8,9},{9,8},{10,11... | collective-permute-start | bytes 1179656 | tf_op jit(solution)/shard_map/ppermute | solution.py:352
  23.0 16.3 %collective-permute-start.9 = (f32[3,2,128,128]{3,2,1,0:T(8,128)S(1)}, f32[3,2,128,128]{3,2,1,0:T(8,128)S(1)}, u32[]{:S(2)}, u32[]{:S(2)}) collective-permute-start(f32[3,2,128,128]{3,2,1,0:T(8,128)S(1)} %collective-permute-done.8.c_high), channel_id=1, source_target_pairs={{0,1},{1,0},{2,3},{3,2},{4,5},{5,4},{6,7},{7,6},{8,9},{9,8},{10,11... | collective-permute-start | bytes 1179656 | tf_op jit(solution)/shard_map/ppermute | solution.py:352
  23.0 15.3 %collective-permute-start.3 = (f32[2,2,128,128]{3,2,1,0:T(8,128)S(1)}, f32[2,2,128,128]{3,2,1,0:T(8,128)S(1)}, u32[]{:S(2)}, u32[]{:S(2)}) collective-permute-start(f32[2,2,128,128]{3,2,1,0:T(8,128)S(1)} %get-tuple-element.41.p_own), channel_id=1, source_target_pairs={{2,0},{3,1},{4,2},{5,3},{6,4},{7,5},{8,6},{9,7},{10,8},{11,9},{12,... | collective-permute-start | bytes 786440 | tf_op jit(solution)/shard_map/ppermute | solution.py:352
  24.3 15.0 %collective-permute-start.1 = (f32[2,2,128,128]{3,2,1,0:T(8,128)S(1)}, f32[2,2,128,128]{3,2,1,0:T(8,128)S(1)}, u32[]{:S(2)}, u32[]{:S(2)}) collective-permute-start(f32[2,2,128,128]{3,2,1,0:T(8,128)S(1)} %get-tuple-element.41.p_own), channel_id=1, source_target_pairs={{0,2},{1,3},{2,4},{3,5},{4,6},{5,7},{6,8},{7,9},{8,10},{9,11},{10,... | collective-permute-start | bytes 786440 | tf_op jit(solution)/shard_map/ppermute | solution.py:352
  39.4 1.0 copy-start.5
  40.4 0.7 copy-start.6
  41.0 31.3 %copy-start.7 = (s32[1,1024]{1,0:T(1,128)S(1)}, s32[1,1024]{1,0:T(1,128)}, u32[]{:S(2)}) copy-start(s32[1,1024]{1,0:T(1,128)} %cells.3) | copy-start | bytes 12292
  41.0 31.3 %copy-start.8 = (f32[1,4,1024]{2,1,0:T(4,128)S(1)}, f32[1,4,1024]{2,1,0:T(4,128)}, u32[]{:S(2)}) copy-start(f32[1,4,1024]{2,1,0:T(4,128)} %param.6) | copy-start | bytes 49156
  72.4 1.1 copy-start.2
  73.5 1.1 copy-start.3
  74.6 1.1 copy-start.4
  90.8 9.8 %all-to-all-start.1 = ((f32[8,24,128]{2,1,0:T(8,128)}), f32[8,24,128]{2,1,0:T(8,128)S(1)}, u32[]{:S(2)}, u32[]{:S(2)}) async-start(f32[8,24,128]{2,1,0:T(8,128)} %get-tuple-element.31), calls=%async_computation.1 | async-start | bytes 196608 | tf_op jit(solution)/shard_map/all_to_all | solution.py:390
  94.2 1.3 collective-permute-start.10
  100.7 1.4 copy-start
  102.1 1.4 copy-start.1
  105.9 1.8 %collective-permute-start.11 = (f32[16,6,8,128]{3,2,1,0:T(8,128)S(1)}, f32[16,6,8,128]{3,2,1,0:T(8,128)S(1)}, u32[]{:S(2)}, u32[]{:S(2)}) collective-permute-start(f32[16,6,8,128]{3,2,1,0:T(8,128)S(1)} %get-tuple-element.38), channel_id=1, source_target_pairs={{0,1},{1,0},{2,3},{3,2},{4,5},{5,4},{6,7},{7,6},{8,9},{9,8},{10,11... | collective-permute-start | bytes 1179656 | tf_op jit(solution)/shard_map/ppermute | solution.py:352
  133.0 19.3 %all-to-all-start.3 = ((f32[16,6,8,128]{3,2,1,0:T(8,128)}), f32[16,6,8,128]{3,2,1,0:T(8,128)S(1)}, u32[]{:S(2)}, u32[]{:S(2)}) async-start(f32[16,6,8,128]{3,2,1,0:T(8,128)} %broadcast_in_dim.2), calls=%async_computation.3 | async-start | bytes 786432 | tf_op jit(solution)/shard_map/all_to_all | solution.py:399

commit v2 on v1

--- a/solution.py
+++ b/solution.py
@@ -8,7 +8,7 @@
 
 F32 = jnp.float32
 BF16 = jnp.bfloat16
-LIMIT = 48 * 1024 * 1024
+MEBI = 1024 * 1024
 DEEP = 12
 KEPT = 4
 CHIPS = 8
@@ -110,15 +110,14 @@
 def forward_kernel(
     p_own, p_pair, p_low, p_low_pair, p_high, p_high_pair,
     c_own, c_pair, c_low, c_low_pair, c_high, c_high_pair, cells,
-    kx, ky, kz, dinv, dg, prim, t0, t1, t2, sent, cond, hot,
+    kx, ky, kz, dinv, dg, prim, t0, t1, t2, sent, cond, hot, left,
 ):
     block = 2 * lax.axis_index("y") + lax.axis_index("xl")
     core = lax.axis_index("c")
     here = pl.ds(2 * core, 2)
-    other = pl.ds(2 - 2 * core, 2)
     for base, first, second in ((0, p_low, p_low_pair), (4, p_own, p_pair), (8, p_high, p_high_pair)):
-        prim[:, pl.ds(base + 2 * core, 2)] = first[...]
-        prim[:, pl.ds(base + 2 - 2 * core, 2)] = second[...]
+        prim[:, pl.ds(base + 2 * core, 2)] = first[here]
+        prim[:, pl.ds(base + 2 - 2 * core, 2)] = second[here]
     for base, first, second in ((0, c_low, c_low_pair), (4, c_own, c_pair), (8, c_high, c_high_pair)):
         cond[:, pl.ds(base + 2 * core, 2)] = first[...]
         cond[:, pl.ds(base + 2 - 2 * core, 2)] = second[...]
@@ -189,14 +188,18 @@
         for piece in range(3):
             hot[pl.ds((piece * 4 + j) * rows, rows)] = rows_hot
     lane_hot = one_hot(lanes, 0, lane_of)
-    samples = []
-    for field in (prim, t0, t1, t2):
+    for f, field in enumerate((prim, t0, t1, t2)):
         for s in range(2):
-            turned = [jnp.transpose(field[s, 4 + j]) for j in range(4)]
-            parts = [pieces_of(x) for x in turned]
-            left = jnp.concatenate([parts[j][k] for k in range(3) for j in range(4)], axis=1)
-            spread = jnp.dot(left, hot[...], preferred_element_type=F32)
-            samples.append(jnp.sum(jnp.where(lane_hot, spread, 0.0), axis=0, keepdims=True))
+            for j in range(4):
+                parts = pieces_of(jnp.transpose(field[s, 4 + j]))
+                for k in range(3):
+                    start = (k * 4 + j) * rows
+                    left[pl.ds((2 * f + s) * lanes, lanes), start : start + rows] = parts[k]
+    spread = jnp.dot(left[...], hot[...], preferred_element_type=F32)
+    samples = [
+        jnp.sum(jnp.where(lane_hot, spread[k * lanes : (k + 1) * lanes], 0.0), axis=0, keepdims=True)
+        for k in range(8)
+    ]
     sample = jnp.concatenate(samples, axis=0)
     for k in range(CHIPS):
         sent[k, :, :count] = sample
@@ -206,7 +209,7 @@
 
 def adjoint_kernel(
     got, observed, cells, kx, ky, kz, dinv, dg, prim, f0, f1, f2,
-    a0, a1, a2, pot, predicted, sent, heavy,
+    a0, a1, a2, pot, predicted, sent, heavy, hot,
 ):
     block = 2 * lax.axis_index("y") + lax.axis_index("xl")
     core = lax.axis_index("c")
@@ -236,21 +239,19 @@
     for s in range(2):
         spread = jnp.where(lane_hot, misfit[s : s + 1], 0.0)
         for k, piece in enumerate(pieces_of(spread)):
-            heavy[pl.ds(s * lanes, lanes), count * k : count * (k + 1)] = piece
-
-    def scatter(i, carry):
-        rows_hot = one_hot(rows, (4 * block - 4 + i) * rows, row_of)
-        rows_hot = jnp.where(rows_hot, 1.0, 0.0).astype(BF16)
-        left = jnp.concatenate([rows_hot] * 3, axis=1)
-        source = lax.dot_general(
-            left, heavy[...], (((1,), (1,)), ((), ())), preferred_element_type=F32
-        )
-        inverse = dinv[i]
+            heavy[k, pl.ds(s * lanes, lanes)] = piece
+    for i in range(10):
+        rows_hot = one_hot(rows, (4 * block - 3 + i) * rows, row_of)
+        hot[pl.ds(i * rows, rows)] = jnp.where(rows_hot, 1.0, 0.0).astype(BF16)
+    placed = [
+        lax.dot_general(hot[...], heavy[k], (((1,), (1,)), ((), ())), preferred_element_type=F32)
+        for k in range(3)
+    ]
+    source = placed[0] + placed[1] + placed[2]
+    for i in range(10):
+        inverse = dinv[i + 1]
         for s in range(2):
-            a0[s, i] = inverse * source[:, s * lanes : (s + 1) * lanes]
-        return carry
-
-    lax.fori_loop(1, 11, scatter, 0)
+            a0[s, i + 1] = inverse * source[i * rows : (i + 1) * rows, s * lanes : (s + 1) * lanes]
     moments = krylov(a0, a1, a2, kx, ky, kz, dinv, dg)
     for k in range(CHIPS):
         sent[k] = moments
@@ -295,7 +296,7 @@
                 target[:, 2 * k + j] = (-0.5 * sums[k]).reshape(rows // 8, 8, lanes)
 
 
-def call(kernel, outs, scratch=()):
+def call(kernel, limit, outs, scratch=()):
     vmem = pl.BlockSpec(memory_space=pltpu.VMEM)
 
     def run(*args):
@@ -305,7 +306,7 @@
             in_specs=[vmem] * len(args),
             out_specs=tuple([vmem] * len(outs)),
             scratch_shapes=list(scratch),
-            compiler_params=pltpu.CompilerParams(vmem_limit_bytes=LIMIT),
+            compiler_params=pltpu.CompilerParams(vmem_limit_bytes=limit * MEBI),
         )(*args)
 
     return run
@@ -331,14 +332,11 @@
 def per_device(high_count, primary, conductivity, observed, receivers):
     chain = CHIPS // 2
     sizes = (high_count, chain)
-    core = lax.axis_index("c")
-
-    def step(by, flip, around):
+    def step(by, around):
         def move(h, y, l, c):
             block = 2 * y + l + by
             if block < 0 or block >= CHIPS:
                 return None
-            c = 1 - c if flip else c
             side = 2 * h + l
             if around:
                 wrap = 1 if (l == 1) else -1
@@ -352,19 +350,17 @@
         return lax.ppermute(x, NAMES, pairs)
 
     fields = primary[0]
-    same = lax.dynamic_slice_in_dim(fields, 2 * core, 2, axis=0)
-    cross = lax.dynamic_slice_in_dim(fields, 2 - 2 * core, 2, axis=0)
     swap = routes(sizes, lambda h, y, l, c: (h, y, l, 1 - c))
-    c_low = send(conductivity, step(1, False, True))
-    c_high = send(conductivity, step(-1, False, True))
-    p_low = send(same, step(1, False, False))
-    p_high = send(same, step(-1, False, False))
-    p_low_pair = send(cross, step(1, True, False))
-    p_high_pair = send(cross, step(-1, True, False))
-    p_pair = send(cross, swap)
+    p_low = send(fields, step(1, False))
+    p_high = send(fields, step(-1, False))
+    c_low = send(conductivity, step(1, True))
+    c_high = send(conductivity, step(-1, True))
+    p_pair = send(fields, swap)
     c_pair = send(conductivity, swap)
     c_low_pair = send(c_low, swap)
     c_high_pair = send(c_high, swap)
+    p_low_pair = send(p_low, swap)
+    p_high_pair = send(p_high, swap)
 
     rows, lanes = primary.shape[3], primary.shape[4]
     count = receivers.shape[1]
@@ -373,24 +369,26 @@
     payload = (CHIPS, 8, count + 384)
     kx, ky, kz, dinv, dg, prim, f0, f1, f2, sent = call(
         forward_kernel,
+        26,
         [deep] * 5 + [pairs] * 4 + [payload],
-        [pltpu.VMEM((3,) + deep, F32), pltpu.VMEM((12 * rows, count), BF16)],
+        [pltpu.VMEM((3,) + deep, F32), pltpu.VMEM((12 * rows, count), BF16), pltpu.VMEM((8 * lanes, 12 * rows), BF16)],
     )(
-        same, p_pair, p_low, p_low_pair, p_high, p_high_pair,
+        fields, p_pair, p_low, p_low_pair, p_high, p_high_pair,
         conductivity, c_pair, c_low, c_low_pair, c_high, c_high_pair, receivers,
     )
     got = lax.all_to_all(sent, ("y", "xl"), 0, 0, tiled=True)
     six = (2, 6, rows, lanes)
     a0, a1, a2, pot, pred, sent = call(
         adjoint_kernel,
+        18,
         [pairs] * 3 + [six, (2, count), (CHIPS, 24, 128)],
-        [pltpu.VMEM((2 * lanes, 3 * count), BF16)],
+        [pltpu.VMEM((3, 2 * lanes, count), BF16), pltpu.VMEM((10 * rows, count), BF16)],
     )(got, observed[0], receivers, kx, ky, kz, dinv, dg, prim, f0, f1, f2)
     pred_pair = send(pred, swap)
     got = lax.all_to_all(sent, ("y", "xl"), 0, 0, tiled=True)
     chunks = (rows // 8, 6, 8, lanes)
     kept, given, predicted = call(
-        gradient_kernel, [chunks, chunks, (2, 2, count)], [pltpu.VMEM(six, F32)]
+        gradient_kernel, 8, [chunks, chunks, (2, 2, count)], [pltpu.VMEM(six, F32)]
     )(got, a0, a1, a2, pot, pred, pred_pair)
     total = kept + send(given, swap)
     parts = lax.all_to_all(total, ("z", "xh"), 0, 0, tiled=True)

time: 155 us -> 132 us (0.85)
  starting transfers between devices: 35.3 us -> 21.9 us
  Pallas kernels: 30.8 us -> 18.1 us
  waiting for transfers between devices: 32.7 us -> 39.1 us
  blocking collectives: 42.4 us -> 40.1 us
  local copies, waits for them, and re-layouts: 11.1 us -> 9.48 us
    ppermute x12, starting transfers between devices: 25.2 us -> 11.8 us  [send(): return lax.ppermute(x, NAMES, pairs)]
    pallas_call x3, Pallas kernels: 30.8 us -> 18.1 us  [run(): pl.pallas_call(kernel, out_shape=tuple((jax.ShapeDtypeStruct(x, F32) for...]
    ppermute x12, waiting for transfers between devices: 15.5 us -> 21.9 us  [send(): return lax.ppermute(x, NAMES, pairs)]
    all_to_all x1, blocking collectives: 18 us -> 15.7 us  [per_device(): got = lax.all_to_all(sent, ('y', 'xl'), 0, 0, tiled=True)]
    unnamed x18 -> x16, local copies, waits for them, and re-layouts: 7.9 us -> 7.31 us
  transfers between devices with their start and end apart: 14 -> 14, of which waited for: 8 -> 7; matrix products, arithmetic and copies ran while one was open for 1% -> 0% of each run, Pallas kernels for 0% -> 0%
where the time goes in v2:
time: 132 us; the launch traced here: 130 us
  blocking collectives  40.1 us (30%)
  waiting for transfers between devices  39.1 us (30%)
  starting transfers between devices  21.9 us (17%)
  Pallas kernels  18.1 us (14%)
  local copies, waits for them, and re-layouts  9.48 us (7%)
    all_to_all x1, blocking collectives, per_device(): parts = lax.all_to_all(total, ('z', 'xh'), 0, 0, tiled=True)  24.4 us
    ppermute x12, waiting for transfers between devices, send(): return lax.ppermute(x, NAMES, pairs)  21.9 us
    pallas_call x3, Pallas kernels, run(): pl.pallas_call(kernel, out_shape=tuple((jax.ShapeDtypeStruct(x, F32) for...  18.1 us
    all_to_all x1, blocking collectives, per_device(): got = lax.all_to_all(sent, ('y', 'xl'), 0, 0, tiled=True)  15.7 us
    all_to_all x1, waiting for transfers between devices, per_device(): whole = lax.all_to_all(spread, ('z', 'xh'), 0, 0, tiled=True)  12 us
    ppermute x12, starting transfers between devices, send(): return lax.ppermute(x, NAMES, pairs)  11.8 us
    unnamed x16, local copies, waits for them, and re-layouts  7.31 us
    all_to_all x1, starting transfers between devices, per_device(): whole = lax.all_to_all(spread, ('z', 'xh'), 0, 0, tiled=True)  6.74 us
  transfers between devices with their start and end apart: 14, of which 7 were waited for; matrix products, arithmetic and copies ran while one was open for 0% of the time, Pallas kernels for 0%

profile of v2, /device:TPU:4, one launch (start us, length us, event | category | flops | bytes accessed | tf_op | source)
XLA Modules:
  0.0 129.5 jit_solution(9209678654343136271)
XLA Ops:
  0.6 1.3 collective-permute-start.3
  1.9 4.6 %collective-permute-start.1 = (f32[4,2,128,128]{3,2,1,0:T(8,128)}, f32[4,2,128,128]{3,2,1,0:T(8,128)S(1)}, u32[]{:S(2)}, u32[]{:S(2)}) collective-permute-start(f32[4,2,128,128]{3,2,1,0:T(8,128)} %bitcast.6), channel_id=1, source_target_pairs={{0,2},{1,3},{2,4},{3,5},{4,6},{5,7},{6,8},{7,9},{8,10},{9,11},{10,... | collective-permute-start | bytes 1572872 | tf_op jit(solution)/shard_map/ppermute | solution.py:350
  6.5 3.3 %collective-permute-start.6 = (f32[3,2,128,128]{3,2,1,0:T(8,128)}, f32[3,2,128,128]{3,2,1,0:T(8,128)S(1)}, u32[]{:S(2)}, u32[]{:S(2)}) collective-permute-start(f32[3,2,128,128]{3,2,1,0:T(8,128)} %c_own.1), channel_id=1, source_target_pairs={{0,18},{1,19},{2,20},{3,21},{4,22},{5,23},{6,24},{7,25},{8,26},{9,... | collective-permute-start | bytes 1179656 | tf_op jit(solution)/shard_map/ppermute | solution.py:350
  9.9 0.1 collective-permute-start.5
  10.0 1.3 collective-permute-start.8
  11.3 6.7 %collective-permute-done.6.c_low = f32[3,2,128,128]{3,2,1,0:T(8,128)S(1)} collective-permute-done((f32[3,2,128,128]{3,2,1,0:T(8,128)}, f32[3,2,128,128]{3,2,1,0:T(8,128)S(1)}, u32[]{:S(2)}, u32[]{:S(2)}) %collective-permute-start.6) | collective-permute-done | bytes 393248 | tf_op jit(solution)/shard_map/ppermute | solution.py:350
  17.9 0.0 collective-permute-start
  17.9 0.0 collective-permute-done.3.p_high
  18.0 0.5 collective-permute-start.4
  18.5 0.0 collective-permute-done.1.p_low
  18.5 0.1 collective-permute-start.2
  18.6 0.0 collective-permute-done.5.c_pair
  18.6 0.4 collective-permute-start.7
  19.0 10.7 %collective-permute-done.8.c_high = f32[3,2,128,128]{3,2,1,0:T(8,128)S(1)} collective-permute-done((f32[3,2,128,128]{3,2,1,0:T(8,128)}, f32[3,2,128,128]{3,2,1,0:T(8,128)S(1)}, u32[]{:S(2)}, u32[]{:S(2)}) %collective-permute-start.8) | collective-permute-done | bytes 393248 | tf_op jit(solution)/shard_map/ppermute | solution.py:350
  29.6 0.0 collective-permute-start.9
  29.6 0.0 collective-permute-done.p_pair
  29.6 0.0 collective-permute-done.7.c_low_pair
  29.6 1.7 %collective-permute-done.9.c_high_pair = f32[3,2,128,128]{3,2,1,0:T(8,128)S(1)} collective-permute-done((f32[3,2,128,128]{3,2,1,0:T(8,128)S(1)}, f32[3,2,128,128]{3,2,1,0:T(8,128)S(1)}, u32[]{:S(2)}, u32[]{:S(2)}) %collective-permute-start.9) | collective-permute-done | bytes 393248 | tf_op jit(solution)/shard_map/ppermute | solution.py:350
  31.4 0.0 collective-permute-done.4.p_high_pair
  31.4 0.0 collective-permute-done.2.p_low_pair
  31.4 0.0 copy-start.4
  31.4 1.0 copy-done.4
  32.4 0.0 copy-start.5
  32.4 1.0 copy-done.5
  33.4 0.0 copy-start.6
  33.4 0.7 copy-done.6
  34.1 10.3 %shard_map.59 = (f32[12,128,128]{2,1,0:T(8,128)S(1)}, f32[12,128,128]{2,1,0:T(8,128)S(1)}, f32[12,128,128]{2,1,0:T(8,128)S(1)}, f32[12,128,128]{2,1,0:T(8,128)S(...) custom-call(f32[4,2,128,128]{3,2,1,0:T(8,128)S(1)} %bitcast.8, ...), custom_call_target="tpu_custom_call" | custom-call | tf_op jit(solution)/shard_map/pallas_call | solution.py:303
  44.5 15.7 %all_to_all.20.got = f32[8,8,1408]{2,1,0:T(8,128)S(1)} all-to-all(f32[8,8,1408]{2,1,0:T(8,128)S(1)} %get-tuple-element.21), channel_id=1, replica_groups=mesh['z'=8,'xh'=2,'y'=4,'xl'=2,'c'=2] {'y','xl'}, dimensions={0} | all-to-all | bytes 720896 | tf_op jit(solution)/shard_map/all_to_all | solution.py:379
  60.2 0.0 copy-done.7
  60.2 6.7 %shard_map.60 = (f32[2,12,128,128]{3,2,1,0:T(8,128)S(1)}, f32[2,12,128,128]{3,2,1,0:T(8,128)S(1)}, f32[2,12,128,128]{3,2,1,0:T(8,128)S(1)}, f32[2,6,128,128]{3,2...) custom-call(f32[8,8,1408]{2,1,0:T(8,128)S(1)} %all_to_all.20.got, f32[4,1024]{1,0:T(4,128)S(1)} %bitcast.9, ...), custom_call_target="tpu_custom_call" | custom-call | tf_op jit(solution)/shard_map/pallas_call | solution.py:303
  66.8 1.2 copy-done
  68.0 0.9 copy-done.2
  68.9 3.4 %all-to-all-start.1 = ((f32[8,24,128]{2,1,0:T(8,128)}), f32[8,24,128]{2,1,0:T(8,128)S(1)}, u32[]{:S(2)}, u32[]{:S(2)}) async-start(f32[8,24,128]{2,1,0:T(8,128)} %get-tuple-element.31), calls=%async_computation.1 | async-start | bytes 196608 | tf_op jit(solution)/shard_map/all_to_all | solution.py:388
  72.3 0.1 collective-permute-start.10
  72.4 1.2 collective-permute-done.10.pred_pair
  73.5 5.2 %all-to-all-done.1.got = f32[8,24,128]{2,1,0:T(8,128)S(1)} async-done(((f32[8,24,128]{2,1,0:T(8,128)}), f32[8,24,128]{2,1,0:T(8,128)S(1)}, u32[]{:S(2)}, u32[]{:S(2)}) %all-to-all-start.1) | async-done | bytes 98336 | tf_op jit(solution)/shard_map/all_to_all | solution.py:388
  78.7 1.4 %copy-done.1 = f32[2,12,128,128]{3,2,1,0:T(8,128)S(1)} copy-done((f32[2,12,128,128]{3,2,1,0:T(8,128)S(1)}, f32[2,12,128,128]{3,2,1,0:T(8,128)}, u32[]{:S(2)}) %copy-start.1) | copy-done | bytes 1572888
  80.1 1.1 copy-done.3
  81.3 1.1 shard_map.61
  82.4 0.1 collective-permute-start.11
  82.5 1.7 %collective-permute-done.11 = f32[16,6,8,128]{3,2,1,0:T(8,128)S(1)} collective-permute-done((f32[16,6,8,128]{3,2,1,0:T(8,128)S(1)}, f32[16,6,8,128]{3,2,1,0:T(8,128)S(1)}, u32[]{:S(2)}, u32[]{:S(2)}) %collective-permute-start.11) | collective-permute-done | bytes 393248 | tf_op jit(solution)/shard_map/ppermute | solution.py:350
  84.2 0.1 add.3
  84.2 24.4 %all_to_all.21 = f32[16,6,8,128]{3,2,1,0:T(8,128)S(1)} all-to-all(f32[16,6,8,128]{3,2,1,0:T(8,128)S(1)} %add.3), channel_id=1, replica_groups=mesh['z'=8,'xh'=2,'y'=4,'xl'=2,'c'=2] {'z','xh'}, dimensions={0} | all-to-all | bytes 786432 | tf_op jit(solution)/shard_map/all_to_all | solution.py:394
  108.6 0.8 broadcast_in_dim.2
  109.4 6.7 %all-to-all-start.3 = ((f32[16,6,8,128]{3,2,1,0:T(8,128)}), f32[16,6,8,128]{3,2,1,0:T(8,128)S(1)}, u32[]{:S(2)}, u32[]{:S(2)}) async-start(f32[16,6,8,128]{3,2,1,0:T(8,128)} %broadcast_in_dim.2), calls=%async_computation.3 | async-start | bytes 786432 | tf_op jit(solution)/shard_map/all_to_all | solution.py:397
  116.1 0.6 reshape.12
  116.8 12.0 %all-to-all-done.3 = f32[16,6,8,128]{3,2,1,0:T(8,128)S(1)} async-done(((f32[16,6,8,128]{3,2,1,0:T(8,128)}), f32[16,6,8,128]{3,2,1,0:T(8,128)S(1)}, u32[]{:S(2)}, u32[]{:S(2)}) %all-to-all-start.3) | async-done | bytes 393248 | tf_op jit(solution)/shard_map/all_to_all | solution.py:397
  128.8 0.8 copy.6
  (6 shorter events, 0.0 us)
Async XLA Ops:
  0.6 17.3 %collective-permute-start.3 = (f32[4,2,128,128]{3,2,1,0:T(8,128)}, f32[4,2,128,128]{3,2,1,0:T(8,128)S(1)}, u32[]{:S(2)}, u32[]{:S(2)}) collective-permute-start(f32[4,2,128,128]{3,2,1,0:T(8,128)} %bitcast.5), channel_id=1, source_target_pairs={{2,0},{3,1},{4,2},{5,3},{6,4},{7,5},{8,6},{9,7},{10,8},{11,9},{12,... | collective-permute-start | bytes 1572872 | tf_op jit(solution)/shard_map/ppermute | solution.py:350
  1.9 16.5 %collective-permute-start.1 = (f32[4,2,128,128]{3,2,1,0:T(8,128)}, f32[4,2,128,128]{3,2,1,0:T(8,128)S(1)}, u32[]{:S(2)}, u32[]{:S(2)}) collective-permute-start(f32[4,2,128,128]{3,2,1,0:T(8,128)} %bitcast.6), channel_id=1, source_target_pairs={{0,2},{1,3},{2,4},{3,5},{4,6},{5,7},{6,8},{7,9},{8,10},{9,11},{10,... | collective-permute-start | bytes 1572872 | tf_op jit(solution)/shard_map/ppermute | solution.py:350
  6.5 11.4 %collective-permute-start.6 = (f32[3,2,128,128]{3,2,1,0:T(8,128)}, f32[3,2,128,128]{3,2,1,0:T(8,128)S(1)}, u32[]{:S(2)}, u32[]{:S(2)}) collective-permute-start(f32[3,2,128,128]{3,2,1,0:T(8,128)} %c_own.1), channel_id=1, source_target_pairs={{0,18},{1,19},{2,20},{3,21},{4,22},{5,23},{6,24},{7,25},{8,26},{9,... | collective-permute-start | bytes 1179656 | tf_op jit(solution)/shard_map/ppermute | solution.py:350
  9.9 8.7 %collective-permute-start.5 = (f32[3,2,128,128]{3,2,1,0:T(8,128)}, f32[3,2,128,128]{3,2,1,0:T(8,128)S(1)}, u32[]{:S(2)}, u32[]{:S(2)}) collective-permute-start(f32[3,2,128,128]{3,2,1,0:T(8,128)} %c_own.1), channel_id=1, source_target_pairs={{0,1},{1,0},{2,3},{3,2},{4,5},{5,4},{6,7},{7,6},{8,9},{9,8},{10,11... | collective-permute-start | bytes 1179656 | tf_op jit(solution)/shard_map/ppermute | solution.py:350
  10.0 19.7 %collective-permute-start.8 = (f32[3,2,128,128]{3,2,1,0:T(8,128)}, f32[3,2,128,128]{3,2,1,0:T(8,128)S(1)}, u32[]{:S(2)}, u32[]{:S(2)}) collective-permute-start(f32[3,2,128,128]{3,2,1,0:T(8,128)} %c_own.1), channel_id=1, source_target_pairs={{2,16},{3,17},{4,18},{5,19},{6,20},{7,21},{8,22},{9,23},{10,24},{1... | collective-permute-start | bytes 1179656 | tf_op jit(solution)/shard_map/ppermute | solution.py:350
  17.9 11.7 %collective-permute-start = (f32[4,2,128,128]{3,2,1,0:T(8,128)}, f32[4,2,128,128]{3,2,1,0:T(8,128)S(1)}, u32[]{:S(2)}, u32[]{:S(2)}) collective-permute-start(f32[4,2,128,128]{3,2,1,0:T(8,128)} %bitcast.7), channel_id=1, source_target_pairs={{0,1},{1,0},{2,3},{3,2},{4,5},{5,4},{6,7},{7,6},{8,9},{9,8},{10,11... | collective-permute-start | bytes 1572872 | tf_op jit(solution)/shard_map/ppermute | solution.py:350
  18.0 13.4 %collective-permute-start.4 = (f32[4,2,128,128]{3,2,1,0:T(8,128)S(1)}, f32[4,2,128,128]{3,2,1,0:T(8,128)S(1)}, u32[]{:S(2)}, u32[]{:S(2)}) collective-permute-start(f32[4,2,128,128]{3,2,1,0:T(8,128)S(1)} %collective-permute-done.3.p_high), channel_id=1, source_target_pairs={{0,1},{1,0},{2,3},{3,2},{4,5},{5,4},{6,7},{7,6},{8,9},{9,8},{10,11... | collective-permute-start | bytes 1572872 | tf_op jit(solution)/shard_map/ppermute | solution.py:350
  18.5 12.9 %collective-permute-start.2 = (f32[4,2,128,128]{3,2,1,0:T(8,128)S(1)}, f32[4,2,128,128]{3,2,1,0:T(8,128)S(1)}, u32[]{:S(2)}, u32[]{:S(2)}) collective-permute-start(f32[4,2,128,128]{3,2,1,0:T(8,128)S(1)} %collective-permute-done.1.p_low), channel_id=1, source_target_pairs={{0,1},{1,0},{2,3},{3,2},{4,5},{5,4},{6,7},{7,6},{8,9},{9,8},{10,11... | collective-permute-start | bytes 1572872 | tf_op jit(solution)/shard_map/ppermute | solution.py:350
  18.6 11.1 %collective-permute-start.7 = (f32[3,2,128,128]{3,2,1,0:T(8,128)S(1)}, f32[3,2,128,128]{3,2,1,0:T(8,128)S(1)}, u32[]{:S(2)}, u32[]{:S(2)}) collective-permute-start(f32[3,2,128,128]{3,2,1,0:T(8,128)S(1)} %collective-permute-done.6.c_low), channel_id=1, source_target_pairs={{0,1},{1,0},{2,3},{3,2},{4,5},{5,4},{6,7},{7,6},{8,9},{9,8},{10,11... | collective-permute-start | bytes 1179656 | tf_op jit(solution)/shard_map/ppermute | solution.py:350
  29.6 1.7 %collective-permute-start.9 = (f32[3,2,128,128]{3,2,1,0:T(8,128)S(1)}, f32[3,2,128,128]{3,2,1,0:T(8,128)S(1)}, u32[]{:S(2)}, u32[]{:S(2)}) collective-permute-start(f32[3,2,128,128]{3,2,1,0:T(8,128)S(1)} %collective-permute-done.8.c_high), channel_id=1, source_target_pairs={{0,1},{1,0},{2,3},{3,2},{4,5},{5,4},{6,7},{7,6},{8,9},{9,8},{10,11... | collective-permute-start | bytes 1179656 | tf_op jit(solution)/shard_map/ppermute | solution.py:350
  31.4 1.0 copy-start.4
  32.4 1.0 copy-start.5
  33.4 0.7 copy-start.6
  34.1 26.1 %copy-start.7 = (f32[1,4,1024]{2,1,0:T(4,128)S(1)}, f32[1,4,1024]{2,1,0:T(4,128)}, u32[]{:S(2)}) copy-start(f32[1,4,1024]{2,1,0:T(4,128)} %param.6) | copy-start | bytes 49156
  66.8 1.2 copy-start
  68.0 0.9 copy-start.2
  68.9 9.8 %all-to-all-start.1 = ((f32[8,24,128]{2,1,0:T(8,128)}), f32[8,24,128]{2,1,0:T(8,128)S(1)}, u32[]{:S(2)}, u32[]{:S(2)}) async-start(f32[8,24,128]{2,1,0:T(8,128)} %get-tuple-element.31), calls=%async_computation.1 | async-start | bytes 196608 | tf_op jit(solution)/shard_map/all_to_all | solution.py:388
  72.3 1.3 collective-permute-start.10
  78.7 1.4 %copy-start.1 = (f32[2,12,128,128]{3,2,1,0:T(8,128)S(1)}, f32[2,12,128,128]{3,2,1,0:T(8,128)}, u32[]{:S(2)}) copy-start(f32[2,12,128,128]{3,2,1,0:T(8,128)} %copy-done) | copy-start | bytes 4718596
  80.1 1.1 copy-start.3
  82.4 1.8 %collective-permute-start.11 = (f32[16,6,8,128]{3,2,1,0:T(8,128)S(1)}, f32[16,6,8,128]{3,2,1,0:T(8,128)S(1)}, u32[]{:S(2)}, u32[]{:S(2)}) collective-permute-start(f32[16,6,8,128]{3,2,1,0:T(8,128)S(1)} %get-tuple-element.38), channel_id=1, source_target_pairs={{0,1},{1,0},{2,3},{3,2},{4,5},{5,4},{6,7},{7,6},{8,9},{9,8},{10,11... | collective-permute-start | bytes 1179656 | tf_op jit(solution)/shard_map/ppermute | solution.py:350
  109.4 19.3 %all-to-all-start.3 = ((f32[16,6,8,128]{3,2,1,0:T(8,128)}), f32[16,6,8,128]{3,2,1,0:T(8,128)S(1)}, u32[]{:S(2)}, u32[]{:S(2)}) async-start(f32[16,6,8,128]{3,2,1,0:T(8,128)} %broadcast_in_dim.2), calls=%async_computation.3 | async-start | bytes 786432 | tf_op jit(solution)/shard_map/all_to_all | solution.py:397

commit v3 on v2

--- a/solution.py
+++ b/solution.py
@@ -75,14 +75,18 @@
 
     zero = jnp.zeros((8, t0.shape[3]), F32)
     sums = lax.fori_loop(4, 8, body, (zero,) * (11 * sources))
-    rows = [jnp.sum(x) * jnp.ones((1, 128), F32) for x in sums]
-    rows = rows + [jnp.zeros((1, 128), F32)] * (24 - len(rows))
-    return jnp.concatenate(rows, axis=0)
+    row_at = lax.broadcasted_iota(jnp.int32, (8, 128), 0)
+    lane_at = lax.broadcasted_iota(jnp.int32, (8, 128), 1)
+    packed = jnp.zeros((8, 128), F32)
+    for n, x in enumerate(sums):
+        here = jnp.logical_and(row_at == n % sources, lane_at == n // sources)
+        packed = jnp.where(here, jnp.sum(x), packed)
+    return packed
 
 
 def weights_of(moments):
-    t = [moments[2 * k : 2 * k + 2] for k in range(6)]
-    m = [t[0]] + [moments[2 * k : 2 * k + 2] for k in range(6, 11)]
+    t = [moments[0:2, k : k + 1] for k in range(6)]
+    m = [t[0]] + [moments[0:2, k : k + 1] for k in range(6, 11)]
     near = t[1] < 0.5 * t[0]
     g = [jnp.where(near, t[k + 1], m[k] - m[k + 1]) for k in range(5)]
     h = [jnp.where(near, t[k], m[k]) for k in range(3)]
@@ -107,51 +111,113 @@
     return place == picked
 
 
+def edges(rows, lanes):
+    row_at = lax.broadcasted_iota(jnp.int32, (rows, lanes), 0)
+    lane_at = lax.broadcasted_iota(jnp.int32, (rows, lanes), 1)
+    mask_y = jnp.where(row_at < rows - 1, 1.0, 0.0).astype(F32)
+    mask_z = jnp.where(lane_at < lanes - 1, 1.0, 0.0).astype(F32)
+    return row_at, lane_at, mask_y, mask_z
+
+
+def in_plane(along_y, along_z):
+    rows, lanes = along_y.shape
+    row_at, lane_at, mask_y, mask_z = edges(rows, lanes)
+    up_y = 0.5 * (along_y + ahead(along_y, 0)) * mask_y
+    up_z = 0.5 * (along_z + ahead(along_z, 1)) * mask_z
+    low_y = jnp.where(row_at == 0, 0.5 * along_y, behind(up_y, 0))
+    low_z = jnp.where(lane_at == 0, 0.5 * along_z, behind(up_z, 1))
+    top_y = jnp.where(row_at == rows - 1, 0.5 * along_y, up_y)
+    top_z = jnp.where(lane_at == lanes - 1, 0.5 * along_z, up_z)
+    return up_y, up_z, top_y + low_y + top_z + low_z
+
+
+def own_kernel(p_own, p_pair, c_own, c_pair, cells, prim, first, ky, kz, plane_dg, hot, hot_own, sample, left):
+    block = 2 * lax.axis_index("y") + lax.axis_index("xl")
+    core = lax.axis_index("c")
+    here = pl.ds(2 * core, 2)
+    other = pl.ds(2 - 2 * core, 2)
+    prim[:, here] = p_own[here]
+    prim[:, other] = p_pair[here]
+    first[here] = c_own[0]
+    first[other] = c_pair[0]
+    rows, lanes = prim.shape[2], prim.shape[3]
+    for source, base in ((c_own, 2 * core), (c_pair, 2 - 2 * core)):
+        for j in range(2):
+            up_y, up_z, part = in_plane(source[1, j], source[2, j])
+            ky[base + j] = up_y
+            kz[base + j] = up_z
+            plane_dg[base + j] = part
+    picked = cells[...]
+    row_of = picked // lanes
+    lane_of = picked - row_of * lanes
+    for i in range(10):
+        rows_hot = one_hot(rows, (4 * block - 3 + i) * rows, row_of)
+        rows_hot = jnp.where(rows_hot, 1.0, 0.0).astype(BF16)
+        hot[pl.ds(i * rows, rows)] = rows_hot
+        if 3 <= i < 7:
+            for piece in range(3):
+                hot_own[pl.ds((piece * KEPT + i - 3) * rows, rows)] = rows_hot
+    gather([(prim, 0)], left, hot_own, one_hot(lanes, 0, lane_of), sample)
+
+
+def gather(fields, left, hot_own, lane_hot, sample):
+    lanes = lane_hot.shape[0]
+    for f, (field, first) in enumerate(fields):
+        rows = field.shape[2]
+        for s in range(2):
+            for j in range(KEPT):
+                parts = pieces_of(jnp.transpose(field[s, first + j]))
+                for k in range(3):
+                    start = (k * KEPT + j) * rows
+                    left[pl.ds((2 * f + s) * lanes, lanes), start : start + rows] = parts[k]
+    spread = jnp.dot(left[...], hot_own[...], preferred_element_type=F32)
+    found = [
+        jnp.sum(jnp.where(lane_hot, spread[k * lanes : (k + 1) * lanes], 0.0), axis=0, keepdims=True)
+        for k in range(2 * len(fields))
+    ]
+    sample[...] = jnp.concatenate(found, axis=0)
+
+
 def forward_kernel(
-    p_own, p_pair, p_low, p_low_pair, p_high, p_high_pair,
-    c_own, c_pair, c_low, c_low_pair, c_high, c_high_pair, cells,
-    kx, ky, kz, dinv, dg, prim, t0, t1, t2, sent, cond, hot, left,
+    p_mid, p_low, p_low_pair, p_high, p_high_pair,
+    c_mid, c_low, c_low_pair, c_high, c_high_pair, ky_mid, kz_mid, dg_mid, cells, hot_own, p_sample,
+    kx, ky, kz, dinv, dg, prim, t0, t1, t2, sent, cond, left, found,
 ):
     block = 2 * lax.axis_index("y") + lax.axis_index("xl")
     core = lax.axis_index("c")
     here = pl.ds(2 * core, 2)
-    for base, first, second in ((0, p_low, p_low_pair), (4, p_own, p_pair), (8, p_high, p_high_pair)):
+    prim[:, 4:8] = p_mid[...]
+    cond[4:8] = c_mid[...]
+    for base, first, second in ((0, p_low, p_low_pair), (8, p_high, p_high_pair)):
         prim[:, pl.ds(base + 2 * core, 2)] = first[here]
         prim[:, pl.ds(base + 2 - 2 * core, 2)] = second[here]
-    for base, first, second in ((0, c_low, c_low_pair), (4, c_own, c_pair), (8, c_high, c_high_pair)):
-        cond[:, pl.ds(base + 2 * core, 2)] = first[...]
-        cond[:, pl.ds(base + 2 - 2 * core, 2)] = second[...]
+    for base, first, second in ((0, c_low, c_low_pair), (8, c_high, c_high_pair)):
+        cond[pl.ds(base + 2 * core, 2)] = first[0]
+        cond[pl.ds(base + 2 - 2 * core, 2)] = second[0]
+        for source, start in ((first, base + 2 * core), (second, base + 2 - 2 * core)):
+            for j in range(2):
+                up_y, up_z, part = in_plane(source[1, j], source[2, j])
+                ky[start + j] = up_y
+                kz[start + j] = up_z
+                dg[start + j] = part
+    ky[4:8] = ky_mid[...]
+    kz[4:8] = kz_mid[...]
+    dg[4:8] = dg_mid[...]
     rows, lanes = prim.shape[2], prim.shape[3]
-    shape = (rows, lanes)
-    row_at = lax.broadcasted_iota(jnp.int32, shape, 0)
-    lane_at = lax.broadcasted_iota(jnp.int32, shape, 1)
-    mask_y = jnp.where(row_at < rows - 1, 1.0, 0.0).astype(F32)
-    mask_z = jnp.where(lane_at < lanes - 1, 1.0, 0.0).astype(F32)
+    row_at, lane_at, mask_y, mask_z = edges(rows, lanes)
     edge = jnp.where(row_at == 0, 0.5, 0.0) + jnp.where(row_at == rows - 1, 0.5, 0.0)
     edge = edge + jnp.where(lane_at == 0, 0.5, 0.0) + jnp.where(lane_at == lanes - 1, 0.5, 0.0)
     unit = (6.0 - edge).astype(F32)
     layers = 4 * CHIPS
 
-    kx[0] = 0.5 * (cond[0, 0] + cond[0, 1])
+    kx[0] = 0.5 * (cond[0] + cond[1])
 
     def coefficients(i, carry):
         layer = 4 * block - 4 + i
         inside = jnp.where(jnp.logical_and(layer >= 0, layer < layers), 1.0, 0.0).astype(F32)
-        first = 0.5 * (cond[0, i] + cond[0, i + 1])
+        first = 0.5 * (cond[i] + cond[i + 1])
         kx[i] = first
-        along_y = cond[1, i]
-        along_z = cond[2, i]
-        up_y = 0.5 * (along_y + ahead(along_y, 0)) * mask_y
-        up_z = 0.5 * (along_z + ahead(along_z, 1)) * mask_z
-        ky[i] = up_y
-        kz[i] = up_z
-        low_y = behind(up_y, 0)
-        low_z = behind(up_z, 1)
-        up_y = jnp.where(row_at == rows - 1, 0.5 * along_y, up_y)
-        up_z = jnp.where(lane_at == lanes - 1, 0.5 * along_z, up_z)
-        low_y = jnp.where(row_at == 0, 0.5 * along_y, low_y)
-        low_z = jnp.where(lane_at == 0, 0.5 * along_z, low_z)
-        diagonal = first + kx[i - 1] + up_y + low_y + up_z + low_z
+        diagonal = first + kx[i - 1] + dg[i]
         inverse = jnp.where(inside > 0.5, 1.0 / diagonal, 0.0)
         dg[i] = diagonal
         dinv[i] = inverse
@@ -179,51 +245,30 @@
     moments = krylov(t0, t1, t2, kx, ky, kz, dinv, dg)
 
     picked = cells[...]
-    row_of = picked // lanes
-    lane_of = picked - row_of * lanes
+    lane_of = picked - (picked // lanes) * lanes
     count = picked.shape[1]
-    for j in range(4):
-        rows_hot = one_hot(rows, (4 * block + j) * rows, row_of)
-        rows_hot = jnp.where(rows_hot, 1.0, 0.0).astype(BF16)
-        for piece in range(3):
-            hot[pl.ds((piece * 4 + j) * rows, rows)] = rows_hot
-    lane_hot = one_hot(lanes, 0, lane_of)
-    for f, field in enumerate((prim, t0, t1, t2)):
-        for s in range(2):
-            for j in range(4):
-                parts = pieces_of(jnp.transpose(field[s, 4 + j]))
-                for k in range(3):
-                    start = (k * 4 + j) * rows
-                    left[pl.ds((2 * f + s) * lanes, lanes), start : start + rows] = parts[k]
-    spread = jnp.dot(left[...], hot[...], preferred_element_type=F32)
-    samples = [
-        jnp.sum(jnp.where(lane_hot, spread[k * lanes : (k + 1) * lanes], 0.0), axis=0, keepdims=True)
-        for k in range(8)
-    ]
-    sample = jnp.concatenate(samples, axis=0)
+    gather([(t0, 4), (t1, 4), (t2, 4)], left, hot_own, one_hot(lanes, 0, lane_of), found)
     for k in range(CHIPS):
-        sent[k, :, :count] = sample
-        for j in range(3):
-            sent[k, :, count + 128 * j : count + 128 * (j + 1)] = moments[8 * j : 8 * j + 8]
+        sent[k, 0:2, :count] = p_sample[...]
+        sent[k, 2:8, :count] = found[...]
+        sent[k, :, count:] = moments
 
 
 def adjoint_kernel(
-    got, observed, cells, kx, ky, kz, dinv, dg, prim, f0, f1, f2,
-    a0, a1, a2, pot, predicted, sent, heavy, hot,
+    got, observed, cells, hot, kx, ky, kz, dinv, dg, prim, f0, f1, f2,
+    a0, a1, a2, pot, predicted, sent, heavy,
 ):
-    block = 2 * lax.axis_index("y") + lax.axis_index("xl")
     core = lax.axis_index("c")
     rows, lanes = prim.shape[2], prim.shape[3]
     count = cells.shape[1]
     total = got[0]
     for k in range(1, CHIPS):
         total = total + got[k]
-    moments = jnp.concatenate([total[:, count + 128 * j : count + 128 * (j + 1)] for j in range(3)], axis=0)
-    weights = weights_of(moments)
+    weights = weights_of(total[:, count:])
     sample = total[:, :count]
     value = sample[0:2]
     for k in range(3):
-        value = value + weights[k][:, 0:1] * sample[2 * k + 2 : 2 * k + 4]
+        value = value + weights[k] * sample[2 * k + 2 : 2 * k + 4]
     predicted[...] = value
     seen = jnp.where(core == 0, observed[0:2], observed[2:4])
     misfit = value - seen
@@ -233,16 +278,12 @@
             pot[s, i] = prim[s, i + 3] + w[0] * f0[s, i + 3] + w[1] * f1[s, i + 3] + w[2] * f2[s, i + 3]
 
     picked = cells[...]
-    row_of = picked // lanes
-    lane_of = picked - row_of * lanes
+    lane_of = picked - (picked // lanes) * lanes
     lane_hot = one_hot(lanes, 0, lane_of)
     for s in range(2):
         spread = jnp.where(lane_hot, misfit[s : s + 1], 0.0)
         for k, piece in enumerate(pieces_of(spread)):
             heavy[k, pl.ds(s * lanes, lanes)] = piece
-    for i in range(10):
-        rows_hot = one_hot(rows, (4 * block - 3 + i) * rows, row_of)
-        hot[pl.ds(i * rows, rows)] = jnp.where(rows_hot, 1.0, 0.0).astype(BF16)
     placed = [
         lax.dot_general(hot[...], heavy[k], (((1,), (1,)), ((), ())), preferred_element_type=F32)
         for k in range(3)
@@ -293,7 +334,7 @@
                 sums[1] = sums[1] + along(mid_p, mid_a, 0, row_at)
                 sums[2] = sums[2] + along(mid_p, mid_a, 1, lane_at)
             for k in range(3):
-                target[:, 2 * k + j] = (-0.5 * sums[k]).reshape(rows // 8, 8, lanes)
+                target[:, 2 * k + j] = (-0.5 * sums[k]).reshape(target.shape[0], target.shape[2], lanes)
 
 
 def call(kernel, limit, outs, scratch=()):
@@ -302,7 +343,7 @@
     def run(*args):
         return pl.pallas_call(
             kernel,
-            out_shape=tuple(jax.ShapeDtypeStruct(x, F32) for x in outs),
+            out_shape=tuple(jax.ShapeDtypeStruct(x, kind) for x, kind in outs),
             in_specs=[vmem] * len(args),
             out_specs=tuple([vmem] * len(outs)),
             scratch_shapes=list(scratch),
@@ -364,37 +405,54 @@
 
     rows, lanes = primary.shape[3], primary.shape[4]
     count = receivers.shape[1]
-    deep = (DEEP, rows, lanes)
-    pairs = (2, DEEP, rows, lanes)
-    payload = (CHIPS, 8, count + 384)
+    f32 = lambda *shape: (shape, F32)
+    deep = f32(DEEP, rows, lanes)
+    pairs = f32(2, DEEP, rows, lanes)
+    four = f32(KEPT, rows, lanes)
+    p_mid, c_mid, ky_mid, kz_mid, dg_mid, hot, hot_own, p_sample = call(
+        own_kernel,
+        14,
+        [
+            f32(2, KEPT, rows, lanes), four, four, four, four,
+            ((10 * rows, count), BF16), ((3 * KEPT * rows, count), BF16), f32(2, count),
+        ],
+        [pltpu.VMEM((2 * lanes, 3 * KEPT * rows), BF16)],
+    )(fields, p_pair, conductivity, c_pair, receivers)
     kx, ky, kz, dinv, dg, prim, f0, f1, f2, sent = call(
         forward_kernel,
-        26,
-        [deep] * 5 + [pairs] * 4 + [payload],
-        [pltpu.VMEM((3,) + deep, F32), pltpu.VMEM((12 * rows, count), BF16), pltpu.VMEM((8 * lanes, 12 * rows), BF16)],
+        20,
+        [deep] * 5 + [pairs] * 4 + [f32(CHIPS, 8, count + 128)],
+        [
+            pltpu.VMEM((DEEP, rows, lanes), F32),
+            pltpu.VMEM((6 * lanes, 3 * KEPT * rows), BF16),
+            pltpu.VMEM((6, count), F32),
+        ],
     )(
-        fields, p_pair, p_low, p_low_pair, p_high, p_high_pair,
-        conductivity, c_pair, c_low, c_low_pair, c_high, c_high_pair, receivers,
+        p_mid, p_low, p_low_pair, p_high, p_high_pair,
+        c_mid, c_low, c_low_pair, c_high, c_high_pair, ky_mid, kz_mid, dg_mid, receivers, hot_own, p_sample,
     )
     got = lax.all_to_all(sent, ("y", "xl"), 0, 0, tiled=True)
     six = (2, 6, rows, lanes)
     a0, a1, a2, pot, pred, sent = call(
         adjoint_kernel,
-        18,
-        [pairs] * 3 + [six, (2, count), (CHIPS, 24, 128)],
-        [pltpu.VMEM((3, 2 * lanes, count), BF16), pltpu.VMEM((10 * rows, count), BF16)],
-    )(got, observed[0], receivers, kx, ky, kz, dinv, dg, prim, f0, f1, f2)
+        16,
+        [pairs] * 3 + [f32(*six), f32(2, count), f32(CHIPS, 8, 128)],
+        [pltpu.VMEM((3, 2 * lanes, count), BF16)],
+    )(got, observed[0], receivers, hot, kx, ky, kz, dinv, dg, prim, f0, f1, f2)
     pred_pair = send(pred, swap)
     got = lax.all_to_all(sent, ("y", "xl"), 0, 0, tiled=True)
-    chunks = (rows // 8, 6, 8, lanes)
+    slabs = lax.axis_size("z")
+    chunks = (slabs, 6, rows // slabs, lanes)
     kept, given, predicted = call(
-        gradient_kernel, 8, [chunks, chunks, (2, 2, count)], [pltpu.VMEM(six, F32)]
+        gradient_kernel, 8, [f32(*chunks), f32(*chunks), f32(2, 2, count)], [pltpu.VMEM(six, F32)]
     )(got, a0, a1, a2, pot, pred, pred_pair)
     total = kept + send(given, swap)
-    parts = lax.all_to_all(total, ("z", "xh"), 0, 0, tiled=True)
+    parts = lax.all_to_all(total, "z", 0, 0, tiled=True)
     share = jnp.sum(parts, axis=0, keepdims=True)
+    if high_count > 1:
+        share = share + lax.ppermute(share, "xh", [(0, 1), (1, 0)])
     spread = jnp.broadcast_to(share, chunks)
-    whole = lax.all_to_all(spread, ("z", "xh"), 0, 0, tiled=True)
+    whole = lax.all_to_all(spread, "z", 0, 0, tiled=True)
     grad = jnp.transpose(whole, (1, 0, 2, 3)).reshape(3, 2, rows, lanes)
     return grad, predicted.reshape(1, 4, count)
 

time: 132 us -> 133 us (level); the launches traced: 130 us -> 133 us
  blocking collectives: 40.1 us -> 50.6 us
  waiting for transfers between devices: 39.1 us -> 33.2 us
  starting transfers between devices: 21.9 us -> 20.1 us
    all_to_all x1, blocking collectives: 15.7 us -> 27.3 us  [per_device(): got = lax.all_to_all(sent, ('y', 'xl'), 0, 0, tiled=True)]
    ppermute x12, waiting for transfers between devices: 21.9 us -> 11.4 us  [send(): return lax.ppermute(x, NAMES, pairs)]
    ppermute x0 -> x1, waiting for transfers between devices: none -> 4.99 us  [per_device(): share = share + lax.ppermute(share, 'xh', [(0, 1), (1, 0)])]
    all_to_all x1, starting transfers between devices: 6.74 us -> 3.45 us  [per_device(): whole = lax.all_to_all(spread, 'z', 0, 0, tiled=True)]
    pallas_call x3 -> x4, Pallas kernels: 18.1 us -> 18.6 us  [run(): pl.pallas_call(kernel, out_shape=tuple((jax.ShapeDtypeStruct(x, kind) for...]
    unnamed x16 -> x18, local copies, waits for them, and re-layouts: 7.31 us -> 7.35 us
  transfers between devices with their start and end apart: 14 -> 15, of which waited for: 7 -> 9; matrix products, arithmetic and copies ran while one was open for 0% -> 0% of each run, Pallas kernels for 0% -> 1%
where the time goes in v3:
time: 133 us
  blocking collectives  50.6 us (38%)
  waiting for transfers between devices  33.2 us (25%)
  starting transfers between devices  20.1 us (15%)
  Pallas kernels  18.6 us (14%)
  local copies, waits for them, and re-layouts  9.53 us (7%)
    all_to_all x1, blocking collectives, per_device(): got = lax.all_to_all(sent, ('y', 'xl'), 0, 0, tiled=True)  27.3 us
    all_to_all x1, blocking collectives, per_device(): parts = lax.all_to_all(total, 'z', 0, 0, tiled=True)  23.3 us
    pallas_call x4, Pallas kernels, run(): pl.pallas_call(kernel, out_shape=tuple((jax.ShapeDtypeStruct(x, kind) for...  18.6 us
    ppermute x12, starting transfers between devices, send(): return lax.ppermute(x, NAMES, pairs)  12.7 us
    all_to_all x1, waiting for transfers between devices, per_device(): whole = lax.all_to_all(spread, 'z', 0, 0, tiled=True)  12 us
    ppermute x12, waiting for transfers between devices, send(): return lax.ppermute(x, NAMES, pairs)  11.4 us
    unnamed x18, local copies, waits for them, and re-layouts  7.35 us
    ppermute x1, waiting for transfers between devices, per_device(): share = share + lax.ppermute(share, 'xh', [(0, 1), (1, 0)])  4.99 us
  transfers between devices with their start and end apart: 15, of which 9 were waited for; matrix products, arithmetic and copies ran while one was open for 0% of the time, Pallas kernels for 1%

profile of v3, /device:TPU:4, one launch (start us, length us, event | category | flops | bytes accessed | tf_op | source)
XLA Modules:
  0.0 132.9 jit_solution(1116986568432104346)
XLA Ops:
  0.6 1.3 collective-permute-start.4
  1.9 4.6 %collective-permute-start.2 = (f32[4,2,128,128]{3,2,1,0:T(8,128)}, f32[4,2,128,128]{3,2,1,0:T(8,128)S(1)}, u32[]{:S(2)}, u32[]{:S(2)}) collective-permute-start(f32[4,2,128,128]{3,2,1,0:T(8,128)} %bitcast.10), channel_id=1, source_target_pairs={{0,2},{1,3},{2,4},{3,5},{4,6},{5,7},{6,8},{7,9},{8,10},{9,11},{10,... | collective-permute-start | bytes 1572872 | tf_op jit(solution)/shard_map/ppermute | solution.py:391
  6.5 0.1 collective-permute-start.1
  6.6 1.3 collective-permute-start.8
  7.9 4.6 %collective-permute-start.6 = (f32[3,2,128,128]{3,2,1,0:T(8,128)}, f32[3,2,128,128]{3,2,1,0:T(8,128)S(1)}, u32[]{:S(2)}, u32[]{:S(2)}) collective-permute-start(f32[3,2,128,128]{3,2,1,0:T(8,128)} %c_own.1), channel_id=1, source_target_pairs={{0,18},{1,19},{2,20},{3,21},{4,22},{5,23},{6,24},{7,25},{8,26},{9,... | collective-permute-start | bytes 1179656 | tf_op jit(solution)/shard_map/ppermute | solution.py:391
  12.5 0.0 collective-permute-done.1.c_pair
  12.5 0.1 collective-permute-start
  12.6 4.9 %collective-permute-done.4.p_high = f32[4,2,128,128]{3,2,1,0:T(8,128)S(1)} collective-permute-done((f32[4,2,128,128]{3,2,1,0:T(8,128)}, f32[4,2,128,128]{3,2,1,0:T(8,128)S(1)}, u32[]{:S(2)}, u32[]{:S(2)}) %collective-permute-start.4) | collective-permute-done | bytes 524320 | tf_op jit(solution)/shard_map/ppermute | solution.py:391
  17.5 0.0 collective-permute-start.5
  17.5 0.1 collective-permute-done.2.p_low
  17.7 0.4 collective-permute-start.3
  18.1 2.6 %collective-permute-done.8.c_high = f32[3,2,128,128]{3,2,1,0:T(8,128)S(1)} collective-permute-done((f32[3,2,128,128]{3,2,1,0:T(8,128)}, f32[3,2,128,128]{3,2,1,0:T(8,128)S(1)}, u32[]{:S(2)}, u32[]{:S(2)}) %collective-permute-start.8) | collective-permute-done | bytes 393248 | tf_op jit(solution)/shard_map/ppermute | solution.py:391
  20.6 0.0 collective-permute-start.9
  20.6 0.9 collective-permute-done.6.c_low
  21.5 0.0 collective-permute-start.7
  21.5 0.0 collective-permute-done.p_pair
  21.5 1.0 copy-done.4
  22.6 1.0 copy-done.5
  23.6 0.7 copy-done.6
  24.2 1.7 %shard_map.59 = (f32[2,4,128,128]{3,2,1,0:T(8,128)S(1)}, f32[4,128,128]{2,1,0:T(8,128)S(1)}, f32[4,128,128]{2,1,0:T(8,128)S(1)}, f32[4,128,128]{2,1,0:T(8,128)S(...) custom-call(f32[4,2,128,128]{3,2,1,0:T(8,128)S(1)} %bitcast.12, ...), custom_call_target="tpu_custom_call" | custom-call | tf_op jit(solution)/shard_map/pallas_call | solution.py:344
  26.0 0.0 collective-permute-done.9.c_high_pair
  26.0 0.0 collective-permute-done.7.c_low_pair
  26.0 0.0 collective-permute-done.5.p_high_pair
  26.0 0.0 collective-permute-done.3.p_low_pair
  26.0 0.0 copy-start.8
  26.1 8.7 %shard_map.60 = (f32[12,128,128]{2,1,0:T(8,128)S(1)}, f32[12,128,128]{2,1,0:T(8,128)S(1)}, f32[12,128,128]{2,1,0:T(8,128)S(1)}, f32[12,128,128]{2,1,0:T(8,128)S(...) custom-call(f32[2,4,128,128]{3,2,1,0:T(8,128)S(1)} %get-tuple-elemen, ...), custom_call_target="tpu_custom_call" | custom-call | tf_op jit(solution)/shard_map/pallas_call | solution.py:344
  34.8 27.3 %all_to_all.20.got = f32[8,8,1152]{2,1,0:T(8,128)S(1)} all-to-all(f32[8,8,1152]{2,1,0:T(8,128)S(1)} %get-tuple-element.36), channel_id=1, replica_groups=mesh['z'=8,'xh'=2,'y'=4,'xl'=2,'c'=2] {'y','xl'}, dimensions={0} | all-to-all | bytes 589824 | tf_op jit(solution)/shard_map/all_to_all | solution.py:434
  62.1 6.9 %shard_map.61 = (f32[2,12,128,128]{3,2,1,0:T(8,128)S(1)}, f32[2,12,128,128]{3,2,1,0:T(8,128)S(1)}, f32[2,12,128,128]{3,2,1,0:T(8,128)S(1)}, f32[2,6,128,128]{3,2...) custom-call(f32[8,8,1152]{2,1,0:T(8,128)S(1)} %all_to_all.20.got, f32[4,1024]{1,0:T(4,128)S(1)} %bitcast.13, ...), custom_call_target="tpu_custom_call" | custom-call | tf_op jit(solution)/shard_map/pallas_call | solution.py:344
  69.0 1.2 copy-done
  70.2 0.9 copy-done.2
  71.1 3.3 %all-to-all-start.1 = ((f32[8,8,128]{2,1,0:T(8,128)}), f32[8,8,128]{2,1,0:T(8,128)S(1)}, u32[]{:S(2)}, u32[]{:S(2)}) async-start(f32[8,8,128]{2,1,0:T(8,128)} %get-tuple-element.47), calls=%async_computation.1 | async-start | bytes 65536 | tf_op jit(solution)/shard_map/all_to_all | solution.py:443
  74.4 0.3 collective-permute-start.10
  74.7 1.2 collective-permute-done.10.pred_pair
  75.8 4.7 %all-to-all-done.1.got = f32[8,8,128]{2,1,0:T(8,128)S(1)} async-done(((f32[8,8,128]{2,1,0:T(8,128)}), f32[8,8,128]{2,1,0:T(8,128)S(1)}, u32[]{:S(2)}, u32[]{:S(2)}) %all-to-all-start.1) | async-done | bytes 32800 | tf_op jit(solution)/shard_map/all_to_all | solution.py:443
  80.6 1.4 %copy-done.1 = f32[2,12,128,128]{3,2,1,0:T(8,128)S(1)} copy-done((f32[2,12,128,128]{3,2,1,0:T(8,128)S(1)}, f32[2,12,128,128]{3,2,1,0:T(8,128)}, u32[]{:S(2)}) %copy-start.1) | copy-done | bytes 1572888
  82.0 1.1 copy-done.3
  83.1 1.2 shard_map.62
  84.4 0.1 collective-permute-start.11
  84.5 1.7 %collective-permute-done.11 = f32[8,6,16,128]{3,2,1,0:T(8,128)S(1)} collective-permute-done((f32[8,6,16,128]{3,2,1,0:T(8,128)S(1)}, f32[8,6,16,128]{3,2,1,0:T(8,128)S(1)}, u32[]{:S(2)}, u32[]{:S(2)}) %collective-permute-start.11) | collective-permute-done | bytes 393248 | tf_op jit(solution)/shard_map/ppermute | solution.py:391
  86.2 0.1 add.6
  86.2 23.3 %all_to_all.21 = f32[8,6,16,128]{3,2,1,0:T(8,128)S(1)} all-to-all(f32[8,6,16,128]{3,2,1,0:T(8,128)S(1)} %add.6), channel_id=1, replica_groups=mesh['z'=8,'xh'=2,'y'=4,'xl'=2,'c'=2] {'z'}, dimensions={0} | all-to-all | bytes 786432 | tf_op jit(solution)/shard_map/all_to_all | solution.py:450
  109.5 0.7 collective-permute-start.12
  110.2 5.0 %collective-permute-done.12 = f32[1,6,16,128]{3,2,1,0:T(8,128)S(1)} collective-permute-done((f32[1,6,16,128]{3,2,1,0:T(8,128)S(1)}, f32[1,6,16,128]{3,2,1,0:T(8,128)S(1)}, u32[]{:S(2)}, u32[]{:S(2)}) %collective-permute-start.12) | collective-permute-done | bytes 49184 | tf_op jit(solution)/shard_map/ppermute | solution.py:453
  115.2 0.8 broadcast_in_dim.12
  116.0 3.5 %all-to-all-start.3 = ((f32[8,6,16,128]{3,2,1,0:T(8,128)}), f32[8,6,16,128]{3,2,1,0:T(8,128)S(1)}, u32[]{:S(2)}, u32[]{:S(2)}) async-start(f32[8,6,16,128]{3,2,1,0:T(8,128)} %broadcast_in_dim.12), calls=%async_computation.3 | async-start | bytes 786432 | tf_op jit(solution)/shard_map/all_to_all | solution.py:455
  119.4 0.6 reshape.11
  120.1 12.0 %all-to-all-done.3 = f32[8,6,16,128]{3,2,1,0:T(8,128)S(1)} async-done(((f32[8,6,16,128]{3,2,1,0:T(8,128)}), f32[8,6,16,128]{3,2,1,0:T(8,128)S(1)}, u32[]{:S(2)}, u32[]{:S(2)}) %all-to-all-start.3) | async-done | bytes 393248 | tf_op jit(solution)/shard_map/all_to_all | solution.py:455
  132.1 0.8 copy.6
  (12 shorter events, 0.1 us)
Async XLA Ops:
  0.6 16.9 %collective-permute-start.4 = (f32[4,2,128,128]{3,2,1,0:T(8,128)}, f32[4,2,128,128]{3,2,1,0:T(8,128)S(1)}, u32[]{:S(2)}, u32[]{:S(2)}) collective-permute-start(f32[4,2,128,128]{3,2,1,0:T(8,128)} %bitcast.9), channel_id=1, source_target_pairs={{2,0},{3,1},{4,2},{5,3},{6,4},{7,5},{8,6},{9,7},{10,8},{11,9},{12,... | collective-permute-start | bytes 1572872 | tf_op jit(solution)/shard_map/ppermute | solution.py:391
  1.9 15.8 %collective-permute-start.2 = (f32[4,2,128,128]{3,2,1,0:T(8,128)}, f32[4,2,128,128]{3,2,1,0:T(8,128)S(1)}, u32[]{:S(2)}, u32[]{:S(2)}) collective-permute-start(f32[4,2,128,128]{3,2,1,0:T(8,128)} %bitcast.10), channel_id=1, source_target_pairs={{0,2},{1,3},{2,4},{3,5},{4,6},{5,7},{6,8},{7,9},{8,10},{9,11},{10,... | collective-permute-start | bytes 1572872 | tf_op jit(solution)/shard_map/ppermute | solution.py:391
  6.5 6.0 %collective-permute-start.1 = (f32[3,2,128,128]{3,2,1,0:T(8,128)}, f32[3,2,128,128]{3,2,1,0:T(8,128)S(1)}, u32[]{:S(2)}, u32[]{:S(2)}) collective-permute-start(f32[3,2,128,128]{3,2,1,0:T(8,128)} %c_own.1), channel_id=1, source_target_pairs={{0,1},{1,0},{2,3},{3,2},{4,5},{5,4},{6,7},{7,6},{8,9},{9,8},{10,11... | collective-permute-start | bytes 1179656 | tf_op jit(solution)/shard_map/ppermute | solution.py:391
  6.6 14.0 %collective-permute-start.8 = (f32[3,2,128,128]{3,2,1,0:T(8,128)}, f32[3,2,128,128]{3,2,1,0:T(8,128)S(1)}, u32[]{:S(2)}, u32[]{:S(2)}) collective-permute-start(f32[3,2,128,128]{3,2,1,0:T(8,128)} %c_own.1), channel_id=1, source_target_pairs={{2,16},{3,17},{4,18},{5,19},{6,20},{7,21},{8,22},{9,23},{10,24},{1... | collective-permute-start | bytes 1179656 | tf_op jit(solution)/shard_map/ppermute | solution.py:391
  7.9 13.6 %collective-permute-start.6 = (f32[3,2,128,128]{3,2,1,0:T(8,128)}, f32[3,2,128,128]{3,2,1,0:T(8,128)S(1)}, u32[]{:S(2)}, u32[]{:S(2)}) collective-permute-start(f32[3,2,128,128]{3,2,1,0:T(8,128)} %c_own.1), channel_id=1, source_target_pairs={{0,18},{1,19},{2,20},{3,21},{4,22},{5,23},{6,24},{7,25},{8,26},{9,... | collective-permute-start | bytes 1179656 | tf_op jit(solution)/shard_map/ppermute | solution.py:391
  12.5 9.0 %collective-permute-start = (f32[4,2,128,128]{3,2,1,0:T(8,128)}, f32[4,2,128,128]{3,2,1,0:T(8,128)S(1)}, u32[]{:S(2)}, u32[]{:S(2)}) collective-permute-start(f32[4,2,128,128]{3,2,1,0:T(8,128)} %bitcast.11), channel_id=1, source_target_pairs={{0,1},{1,0},{2,3},{3,2},{4,5},{5,4},{6,7},{7,6},{8,9},{9,8},{10,11... | collective-permute-start | bytes 1572872 | tf_op jit(solution)/shard_map/ppermute | solution.py:391
  17.5 8.5 %collective-permute-start.5 = (f32[4,2,128,128]{3,2,1,0:T(8,128)S(1)}, f32[4,2,128,128]{3,2,1,0:T(8,128)S(1)}, u32[]{:S(2)}, u32[]{:S(2)}) collective-permute-start(f32[4,2,128,128]{3,2,1,0:T(8,128)S(1)} %collective-permute-done.4.p_high), channel_id=1, source_target_pairs={{0,1},{1,0},{2,3},{3,2},{4,5},{5,4},{6,7},{7,6},{8,9},{9,8},{10,11... | collective-permute-start | bytes 1572872 | tf_op jit(solution)/shard_map/ppermute | solution.py:391
  17.7 8.3 %collective-permute-start.3 = (f32[4,2,128,128]{3,2,1,0:T(8,128)S(1)}, f32[4,2,128,128]{3,2,1,0:T(8,128)S(1)}, u32[]{:S(2)}, u32[]{:S(2)}) collective-permute-start(f32[4,2,128,128]{3,2,1,0:T(8,128)S(1)} %collective-permute-done.2.p_low), channel_id=1, source_target_pairs={{0,1},{1,0},{2,3},{3,2},{4,5},{5,4},{6,7},{7,6},{8,9},{9,8},{10,11... | collective-permute-start | bytes 1572872 | tf_op jit(solution)/shard_map/ppermute | solution.py:391
  20.6 5.4 %collective-permute-start.9 = (f32[3,2,128,128]{3,2,1,0:T(8,128)S(1)}, f32[3,2,128,128]{3,2,1,0:T(8,128)S(1)}, u32[]{:S(2)}, u32[]{:S(2)}) collective-permute-start(f32[3,2,128,128]{3,2,1,0:T(8,128)S(1)} %collective-permute-done.8.c_high), channel_id=1, source_target_pairs={{0,1},{1,0},{2,3},{3,2},{4,5},{5,4},{6,7},{7,6},{8,9},{9,8},{10,11... | collective-permute-start | bytes 1179656 | tf_op jit(solution)/shard_map/ppermute | solution.py:391
  21.5 4.5 %collective-permute-start.7 = (f32[3,2,128,128]{3,2,1,0:T(8,128)S(1)}, f32[3,2,128,128]{3,2,1,0:T(8,128)S(1)}, u32[]{:S(2)}, u32[]{:S(2)}) collective-permute-start(f32[3,2,128,128]{3,2,1,0:T(8,128)S(1)} %collective-permute-done.6.c_low), channel_id=1, source_target_pairs={{0,1},{1,0},{2,3},{3,2},{4,5},{5,4},{6,7},{7,6},{8,9},{9,8},{10,11... | collective-permute-start | bytes 1179656 | tf_op jit(solution)/shard_map/ppermute | solution.py:391
  21.5 1.0 copy-start.4
  22.6 1.0 copy-start.5
  23.6 0.7 copy-start.6
  24.2 1.8 %copy-start.7 = (s32[1,1024]{1,0:T(1,128)S(1)}, s32[1,1024]{1,0:T(1,128)}, u32[]{:S(2)}) copy-start(s32[1,1024]{1,0:T(1,128)} %cells.5) | copy-start | bytes 12292
  26.0 36.1 %copy-start.8 = (f32[1,4,1024]{2,1,0:T(4,128)S(1)}, f32[1,4,1024]{2,1,0:T(4,128)}, u32[]{:S(2)}) copy-start(f32[1,4,1024]{2,1,0:T(4,128)} %param.6) | copy-start | bytes 49156
  69.0 1.2 copy-start
  70.2 0.9 copy-start.2
  71.1 9.5 %all-to-all-start.1 = ((f32[8,8,128]{2,1,0:T(8,128)}), f32[8,8,128]{2,1,0:T(8,128)S(1)}, u32[]{:S(2)}, u32[]{:S(2)}) async-start(f32[8,8,128]{2,1,0:T(8,128)} %get-tuple-element.47), calls=%async_computation.1 | async-start | bytes 65536 | tf_op jit(solution)/shard_map/all_to_all | solution.py:443
  74.4 1.4 %collective-permute-start.10 = (f32[2,1024]{1,0:T(2,128)S(1)}, f32[2,1024]{1,0:T(2,128)S(1)}, u32[]{:S(2)}, u32[]{:S(2)}) collective-permute-start(f32[2,1024]{1,0:T(2,128)S(1)} %get-tuple-element.52.pred), channel_id=1, source_target_pairs={{0,1},{1,0},{2,3},{3,2},{4,5},{5,4},{6,7},{7,6},{8,9},{9,8},{10,11... | collective-permute-start | bytes 24584 | tf_op jit(solution)/shard_map/ppermute | solution.py:391
  80.6 1.4 %copy-start.1 = (f32[2,12,128,128]{3,2,1,0:T(8,128)S(1)}, f32[2,12,128,128]{3,2,1,0:T(8,128)}, u32[]{:S(2)}) copy-start(f32[2,12,128,128]{3,2,1,0:T(8,128)} %copy-done) | copy-start | bytes 4718596
  82.0 1.1 copy-start.3
  84.4 1.8 %collective-permute-start.11 = (f32[8,6,16,128]{3,2,1,0:T(8,128)S(1)}, f32[8,6,16,128]{3,2,1,0:T(8,128)S(1)}, u32[]{:S(2)}, u32[]{:S(2)}) collective-permute-start(f32[8,6,16,128]{3,2,1,0:T(8,128)S(1)} %get-tuple-element.54), channel_id=1, source_target_pairs={{0,1},{1,0},{2,3},{3,2},{4,5},{5,4},{6,7},{7,6},{8,9},{9,8},{10,11... | collective-permute-start | bytes 1179656 | tf_op jit(solution)/shard_map/ppermute | solution.py:391
  109.5 5.7 %collective-permute-start.12 = (f32[1,6,16,128]{3,2,1,0:T(8,128)S(1)}, f32[1,6,16,128]{3,2,1,0:T(8,128)S(1)}, u32[]{:S(2)}, u32[]{:S(2)}) collective-permute-start(f32[1,6,16,128]{3,2,1,0:T(8,128)S(1)} %bitcast.15), channel_id=1, source_target_pairs={{0,16},{16,0},{1,17},{17,1},{2,18},{18,2},{3,19},{19,3},{4,20},{20... | collective-permute-start | bytes 147464 | tf_op jit(solution)/shard_map/ppermute | solution.py:453
  116.0 16.1 %all-to-all-start.3 = ((f32[8,6,16,128]{3,2,1,0:T(8,128)}), f32[8,6,16,128]{3,2,1,0:T(8,128)S(1)}, u32[]{:S(2)}, u32[]{:S(2)}) async-start(f32[8,6,16,128]{3,2,1,0:T(8,128)} %broadcast_in_dim.12), calls=%async_computation.3 | async-start | bytes 786432 | tf_op jit(solution)/shard_map/all_to_all | solution.py:455

commit v4 on v3

--- a/solution.py
+++ b/solution.py
@@ -256,7 +256,7 @@
 
 def adjoint_kernel(
     got, observed, cells, hot, kx, ky, kz, dinv, dg, prim, f0, f1, f2,
-    a0, a1, a2, pot, predicted, sent, heavy,
+    b0, b1, b2, pot, predicted, sent, heavy, a0, a1, a2,
 ):
     core = lax.axis_index("c")
     rows, lanes = prim.shape[2], prim.shape[3]
@@ -296,6 +296,8 @@
     moments = krylov(a0, a1, a2, kx, ky, kz, dinv, dg)
     for k in range(CHIPS):
         sent[k] = moments
+    for near, deep in ((b0, a0), (b1, a1), (b2, a2)):
+        near[...] = deep[:, 3:9]
 
 
 def gradient_kernel(got, a0, a1, a2, pot, pred, pred_pair, kept, given, predicted, adj):
@@ -312,7 +314,7 @@
     for i in range(6):
         for s in range(2):
             w = [weights[k][s : s + 1, :] for k in range(3)]
-            adj[s, i] = w[0] * a0[s, i + 3] + w[1] * a1[s, i + 3] + w[2] * a2[s, i + 3]
+            adj[s, i] = w[0] * a0[s, i] + w[1] * a1[s, i] + w[2] * a2[s, i]
 
     def along(mid_p, mid_a, axis, at):
         last = mid_p.shape[axis] - 1
@@ -337,7 +339,7 @@
                 target[:, 2 * k + j] = (-0.5 * sums[k]).reshape(target.shape[0], target.shape[2], lanes)
 
 
-def call(kernel, limit, outs, scratch=()):
+def call(kernel, limit, outs, scratch=(), flops=0):
     vmem = pl.BlockSpec(memory_space=pltpu.VMEM)
 
     def run(*args):
@@ -347,6 +349,7 @@
             in_specs=[vmem] * len(args),
             out_specs=tuple([vmem] * len(outs)),
             scratch_shapes=list(scratch),
+            cost_estimate=pl.CostEstimate(flops=flops, bytes_accessed=8 * MEBI, transcendentals=0),
             compiler_params=pltpu.CompilerParams(vmem_limit_bytes=limit * MEBI),
         )(*args)
 
@@ -398,10 +401,6 @@
     c_high = send(conductivity, step(-1, True))
     p_pair = send(fields, swap)
     c_pair = send(conductivity, swap)
-    c_low_pair = send(c_low, swap)
-    c_high_pair = send(c_high, swap)
-    p_low_pair = send(p_low, swap)
-    p_high_pair = send(p_high, swap)
 
     rows, lanes = primary.shape[3], primary.shape[4]
     count = receivers.shape[1]
@@ -417,7 +416,12 @@
             ((10 * rows, count), BF16), ((3 * KEPT * rows, count), BF16), f32(2, count),
         ],
         [pltpu.VMEM((2 * lanes, 3 * KEPT * rows), BF16)],
+        flops=10**10,
     )(fields, p_pair, conductivity, c_pair, receivers)
+    c_low, c_high, p_sample = lax.optimization_barrier((c_low, c_high, p_sample))
+    c_low_pair, c_high_pair = send(c_low, swap), send(c_high, swap)
+    p_low, p_high, p_sample = lax.optimization_barrier((p_low, p_high, p_sample))
+    p_low_pair, p_high_pair = send(p_low, swap), send(p_high, swap)
     kx, ky, kz, dinv, dg, prim, f0, f1, f2, sent = call(
         forward_kernel,
         20,
@@ -435,9 +439,9 @@
     six = (2, 6, rows, lanes)
     a0, a1, a2, pot, pred, sent = call(
         adjoint_kernel,
-        16,
-        [pairs] * 3 + [f32(*six), f32(2, count), f32(CHIPS, 8, 128)],
-        [pltpu.VMEM((3, 2 * lanes, count), BF16)],
+        18,
+        [f32(*six)] * 4 + [f32(2, count), f32(CHIPS, 8, 128)],
+        [pltpu.VMEM((3, 2 * lanes, count), BF16)] + [pltpu.VMEM((2, DEEP, rows, lanes), F32)] * 3,
     )(got, observed[0], receivers, hot, kx, ky, kz, dinv, dg, prim, f0, f1, f2)
     pred_pair = send(pred, swap)
     got = lax.all_to_all(sent, ("y", "xl"), 0, 0, tiled=True)

time: 133 us -> 130 us (0.977)
  local copies, waits for them, and re-layouts: 9.53 us -> 4.91 us
  starting transfers between devices: 20.1 us -> 21.9 us
  blocking collectives: 50.6 us -> 48.9 us
  waiting for transfers between devices: 33.2 us -> 34.6 us
    unnamed x18 -> x10, local copies, waits for them, and re-layouts: 7.35 us -> 2.73 us
    ppermute x12, starting transfers between devices: 12.7 us -> 15 us  [send(): return lax.ppermute(x, NAMES, pairs)]
    all_to_all x1, blocking collectives: 27.3 us -> 25.7 us  [per_device(): got = lax.all_to_all(sent, ('y', 'xl'), 0, 0, tiled=True)]
where the time goes in v4:
time: 130 us
  blocking collectives  48.9 us (38%)
  waiting for transfers between devices  34.6 us (27%)
  starting transfers between devices  21.9 us (17%)
  Pallas kernels  18.4 us (14%)
  local copies, waits for them, and re-layouts  4.91 us (4%)
    all_to_all x1, blocking collectives, per_device(): got = lax.all_to_all(sent, ('y', 'xl'), 0, 0, tiled=True)  25.7 us
    all_to_all x1, blocking collectives, per_device(): parts = lax.all_to_all(total, 'z', 0, 0, tiled=True)  23.3 us
    pallas_call x4, Pallas kernels, run(): pl.pallas_call(kernel, out_shape=tuple((jax.ShapeDtypeStruct(x, kind) for...  18.4 us
    ppermute x12, starting transfers between devices, send(): return lax.ppermute(x, NAMES, pairs)  15 us
    ppermute x12, waiting for transfers between devices, send(): return lax.ppermute(x, NAMES, pairs)  12.3 us
    all_to_all x1, waiting for transfers between devices, per_device(): whole = lax.all_to_all(spread, 'z', 0, 0, tiled=True)  12 us
    ppermute x1, waiting for transfers between devices, per_device(): share = share + lax.ppermute(share, 'xh', [(0, 1), (1, 0)])  5.58 us
    all_to_all x1, waiting for transfers between devices, per_device(): got = lax.all_to_all(sent, ('y', 'xl'), 0, 0, tiled=True)  4.74 us
  transfers between devices with their start and end apart: 15, of which 9 were waited for; matrix products, arithmetic and copies ran while one was open for 0% of the time, Pallas kernels for 1%

profile of v4, /device:TPU:4, one launch (start us, length us, event | category | flops | bytes accessed | tf_op | source)
XLA Modules:
  0.0 129.6 jit_solution(17589159356231738791)
XLA Ops:
  0.6 0.1 collective-permute-start
  0.7 0.5 collective-permute-start.1
  1.2 1.3 collective-permute-start.5
  2.5 4.6 %collective-permute-start.4 = (f32[3,2,128,128]{3,2,1,0:T(8,128)}, f32[3,2,128,128]{3,2,1,0:T(8,128)S(1)}, u32[]{:S(2)}, u32[]{:S(2)}) collective-permute-start(f32[3,2,128,128]{3,2,1,0:T(8,128)} %c_own.1), channel_id=1, source_target_pairs={{0,18},{1,19},{2,20},{3,21},{4,22},{5,23},{6,24},{7,25},{8,26},{9,... | collective-permute-start | bytes 1179656 | tf_op jit(solution)/shard_map/ppermute | solution.py:394
  7.1 1.3 collective-permute-start.3
  8.4 0.0 collective-permute-done.1.c_pair
  8.4 5.9 %collective-permute-start.2 = (f32[4,2,128,128]{3,2,1,0:T(8,128)}, f32[4,2,128,128]{3,2,1,0:T(8,128)S(1)}, u32[]{:S(2)}, u32[]{:S(2)}) collective-permute-start(f32[4,2,128,128]{3,2,1,0:T(8,128)} %bitcast.12), channel_id=1, source_target_pairs={{0,2},{1,3},{2,4},{3,5},{4,6},{5,7},{6,8},{7,9},{8,10},{9,11},{10,... | collective-permute-start | bytes 1572872 | tf_op jit(solution)/shard_map/ppermute | solution.py:394
  14.3 0.0 collective-permute-done.p_pair
  14.3 0.0 copy-start.1
  14.3 0.7 copy-done.1
  15.0 0.0 copy-start.3
  15.0 1.0 copy-done.3
  16.0 1.0 copy-done.4
  17.0 1.7 %shard_map.59 = (f32[2,4,128,128]{3,2,1,0:T(8,128)S(1)}, f32[4,128,128]{2,1,0:T(8,128)S(1)}, f32[4,128,128]{2,1,0:T(8,128)S(1)}, f32[4,128,128]{2,1,0:T(8,128)S(...) custom-call(f32[4,2,128,128]{3,2,1,0:T(8,128)S(1)} %bitcast.13, ...), custom_call_target="tpu_custom_call" | custom-call | flops 10000000000 | bytes 8388608 | tf_op jit(solution)/shard_map/pallas_call | solution.py:346
  18.7 0.0 collective-permute-done.5.c_high
  18.7 0.0 collective-permute-done.4.c_low
  18.8 6.5 %collective-permute-done.3.p_high = f32[4,2,128,128]{3,2,1,0:T(8,128)S(1)} collective-permute-done((f32[4,2,128,128]{3,2,1,0:T(8,128)}, f32[4,2,128,128]{3,2,1,0:T(8,128)S(1)}, u32[]{:S(2)}, u32[]{:S(2)}) %collective-permute-start.3) | collective-permute-done | bytes 524320 | tf_op jit(solution)/shard_map/ppermute | solution.py:394
  25.3 0.1 collective-permute-done.2.p_low
  25.4 0.0 collective-permute-start.6
  25.4 0.5 collective-permute-start.7
  25.9 0.0 collective-permute-start.8
  25.9 0.5 collective-permute-start.9
  26.4 2.2 %collective-permute-done.8.c_low_pair = f32[3,2,128,128]{3,2,1,0:T(8,128)S(1)} collective-permute-done((f32[3,2,128,128]{3,2,1,0:T(8,128)S(1)}, f32[3,2,128,128]{3,2,1,0:T(8,128)S(1)}, u32[]{:S(2)}, u32[]{:S(2)}) %collective-permute-start.8) | collective-permute-done | bytes 393248 | tf_op jit(solution)/shard_map/ppermute | solution.py:394
  28.6 0.6 collective-permute-done.9.c_high_pair
  29.2 0.0 collective-permute-done.6.p_low_pair
  29.2 0.0 collective-permute-done.7.p_high_pair
  29.2 0.0 copy-done.2
  29.2 0.0 copy-start
  29.2 8.6 %shard_map.60 = (f32[12,128,128]{2,1,0:T(8,128)S(1)}, f32[12,128,128]{2,1,0:T(8,128)S(1)}, f32[12,128,128]{2,1,0:T(8,128)S(1)}, f32[12,128,128]{2,1,0:T(8,128)S(...) custom-call(f32[2,4,128,128]{3,2,1,0:T(8,128)S(1)} %get-tuple-elemen, ...), custom_call_target="tpu_custom_call" | custom-call | bytes 8388608 | tf_op jit(solution)/shard_map/pallas_call | solution.py:346
  37.9 25.7 %all_to_all.20.got = f32[8,8,1152]{2,1,0:T(8,128)S(1)} all-to-all(f32[8,8,1152]{2,1,0:T(8,128)S(1)} %get-tuple-element.48), channel_id=1, replica_groups=mesh['z'=8,'xh'=2,'y'=4,'xl'=2,'c'=2] {'y','xl'}, dimensions={0} | all-to-all | bytes 589824 | tf_op jit(solution)/shard_map/all_to_all | solution.py:438
  63.6 0.0 copy-done
  63.6 6.8 %shard_map.61 = (f32[2,6,128,128]{3,2,1,0:T(8,128)S(1)}, f32[2,6,128,128]{3,2,1,0:T(8,128)S(1)}, f32[2,6,128,128]{3,2,1,0:T(8,128)S(1)}, f32[2,6,128,128]{3,2,1,...) custom-call(f32[8,8,1152]{2,1,0:T(8,128)S(1)} %all_to_all.20.got, f32[4,1024]{1,0:T(4,128)S(1)} %bitcast.9, ...), custom_call_target="tpu_custom_call" | custom-call | bytes 8388608 | tf_op jit(solution)/shard_map/pallas_call | solution.py:346
  70.4 3.3 %all-to-all-start.1 = ((f32[8,8,128]{2,1,0:T(8,128)}), f32[8,8,128]{2,1,0:T(8,128)S(1)}, u32[]{:S(2)}, u32[]{:S(2)}) async-start(f32[8,8,128]{2,1,0:T(8,128)} %get-tuple-element.59), calls=%async_computation.1 | async-start | bytes 65536 | tf_op jit(solution)/shard_map/all_to_all | solution.py:447
  73.7 0.3 collective-permute-start.10
  74.0 1.2 collective-permute-done.10.pred_pair
  75.2 4.7 %all-to-all-done.1.got = f32[8,8,128]{2,1,0:T(8,128)S(1)} async-done(((f32[8,8,128]{2,1,0:T(8,128)}), f32[8,8,128]{2,1,0:T(8,128)S(1)}, u32[]{:S(2)}, u32[]{:S(2)}) %all-to-all-start.1) | async-done | bytes 32800 | tf_op jit(solution)/shard_map/all_to_all | solution.py:447
  79.9 1.2 shard_map.62
  81.1 0.1 collective-permute-start.11
  81.2 1.7 %collective-permute-done.11 = f32[8,6,16,128]{3,2,1,0:T(8,128)S(1)} collective-permute-done((f32[8,6,16,128]{3,2,1,0:T(8,128)S(1)}, f32[8,6,16,128]{3,2,1,0:T(8,128)S(1)}, u32[]{:S(2)}, u32[]{:S(2)}) %collective-permute-start.11) | collective-permute-done | bytes 393248 | tf_op jit(solution)/shard_map/ppermute | solution.py:394
  82.9 0.1 add.6
  83.0 23.3 %all_to_all.21 = f32[8,6,16,128]{3,2,1,0:T(8,128)S(1)} all-to-all(f32[8,6,16,128]{3,2,1,0:T(8,128)S(1)} %add.6), channel_id=1, replica_groups=mesh['z'=8,'xh'=2,'y'=4,'xl'=2,'c'=2] {'z'}, dimensions={0} | all-to-all | bytes 786432 | tf_op jit(solution)/shard_map/all_to_all | solution.py:454
  106.3 0.1 collective-permute-start.12
  106.4 5.6 %collective-permute-done.12 = f32[1,6,16,128]{3,2,1,0:T(8,128)S(1)} collective-permute-done((f32[1,6,16,128]{3,2,1,0:T(8,128)S(1)}, f32[1,6,16,128]{3,2,1,0:T(8,128)S(1)}, u32[]{:S(2)}, u32[]{:S(2)}) %collective-permute-start.12) | collective-permute-done | bytes 49184 | tf_op jit(solution)/shard_map/ppermute | solution.py:457
  112.0 0.8 broadcast_in_dim.12
  112.7 3.5 %all-to-all-start.3 = ((f32[8,6,16,128]{3,2,1,0:T(8,128)}), f32[8,6,16,128]{3,2,1,0:T(8,128)S(1)}, u32[]{:S(2)}, u32[]{:S(2)}) async-start(f32[8,6,16,128]{3,2,1,0:T(8,128)} %broadcast_in_dim.12), calls=%async_computation.3 | async-start | bytes 786432 | tf_op jit(solution)/shard_map/all_to_all | solution.py:459
  116.2 0.6 reshape.11
  116.8 12.0 %all-to-all-done.3 = f32[8,6,16,128]{3,2,1,0:T(8,128)S(1)} async-done(((f32[8,6,16,128]{3,2,1,0:T(8,128)}), f32[8,6,16,128]{3,2,1,0:T(8,128)S(1)}, u32[]{:S(2)}, u32[]{:S(2)}) %all-to-all-start.3) | async-done | bytes 393248 | tf_op jit(solution)/shard_map/all_to_all | solution.py:459
  128.8 0.8 copy.6
  (4 shorter events, 0.0 us)
Async XLA Ops:
  0.6 13.6 %collective-permute-start = (f32[4,2,128,128]{3,2,1,0:T(8,128)}, f32[4,2,128,128]{3,2,1,0:T(8,128)S(1)}, u32[]{:S(2)}, u32[]{:S(2)}) collective-permute-start(f32[4,2,128,128]{3,2,1,0:T(8,128)} %bitcast.10), channel_id=1, source_target_pairs={{0,1},{1,0},{2,3},{3,2},{4,5},{5,4},{6,7},{7,6},{8,9},{9,8},{10,11... | collective-permute-start | bytes 1572872 | tf_op jit(solution)/shard_map/ppermute | solution.py:394
  0.7 7.7 %collective-permute-start.1 = (f32[3,2,128,128]{3,2,1,0:T(8,128)}, f32[3,2,128,128]{3,2,1,0:T(8,128)S(1)}, u32[]{:S(2)}, u32[]{:S(2)}) collective-permute-start(f32[3,2,128,128]{3,2,1,0:T(8,128)} %c_own.1), channel_id=1, source_target_pairs={{0,1},{1,0},{2,3},{3,2},{4,5},{5,4},{6,7},{7,6},{8,9},{9,8},{10,11... | collective-permute-start | bytes 1179656 | tf_op jit(solution)/shard_map/ppermute | solution.py:394
  1.2 17.5 %collective-permute-start.5 = (f32[3,2,128,128]{3,2,1,0:T(8,128)}, f32[3,2,128,128]{3,2,1,0:T(8,128)S(1)}, u32[]{:S(2)}, u32[]{:S(2)}) collective-permute-start(f32[3,2,128,128]{3,2,1,0:T(8,128)} %c_own.1), channel_id=1, source_target_pairs={{2,16},{3,17},{4,18},{5,19},{6,20},{7,21},{8,22},{9,23},{10,24},{1... | collective-permute-start | bytes 1179656 | tf_op jit(solution)/shard_map/ppermute | solution.py:394
  2.5 16.2 %collective-permute-start.4 = (f32[3,2,128,128]{3,2,1,0:T(8,128)}, f32[3,2,128,128]{3,2,1,0:T(8,128)S(1)}, u32[]{:S(2)}, u32[]{:S(2)}) collective-permute-start(f32[3,2,128,128]{3,2,1,0:T(8,128)} %c_own.1), channel_id=1, source_target_pairs={{0,18},{1,19},{2,20},{3,21},{4,22},{5,23},{6,24},{7,25},{8,26},{9,... | collective-permute-start | bytes 1179656 | tf_op jit(solution)/shard_map/ppermute | solution.py:394
  7.1 18.2 %collective-permute-start.3 = (f32[4,2,128,128]{3,2,1,0:T(8,128)}, f32[4,2,128,128]{3,2,1,0:T(8,128)S(1)}, u32[]{:S(2)}, u32[]{:S(2)}) collective-permute-start(f32[4,2,128,128]{3,2,1,0:T(8,128)} %bitcast.11), channel_id=1, source_target_pairs={{2,0},{3,1},{4,2},{5,3},{6,4},{7,5},{8,6},{9,7},{10,8},{11,9},{12,... | collective-permute-start | bytes 1572872 | tf_op jit(solution)/shard_map/ppermute | solution.py:394
  8.4 17.0 %collective-permute-start.2 = (f32[4,2,128,128]{3,2,1,0:T(8,128)}, f32[4,2,128,128]{3,2,1,0:T(8,128)S(1)}, u32[]{:S(2)}, u32[]{:S(2)}) collective-permute-start(f32[4,2,128,128]{3,2,1,0:T(8,128)} %bitcast.12), channel_id=1, source_target_pairs={{0,2},{1,3},{2,4},{3,5},{4,6},{5,7},{6,8},{7,9},{8,10},{9,11},{10,... | collective-permute-start | bytes 1572872 | tf_op jit(solution)/shard_map/ppermute | solution.py:394
  14.3 0.7 copy-start.1
  15.0 1.0 copy-start.3
  16.0 1.0 copy-start.4
  17.0 12.2 %copy-start.2 = (s32[1,1024]{1,0:T(1,128)S(1)}, s32[1,1024]{1,0:T(1,128)}, u32[]{:S(2)}) copy-start(s32[1,1024]{1,0:T(1,128)} %cells.5) | copy-start | bytes 12292
  25.4 3.8 %collective-permute-start.6 = (f32[4,2,128,128]{3,2,1,0:T(8,128)S(1)}, f32[4,2,128,128]{3,2,1,0:T(8,128)S(1)}, u32[]{:S(2)}, u32[]{:S(2)}) collective-permute-start(f32[4,2,128,128]{3,2,1,0:T(8,128)S(1)} %collective-permute-done.2.p_low), channel_id=1, source_target_pairs={{0,1},{1,0},{2,3},{3,2},{4,5},{5,4},{6,7},{7,6},{8,9},{9,8},{10,11... | collective-permute-start | bytes 1572872 | tf_op jit(solution)/shard_map/ppermute | solution.py:394
  25.4 3.8 %collective-permute-start.7 = (f32[4,2,128,128]{3,2,1,0:T(8,128)S(1)}, f32[4,2,128,128]{3,2,1,0:T(8,128)S(1)}, u32[]{:S(2)}, u32[]{:S(2)}) collective-permute-start(f32[4,2,128,128]{3,2,1,0:T(8,128)S(1)} %collective-permute-done.3.p_high), channel_id=1, source_target_pairs={{0,1},{1,0},{2,3},{3,2},{4,5},{5,4},{6,7},{7,6},{8,9},{9,8},{10,11... | collective-permute-start | bytes 1572872 | tf_op jit(solution)/shard_map/ppermute | solution.py:394
  25.9 2.7 %collective-permute-start.8 = (f32[3,2,128,128]{3,2,1,0:T(8,128)S(1)}, f32[3,2,128,128]{3,2,1,0:T(8,128)S(1)}, u32[]{:S(2)}, u32[]{:S(2)}) collective-permute-start(f32[3,2,128,128]{3,2,1,0:T(8,128)S(1)} %collective-permute-done.4.c_low), channel_id=1, source_target_pairs={{0,1},{1,0},{2,3},{3,2},{4,5},{5,4},{6,7},{7,6},{8,9},{9,8},{10,11... | collective-permute-start | bytes 1179656 | tf_op jit(solution)/shard_map/ppermute | solution.py:394
  25.9 3.3 %collective-permute-start.9 = (f32[3,2,128,128]{3,2,1,0:T(8,128)S(1)}, f32[3,2,128,128]{3,2,1,0:T(8,128)S(1)}, u32[]{:S(2)}, u32[]{:S(2)}) collective-permute-start(f32[3,2,128,128]{3,2,1,0:T(8,128)S(1)} %collective-permute-done.5.c_high), channel_id=1, source_target_pairs={{0,1},{1,0},{2,3},{3,2},{4,5},{5,4},{6,7},{7,6},{8,9},{9,8},{10,11... | collective-permute-start | bytes 1179656 | tf_op jit(solution)/shard_map/ppermute | solution.py:394
  29.2 34.4 %copy-start = (f32[1,4,1024]{2,1,0:T(4,128)S(1)}, f32[1,4,1024]{2,1,0:T(4,128)}, u32[]{:S(2)}) copy-start(f32[1,4,1024]{2,1,0:T(4,128)} %param.6) | copy-start | bytes 49156
  70.4 9.5 %all-to-all-start.1 = ((f32[8,8,128]{2,1,0:T(8,128)}), f32[8,8,128]{2,1,0:T(8,128)S(1)}, u32[]{:S(2)}, u32[]{:S(2)}) async-start(f32[8,8,128]{2,1,0:T(8,128)} %get-tuple-element.59), calls=%async_computation.1 | async-start | bytes 65536 | tf_op jit(solution)/shard_map/all_to_all | solution.py:447
  73.7 1.4 %collective-permute-start.10 = (f32[2,1024]{1,0:T(2,128)S(1)}, f32[2,1024]{1,0:T(2,128)S(1)}, u32[]{:S(2)}, u32[]{:S(2)}) collective-permute-start(f32[2,1024]{1,0:T(2,128)S(1)} %get-tuple-element.64.pred), channel_id=1, source_target_pairs={{0,1},{1,0},{2,3},{3,2},{4,5},{5,4},{6,7},{7,6},{8,9},{9,8},{10,11... | collective-permute-start | bytes 24584 | tf_op jit(solution)/shard_map/ppermute | solution.py:394
  81.1 1.8 %collective-permute-start.11 = (f32[8,6,16,128]{3,2,1,0:T(8,128)S(1)}, f32[8,6,16,128]{3,2,1,0:T(8,128)S(1)}, u32[]{:S(2)}, u32[]{:S(2)}) collective-permute-start(f32[8,6,16,128]{3,2,1,0:T(8,128)S(1)} %get-tuple-element.66), channel_id=1, source_target_pairs={{0,1},{1,0},{2,3},{3,2},{4,5},{5,4},{6,7},{7,6},{8,9},{9,8},{10,11... | collective-permute-start | bytes 1179656 | tf_op jit(solution)/shard_map/ppermute | solution.py:394
  106.3 5.7 %collective-permute-start.12 = (f32[1,6,16,128]{3,2,1,0:T(8,128)S(1)}, f32[1,6,16,128]{3,2,1,0:T(8,128)S(1)}, u32[]{:S(2)}, u32[]{:S(2)}) collective-permute-start(f32[1,6,16,128]{3,2,1,0:T(8,128)S(1)} %bitcast.15), channel_id=1, source_target_pairs={{0,16},{16,0},{1,17},{17,1},{2,18},{18,2},{3,19},{19,3},{4,20},{20... | collective-permute-start | bytes 147464 | tf_op jit(solution)/shard_map/ppermute | solution.py:457
  112.7 16.1 %all-to-all-start.3 = ((f32[8,6,16,128]{3,2,1,0:T(8,128)}), f32[8,6,16,128]{3,2,1,0:T(8,128)S(1)}, u32[]{:S(2)}, u32[]{:S(2)}) async-start(f32[8,6,16,128]{3,2,1,0:T(8,128)} %broadcast_in_dim.12), calls=%async_computation.3 | async-start | bytes 786432 | tf_op jit(solution)/shard_map/all_to_all | solution.py:459

commit v5 on v4

--- a/solution.py
+++ b/solution.py
@@ -300,7 +300,7 @@
         near[...] = deep[:, 3:9]
 
 
-def gradient_kernel(got, a0, a1, a2, pot, pred, pred_pair, kept, given, predicted, adj):
+def gradient_kernel(got, a0, a1, a2, pot, kept, given, adj):
     core = lax.axis_index("c")
     moments = got[0]
     for k in range(1, CHIPS):
@@ -309,8 +309,6 @@
     rows, lanes = pot.shape[2], pot.shape[3]
     row_at = lax.broadcasted_iota(jnp.int32, (rows, lanes), 0)
     lane_at = lax.broadcasted_iota(jnp.int32, (rows, lanes), 1)
-    predicted[pl.ds(core, 1)] = pred[...][None]
-    predicted[pl.ds(1 - core, 1)] = pred_pair[...][None]
     for i in range(6):
         for s in range(2):
             w = [weights[k][s : s + 1, :] for k in range(3)]
@@ -339,7 +337,7 @@
                 target[:, 2 * k + j] = (-0.5 * sums[k]).reshape(target.shape[0], target.shape[2], lanes)
 
 
-def call(kernel, limit, outs, scratch=(), flops=0):
+def call(kernel, limit, outs, scratch=()):
     vmem = pl.BlockSpec(memory_space=pltpu.VMEM)
 
     def run(*args):
@@ -349,7 +347,6 @@
             in_specs=[vmem] * len(args),
             out_specs=tuple([vmem] * len(outs)),
             scratch_shapes=list(scratch),
-            cost_estimate=pl.CostEstimate(flops=flops, bytes_accessed=8 * MEBI, transcendentals=0),
             compiler_params=pltpu.CompilerParams(vmem_limit_bytes=limit * MEBI),
         )(*args)
 
@@ -416,7 +413,6 @@
             ((10 * rows, count), BF16), ((3 * KEPT * rows, count), BF16), f32(2, count),
         ],
         [pltpu.VMEM((2 * lanes, 3 * KEPT * rows), BF16)],
-        flops=10**10,
     )(fields, p_pair, conductivity, c_pair, receivers)
     c_low, c_high, p_sample = lax.optimization_barrier((c_low, c_high, p_sample))
     c_low_pair, c_high_pair = send(c_low, swap), send(c_high, swap)
@@ -443,14 +439,15 @@
         [f32(*six)] * 4 + [f32(2, count), f32(CHIPS, 8, 128)],
         [pltpu.VMEM((3, 2 * lanes, count), BF16)] + [pltpu.VMEM((2, DEEP, rows, lanes), F32)] * 3,
     )(got, observed[0], receivers, hot, kx, ky, kz, dinv, dg, prim, f0, f1, f2)
-    pred_pair = send(pred, swap)
     got = lax.all_to_all(sent, ("y", "xl"), 0, 0, tiled=True)
     slabs = lax.axis_size("z")
     chunks = (slabs, 6, rows // slabs, lanes)
-    kept, given, predicted = call(
-        gradient_kernel, 8, [f32(*chunks), f32(*chunks), f32(2, 2, count)], [pltpu.VMEM(six, F32)]
-    )(got, a0, a1, a2, pot, pred, pred_pair)
+    kept, given = call(gradient_kernel, 8, [f32(*chunks)] * 2, [pltpu.VMEM(six, F32)])(got, a0, a1, a2, pot)
+    given, pred = lax.optimization_barrier((given, pred))
     total = kept + send(given, swap)
+    pred_pair = send(pred, swap)
+    even = lax.axis_index("c") == 0
+    predicted = jnp.where(even, jnp.concatenate([pred, pred_pair]), jnp.concatenate([pred_pair, pred]))
     parts = lax.all_to_all(total, "z", 0, 0, tiled=True)
     share = jnp.sum(parts, axis=0, keepdims=True)
     if high_count > 1:
@@ -458,7 +455,7 @@
     spread = jnp.broadcast_to(share, chunks)
     whole = lax.all_to_all(spread, "z", 0, 0, tiled=True)
     grad = jnp.transpose(whole, (1, 0, 2, 3)).reshape(3, 2, rows, lanes)
-    return grad, predicted.reshape(1, 4, count)
+    return grad, predicted[None]
 
 
 def solution(mesh):

time: 130 us -> 128 us (0.985)
  waiting for transfers between devices: 34.6 us -> 40.9 us
  starting transfers between devices: 21.9 us -> 15.7 us
  blocking collectives: 48.9 us -> 47.5 us
    ppermute x12, waiting for transfers between devices: 12.3 us -> 25.3 us  [send(): return lax.ppermute(x, NAMES, pairs)]
    all_to_all x1 -> x0, waiting for transfers between devices: 4.74 us -> none  [per_device(): got = lax.all_to_all(sent, ('y', 'xl'), 0, 0, tiled=True)]
    ppermute x12, starting transfers between devices: 15 us -> 11.4 us  [send(): return lax.ppermute(x, NAMES, pairs)]
    all_to_all x1 -> x0, starting transfers between devices: 3.34 us -> none  [per_device(): got = lax.all_to_all(sent, ('y', 'xl'), 0, 0, tiled=True)]
    all_to_all x1 -> x2, blocking collectives: 25.7 us -> 24.2 us  [per_device(): got = lax.all_to_all(sent, ('y', 'xl'), 0, 0, tiled=True)]
  transfers between devices with their start and end apart: 15 -> 14, of which waited for: 9 -> 8; matrix products, arithmetic and copies ran while one was open for 0% -> 0% of each run, Pallas kernels for 1% -> 1%
where the time goes in v5:
time: 128 us
  blocking collectives  47.5 us (37%)
  waiting for transfers between devices  40.9 us (32%)
  Pallas kernels  17.9 us (14%)
  starting transfers between devices  15.7 us (12%)
  local copies, waits for them, and re-layouts  4.29 us (3%)
    ppermute x12, waiting for transfers between devices, send(): return lax.ppermute(x, NAMES, pairs)  25.3 us
    all_to_all x2, blocking collectives, per_device(): got = lax.all_to_all(sent, ('y', 'xl'), 0, 0, tiled=True)  24.2 us
    all_to_all x1, blocking collectives, per_device(): parts = lax.all_to_all(total, 'z', 0, 0, tiled=True)  23.3 us
    pallas_call x4, Pallas kernels, run(): pl.pallas_call(kernel, out_shape=tuple((jax.ShapeDtypeStruct(x, kind) for...  17.9 us
    ppermute x12, starting transfers between devices, send(): return lax.ppermute(x, NAMES, pairs)  11.4 us
    all_to_all x1, waiting for transfers between devices, per_device(): whole = lax.all_to_all(spread, 'z', 0, 0, tiled=True)  10.8 us
    ppermute x1, waiting for transfers between devices, per_device(): share = share + lax.ppermute(share, 'xh', [(0, 1), (1, 0)])  4.79 us
    all_to_all x1, starting transfers between devices, per_device(): whole = lax.all_to_all(spread, 'z', 0, 0, tiled=True)  3.45 us
  transfers between devices with their start and end apart: 14, of which 8 were waited for; matrix products, arithmetic and copies ran while one was open for 0% of the time, Pallas kernels for 1%

profile of v5, /device:TPU:4, one launch (start us, length us, event | category | flops | bytes accessed | tf_op | source)
XLA Modules:
  0.0 127.8 jit_solution(4813766843679844)
XLA Ops:
  0.6 0.1 collective-permute-start.1
  0.7 0.5 collective-permute-start
  1.2 3.1 %collective-permute-start.2 = (f32[4,2,128,128]{3,2,1,0:T(8,128)}, f32[4,2,128,128]{3,2,1,0:T(8,128)S(1)}, u32[]{:S(2)}, u32[]{:S(2)}) collective-permute-start(f32[4,2,128,128]{3,2,1,0:T(8,128)} %bitcast.12), channel_id=1, source_target_pairs={{0,2},{1,3},{2,4},{3,5},{4,6},{5,7},{6,8},{7,9},{8,10},{9,11},{10,... | collective-permute-start | bytes 1572872 | tf_op jit(solution)/shard_map/ppermute | solution.py:391
  4.4 1.3 %collective-permute-start.3 = (f32[4,2,128,128]{3,2,1,0:T(8,128)}, f32[4,2,128,128]{3,2,1,0:T(8,128)S(1)}, u32[]{:S(2)}, u32[]{:S(2)}) collective-permute-start(f32[4,2,128,128]{3,2,1,0:T(8,128)} %bitcast.13), channel_id=1, source_target_pairs={{2,0},{3,1},{4,2},{5,3},{6,4},{7,5},{8,6},{9,7},{10,8},{11,9},{12,... | collective-permute-start | bytes 1572872 | tf_op jit(solution)/shard_map/ppermute | solution.py:391
  5.7 3.9 %collective-permute-start.4 = (f32[3,2,128,128]{3,2,1,0:T(8,128)}, f32[3,2,128,128]{3,2,1,0:T(8,128)S(1)}, u32[]{:S(2)}, u32[]{:S(2)}) collective-permute-start(f32[3,2,128,128]{3,2,1,0:T(8,128)} %c_own.1), channel_id=1, source_target_pairs={{0,18},{1,19},{2,20},{3,21},{4,22},{5,23},{6,24},{7,25},{8,26},{9,... | collective-permute-start | bytes 1179656 | tf_op jit(solution)/shard_map/ppermute | solution.py:391
  9.6 0.0 collective-permute-done.1.c_pair
  9.6 1.3 %collective-permute-start.5 = (f32[3,2,128,128]{3,2,1,0:T(8,128)}, f32[3,2,128,128]{3,2,1,0:T(8,128)S(1)}, u32[]{:S(2)}, u32[]{:S(2)}) collective-permute-start(f32[3,2,128,128]{3,2,1,0:T(8,128)} %c_own.1), channel_id=1, source_target_pairs={{2,16},{3,17},{4,18},{5,19},{6,20},{7,21},{8,22},{9,23},{10,24},{1... | collective-permute-start | bytes 1179656 | tf_op jit(solution)/shard_map/ppermute | solution.py:391
  10.9 0.0 collective-permute-done.p_pair
  10.9 0.0 copy-start
  10.9 1.0 copy-done
  11.9 0.0 copy-start.1
  11.9 1.0 copy-done.1
  12.9 0.0 copy-start.2
  12.9 0.7 copy-done.2
  13.6 1.7 %shard_map.59 = (f32[2,4,128,128]{3,2,1,0:T(8,128)S(1)}, f32[4,128,128]{2,1,0:T(8,128)S(1)}, f32[4,128,128]{2,1,0:T(8,128)S(1)}, f32[4,128,128]{2,1,0:T(8,128)S(...) custom-call(f32[4,2,128,128]{3,2,1,0:T(8,128)S(1)} %bitcast.14, ...), custom_call_target="tpu_custom_call" | custom-call | tf_op jit(solution)/shard_map/pallas_call | solution.py:344
  15.4 2.6 %collective-permute-done.4.c_low = f32[3,2,128,128]{3,2,1,0:T(8,128)S(1)} collective-permute-done((f32[3,2,128,128]{3,2,1,0:T(8,128)}, f32[3,2,128,128]{3,2,1,0:T(8,128)S(1)}, u32[]{:S(2)}, u32[]{:S(2)}) %collective-permute-start.4) | collective-permute-done | bytes 393248 | tf_op jit(solution)/shard_map/ppermute | solution.py:391
  17.9 17.1 %collective-permute-done.5.c_high = f32[3,2,128,128]{3,2,1,0:T(8,128)S(1)} collective-permute-done((f32[3,2,128,128]{3,2,1,0:T(8,128)}, f32[3,2,128,128]{3,2,1,0:T(8,128)S(1)}, u32[]{:S(2)}, u32[]{:S(2)}) %collective-permute-start.5) | collective-permute-done | bytes 393248 | tf_op jit(solution)/shard_map/ppermute | solution.py:391
  35.1 0.0 collective-permute-done.2.p_low
  35.1 0.0 collective-permute-done.3.p_high
  35.1 0.0 collective-permute-start.6
  35.1 0.5 collective-permute-start.7
  35.6 0.1 collective-permute-start.8
  35.7 0.4 collective-permute-start.9
  36.1 2.2 %collective-permute-done.8.c_low_pair = f32[3,2,128,128]{3,2,1,0:T(8,128)S(1)} collective-permute-done((f32[3,2,128,128]{3,2,1,0:T(8,128)S(1)}, f32[3,2,128,128]{3,2,1,0:T(8,128)S(1)}, u32[]{:S(2)}, u32[]{:S(2)}) %collective-permute-start.8) | collective-permute-done | bytes 393248 | tf_op jit(solution)/shard_map/ppermute | solution.py:391
  38.3 0.6 collective-permute-done.9.c_high_pair
  38.9 0.0 collective-permute-done.6.p_low_pair
  38.9 0.0 collective-permute-done.7.p_high_pair
  38.9 0.0 copy-done.3
  38.9 0.0 copy-start.4
  38.9 8.7 %shard_map.60 = (f32[12,128,128]{2,1,0:T(8,128)S(1)}, f32[12,128,128]{2,1,0:T(8,128)S(1)}, f32[12,128,128]{2,1,0:T(8,128)S(1)}, f32[12,128,128]{2,1,0:T(8,128)S(...) custom-call(f32[2,4,128,128]{3,2,1,0:T(8,128)S(1)} %get-tuple-elemen, ...), custom_call_target="tpu_custom_call" | custom-call | tf_op jit(solution)/shard_map/pallas_call | solution.py:344
  47.5 15.6 %all_to_all.20.got = f32[8,8,1152]{2,1,0:T(8,128)S(1)} all-to-all(f32[8,8,1152]{2,1,0:T(8,128)S(1)} %get-tuple-element.49), channel_id=1, replica_groups=mesh['z'=8,'xh'=2,'y'=4,'xl'=2,'c'=2] {'y','xl'}, dimensions={0} | all-to-all | bytes 589824 | tf_op jit(solution)/shard_map/all_to_all | solution.py:434
  63.1 0.0 copy-done.4
  63.1 6.2 %shard_map.61 = (f32[2,6,128,128]{3,2,1,0:T(8,128)S(1)}, f32[2,6,128,128]{3,2,1,0:T(8,128)S(1)}, f32[2,6,128,128]{3,2,1,0:T(8,128)S(1)}, f32[2,6,128,128]{3,2,1,...) custom-call(f32[8,8,1152]{2,1,0:T(8,128)S(1)} %all_to_all.20.got, f32[4,1024]{1,0:T(4,128)S(1)} %bitcast.15, ...), custom_call_target="tpu_custom_call" | custom-call | tf_op jit(solution)/shard_map/pallas_call | solution.py:344
  69.4 8.6 %all_to_all.21.got = f32[8,8,128]{2,1,0:T(8,128)S(1)} all-to-all(f32[8,8,128]{2,1,0:T(8,128)S(1)} %get-tuple-element.60), channel_id=1, replica_groups=mesh['z'=8,'xh'=2,'y'=4,'xl'=2,'c'=2] {'y','xl'}, dimensions={0} | all-to-all | bytes 65536 | tf_op jit(solution)/shard_map/all_to_all | solution.py:442
  78.0 1.3 shard_map.62
  79.3 0.1 collective-permute-start.10
  79.4 1.7 %collective-permute-done.10 = f32[8,6,16,128]{3,2,1,0:T(8,128)S(1)} collective-permute-done((f32[8,6,16,128]{3,2,1,0:T(8,128)S(1)}, f32[8,6,16,128]{3,2,1,0:T(8,128)S(1)}, u32[]{:S(2)}, u32[]{:S(2)}) %collective-permute-start.10) | collective-permute-done | bytes 393248 | tf_op jit(solution)/shard_map/ppermute | solution.py:391
  81.1 0.1 add.6
  81.1 23.3 %all_to_all.22 = f32[8,6,16,128]{3,2,1,0:T(8,128)S(1)} all-to-all(f32[8,6,16,128]{3,2,1,0:T(8,128)S(1)} %add.6), channel_id=1, replica_groups=mesh['z'=8,'xh'=2,'y'=4,'xl'=2,'c'=2] {'z'}, dimensions={0} | all-to-all | bytes 786432 | tf_op jit(solution)/shard_map/all_to_all | solution.py:451
  104.4 0.9 collective-permute-start.11
  105.3 4.8 %collective-permute-done.11 = f32[1,6,16,128]{3,2,1,0:T(8,128)S(1)} collective-permute-done((f32[1,6,16,128]{3,2,1,0:T(8,128)S(1)}, f32[1,6,16,128]{3,2,1,0:T(8,128)S(1)}, u32[]{:S(2)}, u32[]{:S(2)}) %collective-permute-start.11) | collective-permute-done | bytes 49184 | tf_op jit(solution)/shard_map/ppermute | solution.py:454
  110.1 0.8 broadcast_in_dim.13
  110.9 3.5 %all-to-all-start.3 = ((f32[8,6,16,128]{3,2,1,0:T(8,128)}), f32[8,6,16,128]{3,2,1,0:T(8,128)S(1)}, u32[]{:S(2)}, u32[]{:S(2)}) async-start(f32[8,6,16,128]{3,2,1,0:T(8,128)} %broadcast_in_dim.13), calls=%async_computation.3 | async-start | bytes 786432 | tf_op jit(solution)/shard_map/all_to_all | solution.py:456
  114.4 0.1 collective-permute-start.12
  114.5 1.2 collective-permute-done.12
  115.6 0.6 maximum_select_fusion
  116.2 10.8 %all-to-all-done.3 = f32[8,6,16,128]{3,2,1,0:T(8,128)S(1)} async-done(((f32[8,6,16,128]{3,2,1,0:T(8,128)}), f32[8,6,16,128]{3,2,1,0:T(8,128)S(1)}, u32[]{:S(2)}, u32[]{:S(2)}) %all-to-all-start.3) | async-done | bytes 393248 | tf_op jit(solution)/shard_map/all_to_all | solution.py:456
  127.0 0.8 copy.6
  (3 shorter events, 0.0 us)
Async XLA Ops:
  0.6 8.9 %collective-permute-start.1 = (f32[3,2,128,128]{3,2,1,0:T(8,128)}, f32[3,2,128,128]{3,2,1,0:T(8,128)S(1)}, u32[]{:S(2)}, u32[]{:S(2)}) collective-permute-start(f32[3,2,128,128]{3,2,1,0:T(8,128)} %c_own.1), channel_id=1, source_target_pairs={{0,1},{1,0},{2,3},{3,2},{4,5},{5,4},{6,7},{7,6},{8,9},{9,8},{10,11... | collective-permute-start | bytes 1179656 | tf_op jit(solution)/shard_map/ppermute | solution.py:391
  0.7 10.2 %collective-permute-start = (f32[4,2,128,128]{3,2,1,0:T(8,128)}, f32[4,2,128,128]{3,2,1,0:T(8,128)S(1)}, u32[]{:S(2)}, u32[]{:S(2)}) collective-permute-start(f32[4,2,128,128]{3,2,1,0:T(8,128)} %bitcast.11), channel_id=1, source_target_pairs={{0,1},{1,0},{2,3},{3,2},{4,5},{5,4},{6,7},{7,6},{8,9},{9,8},{10,11... | collective-permute-start | bytes 1572872 | tf_op jit(solution)/shard_map/ppermute | solution.py:391
  1.2 33.8 %collective-permute-start.2 = (f32[4,2,128,128]{3,2,1,0:T(8,128)}, f32[4,2,128,128]{3,2,1,0:T(8,128)S(1)}, u32[]{:S(2)}, u32[]{:S(2)}) collective-permute-start(f32[4,2,128,128]{3,2,1,0:T(8,128)} %bitcast.12), channel_id=1, source_target_pairs={{0,2},{1,3},{2,4},{3,5},{4,6},{5,7},{6,8},{7,9},{8,10},{9,11},{10,... | collective-permute-start | bytes 1572872 | tf_op jit(solution)/shard_map/ppermute | solution.py:391
  4.4 30.7 %collective-permute-start.3 = (f32[4,2,128,128]{3,2,1,0:T(8,128)}, f32[4,2,128,128]{3,2,1,0:T(8,128)S(1)}, u32[]{:S(2)}, u32[]{:S(2)}) collective-permute-start(f32[4,2,128,128]{3,2,1,0:T(8,128)} %bitcast.13), channel_id=1, source_target_pairs={{2,0},{3,1},{4,2},{5,3},{6,4},{7,5},{8,6},{9,7},{10,8},{11,9},{12,... | collective-permute-start | bytes 1572872 | tf_op jit(solution)/shard_map/ppermute | solution.py:391
  5.7 12.3 %collective-permute-start.4 = (f32[3,2,128,128]{3,2,1,0:T(8,128)}, f32[3,2,128,128]{3,2,1,0:T(8,128)S(1)}, u32[]{:S(2)}, u32[]{:S(2)}) collective-permute-start(f32[3,2,128,128]{3,2,1,0:T(8,128)} %c_own.1), channel_id=1, source_target_pairs={{0,18},{1,19},{2,20},{3,21},{4,22},{5,23},{6,24},{7,25},{8,26},{9,... | collective-permute-start | bytes 1179656 | tf_op jit(solution)/shard_map/ppermute | solution.py:391
  9.6 25.5 %collective-permute-start.5 = (f32[3,2,128,128]{3,2,1,0:T(8,128)}, f32[3,2,128,128]{3,2,1,0:T(8,128)S(1)}, u32[]{:S(2)}, u32[]{:S(2)}) collective-permute-start(f32[3,2,128,128]{3,2,1,0:T(8,128)} %c_own.1), channel_id=1, source_target_pairs={{2,16},{3,17},{4,18},{5,19},{6,20},{7,21},{8,22},{9,23},{10,24},{1... | collective-permute-start | bytes 1179656 | tf_op jit(solution)/shard_map/ppermute | solution.py:391
  10.9 1.0 copy-start
  11.9 1.0 copy-start.1
  12.9 0.7 copy-start.2
  13.6 25.2 %copy-start.3 = (s32[1,1024]{1,0:T(1,128)S(1)}, s32[1,1024]{1,0:T(1,128)}, u32[]{:S(2)}) copy-start(s32[1,1024]{1,0:T(1,128)} %cells.5) | copy-start | bytes 12292
  35.1 3.8 %collective-permute-start.6 = (f32[4,2,128,128]{3,2,1,0:T(8,128)S(1)}, f32[4,2,128,128]{3,2,1,0:T(8,128)S(1)}, u32[]{:S(2)}, u32[]{:S(2)}) collective-permute-start(f32[4,2,128,128]{3,2,1,0:T(8,128)S(1)} %collective-permute-done.2.p_low), channel_id=1, source_target_pairs={{0,1},{1,0},{2,3},{3,2},{4,5},{5,4},{6,7},{7,6},{8,9},{9,8},{10,11... | collective-permute-start | bytes 1572872 | tf_op jit(solution)/shard_map/ppermute | solution.py:391
  35.1 3.8 %collective-permute-start.7 = (f32[4,2,128,128]{3,2,1,0:T(8,128)S(1)}, f32[4,2,128,128]{3,2,1,0:T(8,128)S(1)}, u32[]{:S(2)}, u32[]{:S(2)}) collective-permute-start(f32[4,2,128,128]{3,2,1,0:T(8,128)S(1)} %collective-permute-done.3.p_high), channel_id=1, source_target_pairs={{0,1},{1,0},{2,3},{3,2},{4,5},{5,4},{6,7},{7,6},{8,9},{9,8},{10,11... | collective-permute-start | bytes 1572872 | tf_op jit(solution)/shard_map/ppermute | solution.py:391
  35.6 2.7 %collective-permute-start.8 = (f32[3,2,128,128]{3,2,1,0:T(8,128)S(1)}, f32[3,2,128,128]{3,2,1,0:T(8,128)S(1)}, u32[]{:S(2)}, u32[]{:S(2)}) collective-permute-start(f32[3,2,128,128]{3,2,1,0:T(8,128)S(1)} %collective-permute-done.4.c_low), channel_id=1, source_target_pairs={{0,1},{1,0},{2,3},{3,2},{4,5},{5,4},{6,7},{7,6},{8,9},{9,8},{10,11... | collective-permute-start | bytes 1179656 | tf_op jit(solution)/shard_map/ppermute | solution.py:391
  35.7 3.2 %collective-permute-start.9 = (f32[3,2,128,128]{3,2,1,0:T(8,128)S(1)}, f32[3,2,128,128]{3,2,1,0:T(8,128)S(1)}, u32[]{:S(2)}, u32[]{:S(2)}) collective-permute-start(f32[3,2,128,128]{3,2,1,0:T(8,128)S(1)} %collective-permute-done.5.c_high), channel_id=1, source_target_pairs={{0,1},{1,0},{2,3},{3,2},{4,5},{5,4},{6,7},{7,6},{8,9},{9,8},{10,11... | collective-permute-start | bytes 1179656 | tf_op jit(solution)/shard_map/ppermute | solution.py:391
  38.9 24.3 %copy-start.4 = (f32[1,4,1024]{2,1,0:T(4,128)S(1)}, f32[1,4,1024]{2,1,0:T(4,128)}, u32[]{:S(2)}) copy-start(f32[1,4,1024]{2,1,0:T(4,128)} %param.6) | copy-start | bytes 49156
  79.3 1.8 %collective-permute-start.10 = (f32[8,6,16,128]{3,2,1,0:T(8,128)S(1)}, f32[8,6,16,128]{3,2,1,0:T(8,128)S(1)}, u32[]{:S(2)}, u32[]{:S(2)}) collective-permute-start(f32[8,6,16,128]{3,2,1,0:T(8,128)S(1)} %get-tuple-element.68), channel_id=1, source_target_pairs={{0,1},{1,0},{2,3},{3,2},{4,5},{5,4},{6,7},{7,6},{8,9},{9,8},{10,11... | collective-permute-start | bytes 1179656 | tf_op jit(solution)/shard_map/ppermute | solution.py:391
  104.4 5.7 %collective-permute-start.11 = (f32[1,6,16,128]{3,2,1,0:T(8,128)S(1)}, f32[1,6,16,128]{3,2,1,0:T(8,128)S(1)}, u32[]{:S(2)}, u32[]{:S(2)}) collective-permute-start(f32[1,6,16,128]{3,2,1,0:T(8,128)S(1)} %bitcast.18), channel_id=1, source_target_pairs={{0,16},{16,0},{1,17},{17,1},{2,18},{18,2},{3,19},{19,3},{4,20},{20... | collective-permute-start | bytes 147464 | tf_op jit(solution)/shard_map/ppermute | solution.py:454
  110.9 16.1 %all-to-all-start.3 = ((f32[8,6,16,128]{3,2,1,0:T(8,128)}), f32[8,6,16,128]{3,2,1,0:T(8,128)S(1)}, u32[]{:S(2)}, u32[]{:S(2)}) async-start(f32[8,6,16,128]{3,2,1,0:T(8,128)} %broadcast_in_dim.13), calls=%async_computation.3 | async-start | bytes 786432 | tf_op jit(solution)/shard_map/all_to_all | solution.py:456
  114.4 1.3 collective-permute-start.12

commit v6 on v5

--- a/solution.py
+++ b/solution.py
@@ -12,6 +12,7 @@
 DEEP = 12
 KEPT = 4
 CHIPS = 8
+LANES = 128
 
 
 def pieces_of(values):
@@ -50,7 +51,7 @@
                 target[s, i] = source[s, i] - dinv[i] * neighbours(source, s, i, kx, ky, kz)
             return carry
 
-        lax.fori_loop(first, last + 1, body, 0)
+        lax.fori_loop(first, last + 1, body, 0, unroll=True)
 
     apply_planes(t0, t1, 2, 9)
     apply_planes(t1, t2, 3, 8)
@@ -74,7 +75,7 @@
         return tuple(sums)
 
     zero = jnp.zeros((8, t0.shape[3]), F32)
-    sums = lax.fori_loop(4, 8, body, (zero,) * (11 * sources))
+    sums = lax.fori_loop(4, 8, body, (zero,) * (11 * sources), unroll=True)
     row_at = lax.broadcasted_iota(jnp.int32, (8, 128), 0)
     lane_at = lax.broadcasted_iota(jnp.int32, (8, 128), 1)
     packed = jnp.zeros((8, 128), F32)
@@ -131,8 +132,20 @@
     return up_y, up_z, top_y + low_y + top_z + low_z
 
 
-def own_kernel(p_own, p_pair, c_own, c_pair, cells, prim, first, ky, kz, plane_dg, hot, hot_own, sample, left):
+def hot_kernel(cells, hot, hot_own):
     block = 2 * lax.axis_index("y") + lax.axis_index("xl")
+    rows = hot.shape[0] // 10
+    row_of = cells[...] // LANES
+    for i in range(10):
+        rows_hot = one_hot(rows, (4 * block - 3 + i) * rows, row_of)
+        rows_hot = jnp.where(rows_hot, 1.0, 0.0).astype(BF16)
+        hot[pl.ds(i * rows, rows)] = rows_hot
+        if 3 <= i < 7:
+            for piece in range(3):
+                hot_own[pl.ds((piece * KEPT + i - 3) * rows, rows)] = rows_hot
+
+
+def own_kernel(p_own, p_pair, c_own, c_pair, cells, hot_own, prim, first, ky, kz, plane_dg, sample, left):
     core = lax.axis_index("c")
     here = pl.ds(2 * core, 2)
     other = pl.ds(2 - 2 * core, 2)
@@ -148,15 +161,7 @@
             kz[base + j] = up_z
             plane_dg[base + j] = part
     picked = cells[...]
-    row_of = picked // lanes
-    lane_of = picked - row_of * lanes
-    for i in range(10):
-        rows_hot = one_hot(rows, (4 * block - 3 + i) * rows, row_of)
-        rows_hot = jnp.where(rows_hot, 1.0, 0.0).astype(BF16)
-        hot[pl.ds(i * rows, rows)] = rows_hot
-        if 3 <= i < 7:
-            for piece in range(3):
-                hot_own[pl.ds((piece * KEPT + i - 3) * rows, rows)] = rows_hot
+    lane_of = picked - (picked // lanes) * lanes
     gather([(prim, 0)], left, hot_own, one_hot(lanes, 0, lane_of), sample)
 
 
@@ -241,7 +246,7 @@
             t0[s, i] = inverse * total
         return carry
 
-    lax.fori_loop(1, 11, right_side, 0)
+    lax.fori_loop(1, 11, right_side, 0, unroll=True)
     moments = krylov(t0, t1, t2, kx, ky, kz, dinv, dg)
 
     picked = cells[...]
@@ -396,8 +401,6 @@
     p_high = send(fields, step(-1, False))
     c_low = send(conductivity, step(1, True))
     c_high = send(conductivity, step(-1, True))
-    p_pair = send(fields, swap)
-    c_pair = send(conductivity, swap)
 
     rows, lanes = primary.shape[3], primary.shape[4]
     count = receivers.shape[1]
@@ -405,15 +408,17 @@
     deep = f32(DEEP, rows, lanes)
     pairs = f32(2, DEEP, rows, lanes)
     four = f32(KEPT, rows, lanes)
-    p_mid, c_mid, ky_mid, kz_mid, dg_mid, hot, hot_own, p_sample = call(
+    hot, hot_own = call(
+        hot_kernel, 4, [((10 * rows, count), BF16), ((3 * KEPT * rows, count), BF16)]
+    )(receivers)
+    own_c, p_pair = lax.optimization_barrier((conductivity, send(fields, swap)))
+    c_pair = send(own_c, swap)
+    p_mid, c_mid, ky_mid, kz_mid, dg_mid, p_sample = call(
         own_kernel,
-        14,
-        [
-            f32(2, KEPT, rows, lanes), four, four, four, four,
-            ((10 * rows, count), BF16), ((3 * KEPT * rows, count), BF16), f32(2, count),
-        ],
+        8,
+        [f32(2, KEPT, rows, lanes), four, four, four, four, f32(2, count)],
         [pltpu.VMEM((2 * lanes, 3 * KEPT * rows), BF16)],
-    )(fields, p_pair, conductivity, c_pair, receivers)
+    )(fields, p_pair, conductivity, c_pair, receivers, hot_own)
     c_low, c_high, p_sample = lax.optimization_barrier((c_low, c_high, p_sample))
     c_low_pair, c_high_pair = send(c_low, swap), send(c_high, swap)
     p_low, p_high, p_sample = lax.optimization_barrier((p_low, p_high, p_sample))

time: 128 us -> 126 us (0.984)
  Pallas kernels: 17.9 us -> 15.9 us
    pallas_call x4 -> x5, Pallas kernels: 17.9 us -> 15.9 us  [run(): pl.pallas_call(kernel, out_shape=tuple((jax.ShapeDtypeStruct(x, kind) for...]
where the time goes in v6:
time: 126 us
  blocking collectives  47.5 us (38%)
  waiting for transfers between devices  41.1 us (33%)
  Pallas kernels  15.9 us (13%)
  starting transfers between devices  15.4 us (12%)
  local copies, waits for them, and re-layouts  4.29 us (3%)
    ppermute x12, waiting for transfers between devices, send(): return lax.ppermute(x, NAMES, pairs)  25.5 us
    all_to_all x2, blocking collectives, per_device(): got = lax.all_to_all(sent, ('y', 'xl'), 0, 0, tiled=True)  24.2 us
    all_to_all x1, blocking collectives, per_device(): parts = lax.all_to_all(total, 'z', 0, 0, tiled=True)  23.2 us
    pallas_call x5, Pallas kernels, run(): pl.pallas_call(kernel, out_shape=tuple((jax.ShapeDtypeStruct(x, kind) for...  15.9 us
    ppermute x12, starting transfers between devices, send(): return lax.ppermute(x, NAMES, pairs)  11 us
    all_to_all x1, waiting for transfers between devices, per_device(): whole = lax.all_to_all(spread, 'z', 0, 0, tiled=True)  10.8 us
    ppermute x1, waiting for transfers between devices, per_device(): share = share + lax.ppermute(share, 'xh', [(0, 1), (1, 0)])  4.78 us
    all_to_all x1, starting transfers between devices, per_device(): whole = lax.all_to_all(spread, 'z', 0, 0, tiled=True)  3.45 us
  transfers between devices with their start and end apart: 14, of which 8 were waited for; matrix products, arithmetic and copies ran while one was open for 0% of the time, Pallas kernels for 1%

profile of v6, /device:TPU:4, one launch (start us, length us, event | category | flops | bytes accessed | tf_op | source)
XLA Modules:
  0.0 125.6 jit_solution(15241040649382579694)
XLA Ops:
  0.6 0.1 collective-permute-start
  0.7 3.1 %collective-permute-start.2 = (f32[4,2,128,128]{3,2,1,0:T(8,128)}, f32[4,2,128,128]{3,2,1,0:T(8,128)S(1)}, u32[]{:S(2)}, u32[]{:S(2)}) collective-permute-start(f32[4,2,128,128]{3,2,1,0:T(8,128)} %bitcast.12), channel_id=1, source_target_pairs={{0,2},{1,3},{2,4},{3,5},{4,6},{5,7},{6,8},{7,9},{8,10},{9,11},{10,... | collective-permute-start | bytes 1572872 | tf_op jit(solution)/shard_map/ppermute | solution.py:396
  3.9 1.3 %collective-permute-start.3 = (f32[4,2,128,128]{3,2,1,0:T(8,128)}, f32[4,2,128,128]{3,2,1,0:T(8,128)S(1)}, u32[]{:S(2)}, u32[]{:S(2)}) collective-permute-start(f32[4,2,128,128]{3,2,1,0:T(8,128)} %bitcast.13), channel_id=1, source_target_pairs={{2,0},{3,1},{4,2},{5,3},{6,4},{7,5},{8,6},{9,7},{10,8},{11,9},{12,... | collective-permute-start | bytes 1572872 | tf_op jit(solution)/shard_map/ppermute | solution.py:396
  5.2 0.0 collective-permute-done.p_pair
  5.2 0.3 collective-permute-start.1
  5.5 3.7 %collective-permute-start.4 = (f32[3,2,128,128]{3,2,1,0:T(8,128)}, f32[3,2,128,128]{3,2,1,0:T(8,128)S(1)}, u32[]{:S(2)}, u32[]{:S(2)}) collective-permute-start(f32[3,2,128,128]{3,2,1,0:T(8,128)} %c_own.1), channel_id=1, source_target_pairs={{0,18},{1,19},{2,20},{3,21},{4,22},{5,23},{6,24},{7,25},{8,26},{9,... | collective-permute-start | bytes 1179656 | tf_op jit(solution)/shard_map/ppermute | solution.py:396
  9.2 1.3 %collective-permute-start.5 = (f32[3,2,128,128]{3,2,1,0:T(8,128)}, f32[3,2,128,128]{3,2,1,0:T(8,128)S(1)}, u32[]{:S(2)}, u32[]{:S(2)}) collective-permute-start(f32[3,2,128,128]{3,2,1,0:T(8,128)} %c_own.1), channel_id=1, source_target_pairs={{2,16},{3,17},{4,18},{5,19},{6,20},{7,21},{8,22},{9,23},{10,24},{1... | collective-permute-start | bytes 1179656 | tf_op jit(solution)/shard_map/ppermute | solution.py:396
  10.5 0.0 copy-start.2
  10.5 0.7 copy-done.2
  11.2 0.5 shard_map.59
  11.7 0.0 collective-permute-done.1.c_pair
  11.8 0.0 copy-start
  11.8 1.0 copy-done
  12.8 1.0 copy-done.1
  13.8 1.3 %shard_map.60 = (f32[2,4,128,128]{3,2,1,0:T(8,128)S(1)}, f32[4,128,128]{2,1,0:T(8,128)S(1)}, f32[4,128,128]{2,1,0:T(8,128)S(1)}, f32[4,128,128]{2,1,0:T(8,128)S(...) custom-call(f32[4,2,128,128]{3,2,1,0:T(8,128)S(1)} %bitcast.14, ...), custom_call_target="tpu_custom_call" | custom-call | tf_op jit(solution)/shard_map/pallas_call | solution.py:349
  15.1 3.4 %collective-permute-done.4.c_low = f32[3,2,128,128]{3,2,1,0:T(8,128)S(1)} collective-permute-done((f32[3,2,128,128]{3,2,1,0:T(8,128)}, f32[3,2,128,128]{3,2,1,0:T(8,128)S(1)}, u32[]{:S(2)}, u32[]{:S(2)}) %collective-permute-start.4) | collective-permute-done | bytes 393248 | tf_op jit(solution)/shard_map/ppermute | solution.py:396
  18.5 16.5 %collective-permute-done.5.c_high = f32[3,2,128,128]{3,2,1,0:T(8,128)S(1)} collective-permute-done((f32[3,2,128,128]{3,2,1,0:T(8,128)}, f32[3,2,128,128]{3,2,1,0:T(8,128)S(1)}, u32[]{:S(2)}, u32[]{:S(2)}) %collective-permute-start.5) | collective-permute-done | bytes 393248 | tf_op jit(solution)/shard_map/ppermute | solution.py:396
  35.0 0.0 collective-permute-done.2.p_low
  35.0 0.0 collective-permute-done.3.p_high
  35.0 0.0 collective-permute-start.6
  35.0 0.5 collective-permute-start.7
  35.5 0.1 collective-permute-start.8
  35.6 0.4 collective-permute-start.9
  36.0 2.2 %collective-permute-done.8.c_low_pair = f32[3,2,128,128]{3,2,1,0:T(8,128)S(1)} collective-permute-done((f32[3,2,128,128]{3,2,1,0:T(8,128)S(1)}, f32[3,2,128,128]{3,2,1,0:T(8,128)S(1)}, u32[]{:S(2)}, u32[]{:S(2)}) %collective-permute-start.8) | collective-permute-done | bytes 393248 | tf_op jit(solution)/shard_map/ppermute | solution.py:396
  38.2 0.6 collective-permute-done.9.c_high_pair
  38.8 0.0 collective-permute-done.6.p_low_pair
  38.8 0.0 collective-permute-done.7.p_high_pair
  38.8 0.0 copy-done.3
  38.8 0.0 copy-start.4
  38.8 7.3 %shard_map.61 = (f32[12,128,128]{2,1,0:T(8,128)S(1)}, f32[12,128,128]{2,1,0:T(8,128)S(1)}, f32[12,128,128]{2,1,0:T(8,128)S(1)}, f32[12,128,128]{2,1,0:T(8,128)S(...) custom-call(f32[2,4,128,128]{3,2,1,0:T(8,128)S(1)} %get-tuple-elemen, ...), custom_call_target="tpu_custom_call" | custom-call | tf_op jit(solution)/shard_map/pallas_call | solution.py:349
  46.1 15.6 %all_to_all.20.got = f32[8,8,1152]{2,1,0:T(8,128)S(1)} all-to-all(f32[8,8,1152]{2,1,0:T(8,128)S(1)} %get-tuple-element.53), channel_id=1, replica_groups=mesh['z'=8,'xh'=2,'y'=4,'xl'=2,'c'=2] {'y','xl'}, dimensions={0} | all-to-all | bytes 589824 | tf_op jit(solution)/shard_map/all_to_all | solution.py:439
  61.7 0.0 copy-done.4
  61.7 5.4 %shard_map.62 = (f32[2,6,128,128]{3,2,1,0:T(8,128)S(1)}, f32[2,6,128,128]{3,2,1,0:T(8,128)S(1)}, f32[2,6,128,128]{3,2,1,0:T(8,128)S(1)}, f32[2,6,128,128]{3,2,1,...) custom-call(f32[8,8,1152]{2,1,0:T(8,128)S(1)} %all_to_all.20.got, f32[4,1024]{1,0:T(4,128)S(1)} %bitcast.15, ...), custom_call_target="tpu_custom_call" | custom-call | tf_op jit(solution)/shard_map/pallas_call | solution.py:349
  67.2 8.6 %all_to_all.21.got = f32[8,8,128]{2,1,0:T(8,128)S(1)} all-to-all(f32[8,8,128]{2,1,0:T(8,128)S(1)} %get-tuple-element.64), channel_id=1, replica_groups=mesh['z'=8,'xh'=2,'y'=4,'xl'=2,'c'=2] {'y','xl'}, dimensions={0} | all-to-all | bytes 65536 | tf_op jit(solution)/shard_map/all_to_all | solution.py:447
  75.8 1.3 %shard_map.63 = (f32[8,6,16,128]{3,2,1,0:T(8,128)S(1)}, f32[8,6,16,128]{3,2,1,0:T(8,128)S(1)}) custom-call(f32[8,8,128]{2,1,0:T(8,128)S(1)} %all_to_all.21.got, f32[2,6,128,128]{3,2,1,0:T(8,128)S(1)} %get-tuple-element.65.a0, f32[2,6,128,128]{3,2,1,0:T(8,128)S(1)} %get-tuple-element.66.a1, f32[2,6,128,128]{3,2,1,0:T(8,128)S(1)} %get-tuple-element.67.a2, ...), custom_call_target="tpu_custom_call" | custom-call | tf_op jit(solution)/shard_map/pallas_call | solution.py:349
  77.1 0.1 collective-permute-start.10
  77.2 1.7 %collective-permute-done.10 = f32[8,6,16,128]{3,2,1,0:T(8,128)S(1)} collective-permute-done((f32[8,6,16,128]{3,2,1,0:T(8,128)S(1)}, f32[8,6,16,128]{3,2,1,0:T(8,128)S(1)}, u32[]{:S(2)}, u32[]{:S(2)}) %collective-permute-start.10) | collective-permute-done | bytes 393248 | tf_op jit(solution)/shard_map/ppermute | solution.py:396
  78.9 0.1 add.6
  78.9 23.2 %all_to_all.22 = f32[8,6,16,128]{3,2,1,0:T(8,128)S(1)} all-to-all(f32[8,6,16,128]{3,2,1,0:T(8,128)S(1)} %add.6), channel_id=1, replica_groups=mesh['z'=8,'xh'=2,'y'=4,'xl'=2,'c'=2] {'z'}, dimensions={0} | all-to-all | bytes 786432 | tf_op jit(solution)/shard_map/all_to_all | solution.py:456
  102.2 0.9 collective-permute-start.11
  103.1 4.8 %collective-permute-done.11 = f32[1,6,16,128]{3,2,1,0:T(8,128)S(1)} collective-permute-done((f32[1,6,16,128]{3,2,1,0:T(8,128)S(1)}, f32[1,6,16,128]{3,2,1,0:T(8,128)S(1)}, u32[]{:S(2)}, u32[]{:S(2)}) %collective-permute-start.11) | collective-permute-done | bytes 49184 | tf_op jit(solution)/shard_map/ppermute | solution.py:459
  107.9 0.8 broadcast_in_dim.13
  108.7 3.5 %all-to-all-start.3 = ((f32[8,6,16,128]{3,2,1,0:T(8,128)}), f32[8,6,16,128]{3,2,1,0:T(8,128)S(1)}, u32[]{:S(2)}, u32[]{:S(2)}) async-start(f32[8,6,16,128]{3,2,1,0:T(8,128)} %broadcast_in_dim.13), calls=%async_computation.3 | async-start | bytes 786432 | tf_op jit(solution)/shard_map/all_to_all | solution.py:461
  112.1 0.1 collective-permute-start.12
  112.3 1.2 collective-permute-done.12
  113.4 0.6 maximum_select_fusion
  114.0 10.8 %all-to-all-done.3 = f32[8,6,16,128]{3,2,1,0:T(8,128)S(1)} async-done(((f32[8,6,16,128]{3,2,1,0:T(8,128)}), f32[8,6,16,128]{3,2,1,0:T(8,128)S(1)}, u32[]{:S(2)}, u32[]{:S(2)}) %all-to-all-start.3) | async-done | bytes 393248 | tf_op jit(solution)/shard_map/all_to_all | solution.py:461
  124.8 0.8 copy.6
  (4 shorter events, 0.0 us)
Async XLA Ops:
  0.6 4.5 %collective-permute-start = (f32[4,2,128,128]{3,2,1,0:T(8,128)}, f32[4,2,128,128]{3,2,1,0:T(8,128)S(1)}, u32[]{:S(2)}, u32[]{:S(2)}) collective-permute-start(f32[4,2,128,128]{3,2,1,0:T(8,128)} %bitcast.11), channel_id=1, source_target_pairs={{0,1},{1,0},{2,3},{3,2},{4,5},{5,4},{6,7},{7,6},{8,9},{9,8},{10,11... | collective-permute-start | bytes 1572872 | tf_op jit(solution)/shard_map/ppermute | solution.py:396
  0.7 34.2 %collective-permute-start.2 = (f32[4,2,128,128]{3,2,1,0:T(8,128)}, f32[4,2,128,128]{3,2,1,0:T(8,128)S(1)}, u32[]{:S(2)}, u32[]{:S(2)}) collective-permute-start(f32[4,2,128,128]{3,2,1,0:T(8,128)} %bitcast.12), channel_id=1, source_target_pairs={{0,2},{1,3},{2,4},{3,5},{4,6},{5,7},{6,8},{7,9},{8,10},{9,11},{10,... | collective-permute-start | bytes 1572872 | tf_op jit(solution)/shard_map/ppermute | solution.py:396
  3.9 31.1 %collective-permute-start.3 = (f32[4,2,128,128]{3,2,1,0:T(8,128)}, f32[4,2,128,128]{3,2,1,0:T(8,128)S(1)}, u32[]{:S(2)}, u32[]{:S(2)}) collective-permute-start(f32[4,2,128,128]{3,2,1,0:T(8,128)} %bitcast.13), channel_id=1, source_target_pairs={{2,0},{3,1},{4,2},{5,3},{6,4},{7,5},{8,6},{9,7},{10,8},{11,9},{12,... | collective-permute-start | bytes 1572872 | tf_op jit(solution)/shard_map/ppermute | solution.py:396
  5.2 6.6 %collective-permute-start.1 = (f32[3,2,128,128]{3,2,1,0:T(8,128)}, f32[3,2,128,128]{3,2,1,0:T(8,128)S(1)}, u32[]{:S(2)}, u32[]{:S(2)}) collective-permute-start(f32[3,2,128,128]{3,2,1,0:T(8,128)} %c_own.1), channel_id=1, source_target_pairs={{0,1},{1,0},{2,3},{3,2},{4,5},{5,4},{6,7},{7,6},{8,9},{9,8},{10,11... | collective-permute-start | bytes 1179656 | tf_op jit(solution)/shard_map/ppermute | solution.py:396
  5.5 13.0 %collective-permute-start.4 = (f32[3,2,128,128]{3,2,1,0:T(8,128)}, f32[3,2,128,128]{3,2,1,0:T(8,128)S(1)}, u32[]{:S(2)}, u32[]{:S(2)}) collective-permute-start(f32[3,2,128,128]{3,2,1,0:T(8,128)} %c_own.1), channel_id=1, source_target_pairs={{0,18},{1,19},{2,20},{3,21},{4,22},{5,23},{6,24},{7,25},{8,26},{9,... | collective-permute-start | bytes 1179656 | tf_op jit(solution)/shard_map/ppermute | solution.py:396
  9.2 25.8 %collective-permute-start.5 = (f32[3,2,128,128]{3,2,1,0:T(8,128)}, f32[3,2,128,128]{3,2,1,0:T(8,128)S(1)}, u32[]{:S(2)}, u32[]{:S(2)}) collective-permute-start(f32[3,2,128,128]{3,2,1,0:T(8,128)} %c_own.1), channel_id=1, source_target_pairs={{2,16},{3,17},{4,18},{5,19},{6,20},{7,21},{8,22},{9,23},{10,24},{1... | collective-permute-start | bytes 1179656 | tf_op jit(solution)/shard_map/ppermute | solution.py:396
  10.5 0.7 copy-start.2
  11.8 1.0 copy-start
  12.8 1.0 copy-start.1
  13.8 25.0 %copy-start.3 = (s32[1,1024]{1,0:T(1,128)S(1)}, s32[1,1024]{1,0:T(1,128)}, u32[]{:S(2)}) copy-start(s32[1,1024]{1,0:T(1,128)} %cells.7) | copy-start | bytes 12292
  35.0 3.8 %collective-permute-start.6 = (f32[4,2,128,128]{3,2,1,0:T(8,128)S(1)}, f32[4,2,128,128]{3,2,1,0:T(8,128)S(1)}, u32[]{:S(2)}, u32[]{:S(2)}) collective-permute-start(f32[4,2,128,128]{3,2,1,0:T(8,128)S(1)} %collective-permute-done.2.p_low), channel_id=1, source_target_pairs={{0,1},{1,0},{2,3},{3,2},{4,5},{5,4},{6,7},{7,6},{8,9},{9,8},{10,11... | collective-permute-start | bytes 1572872 | tf_op jit(solution)/shard_map/ppermute | solution.py:396
  35.0 3.8 %collective-permute-start.7 = (f32[4,2,128,128]{3,2,1,0:T(8,128)S(1)}, f32[4,2,128,128]{3,2,1,0:T(8,128)S(1)}, u32[]{:S(2)}, u32[]{:S(2)}) collective-permute-start(f32[4,2,128,128]{3,2,1,0:T(8,128)S(1)} %collective-permute-done.3.p_high), channel_id=1, source_target_pairs={{0,1},{1,0},{2,3},{3,2},{4,5},{5,4},{6,7},{7,6},{8,9},{9,8},{10,11... | collective-permute-start | bytes 1572872 | tf_op jit(solution)/shard_map/ppermute | solution.py:396
  35.5 2.7 %collective-permute-start.8 = (f32[3,2,128,128]{3,2,1,0:T(8,128)S(1)}, f32[3,2,128,128]{3,2,1,0:T(8,128)S(1)}, u32[]{:S(2)}, u32[]{:S(2)}) collective-permute-start(f32[3,2,128,128]{3,2,1,0:T(8,128)S(1)} %collective-permute-done.4.c_low), channel_id=1, source_target_pairs={{0,1},{1,0},{2,3},{3,2},{4,5},{5,4},{6,7},{7,6},{8,9},{9,8},{10,11... | collective-permute-start | bytes 1179656 | tf_op jit(solution)/shard_map/ppermute | solution.py:396
  35.6 3.2 %collective-permute-start.9 = (f32[3,2,128,128]{3,2,1,0:T(8,128)S(1)}, f32[3,2,128,128]{3,2,1,0:T(8,128)S(1)}, u32[]{:S(2)}, u32[]{:S(2)}) collective-permute-start(f32[3,2,128,128]{3,2,1,0:T(8,128)S(1)} %collective-permute-done.5.c_high), channel_id=1, source_target_pairs={{0,1},{1,0},{2,3},{3,2},{4,5},{5,4},{6,7},{7,6},{8,9},{9,8},{10,11... | collective-permute-start | bytes 1179656 | tf_op jit(solution)/shard_map/ppermute | solution.py:396
  38.8 23.0 %copy-start.4 = (f32[1,4,1024]{2,1,0:T(4,128)S(1)}, f32[1,4,1024]{2,1,0:T(4,128)}, u32[]{:S(2)}) copy-start(f32[1,4,1024]{2,1,0:T(4,128)} %param.6) | copy-start | bytes 49156
  77.1 1.8 %collective-permute-start.10 = (f32[8,6,16,128]{3,2,1,0:T(8,128)S(1)}, f32[8,6,16,128]{3,2,1,0:T(8,128)S(1)}, u32[]{:S(2)}, u32[]{:S(2)}) collective-permute-start(f32[8,6,16,128]{3,2,1,0:T(8,128)S(1)} %get-tuple-element.72), channel_id=1, source_target_pairs={{0,1},{1,0},{2,3},{3,2},{4,5},{5,4},{6,7},{7,6},{8,9},{9,8},{10,11... | collective-permute-start | bytes 1179656 | tf_op jit(solution)/shard_map/ppermute | solution.py:396
  102.2 5.7 %collective-permute-start.11 = (f32[1,6,16,128]{3,2,1,0:T(8,128)S(1)}, f32[1,6,16,128]{3,2,1,0:T(8,128)S(1)}, u32[]{:S(2)}, u32[]{:S(2)}) collective-permute-start(f32[1,6,16,128]{3,2,1,0:T(8,128)S(1)} %bitcast.18), channel_id=1, source_target_pairs={{0,16},{16,0},{1,17},{17,1},{2,18},{18,2},{3,19},{19,3},{4,20},{20... | collective-permute-start | bytes 147464 | tf_op jit(solution)/shard_map/ppermute | solution.py:459
  108.7 16.1 %all-to-all-start.3 = ((f32[8,6,16,128]{3,2,1,0:T(8,128)}), f32[8,6,16,128]{3,2,1,0:T(8,128)S(1)}, u32[]{:S(2)}, u32[]{:S(2)}) async-start(f32[8,6,16,128]{3,2,1,0:T(8,128)} %broadcast_in_dim.13), calls=%async_computation.3 | async-start | bytes 786432 | tf_op jit(solution)/shard_map/all_to_all | solution.py:461
  112.1 1.3 %collective-permute-start.12 = (f32[2,1024]{1,0:T(2,128)S(1)}, f32[2,1024]{1,0:T(2,128)S(1)}, u32[]{:S(2)}, u32[]{:S(2)}) collective-permute-start(f32[2,1024]{1,0:T(2,128)S(1)} %get-tuple-element.73), channel_id=1, source_target_pairs={{0,1},{1,0},{2,3},{3,2},{4,5},{5,4},{6,7},{7,6},{8,9},{9,8},{10,11... | collective-permute-start | bytes 24584 | tf_op jit(solution)/shard_map/ppermute | solution.py:396

commit v7 on v6

--- a/solution.py
+++ b/solution.py
@@ -419,10 +419,12 @@
         [f32(2, KEPT, rows, lanes), four, four, four, four, f32(2, count)],
         [pltpu.VMEM((2 * lanes, 3 * KEPT * rows), BF16)],
     )(fields, p_pair, conductivity, c_pair, receivers, hot_own)
-    c_low, c_high, p_sample = lax.optimization_barrier((c_low, c_high, p_sample))
-    c_low_pair, c_high_pair = send(c_low, swap), send(c_high, swap)
-    p_low, p_high, p_sample = lax.optimization_barrier((p_low, p_high, p_sample))
-    p_low_pair, p_high_pair = send(p_low, swap), send(p_high, swap)
+    ready = p_sample
+    pairs_of = []
+    for x in (p_low, p_high, c_low, c_high):
+        x, token = lax.optimization_barrier((x, ready))
+        pairs_of.append(send(x, swap))
+    p_low_pair, p_high_pair, c_low_pair, c_high_pair = pairs_of
     kx, ky, kz, dinv, dg, prim, f0, f1, f2, sent = call(
         forward_kernel,
         20,

time: 126 us -> 125 us (level)
  starting transfers between devices: 15.4 us -> 14.1 us
  blocking collectives: 47.5 us -> 48.8 us
    ppermute x12, waiting for transfers between devices: 25.5 us -> 24 us  [send(): return lax.ppermute(x, NAMES, pairs)]
    all_to_all x2, blocking collectives: 24.2 us -> 25.5 us  [per_device(): got = lax.all_to_all(sent, ('y', 'xl'), 0, 0, tiled=True)]
where the time goes in v7:
time: 125 us
  blocking collectives  48.8 us (39%)
  waiting for transfers between devices  40.3 us (32%)
  Pallas kernels  15.9 us (13%)
  starting transfers between devices  14.1 us (11%)
  local copies, waits for them, and re-layouts  4.29 us (3%)
    all_to_all x2, blocking collectives, per_device(): got = lax.all_to_all(sent, ('y', 'xl'), 0, 0, tiled=True)  25.5 us
    ppermute x12, waiting for transfers between devices, send(): return lax.ppermute(x, NAMES, pairs)  24 us
    all_to_all x1, blocking collectives, per_device(): parts = lax.all_to_all(total, 'z', 0, 0, tiled=True)  23.2 us
    pallas_call x5, Pallas kernels, run(): pl.pallas_call(kernel, out_shape=tuple((jax.ShapeDtypeStruct(x, kind) for...  15.9 us
    all_to_all x1, waiting for transfers between devices, per_device(): whole = lax.all_to_all(spread, 'z', 0, 0, tiled=True)  10.8 us
    ppermute x12, starting transfers between devices, send(): return lax.ppermute(x, NAMES, pairs)  10.5 us
    ppermute x1, waiting for transfers between devices, per_device(): share = share + lax.ppermute(share, 'xh', [(0, 1), (1, 0)])  5.58 us
    all_to_all x1, starting transfers between devices, per_device(): whole = lax.all_to_all(spread, 'z', 0, 0, tiled=True)  3.45 us
  transfers between devices with their start and end apart: 14, of which 8 were waited for; matrix products, arithmetic and copies ran while one was open for 0% of the time, Pallas kernels for 1%

profile of v7, /device:TPU:4, one launch (start us, length us, event | category | flops | bytes accessed | tf_op | source)
XLA Modules:
  0.0 124.8 jit_solution(14752035744435137446)
XLA Ops:
  0.6 0.1 collective-permute-start
  0.7 3.1 %collective-permute-start.2 = (f32[4,2,128,128]{3,2,1,0:T(8,128)}, f32[4,2,128,128]{3,2,1,0:T(8,128)S(1)}, u32[]{:S(2)}, u32[]{:S(2)}) collective-permute-start(f32[4,2,128,128]{3,2,1,0:T(8,128)} %bitcast.12), channel_id=1, source_target_pairs={{0,2},{1,3},{2,4},{3,5},{4,6},{5,7},{6,8},{7,9},{8,10},{9,11},{10,... | collective-permute-start | bytes 1572872 | tf_op jit(solution)/shard_map/ppermute | solution.py:396
  3.9 1.3 %collective-permute-start.4 = (f32[4,2,128,128]{3,2,1,0:T(8,128)}, f32[4,2,128,128]{3,2,1,0:T(8,128)S(1)}, u32[]{:S(2)}, u32[]{:S(2)}) collective-permute-start(f32[4,2,128,128]{3,2,1,0:T(8,128)} %bitcast.13), channel_id=1, source_target_pairs={{2,0},{3,1},{4,2},{5,3},{6,4},{7,5},{8,6},{9,7},{10,8},{11,9},{12,... | collective-permute-start | bytes 1572872 | tf_op jit(solution)/shard_map/ppermute | solution.py:396
  5.2 0.0 collective-permute-done.p_pair
  5.2 0.3 collective-permute-start.1
  5.5 3.7 %collective-permute-start.6 = (f32[3,2,128,128]{3,2,1,0:T(8,128)}, f32[3,2,128,128]{3,2,1,0:T(8,128)S(1)}, u32[]{:S(2)}, u32[]{:S(2)}) collective-permute-start(f32[3,2,128,128]{3,2,1,0:T(8,128)} %c_own.1), channel_id=1, source_target_pairs={{0,18},{1,19},{2,20},{3,21},{4,22},{5,23},{6,24},{7,25},{8,26},{9,... | collective-permute-start | bytes 1179656 | tf_op jit(solution)/shard_map/ppermute | solution.py:396
  9.2 1.3 %collective-permute-start.8 = (f32[3,2,128,128]{3,2,1,0:T(8,128)}, f32[3,2,128,128]{3,2,1,0:T(8,128)S(1)}, u32[]{:S(2)}, u32[]{:S(2)}) collective-permute-start(f32[3,2,128,128]{3,2,1,0:T(8,128)} %c_own.1), channel_id=1, source_target_pairs={{2,16},{3,17},{4,18},{5,19},{6,20},{7,21},{8,22},{9,23},{10,24},{1... | collective-permute-start | bytes 1179656 | tf_op jit(solution)/shard_map/ppermute | solution.py:396
  10.5 0.0 copy-start.2
  10.5 0.7 copy-done.2
  11.2 0.5 shard_map.59
  11.7 0.0 collective-permute-done.1.c_pair
  11.8 0.0 copy-start
  11.8 1.0 copy-done
  12.8 1.0 copy-done.1
  13.8 1.3 %shard_map.60 = (f32[2,4,128,128]{3,2,1,0:T(8,128)S(1)}, f32[4,128,128]{2,1,0:T(8,128)S(1)}, f32[4,128,128]{2,1,0:T(8,128)S(1)}, f32[4,128,128]{2,1,0:T(8,128)S(...) custom-call(f32[4,2,128,128]{3,2,1,0:T(8,128)S(1)} %bitcast.14, ...), custom_call_target="tpu_custom_call" | custom-call | tf_op jit(solution)/shard_map/pallas_call | solution.py:349
  15.1 0.9 collective-permute-done.2.p_low
  16.0 0.0 collective-permute-start.3
  16.0 16.4 %collective-permute-done.4.p_high = f32[4,2,128,128]{3,2,1,0:T(8,128)S(1)} collective-permute-done((f32[4,2,128,128]{3,2,1,0:T(8,128)}, f32[4,2,128,128]{3,2,1,0:T(8,128)S(1)}, u32[]{:S(2)}, u32[]{:S(2)}) %collective-permute-start.4) | collective-permute-done | bytes 524320 | tf_op jit(solution)/shard_map/ppermute | solution.py:396
  32.3 0.0 collective-permute-start.5
  32.3 0.0 collective-permute-done.6.c_low
  32.3 0.5 collective-permute-start.7
  32.9 2.1 %collective-permute-done.8.c_high = f32[3,2,128,128]{3,2,1,0:T(8,128)S(1)} collective-permute-done((f32[3,2,128,128]{3,2,1,0:T(8,128)}, f32[3,2,128,128]{3,2,1,0:T(8,128)S(1)}, u32[]{:S(2)}, u32[]{:S(2)}) %collective-permute-start.8) | collective-permute-done | bytes 393248 | tf_op jit(solution)/shard_map/ppermute | solution.py:396
  35.0 0.0 collective-permute-start.9
  35.0 0.0 collective-permute-done.7.c_low_pair
  35.0 1.7 %collective-permute-done.9.c_high_pair = f32[3,2,128,128]{3,2,1,0:T(8,128)S(1)} collective-permute-done((f32[3,2,128,128]{3,2,1,0:T(8,128)S(1)}, f32[3,2,128,128]{3,2,1,0:T(8,128)S(1)}, u32[]{:S(2)}, u32[]{:S(2)}) %collective-permute-start.9) | collective-permute-done | bytes 393248 | tf_op jit(solution)/shard_map/ppermute | solution.py:396
  36.7 0.0 collective-permute-done.3.p_low_pair
  36.7 0.0 collective-permute-done.5.p_high_pair
  36.7 0.0 copy-done.3
  36.7 0.0 copy-start.4
  36.7 7.3 %shard_map.61 = (f32[12,128,128]{2,1,0:T(8,128)S(1)}, f32[12,128,128]{2,1,0:T(8,128)S(1)}, f32[12,128,128]{2,1,0:T(8,128)S(1)}, f32[12,128,128]{2,1,0:T(8,128)S(...) custom-call(f32[2,4,128,128]{3,2,1,0:T(8,128)S(1)} %get-tuple-elemen, ...), custom_call_target="tpu_custom_call" | custom-call | tf_op jit(solution)/shard_map/pallas_call | solution.py:349
  44.1 16.9 %all_to_all.20.got = f32[8,8,1152]{2,1,0:T(8,128)S(1)} all-to-all(f32[8,8,1152]{2,1,0:T(8,128)S(1)} %get-tuple-element.49), channel_id=1, replica_groups=mesh['z'=8,'xh'=2,'y'=4,'xl'=2,'c'=2] {'y','xl'}, dimensions={0} | all-to-all | bytes 589824 | tf_op jit(solution)/shard_map/all_to_all | solution.py:441
  61.0 0.0 copy-done.4
  61.0 5.4 %shard_map.62 = (f32[2,6,128,128]{3,2,1,0:T(8,128)S(1)}, f32[2,6,128,128]{3,2,1,0:T(8,128)S(1)}, f32[2,6,128,128]{3,2,1,0:T(8,128)S(1)}, f32[2,6,128,128]{3,2,1,...) custom-call(f32[8,8,1152]{2,1,0:T(8,128)S(1)} %all_to_all.20.got, f32[4,1024]{1,0:T(4,128)S(1)} %bitcast.15, ...), custom_call_target="tpu_custom_call" | custom-call | tf_op jit(solution)/shard_map/pallas_call | solution.py:349
  66.4 8.6 %all_to_all.21.got = f32[8,8,128]{2,1,0:T(8,128)S(1)} all-to-all(f32[8,8,128]{2,1,0:T(8,128)S(1)} %get-tuple-element.60), channel_id=1, replica_groups=mesh['z'=8,'xh'=2,'y'=4,'xl'=2,'c'=2] {'y','xl'}, dimensions={0} | all-to-all | bytes 65536 | tf_op jit(solution)/shard_map/all_to_all | solution.py:449
  75.1 1.3 %shard_map.63 = (f32[8,6,16,128]{3,2,1,0:T(8,128)S(1)}, f32[8,6,16,128]{3,2,1,0:T(8,128)S(1)}) custom-call(f32[8,8,128]{2,1,0:T(8,128)S(1)} %all_to_all.21.got, f32[2,6,128,128]{3,2,1,0:T(8,128)S(1)} %get-tuple-element.61.a0, f32[2,6,128,128]{3,2,1,0:T(8,128)S(1)} %get-tuple-element.62.a1, f32[2,6,128,128]{3,2,1,0:T(8,128)S(1)} %get-tuple-element.63.a2, ...), custom_call_target="tpu_custom_call" | custom-call | tf_op jit(solution)/shard_map/pallas_call | solution.py:349
  76.3 0.1 collective-permute-start.10
  76.4 1.7 %collective-permute-done.10 = f32[8,6,16,128]{3,2,1,0:T(8,128)S(1)} collective-permute-done((f32[8,6,16,128]{3,2,1,0:T(8,128)S(1)}, f32[8,6,16,128]{3,2,1,0:T(8,128)S(1)}, u32[]{:S(2)}, u32[]{:S(2)}) %collective-permute-start.10) | collective-permute-done | bytes 393248 | tf_op jit(solution)/shard_map/ppermute | solution.py:396
  78.1 0.1 add.6
  78.2 23.2 %all_to_all.22 = f32[8,6,16,128]{3,2,1,0:T(8,128)S(1)} all-to-all(f32[8,6,16,128]{3,2,1,0:T(8,128)S(1)} %add.6), channel_id=1, replica_groups=mesh['z'=8,'xh'=2,'y'=4,'xl'=2,'c'=2] {'z'}, dimensions={0} | all-to-all | bytes 786432 | tf_op jit(solution)/shard_map/all_to_all | solution.py:458
  101.5 0.1 collective-permute-start.11
  101.6 5.6 %collective-permute-done.11 = f32[1,6,16,128]{3,2,1,0:T(8,128)S(1)} collective-permute-done((f32[1,6,16,128]{3,2,1,0:T(8,128)S(1)}, f32[1,6,16,128]{3,2,1,0:T(8,128)S(1)}, u32[]{:S(2)}, u32[]{:S(2)}) %collective-permute-start.11) | collective-permute-done | bytes 49184 | tf_op jit(solution)/shard_map/ppermute | solution.py:461
  107.2 0.8 broadcast_in_dim.13
  107.9 3.5 %all-to-all-start.3 = ((f32[8,6,16,128]{3,2,1,0:T(8,128)}), f32[8,6,16,128]{3,2,1,0:T(8,128)S(1)}, u32[]{:S(2)}, u32[]{:S(2)}) async-start(f32[8,6,16,128]{3,2,1,0:T(8,128)} %broadcast_in_dim.13), calls=%async_computation.3 | async-start | bytes 786432 | tf_op jit(solution)/shard_map/all_to_all | solution.py:463
  111.4 0.1 collective-permute-start.12
  111.5 1.2 collective-permute-done.12
  112.7 0.6 maximum_select_fusion
  113.3 10.8 %all-to-all-done.3 = f32[8,6,16,128]{3,2,1,0:T(8,128)S(1)} async-done(((f32[8,6,16,128]{3,2,1,0:T(8,128)}), f32[8,6,16,128]{3,2,1,0:T(8,128)S(1)}, u32[]{:S(2)}, u32[]{:S(2)}) %all-to-all-start.3) | async-done | bytes 393248 | tf_op jit(solution)/shard_map/all_to_all | solution.py:463
  124.0 0.8 copy.6
  (4 shorter events, 0.0 us)
Async XLA Ops:
  0.6 4.5 %collective-permute-start = (f32[4,2,128,128]{3,2,1,0:T(8,128)}, f32[4,2,128,128]{3,2,1,0:T(8,128)S(1)}, u32[]{:S(2)}, u32[]{:S(2)}) collective-permute-start(f32[4,2,128,128]{3,2,1,0:T(8,128)} %bitcast.11), channel_id=1, source_target_pairs={{0,1},{1,0},{2,3},{3,2},{4,5},{5,4},{6,7},{7,6},{8,9},{9,8},{10,11... | collective-permute-start | bytes 1572872 | tf_op jit(solution)/shard_map/ppermute | solution.py:396
  0.7 15.2 %collective-permute-start.2 = (f32[4,2,128,128]{3,2,1,0:T(8,128)}, f32[4,2,128,128]{3,2,1,0:T(8,128)S(1)}, u32[]{:S(2)}, u32[]{:S(2)}) collective-permute-start(f32[4,2,128,128]{3,2,1,0:T(8,128)} %bitcast.12), channel_id=1, source_target_pairs={{0,2},{1,3},{2,4},{3,5},{4,6},{5,7},{6,8},{7,9},{8,10},{9,11},{10,... | collective-permute-start | bytes 1572872 | tf_op jit(solution)/shard_map/ppermute | solution.py:396
  3.9 28.5 %collective-permute-start.4 = (f32[4,2,128,128]{3,2,1,0:T(8,128)}, f32[4,2,128,128]{3,2,1,0:T(8,128)S(1)}, u32[]{:S(2)}, u32[]{:S(2)}) collective-permute-start(f32[4,2,128,128]{3,2,1,0:T(8,128)} %bitcast.13), channel_id=1, source_target_pairs={{2,0},{3,1},{4,2},{5,3},{6,4},{7,5},{8,6},{9,7},{10,8},{11,9},{12,... | collective-permute-start | bytes 1572872 | tf_op jit(solution)/shard_map/ppermute | solution.py:396
  5.2 6.6 %collective-permute-start.1 = (f32[3,2,128,128]{3,2,1,0:T(8,128)}, f32[3,2,128,128]{3,2,1,0:T(8,128)S(1)}, u32[]{:S(2)}, u32[]{:S(2)}) collective-permute-start(f32[3,2,128,128]{3,2,1,0:T(8,128)} %c_own.1), channel_id=1, source_target_pairs={{0,1},{1,0},{2,3},{3,2},{4,5},{5,4},{6,7},{7,6},{8,9},{9,8},{10,11... | collective-permute-start | bytes 1179656 | tf_op jit(solution)/shard_map/ppermute | solution.py:396
  5.5 26.9 %collective-permute-start.6 = (f32[3,2,128,128]{3,2,1,0:T(8,128)}, f32[3,2,128,128]{3,2,1,0:T(8,128)S(1)}, u32[]{:S(2)}, u32[]{:S(2)}) collective-permute-start(f32[3,2,128,128]{3,2,1,0:T(8,128)} %c_own.1), channel_id=1, source_target_pairs={{0,18},{1,19},{2,20},{3,21},{4,22},{5,23},{6,24},{7,25},{8,26},{9,... | collective-permute-start | bytes 1179656 | tf_op jit(solution)/shard_map/ppermute | solution.py:396
  9.2 25.8 %collective-permute-start.8 = (f32[3,2,128,128]{3,2,1,0:T(8,128)}, f32[3,2,128,128]{3,2,1,0:T(8,128)S(1)}, u32[]{:S(2)}, u32[]{:S(2)}) collective-permute-start(f32[3,2,128,128]{3,2,1,0:T(8,128)} %c_own.1), channel_id=1, source_target_pairs={{2,16},{3,17},{4,18},{5,19},{6,20},{7,21},{8,22},{9,23},{10,24},{1... | collective-permute-start | bytes 1179656 | tf_op jit(solution)/shard_map/ppermute | solution.py:396
  10.5 0.7 copy-start.2
  11.8 1.0 copy-start
  12.8 1.0 copy-start.1
  13.8 22.9 %copy-start.3 = (s32[1,1024]{1,0:T(1,128)S(1)}, s32[1,1024]{1,0:T(1,128)}, u32[]{:S(2)}) copy-start(s32[1,1024]{1,0:T(1,128)} %cells.7) | copy-start | bytes 12292
  16.0 20.7 %collective-permute-start.3 = (f32[4,2,128,128]{3,2,1,0:T(8,128)S(1)}, f32[4,2,128,128]{3,2,1,0:T(8,128)S(1)}, u32[]{:S(2)}, u32[]{:S(2)}) collective-permute-start(f32[4,2,128,128]{3,2,1,0:T(8,128)S(1)} %collective-permute-done.2.p_low), channel_id=1, source_target_pairs={{0,1},{1,0},{2,3},{3,2},{4,5},{5,4},{6,7},{7,6},{8,9},{9,8},{10,11... | collective-permute-start | bytes 1572872 | tf_op jit(solution)/shard_map/ppermute | solution.py:396
  32.3 4.4 %collective-permute-start.5 = (f32[4,2,128,128]{3,2,1,0:T(8,128)S(1)}, f32[4,2,128,128]{3,2,1,0:T(8,128)S(1)}, u32[]{:S(2)}, u32[]{:S(2)}) collective-permute-start(f32[4,2,128,128]{3,2,1,0:T(8,128)S(1)} %collective-permute-done.4.p_high), channel_id=1, source_target_pairs={{0,1},{1,0},{2,3},{3,2},{4,5},{5,4},{6,7},{7,6},{8,9},{9,8},{10,11... | collective-permute-start | bytes 1572872 | tf_op jit(solution)/shard_map/ppermute | solution.py:396
  32.3 2.6 %collective-permute-start.7 = (f32[3,2,128,128]{3,2,1,0:T(8,128)S(1)}, f32[3,2,128,128]{3,2,1,0:T(8,128)S(1)}, u32[]{:S(2)}, u32[]{:S(2)}) collective-permute-start(f32[3,2,128,128]{3,2,1,0:T(8,128)S(1)} %collective-permute-done.6.c_low), channel_id=1, source_target_pairs={{0,1},{1,0},{2,3},{3,2},{4,5},{5,4},{6,7},{7,6},{8,9},{9,8},{10,11... | collective-permute-start | bytes 1179656 | tf_op jit(solution)/shard_map/ppermute | solution.py:396
  35.0 1.7 %collective-permute-start.9 = (f32[3,2,128,128]{3,2,1,0:T(8,128)S(1)}, f32[3,2,128,128]{3,2,1,0:T(8,128)S(1)}, u32[]{:S(2)}, u32[]{:S(2)}) collective-permute-start(f32[3,2,128,128]{3,2,1,0:T(8,128)S(1)} %collective-permute-done.8.c_high), channel_id=1, source_target_pairs={{0,1},{1,0},{2,3},{3,2},{4,5},{5,4},{6,7},{7,6},{8,9},{9,8},{10,11... | collective-permute-start | bytes 1179656 | tf_op jit(solution)/shard_map/ppermute | solution.py:396
  36.7 24.3 %copy-start.4 = (f32[1,4,1024]{2,1,0:T(4,128)S(1)}, f32[1,4,1024]{2,1,0:T(4,128)}, u32[]{:S(2)}) copy-start(f32[1,4,1024]{2,1,0:T(4,128)} %param.6) | copy-start | bytes 49156
  76.3 1.8 %collective-permute-start.10 = (f32[8,6,16,128]{3,2,1,0:T(8,128)S(1)}, f32[8,6,16,128]{3,2,1,0:T(8,128)S(1)}, u32[]{:S(2)}, u32[]{:S(2)}) collective-permute-start(f32[8,6,16,128]{3,2,1,0:T(8,128)S(1)} %get-tuple-element.68), channel_id=1, source_target_pairs={{0,1},{1,0},{2,3},{3,2},{4,5},{5,4},{6,7},{7,6},{8,9},{9,8},{10,11... | collective-permute-start | bytes 1179656 | tf_op jit(solution)/shard_map/ppermute | solution.py:396
  101.5 5.7 %collective-permute-start.11 = (f32[1,6,16,128]{3,2,1,0:T(8,128)S(1)}, f32[1,6,16,128]{3,2,1,0:T(8,128)S(1)}, u32[]{:S(2)}, u32[]{:S(2)}) collective-permute-start(f32[1,6,16,128]{3,2,1,0:T(8,128)S(1)} %bitcast.18), channel_id=1, source_target_pairs={{0,16},{16,0},{1,17},{17,1},{2,18},{18,2},{3,19},{19,3},{4,20},{20... | collective-permute-start | bytes 147464 | tf_op jit(solution)/shard_map/ppermute | solution.py:461
  107.9 16.1 %all-to-all-start.3 = ((f32[8,6,16,128]{3,2,1,0:T(8,128)}), f32[8,6,16,128]{3,2,1,0:T(8,128)S(1)}, u32[]{:S(2)}, u32[]{:S(2)}) async-start(f32[8,6,16,128]{3,2,1,0:T(8,128)} %broadcast_in_dim.13), calls=%async_computation.3 | async-start | bytes 786432 | tf_op jit(solution)/shard_map/all_to_all | solution.py:463
  111.4 1.3 %collective-permute-start.12 = (f32[2,1024]{1,0:T(2,128)S(1)}, f32[2,1024]{1,0:T(2,128)S(1)}, u32[]{:S(2)}, u32[]{:S(2)}) collective-permute-start(f32[2,1024]{1,0:T(2,128)S(1)} %get-tuple-element.69), channel_id=1, source_target_pairs={{0,1},{1,0},{2,3},{3,2},{4,5},{5,4},{6,7},{7,6},{8,9},{9,8},{10,11... | collective-permute-start | bytes 24584 | tf_op jit(solution)/shard_map/ppermute | solution.py:396

commit v8 on v6

--- a/solution.py
+++ b/solution.py
@@ -23,6 +23,24 @@
     return first, second, third
 
 
+class Planes:
+    def __init__(self, low, high, cut):
+        self.low, self.high, self.cut = low, high, cut
+        self.shape = low.shape
+
+    def place(self, key):
+        lead, i = (key[:-1], key[-1]) if isinstance(key, tuple) else ((), key)
+        return (self.low, lead + (i,)) if i < self.cut else (self.high, lead + (i - self.cut,))
+
+    def __getitem__(self, key):
+        ref, at = self.place(key)
+        return ref[at]
+
+    def __setitem__(self, key, value):
+        ref, at = self.place(key)
+        ref[at] = value
+
+
 def fold(plane):
     return jnp.sum(plane.reshape(plane.shape[0] // 8, 8, plane.shape[1]), axis=0)
 
@@ -42,19 +60,16 @@
     return total + kz[i] * ahead(mid, 1) + behind(kz[i] * mid, 1)
 
 
-def krylov(t0, t1, t2, kx, ky, kz, dinv, dg):
+def apply_planes(source, target, first, last, kx, ky, kz, dinv):
+    for i in range(first, last + 1):
+        for s in range(source.shape[0]):
+            target[s, i] = source[s, i] - dinv[i] * neighbours(source, s, i, kx, ky, kz)
+
+
+def krylov(t0, t1, t2, kx, ky, kz, dinv, dg, first=(2, 3)):
     sources = t0.shape[0]
-
-    def apply_planes(source, target, first, last):
-        def body(i, carry):
-            for s in range(sources):
-                target[s, i] = source[s, i] - dinv[i] * neighbours(source, s, i, kx, ky, kz)
-            return carry
-
-        lax.fori_loop(first, last + 1, body, 0, unroll=True)
-
-    apply_planes(t0, t1, 2, 9)
-    apply_planes(t1, t2, 3, 8)
+    apply_planes(t0, t1, first[0], 9, kx, ky, kz, dinv)
+    apply_planes(t1, t2, first[1], 8, kx, ky, kz, dinv)
 
     def body(i, sums):
         sums = list(sums)
@@ -74,8 +89,9 @@
                 sums[k * sources + s] = sums[k * sources + s] + fold(term)
         return tuple(sums)
 
-    zero = jnp.zeros((8, t0.shape[3]), F32)
-    sums = lax.fori_loop(4, 8, body, (zero,) * (11 * sources), unroll=True)
+    sums = (jnp.zeros((8, t0.shape[3]), F32),) * (11 * sources)
+    for i in range(4, 8):
+        sums = body(i, sums)
     row_at = lax.broadcasted_iota(jnp.int32, (8, 128), 0)
     lane_at = lax.broadcasted_iota(jnp.int32, (8, 128), 1)
     packed = jnp.zeros((8, 128), F32)
@@ -183,54 +199,39 @@
     sample[...] = jnp.concatenate(found, axis=0)
 
 
-def forward_kernel(
-    p_mid, p_low, p_low_pair, p_high, p_high_pair,
-    c_mid, c_low, c_low_pair, c_high, c_high_pair, ky_mid, kz_mid, dg_mid, cells, hot_own, p_sample,
-    kx, ky, kz, dinv, dg, prim, t0, t1, t2, sent, cond, left, found,
-):
-    block = 2 * lax.axis_index("y") + lax.axis_index("xl")
-    core = lax.axis_index("c")
-    here = pl.ds(2 * core, 2)
-    prim[:, 4:8] = p_mid[...]
-    cond[4:8] = c_mid[...]
-    for base, first, second in ((0, p_low, p_low_pair), (8, p_high, p_high_pair)):
-        prim[:, pl.ds(base + 2 * core, 2)] = first[here]
-        prim[:, pl.ds(base + 2 - 2 * core, 2)] = second[here]
-    for base, first, second in ((0, c_low, c_low_pair), (8, c_high, c_high_pair)):
-        cond[pl.ds(base + 2 * core, 2)] = first[0]
-        cond[pl.ds(base + 2 - 2 * core, 2)] = second[0]
-        for source, start in ((first, base + 2 * core), (second, base + 2 - 2 * core)):
-            for j in range(2):
-                up_y, up_z, part = in_plane(source[1, j], source[2, j])
-                ky[start + j] = up_y
-                kz[start + j] = up_z
-                dg[start + j] = part
-    ky[4:8] = ky_mid[...]
-    kz[4:8] = kz_mid[...]
-    dg[4:8] = dg_mid[...]
-    rows, lanes = prim.shape[2], prim.shape[3]
+def unit_of(rows, lanes):
     row_at, lane_at, mask_y, mask_z = edges(rows, lanes)
     edge = jnp.where(row_at == 0, 0.5, 0.0) + jnp.where(row_at == rows - 1, 0.5, 0.0)
     edge = edge + jnp.where(lane_at == 0, 0.5, 0.0) + jnp.where(lane_at == lanes - 1, 0.5, 0.0)
-    unit = (6.0 - edge).astype(F32)
+    return mask_y, mask_z, (6.0 - edge).astype(F32)
+
+
+def halo_planes(base, core, fields, conductivities, prim, cond, ky, kz, dg):
+    here = pl.ds(2 * core, 2)
+    starts = (base + 2 * core, base + 2 - 2 * core)
+    for source, start in zip(fields, starts):
+        prim[:, pl.ds(start, 2)] = source[here]
+    for source, start in zip(conductivities, starts):
+        cond[pl.ds(start, 2)] = source[0]
+        for j in range(2):
+            up_y, up_z, part = in_plane(source[1, j], source[2, j])
+            ky[start + j] = up_y
+            kz[start + j] = up_z
+            dg[start + j] = part
+
+
+def start_planes(block, planes, flat, cond, kx, ky, kz, dinv, dg, prim, t0):
     layers = 4 * CHIPS
-
-    kx[0] = 0.5 * (cond[0] + cond[1])
-
-    def coefficients(i, carry):
+    mask_y, mask_z, unit = unit_of(prim.shape[2], prim.shape[3])
+    for i in planes:
         layer = 4 * block - 4 + i
         inside = jnp.where(jnp.logical_and(layer >= 0, layer < layers), 1.0, 0.0).astype(F32)
         first = 0.5 * (cond[i] + cond[i + 1])
         kx[i] = first
-        diagonal = first + kx[i - 1] + dg[i]
-        inverse = jnp.where(inside > 0.5, 1.0 / diagonal, 0.0)
+        diagonal = first + kx[i - 1] + flat[i]
         dg[i] = diagonal
-        dinv[i] = inverse
-        return carry
-
-    lax.fori_loop(1, 11, coefficients, 0)
-
-    def right_side(i, carry):
+        dinv[i] = jnp.where(inside > 0.5, 1.0 / diagonal, 0.0)
+    for i in planes:
         layer = 4 * block - 4 + i
         outer = jnp.where(jnp.logical_or(layer == 0, layer == layers - 1), 0.5, 0.0).astype(F32)
         diagonal = (unit - outer) - dg[i]
@@ -244,12 +245,54 @@
             total = total - diff_y * ahead(mid, 0) - behind(diff_y * mid, 0)
             total = total - diff_z * ahead(mid, 1) - behind(diff_z * mid, 1)
             t0[s, i] = inverse * total
-        return carry
-
-    lax.fori_loop(1, 11, right_side, 0, unroll=True)
-    moments = krylov(t0, t1, t2, kx, ky, kz, dinv, dg)
+
+
+CUTS = (7, 8, 8, 7, 7, 8, 7, 6, 5)
+
+
+def low_kernel(
+    p_mid, p_low, p_low_pair, c_mid, c_low, c_low_pair, ky_mid, kz_mid, dg_mid,
+    kx, ky, kz, dinv, dg, prim, t0, t1, t2, cond, flat,
+):
+    block = 2 * lax.axis_index("y") + lax.axis_index("xl")
+    core = lax.axis_index("c")
+    prim[:, 4:8] = p_mid[...]
+    cond[4:8] = c_mid[...]
+    ky[4:8] = ky_mid[...]
+    kz[4:8] = kz_mid[...]
+    flat[4:8] = dg_mid[...]
+    halo_planes(0, core, (p_low, p_low_pair), (c_low, c_low_pair), prim, cond, ky, kz, flat)
+    kx[0] = 0.5 * (cond[0] + cond[1])
+    start_planes(block, range(1, 7), flat, cond, kx, ky, kz, dinv, dg, prim, t0)
+    apply_planes(t0, t1, 2, 5, kx, ky, kz, dinv)
+    apply_planes(t1, t2, 3, 4, kx, ky, kz, dinv)
+
+
+def high_kernel(*refs):
+    lows, refs = refs[:9], refs[9:]
+    p_high, p_high_pair, c_mid, c_high, c_high_pair, dg_mid, cells, hot_own, p_sample = refs[:9]
+    highs, (sent, cond, flat, left, found) = refs[9:18], refs[18:]
+    block = 2 * lax.axis_index("y") + lax.axis_index("xl")
+    core = lax.axis_index("c")
+    kx, ky, kz, dinv, dg, prim, t0, t1, t2 = (Planes(*x) for x in zip(lows, highs, CUTS))
+    cond[3] = c_mid[3]
+    flat[3] = dg_mid[3]
+    here = pl.ds(2 * core, 2)
+    starts = (2 * core, 2 - 2 * core)
+    for source, start in zip((p_high, p_high_pair), starts):
+        prim.high[:, pl.ds(start, 2)] = source[here]
+    for source, start in zip((c_high, c_high_pair), starts):
+        cond[pl.ds(4 + start, 2)] = source[0]
+        for j in range(2):
+            up_y, up_z, part = in_plane(source[1, j], source[2, j])
+            ky.high[start + j] = up_y
+            kz.high[start + j] = up_z
+            flat[4 + start + j] = part
+    start_planes(block, range(7, 11), Planes(flat, flat, 4), Planes(cond, cond, 4), kx, ky, kz, dinv, dg, prim, t0)
+    moments = krylov(t0, t1, t2, kx, ky, kz, dinv, dg, (6, 5))
 
     picked = cells[...]
+    lanes = prim.shape[3]
     lane_of = picked - (picked // lanes) * lanes
     count = picked.shape[1]
     gather([(t0, 4), (t1, 4), (t2, 4)], left, hot_own, one_hot(lanes, 0, lane_of), found)
@@ -259,10 +302,10 @@
         sent[k, :, count:] = moments
 
 
-def adjoint_kernel(
-    got, observed, cells, hot, kx, ky, kz, dinv, dg, prim, f0, f1, f2,
-    b0, b1, b2, pot, predicted, sent, heavy, a0, a1, a2,
-):
+def adjoint_kernel(got, observed, cells, hot, *refs):
+    lows, highs = refs[:9], refs[9:18]
+    b0, b1, b2, pot, predicted, sent, heavy, a0, a1, a2 = refs[18:]
+    kx, ky, kz, dinv, dg, prim, f0, f1, f2 = (Planes(*x) for x in zip(lows, highs, CUTS))
     core = lax.axis_index("c")
     rows, lanes = prim.shape[2], prim.shape[3]
     count = cells.shape[1]
@@ -405,8 +448,6 @@
     rows, lanes = primary.shape[3], primary.shape[4]
     count = receivers.shape[1]
     f32 = lambda *shape: (shape, F32)
-    deep = f32(DEEP, rows, lanes)
-    pairs = f32(2, DEEP, rows, lanes)
     four = f32(KEPT, rows, lanes)
     hot, hot_own = call(
         hot_kernel, 4, [((10 * rows, count), BF16), ((3 * KEPT * rows, count), BF16)]
@@ -419,22 +460,35 @@
         [f32(2, KEPT, rows, lanes), four, four, four, four, f32(2, count)],
         [pltpu.VMEM((2 * lanes, 3 * KEPT * rows), BF16)],
     )(fields, p_pair, conductivity, c_pair, receivers, hot_own)
-    c_low, c_high, p_sample = lax.optimization_barrier((c_low, c_high, p_sample))
-    c_low_pair, c_high_pair = send(c_low, swap), send(c_high, swap)
-    p_low, p_high, p_sample = lax.optimization_barrier((p_low, p_high, p_sample))
-    p_low_pair, p_high_pair = send(p_low, swap), send(p_high, swap)
-    kx, ky, kz, dinv, dg, prim, f0, f1, f2, sent = call(
-        forward_kernel,
-        20,
-        [deep] * 5 + [pairs] * 4 + [f32(CHIPS, 8, count + 128)],
+    def paired(x, ready):
+        x, ready = lax.optimization_barrier((x, ready))
+        return x, send(x, swap)
+
+    p_low, p_low_pair = paired(p_low, p_sample)
+    c_low, c_low_pair = paired(c_low, p_sample)
+    eight = f32(8, rows, lanes)
+    lows = call(
+        low_kernel,
+        10,
+        [eight] * 5 + [f32(2, 8, rows, lanes)] * 4,
+        [pltpu.VMEM((8, rows, lanes), F32)] * 2,
+    )(p_mid, p_low, p_low_pair, c_mid, c_low, c_low_pair, ky_mid, kz_mid, dg_mid)
+    p_high, p_high_pair = paired(p_high, lows[7])
+    c_high, c_high_pair = paired(c_high, lows[7])
+    *highs, sent = call(
+        high_kernel,
+        18,
+        [f32(DEEP - cut, rows, lanes) for cut in CUTS[:5]]
+        + [f32(2, DEEP - cut, rows, lanes) for cut in CUTS[5:]]
+        + [f32(CHIPS, 8, count + 128)],
         [
-            pltpu.VMEM((DEEP, rows, lanes), F32),
+            pltpu.VMEM((8, rows, lanes), F32),
+            pltpu.VMEM((8, rows, lanes), F32),
             pltpu.VMEM((6 * lanes, 3 * KEPT * rows), BF16),
             pltpu.VMEM((6, count), F32),
         ],
     )(
-        p_mid, p_low, p_low_pair, p_high, p_high_pair,
-        c_mid, c_low, c_low_pair, c_high, c_high_pair, ky_mid, kz_mid, dg_mid, receivers, hot_own, p_sample,
+        *lows, p_high, p_high_pair, c_mid, c_high, c_high_pair, dg_mid, receivers, hot_own, p_sample,
     )
     got = lax.all_to_all(sent, ("y", "xl"), 0, 0, tiled=True)
     six = (2, 6, rows, lanes)
@@ -443,7 +497,7 @@
         18,
         [f32(*six)] * 4 + [f32(2, count), f32(CHIPS, 8, 128)],
         [pltpu.VMEM((3, 2 * lanes, count), BF16)] + [pltpu.VMEM((2, DEEP, rows, lanes), F32)] * 3,
-    )(got, observed[0], receivers, hot, kx, ky, kz, dinv, dg, prim, f0, f1, f2)
+    )(got, observed[0], receivers, hot, *lows, *highs)
     got = lax.all_to_all(sent, ("y", "xl"), 0, 0, tiled=True)
     slabs = lax.axis_size("z")
     chunks = (slabs, 6, rows // slabs, lanes)

time: 126 us -> 136 us (1.079)
  blocking collectives: 47.5 us -> 56.1 us
  waiting for transfers between devices: 41.1 us -> 43.9 us
  starting transfers between devices: 15.4 us -> 13.9 us
  Pallas kernels: 15.9 us -> 17.3 us
    all_to_all x2, blocking collectives: 24.2 us -> 32.9 us  [per_device(): got = lax.all_to_all(sent, ('y', 'xl'), 0, 0, tiled=True)]
    ppermute x12, waiting for transfers between devices: 25.5 us -> 27.8 us  [send(): return lax.ppermute(x, NAMES, pairs)]
    pallas_call x5 -> x6, Pallas kernels: 15.9 us -> 17.3 us  [run(): pl.pallas_call(kernel, out_shape=tuple((jax.ShapeDtypeStruct(x, kind) for...]
    unnamed x10 -> x8, local copies, waits for them, and re-layouts: 2.72 us -> 1.37 us
  transfers between devices with their start and end apart: 14 -> 14, of which waited for: 8 -> 8; matrix products, arithmetic and copies ran while one was open for 0% -> 0% of each run, Pallas kernels for 1% -> 4%
where the time goes in v8:
time: 136 us
  blocking collectives  56.1 us (41%)
  waiting for transfers between devices  43.9 us (32%)
  Pallas kernels  17.3 us (13%)
  starting transfers between devices  13.9 us (10%)
  local copies, waits for them, and re-layouts  2.93 us (2%)
    all_to_all x2, blocking collectives, per_device(): got = lax.all_to_all(sent, ('y', 'xl'), 0, 0, tiled=True)  32.9 us
    ppermute x12, waiting for transfers between devices, send(): return lax.ppermute(x, NAMES, pairs)  27.8 us
    all_to_all x1, blocking collectives, per_device(): parts = lax.all_to_all(total, 'z', 0, 0, tiled=True)  23.2 us
    pallas_call x6, Pallas kernels, run(): pl.pallas_call(kernel, out_shape=tuple((jax.ShapeDtypeStruct(x, kind) for...  17.3 us
    all_to_all x1, waiting for transfers between devices, per_device(): whole = lax.all_to_all(spread, 'z', 0, 0, tiled=True)  10.8 us
    ppermute x12, starting transfers between devices, send(): return lax.ppermute(x, NAMES, pairs)  10.1 us
    ppermute x1, waiting for transfers between devices, per_device(): share = share + lax.ppermute(share, 'xh', [(0, 1), (1, 0)])  5.41 us
    all_to_all x1, starting transfers between devices, per_device(): whole = lax.all_to_all(spread, 'z', 0, 0, tiled=True)  3.45 us
  transfers between devices with their start and end apart: 14, of which 8 were waited for; matrix products, arithmetic and copies ran while one was open for 0% of the time, Pallas kernels for 4%

profile of v8, /device:TPU:4, one launch (start us, length us, event | category | flops | bytes accessed | tf_op | source)
XLA Modules:
  0.0 135.7 jit_solution(9430080885886357316)
XLA Ops:
  0.6 0.1 collective-permute-start
  0.7 3.1 %collective-permute-start.2 = (f32[4,2,128,128]{3,2,1,0:T(8,128)}, f32[4,2,128,128]{3,2,1,0:T(8,128)S(1)}, u32[]{:S(2)}, u32[]{:S(2)}) collective-permute-start(f32[4,2,128,128]{3,2,1,0:T(8,128)} %bitcast.p_own), channel_id=1, source_target_pairs={{0,2},{1,3},{2,4},{3,5},{4,6},{5,7},{6,8},{7,9},{8,10},{9,11},{10,... | collective-permute-start | bytes 1572872 | tf_op jit(solution)/shard_map/ppermute | solution.py:439
  3.9 0.0 collective-permute-done.p_pair
  3.9 0.3 collective-permute-start.1
  4.2 2.8 %collective-permute-start.4 = (f32[3,2,128,128]{3,2,1,0:T(8,128)}, f32[3,2,128,128]{3,2,1,0:T(8,128)S(1)}, u32[]{:S(2)}, u32[]{:S(2)}) collective-permute-start(f32[3,2,128,128]{3,2,1,0:T(8,128)} %c_own.1), channel_id=1, source_target_pairs={{0,18},{1,19},{2,20},{3,21},{4,22},{5,23},{6,24},{7,25},{8,26},{9,... | collective-permute-start | bytes 1179656 | tf_op jit(solution)/shard_map/ppermute | solution.py:439
  7.0 0.0 copy-start
  7.0 0.7 copy-done
  7.6 0.5 shard_map.59
  8.2 0.0 collective-permute-done.1.c_pair
  8.2 0.0 copy-start.1
  8.2 0.7 copy-done.1
  8.9 0.0 copy-start.2
  8.9 2.4 %shard_map.60 = (f32[2,4,128,128]{3,2,1,0:T(8,128)S(1)}, f32[4,128,128]{2,1,0:T(8,128)S(1)}, f32[4,128,128]{2,1,0:T(8,128)S(1)}, f32[4,128,128]{2,1,0:T(8,128)S(...) custom-call(f32[4,2,128,128]{3,2,1,0:T(8,128)} %bitcast.p_own, ...), custom_call_target="tpu_custom_call" | custom-call | tf_op jit(solution)/shard_map/pallas_call | solution.py:392
  11.3 4.6 %collective-permute-done.2.p_low = f32[4,2,128,128]{3,2,1,0:T(8,128)S(1)} collective-permute-done((f32[4,2,128,128]{3,2,1,0:T(8,128)}, f32[4,2,128,128]{3,2,1,0:T(8,128)S(1)}, u32[]{:S(2)}, u32[]{:S(2)}) %collective-permute-start.2) | collective-permute-done | bytes 524320 | tf_op jit(solution)/shard_map/ppermute | solution.py:439
  16.0 0.0 collective-permute-start.3
  16.0 1.3 collective-permute-start.6
  17.3 0.0 collective-permute-done.4.c_low
  17.3 0.6 collective-permute-start.5
  17.9 1.3 collective-permute-start.8
  19.2 0.1 collective-permute-done.5.c_low_pair
  19.2 0.0 collective-permute-done.3.p_low_pair
  19.2 2.0 %shard_map.61 = (f32[8,128,128]{2,1,0:T(8,128)S(1)}, f32[8,128,128]{2,1,0:T(8,128)S(1)}, f32[8,128,128]{2,1,0:T(8,128)S(1)}, f32[8,128,128]{2,1,0:T(8,128)S(1)},...) custom-call(f32[2,4,128,128]{3,2,1,0:T(8,128)S(1)} %get-tuple-elemen, ...), custom_call_target="tpu_custom_call" | custom-call | tf_op jit(solution)/shard_map/pallas_call | solution.py:392
  21.3 18.2 %collective-permute-done.6.refs_9_ = f32[4,2,128,128]{3,2,1,0:T(8,128)S(1)} collective-permute-done((f32[4,2,128,128]{3,2,1,0:T(8,128)}, f32[4,2,128,128]{3,2,1,0:T(8,128)S(1)}, u32[]{:S(2)}, u32[]{:S(2)}) %collective-permute-start.6) | collective-permute-done | bytes 524320 | tf_op jit(solution)/shard_map/ppermute | solution.py:439
  39.5 0.0 collective-permute-start.7
  39.5 0.0 collective-permute-done.8.refs_12_
  39.5 0.5 collective-permute-start.9
  40.0 2.0 %collective-permute-done.9.refs_13_ = f32[3,2,128,128]{3,2,1,0:T(8,128)S(1)} collective-permute-done((f32[3,2,128,128]{3,2,1,0:T(8,128)S(1)}, f32[3,2,128,128]{3,2,1,0:T(8,128)S(1)}, u32[]{:S(2)}, u32[]{:S(2)}) %collective-permute-start.9) | collective-permute-done | bytes 393248 | tf_op jit(solution)/shard_map/ppermute | solution.py:439
  42.0 0.0 collective-permute-done.7.refs_10_
  42.0 0.0 copy-done.2
  42.0 5.6 %shard_map.62 = (f32[5,128,128]{2,1,0:T(8,128)S(1)}, f32[4,128,128]{2,1,0:T(8,128)S(1)}, f32[4,128,128]{2,1,0:T(8,128)S(1)}, f32[5,128,128]{2,1,0:T(8,128)S(1)},...) custom-call(f32[8,128,128]{2,1,0:T(8,128)S(1)} %get-tuple-element.56, ...), custom_call_target="tpu_custom_call" | custom-call | tf_op jit(solution)/shard_map/pallas_call | solution.py:392
  47.6 24.3 %all_to_all.20.got = f32[8,8,1152]{2,1,0:T(8,128)S(1)} all-to-all(f32[8,8,1152]{2,1,0:T(8,128)S(1)} %get-tuple-element.67), channel_id=1, replica_groups=mesh['z'=8,'xh'=2,'y'=4,'xl'=2,'c'=2] {'y','xl'}, dimensions={0} | all-to-all | bytes 589824 | tf_op jit(solution)/shard_map/all_to_all | solution.py:493
  71.9 0.0 copy-done.3
  71.9 5.4 %shard_map.63 = (f32[2,6,128,128]{3,2,1,0:T(8,128)S(1)}, f32[2,6,128,128]{3,2,1,0:T(8,128)S(1)}, f32[2,6,128,128]{3,2,1,0:T(8,128)S(1)}, f32[2,6,128,128]{3,2,1,...) custom-call(f32[8,8,1152]{2,1,0:T(8,128)S(1)} %all_to_all.20.got, f32[4,1024]{1,0:T(4,128)S(1)} %bitcast.11, ...), custom_call_target="tpu_custom_call" | custom-call | tf_op jit(solution)/shard_map/pallas_call | solution.py:392
  77.3 8.6 %all_to_all.21.got = f32[8,8,128]{2,1,0:T(8,128)S(1)} all-to-all(f32[8,8,128]{2,1,0:T(8,128)S(1)} %get-tuple-element.78), channel_id=1, replica_groups=mesh['z'=8,'xh'=2,'y'=4,'xl'=2,'c'=2] {'y','xl'}, dimensions={0} | all-to-all | bytes 65536 | tf_op jit(solution)/shard_map/all_to_all | solution.py:501
  85.9 1.3 shard_map.64
  87.2 0.1 collective-permute-start.10
  87.3 1.7 %collective-permute-done.10 = f32[8,6,16,128]{3,2,1,0:T(8,128)S(1)} collective-permute-done((f32[8,6,16,128]{3,2,1,0:T(8,128)S(1)}, f32[8,6,16,128]{3,2,1,0:T(8,128)S(1)}, u32[]{:S(2)}, u32[]{:S(2)}) %collective-permute-start.10) | collective-permute-done | bytes 393248 | tf_op jit(solution)/shard_map/ppermute | solution.py:439
  89.0 0.1 add.6
  89.1 23.2 %all_to_all.22 = f32[8,6,16,128]{3,2,1,0:T(8,128)S(1)} all-to-all(f32[8,6,16,128]{3,2,1,0:T(8,128)S(1)} %add.6), channel_id=1, replica_groups=mesh['z'=8,'xh'=2,'y'=4,'xl'=2,'c'=2] {'z'}, dimensions={0} | all-to-all | bytes 786432 | tf_op jit(solution)/shard_map/all_to_all | solution.py:510
  112.3 0.3 collective-permute-start.11
  112.6 5.4 %collective-permute-done.11 = f32[1,6,16,128]{3,2,1,0:T(8,128)S(1)} collective-permute-done((f32[1,6,16,128]{3,2,1,0:T(8,128)S(1)}, f32[1,6,16,128]{3,2,1,0:T(8,128)S(1)}, u32[]{:S(2)}, u32[]{:S(2)}) %collective-permute-start.11) | collective-permute-done | bytes 49184 | tf_op jit(solution)/shard_map/ppermute | solution.py:513
  118.0 0.8 broadcast_in_dim.13
  118.8 3.5 %all-to-all-start.3 = ((f32[8,6,16,128]{3,2,1,0:T(8,128)}), f32[8,6,16,128]{3,2,1,0:T(8,128)S(1)}, u32[]{:S(2)}, u32[]{:S(2)}) async-start(f32[8,6,16,128]{3,2,1,0:T(8,128)} %broadcast_in_dim.13), calls=%async_computation.3 | async-start | bytes 786432 | tf_op jit(solution)/shard_map/all_to_all | solution.py:515
  122.3 0.1 collective-permute-start.12
  122.4 1.2 collective-permute-done.12
  123.5 0.6 maximum_select_fusion
  124.1 10.8 %all-to-all-done.3 = f32[8,6,16,128]{3,2,1,0:T(8,128)S(1)} async-done(((f32[8,6,16,128]{3,2,1,0:T(8,128)}), f32[8,6,16,128]{3,2,1,0:T(8,128)S(1)}, u32[]{:S(2)}, u32[]{:S(2)}) %all-to-all-start.3) | async-done | bytes 393248 | tf_op jit(solution)/shard_map/all_to_all | solution.py:515
  134.9 0.8 copy.6
  (3 shorter events, 0.0 us)
Async XLA Ops:
  0.6 3.2 %collective-permute-start = (f32[4,2,128,128]{3,2,1,0:T(8,128)}, f32[4,2,128,128]{3,2,1,0:T(8,128)S(1)}, u32[]{:S(2)}, u32[]{:S(2)}) collective-permute-start(f32[4,2,128,128]{3,2,1,0:T(8,128)} %bitcast.p_own), channel_id=1, source_target_pairs={{0,1},{1,0},{2,3},{3,2},{4,5},{5,4},{6,7},{7,6},{8,9},{9,8},{10,11... | collective-permute-start | bytes 1572872 | tf_op jit(solution)/shard_map/ppermute | solution.py:439
  0.7 15.2 %collective-permute-start.2 = (f32[4,2,128,128]{3,2,1,0:T(8,128)}, f32[4,2,128,128]{3,2,1,0:T(8,128)S(1)}, u32[]{:S(2)}, u32[]{:S(2)}) collective-permute-start(f32[4,2,128,128]{3,2,1,0:T(8,128)} %bitcast.p_own), channel_id=1, source_target_pairs={{0,2},{1,3},{2,4},{3,5},{4,6},{5,7},{6,8},{7,9},{8,10},{9,11},{10,... | collective-permute-start | bytes 1572872 | tf_op jit(solution)/shard_map/ppermute | solution.py:439
  3.9 4.3 %collective-permute-start.1 = (f32[3,2,128,128]{3,2,1,0:T(8,128)}, f32[3,2,128,128]{3,2,1,0:T(8,128)S(1)}, u32[]{:S(2)}, u32[]{:S(2)}) collective-permute-start(f32[3,2,128,128]{3,2,1,0:T(8,128)} %c_own.1), channel_id=1, source_target_pairs={{0,1},{1,0},{2,3},{3,2},{4,5},{5,4},{6,7},{7,6},{8,9},{9,8},{10,11... | collective-permute-start | bytes 1179656 | tf_op jit(solution)/shard_map/ppermute | solution.py:439
  4.2 13.1 %collective-permute-start.4 = (f32[3,2,128,128]{3,2,1,0:T(8,128)}, f32[3,2,128,128]{3,2,1,0:T(8,128)S(1)}, u32[]{:S(2)}, u32[]{:S(2)}) collective-permute-start(f32[3,2,128,128]{3,2,1,0:T(8,128)} %c_own.1), channel_id=1, source_target_pairs={{0,18},{1,19},{2,20},{3,21},{4,22},{5,23},{6,24},{7,25},{8,26},{9,... | collective-permute-start | bytes 1179656 | tf_op jit(solution)/shard_map/ppermute | solution.py:439
  7.0 0.7 copy-start
  8.2 0.7 copy-start.1
  8.9 33.1 %copy-start.2 = (s32[1,1024]{1,0:T(1,128)S(1)}, s32[1,1024]{1,0:T(1,128)}, u32[]{:S(2)}) copy-start(s32[1,1024]{1,0:T(1,128)} %cells.5) | copy-start | bytes 12292
  16.0 3.2 %collective-permute-start.3 = (f32[4,2,128,128]{3,2,1,0:T(8,128)S(1)}, f32[4,2,128,128]{3,2,1,0:T(8,128)S(1)}, u32[]{:S(2)}, u32[]{:S(2)}) collective-permute-start(f32[4,2,128,128]{3,2,1,0:T(8,128)S(1)} %collective-permute-done.2.p_low), channel_id=1, source_target_pairs={{0,1},{1,0},{2,3},{3,2},{4,5},{5,4},{6,7},{7,6},{8,9},{9,8},{10,11... | collective-permute-start | bytes 1572872 | tf_op jit(solution)/shard_map/ppermute | solution.py:439
  16.0 23.5 %collective-permute-start.6 = (f32[4,2,128,128]{3,2,1,0:T(8,128)}, f32[4,2,128,128]{3,2,1,0:T(8,128)S(1)}, u32[]{:S(2)}, u32[]{:S(2)}) collective-permute-start(f32[4,2,128,128]{3,2,1,0:T(8,128)} %bitcast.p_own), channel_id=1, source_target_pairs={{2,0},{3,1},{4,2},{5,3},{6,4},{7,5},{8,6},{9,7},{10,8},{11,9},{12,... | collective-permute-start | bytes 1572872 | tf_op jit(solution)/shard_map/ppermute | solution.py:439
  17.3 1.9 %collective-permute-start.5 = (f32[3,2,128,128]{3,2,1,0:T(8,128)S(1)}, f32[3,2,128,128]{3,2,1,0:T(8,128)S(1)}, u32[]{:S(2)}, u32[]{:S(2)}) collective-permute-start(f32[3,2,128,128]{3,2,1,0:T(8,128)S(1)} %collective-permute-done.4.c_low), channel_id=1, source_target_pairs={{0,1},{1,0},{2,3},{3,2},{4,5},{5,4},{6,7},{7,6},{8,9},{9,8},{10,11... | collective-permute-start | bytes 1179656 | tf_op jit(solution)/shard_map/ppermute | solution.py:439
  17.9 21.6 %collective-permute-start.8 = (f32[3,2,128,128]{3,2,1,0:T(8,128)}, f32[3,2,128,128]{3,2,1,0:T(8,128)S(1)}, u32[]{:S(2)}, u32[]{:S(2)}) collective-permute-start(f32[3,2,128,128]{3,2,1,0:T(8,128)} %c_own.1), channel_id=1, source_target_pairs={{2,16},{3,17},{4,18},{5,19},{6,20},{7,21},{8,22},{9,23},{10,24},{1... | collective-permute-start | bytes 1179656 | tf_op jit(solution)/shard_map/ppermute | solution.py:439
  39.5 2.5 %collective-permute-start.7 = (f32[4,2,128,128]{3,2,1,0:T(8,128)S(1)}, f32[4,2,128,128]{3,2,1,0:T(8,128)S(1)}, u32[]{:S(2)}, u32[]{:S(2)}) collective-permute-start(f32[4,2,128,128]{3,2,1,0:T(8,128)S(1)} %collective-permute-done.6.refs_9_), channel_id=1, source_target_pairs={{0,1},{1,0},{2,3},{3,2},{4,5},{5,4},{6,7},{7,6},{8,9},{9,8},{10,11... | collective-permute-start | bytes 1572872 | tf_op jit(solution)/shard_map/ppermute | solution.py:439
  39.5 2.5 %collective-permute-start.9 = (f32[3,2,128,128]{3,2,1,0:T(8,128)S(1)}, f32[3,2,128,128]{3,2,1,0:T(8,128)S(1)}, u32[]{:S(2)}, u32[]{:S(2)}) collective-permute-start(f32[3,2,128,128]{3,2,1,0:T(8,128)S(1)} %collective-permute-done.8.refs_12_), channel_id=1, source_target_pairs={{0,1},{1,0},{2,3},{3,2},{4,5},{5,4},{6,7},{7,6},{8,9},{9,8},{10,11... | collective-permute-start | bytes 1179656 | tf_op jit(solution)/shard_map/ppermute | solution.py:439
  42.0 29.9 %copy-start.3 = (f32[1,4,1024]{2,1,0:T(4,128)S(1)}, f32[1,4,1024]{2,1,0:T(4,128)}, u32[]{:S(2)}) copy-start(f32[1,4,1024]{2,1,0:T(4,128)} %param.6) | copy-start | bytes 49156
  87.2 1.8 %collective-permute-start.10 = (f32[8,6,16,128]{3,2,1,0:T(8,128)S(1)}, f32[8,6,16,128]{3,2,1,0:T(8,128)S(1)}, u32[]{:S(2)}, u32[]{:S(2)}) collective-permute-start(f32[8,6,16,128]{3,2,1,0:T(8,128)S(1)} %get-tuple-element.86), channel_id=1, source_target_pairs={{0,1},{1,0},{2,3},{3,2},{4,5},{5,4},{6,7},{7,6},{8,9},{9,8},{10,11... | collective-permute-start | bytes 1179656 | tf_op jit(solution)/shard_map/ppermute | solution.py:439
  112.3 5.7 %collective-permute-start.11 = (f32[1,6,16,128]{3,2,1,0:T(8,128)S(1)}, f32[1,6,16,128]{3,2,1,0:T(8,128)S(1)}, u32[]{:S(2)}, u32[]{:S(2)}) collective-permute-start(f32[1,6,16,128]{3,2,1,0:T(8,128)S(1)} %bitcast.14), channel_id=1, source_target_pairs={{0,16},{16,0},{1,17},{17,1},{2,18},{18,2},{3,19},{19,3},{4,20},{20... | collective-permute-start | bytes 147464 | tf_op jit(solution)/shard_map/ppermute | solution.py:513
  118.8 16.1 %all-to-all-start.3 = ((f32[8,6,16,128]{3,2,1,0:T(8,128)}), f32[8,6,16,128]{3,2,1,0:T(8,128)S(1)}, u32[]{:S(2)}, u32[]{:S(2)}) async-start(f32[8,6,16,128]{3,2,1,0:T(8,128)} %broadcast_in_dim.13), calls=%async_computation.3 | async-start | bytes 786432 | tf_op jit(solution)/shard_map/all_to_all | solution.py:515
  122.3 1.3 collective-permute-start.12

commit v9 on v7

--- a/solution.py
+++ b/solution.py
@@ -184,8 +184,8 @@
 
 
 def forward_kernel(
-    p_mid, p_low, p_low_pair, p_high, p_high_pair,
-    c_mid, c_low, c_low_pair, c_high, c_high_pair, ky_mid, kz_mid, dg_mid, cells, hot_own, p_sample,
+    p_mid, p_near, p_near_pair, p_far, p_far_pair,
+    c_mid, c_near, c_near_pair, c_far, c_far_pair, ky_mid, kz_mid, dg_mid, cells, hot_own, p_sample,
     kx, ky, kz, dinv, dg, prim, t0, t1, t2, sent, cond, left, found,
 ):
     block = 2 * lax.axis_index("y") + lax.axis_index("xl")
@@ -193,10 +193,12 @@
     here = pl.ds(2 * core, 2)
     prim[:, 4:8] = p_mid[...]
     cond[4:8] = c_mid[...]
-    for base, first, second in ((0, p_low, p_low_pair), (8, p_high, p_high_pair)):
+    far = 8 * lax.axis_index("xl")
+    near = 8 - far
+    for base, first, second in ((near, p_near, p_near_pair), (far, p_far, p_far_pair)):
         prim[:, pl.ds(base + 2 * core, 2)] = first[here]
         prim[:, pl.ds(base + 2 - 2 * core, 2)] = second[here]
-    for base, first, second in ((0, c_low, c_low_pair), (8, c_high, c_high_pair)):
+    for base, first, second in ((near, c_near, c_near_pair), (far, c_far, c_far_pair)):
         cond[pl.ds(base + 2 * core, 2)] = first[0]
         cond[pl.ds(base + 2 - 2 * core, 2)] = second[0]
         for source, start in ((first, base + 2 * core), (second, base + 2 - 2 * core)):
@@ -378,17 +380,17 @@
 def per_device(high_count, primary, conductivity, observed, receivers):
     chain = CHIPS // 2
     sizes = (high_count, chain)
-    def step(by, around):
+    def beside(h, y, l, c):
+        return (h, y, 1 - l, c)
+
+    def around(h, y, l, c):
+        side = (2 * h + l + (1 if l == 1 else -1)) % (2 * high_count)
+        return (side // 2, y, side % 2, c)
+
+    def along(sign):
         def move(h, y, l, c):
-            block = 2 * y + l + by
-            if block < 0 or block >= CHIPS:
-                return None
-            side = 2 * h + l
-            if around:
-                wrap = 1 if (l == 1) else -1
-                side = (side + wrap) % (2 * high_count)
-                return (side // 2, block // 2, side % 2, c)
-            return (h, block // 2, block % 2, c)
+            target = y + sign * (1 if l == 0 else -1)
+            return (h, target, l, c) if 0 <= target < chain else None
 
         return routes(sizes, move)
 
@@ -397,10 +399,11 @@
 
     fields = primary[0]
     swap = routes(sizes, lambda h, y, l, c: (h, y, l, 1 - c))
-    p_low = send(fields, step(1, False))
-    p_high = send(fields, step(-1, False))
-    c_low = send(conductivity, step(1, True))
-    c_high = send(conductivity, step(-1, True))
+    p_near = send(fields, routes(sizes, beside))
+    c_near = send(conductivity, routes(sizes, around))
+    c_next = send(conductivity, along(-1))
+    p_far = send(p_near, along(1))
+    c_far = send(c_next, routes(sizes, beside))
 
     rows, lanes = primary.shape[3], primary.shape[4]
     count = receivers.shape[1]
@@ -421,10 +424,10 @@
     )(fields, p_pair, conductivity, c_pair, receivers, hot_own)
     ready = p_sample
     pairs_of = []
-    for x in (p_low, p_high, c_low, c_high):
+    for x in (p_near, c_near, c_far, p_far):
         x, token = lax.optimization_barrier((x, ready))
         pairs_of.append(send(x, swap))
-    p_low_pair, p_high_pair, c_low_pair, c_high_pair = pairs_of
+    p_near_pair, c_near_pair, c_far_pair, p_far_pair = pairs_of
     kx, ky, kz, dinv, dg, prim, f0, f1, f2, sent = call(
         forward_kernel,
         20,
@@ -435,8 +438,8 @@
             pltpu.VMEM((6, count), F32),
         ],
     )(
-        p_mid, p_low, p_low_pair, p_high, p_high_pair,
-        c_mid, c_low, c_low_pair, c_high, c_high_pair, ky_mid, kz_mid, dg_mid, receivers, hot_own, p_sample,
+        p_mid, p_near, p_near_pair, p_far, p_far_pair,
+        c_mid, c_near, c_near_pair, c_far, c_far_pair, ky_mid, kz_mid, dg_mid, receivers, hot_own, p_sample,
     )
     got = lax.all_to_all(sent, ("y", "xl"), 0, 0, tiled=True)
     six = (2, 6, rows, lanes)

time: 125 us -> 118 us (0.944)
  blocking collectives: 48.8 us -> 46 us
  starting transfers between devices: 14.1 us -> 11.5 us
  waiting for transfers between devices: 40.3 us -> 38.3 us
    all_to_all x2, blocking collectives: 25.5 us -> 22.7 us  [per_device(): got = lax.all_to_all(sent, ('y', 'xl'), 0, 0, tiled=True)]
    ppermute x12 -> x13, starting transfers between devices: 10.5 us -> 7.92 us  [send(): return lax.ppermute(x, NAMES, pairs)]
    ppermute x12 -> x13, waiting for transfers between devices: 24 us -> 21.9 us  [send(): return lax.ppermute(x, NAMES, pairs)]
  transfers between devices with their start and end apart: 14 -> 15, of which waited for: 8 -> 10; matrix products, arithmetic and copies ran while one was open for 0% -> 1% of each run, Pallas kernels for 1% -> 2%
where the time goes in v9:
time: 118 us; the launch traced here: 117 us
  blocking collectives  46 us (39%)
  waiting for transfers between devices  38.3 us (32%)
  Pallas kernels  15.9 us (13%)
  starting transfers between devices  11.5 us (10%)
  local copies, waits for them, and re-layouts  4.29 us (4%)
    all_to_all x1, blocking collectives, per_device(): parts = lax.all_to_all(total, 'z', 0, 0, tiled=True)  23.3 us
    all_to_all x2, blocking collectives, per_device(): got = lax.all_to_all(sent, ('y', 'xl'), 0, 0, tiled=True)  22.7 us
    ppermute x13, waiting for transfers between devices, send(): return lax.ppermute(x, NAMES, pairs)  21.9 us
    pallas_call x5, Pallas kernels, run(): pl.pallas_call(kernel, out_shape=tuple((jax.ShapeDtypeStruct(x, kind) for...  15.9 us
    all_to_all x1, waiting for transfers between devices, per_device(): whole = lax.all_to_all(spread, 'z', 0, 0, tiled=True)  10.8 us
    ppermute x13, starting transfers between devices, send(): return lax.ppermute(x, NAMES, pairs)  7.92 us
    ppermute x1, waiting for transfers between devices, per_device(): share = share + lax.ppermute(share, 'xh', [(0, 1), (1, 0)])  5.58 us
    all_to_all x1, starting transfers between devices, per_device(): whole = lax.all_to_all(spread, 'z', 0, 0, tiled=True)  3.45 us
  transfers between devices with their start and end apart: 15, of which 10 were waited for; matrix products, arithmetic and copies ran while one was open for 1% of the time, Pallas kernels for 2%

profile of v9, /device:TPU:4, one launch (start us, length us, event | category | flops | bytes accessed | tf_op | source)
XLA Modules:
  0.0 117.4 jit_solution(2547502264054767296)
XLA Ops:
  0.6 1.3 %collective-permute-start.2 = (f32[4,2,128,128]{3,2,1,0:T(8,128)}, f32[4,2,128,128]{3,2,1,0:T(8,128)S(1)}, u32[]{:S(2)}, u32[]{:S(2)}) collective-permute-start(f32[4,2,128,128]{3,2,1,0:T(8,128)} %bitcast.11), channel_id=1, source_target_pairs={{0,2},{1,3},{2,0},{3,1},{4,6},{5,7},{6,4},{7,5},{8,10},{9,11},{10,... | collective-permute-start | bytes 1572872 | tf_op jit(solution)/shard_map/ppermute | solution.py:398
  1.9 0.0 collective-permute-start
  1.9 1.3 %collective-permute-start.8 = (f32[3,2,128,128]{3,2,1,0:T(8,128)}, f32[3,2,128,128]{3,2,1,0:T(8,128)S(1)}, u32[]{:S(2)}, u32[]{:S(2)}) collective-permute-start(f32[3,2,128,128]{3,2,1,0:T(8,128)} %c_own.1), channel_id=1, source_target_pairs={{2,6},{3,7},{4,0},{5,1},{6,10},{7,11},{8,4},{9,5},{10,14},{11,15},... | collective-permute-start | bytes 1179656 | tf_op jit(solution)/shard_map/ppermute | solution.py:398
  3.2 11.4 %collective-permute-done.2.p_near = f32[4,2,128,128]{3,2,1,0:T(8,128)S(1)} collective-permute-done((f32[4,2,128,128]{3,2,1,0:T(8,128)}, f32[4,2,128,128]{3,2,1,0:T(8,128)S(1)}, u32[]{:S(2)}, u32[]{:S(2)}) %collective-permute-start.2) | collective-permute-done | bytes 524320 | tf_op jit(solution)/shard_map/ppermute | solution.py:398
  14.6 3.5 %collective-permute-start.4 = (f32[4,2,128,128]{3,2,1,0:T(8,128)S(1)}, f32[4,2,128,128]{3,2,1,0:T(8,128)S(1)}, u32[]{:S(2)}, u32[]{:S(2)}) collective-permute-start(f32[4,2,128,128]{3,2,1,0:T(8,128)S(1)} %collective-permute-done.2.p_near), channel_id=1, source_target_pairs={{0,4},{1,5},{4,8},{5,9},{6,2},{7,3},{8,12},{9,13},{10,6},{11,7},{1... | collective-permute-start | bytes 1572872 | tf_op jit(solution)/shard_map/ppermute | solution.py:398
  18.1 0.0 collective-permute-done.p_pair
  18.1 0.1 collective-permute-start.1
  18.2 0.0 collective-permute-done.8
  18.2 0.1 collective-permute-start.9
  18.3 1.1 collective-permute-start.6
  19.4 0.7 copy-done.2
  20.1 0.5 shard_map.59
  20.6 0.0 collective-permute-done.1.c_pair
  20.6 0.0 copy-start
  20.6 1.0 copy-done
  21.7 1.0 copy-done.1
  22.7 1.3 %shard_map.60 = (f32[2,4,128,128]{3,2,1,0:T(8,128)S(1)}, f32[4,128,128]{2,1,0:T(8,128)S(1)}, f32[4,128,128]{2,1,0:T(8,128)S(1)}, f32[4,128,128]{2,1,0:T(8,128)S(...) custom-call(f32[4,2,128,128]{3,2,1,0:T(8,128)S(1)} %bitcast.13, ...), custom_call_target="tpu_custom_call" | custom-call | tf_op jit(solution)/shard_map/pallas_call | solution.py:351
  24.0 0.1 collective-permute-start.3
  24.1 4.3 %collective-permute-done.4.p_far = f32[4,2,128,128]{3,2,1,0:T(8,128)S(1)} collective-permute-done((f32[4,2,128,128]{3,2,1,0:T(8,128)S(1)}, f32[4,2,128,128]{3,2,1,0:T(8,128)S(1)}, u32[]{:S(2)}, u32[]{:S(2)}) %collective-permute-start.4) | collective-permute-done | bytes 524320 | tf_op jit(solution)/shard_map/ppermute | solution.py:398
  28.4 0.0 collective-permute-start.5
  28.4 1.4 %collective-permute-done.9.c_far = f32[3,2,128,128]{3,2,1,0:T(8,128)S(1)} collective-permute-done((f32[3,2,128,128]{3,2,1,0:T(8,128)S(1)}, f32[3,2,128,128]{3,2,1,0:T(8,128)S(1)}, u32[]{:S(2)}, u32[]{:S(2)}) %collective-permute-start.9) | collective-permute-done | bytes 393248 | tf_op jit(solution)/shard_map/ppermute | solution.py:398
  29.8 0.0 collective-permute-start.10
  29.8 0.2 collective-permute-done.6.c_near
  29.9 0.3 collective-permute-start.7
  30.3 1.2 %collective-permute-done.10.c_far_pair = f32[3,2,128,128]{3,2,1,0:T(8,128)S(1)} collective-permute-done((f32[3,2,128,128]{3,2,1,0:T(8,128)S(1)}, f32[3,2,128,128]{3,2,1,0:T(8,128)S(1)}, u32[]{:S(2)}, u32[]{:S(2)}) %collective-permute-start.10) | collective-permute-done | bytes 393248 | tf_op jit(solution)/shard_map/ppermute | solution.py:398
  31.5 0.6 collective-permute-done.7.c_near_pair
  32.0 0.0 collective-permute-done.3.p_near_pair
  32.0 0.0 collective-permute-done.5.p_far_pair
  32.1 0.0 copy-done.3
  32.1 0.0 copy-start.4
  32.1 7.4 %shard_map.61 = (f32[12,128,128]{2,1,0:T(8,128)S(1)}, f32[12,128,128]{2,1,0:T(8,128)S(1)}, f32[12,128,128]{2,1,0:T(8,128)S(1)}, f32[12,128,128]{2,1,0:T(8,128)S(...) custom-call(f32[2,4,128,128]{3,2,1,0:T(8,128)S(1)} %get-tuple-elemen, ...), custom_call_target="tpu_custom_call" | custom-call | tf_op jit(solution)/shard_map/pallas_call | solution.py:351
  39.5 14.1 %all_to_all.20.got = f32[8,8,1152]{2,1,0:T(8,128)S(1)} all-to-all(f32[8,8,1152]{2,1,0:T(8,128)S(1)} %get-tuple-element.49), channel_id=1, replica_groups=mesh['z'=8,'xh'=2,'y'=4,'xl'=2,'c'=2] {'y','xl'}, dimensions={0} | all-to-all | bytes 589824 | tf_op jit(solution)/shard_map/all_to_all | solution.py:444
  53.6 5.4 %shard_map.62 = (f32[2,6,128,128]{3,2,1,0:T(8,128)S(1)}, f32[2,6,128,128]{3,2,1,0:T(8,128)S(1)}, f32[2,6,128,128]{3,2,1,0:T(8,128)S(1)}, f32[2,6,128,128]{3,2,1,...) custom-call(f32[8,8,1152]{2,1,0:T(8,128)S(1)} %all_to_all.20.got, f32[4,1024]{1,0:T(4,128)S(1)} %bitcast.14, ...), custom_call_target="tpu_custom_call" | custom-call | tf_op jit(solution)/shard_map/pallas_call | solution.py:351
  59.0 8.6 %all_to_all.21.got = f32[8,8,128]{2,1,0:T(8,128)S(1)} all-to-all(f32[8,8,128]{2,1,0:T(8,128)S(1)} %get-tuple-element.60), channel_id=1, replica_groups=mesh['z'=8,'xh'=2,'y'=4,'xl'=2,'c'=2] {'y','xl'}, dimensions={0} | all-to-all | bytes 65536 | tf_op jit(solution)/shard_map/all_to_all | solution.py:452
  67.6 1.3 %shard_map.63 = (f32[8,6,16,128]{3,2,1,0:T(8,128)S(1)}, f32[8,6,16,128]{3,2,1,0:T(8,128)S(1)}) custom-call(f32[8,8,128]{2,1,0:T(8,128)S(1)} %all_to_all.21.got, f32[2,6,128,128]{3,2,1,0:T(8,128)S(1)} %get-tuple-element.61.a0, f32[2,6,128,128]{3,2,1,0:T(8,128)S(1)} %get-tuple-element.62.a1, f32[2,6,128,128]{3,2,1,0:T(8,128)S(1)} %get-tuple-element.63.a2, ...), custom_call_target="tpu_custom_call" | custom-call | tf_op jit(solution)/shard_map/pallas_call | solution.py:351
  68.9 0.1 collective-permute-start.11
  69.0 1.7 %collective-permute-done.11 = f32[8,6,16,128]{3,2,1,0:T(8,128)S(1)} collective-permute-done((f32[8,6,16,128]{3,2,1,0:T(8,128)S(1)}, f32[8,6,16,128]{3,2,1,0:T(8,128)S(1)}, u32[]{:S(2)}, u32[]{:S(2)}) %collective-permute-start.11) | collective-permute-done | bytes 393248 | tf_op jit(solution)/shard_map/ppermute | solution.py:398
  70.7 0.1 add.6
  70.8 23.3 %all_to_all.22 = f32[8,6,16,128]{3,2,1,0:T(8,128)S(1)} all-to-all(f32[8,6,16,128]{3,2,1,0:T(8,128)S(1)} %add.6), channel_id=1, replica_groups=mesh['z'=8,'xh'=2,'y'=4,'xl'=2,'c'=2] {'z'}, dimensions={0} | all-to-all | bytes 786432 | tf_op jit(solution)/shard_map/all_to_all | solution.py:461
  94.1 0.1 collective-permute-start.12
  94.2 5.6 %collective-permute-done.12 = f32[1,6,16,128]{3,2,1,0:T(8,128)S(1)} collective-permute-done((f32[1,6,16,128]{3,2,1,0:T(8,128)S(1)}, f32[1,6,16,128]{3,2,1,0:T(8,128)S(1)}, u32[]{:S(2)}, u32[]{:S(2)}) %collective-permute-start.12) | collective-permute-done | bytes 49184 | tf_op jit(solution)/shard_map/ppermute | solution.py:464
  99.8 0.8 broadcast_in_dim.13
  100.5 3.5 %all-to-all-start.3 = ((f32[8,6,16,128]{3,2,1,0:T(8,128)}), f32[8,6,16,128]{3,2,1,0:T(8,128)S(1)}, u32[]{:S(2)}, u32[]{:S(2)}) async-start(f32[8,6,16,128]{3,2,1,0:T(8,128)} %broadcast_in_dim.13), calls=%async_computation.3 | async-start | bytes 786432 | tf_op jit(solution)/shard_map/all_to_all | solution.py:466
  104.0 0.1 collective-permute-start.13
  104.1 1.2 collective-permute-done.13
  105.3 0.6 maximum_select_fusion
  105.9 10.8 %all-to-all-done.3 = f32[8,6,16,128]{3,2,1,0:T(8,128)S(1)} async-done(((f32[8,6,16,128]{3,2,1,0:T(8,128)}), f32[8,6,16,128]{3,2,1,0:T(8,128)S(1)}, u32[]{:S(2)}, u32[]{:S(2)}) %all-to-all-start.3) | async-done | bytes 393248 | tf_op jit(solution)/shard_map/all_to_all | solution.py:466
  116.6 0.8 copy.6
  (6 shorter events, 0.0 us)
Async XLA Ops:
  0.6 14.0 %collective-permute-start.2 = (f32[4,2,128,128]{3,2,1,0:T(8,128)}, f32[4,2,128,128]{3,2,1,0:T(8,128)S(1)}, u32[]{:S(2)}, u32[]{:S(2)}) collective-permute-start(f32[4,2,128,128]{3,2,1,0:T(8,128)} %bitcast.11), channel_id=1, source_target_pairs={{0,2},{1,3},{2,0},{3,1},{4,6},{5,7},{6,4},{7,5},{8,10},{9,11},{10,... | collective-permute-start | bytes 1572872 | tf_op jit(solution)/shard_map/ppermute | solution.py:398
  1.9 16.2 %collective-permute-start = (f32[4,2,128,128]{3,2,1,0:T(8,128)}, f32[4,2,128,128]{3,2,1,0:T(8,128)S(1)}, u32[]{:S(2)}, u32[]{:S(2)}) collective-permute-start(f32[4,2,128,128]{3,2,1,0:T(8,128)} %bitcast.12), channel_id=1, source_target_pairs={{0,1},{1,0},{2,3},{3,2},{4,5},{5,4},{6,7},{7,6},{8,9},{9,8},{10,11... | collective-permute-start | bytes 1572872 | tf_op jit(solution)/shard_map/ppermute | solution.py:398
  1.9 16.3 %collective-permute-start.8 = (f32[3,2,128,128]{3,2,1,0:T(8,128)}, f32[3,2,128,128]{3,2,1,0:T(8,128)S(1)}, u32[]{:S(2)}, u32[]{:S(2)}) collective-permute-start(f32[3,2,128,128]{3,2,1,0:T(8,128)} %c_own.1), channel_id=1, source_target_pairs={{2,6},{3,7},{4,0},{5,1},{6,10},{7,11},{8,4},{9,5},{10,14},{11,15},... | collective-permute-start | bytes 1179656 | tf_op jit(solution)/shard_map/ppermute | solution.py:398
  14.6 13.8 %collective-permute-start.4 = (f32[4,2,128,128]{3,2,1,0:T(8,128)S(1)}, f32[4,2,128,128]{3,2,1,0:T(8,128)S(1)}, u32[]{:S(2)}, u32[]{:S(2)}) collective-permute-start(f32[4,2,128,128]{3,2,1,0:T(8,128)S(1)} %collective-permute-done.2.p_near), channel_id=1, source_target_pairs={{0,4},{1,5},{4,8},{5,9},{6,2},{7,3},{8,12},{9,13},{10,6},{11,7},{1... | collective-permute-start | bytes 1572872 | tf_op jit(solution)/shard_map/ppermute | solution.py:398
  18.1 2.5 %collective-permute-start.1 = (f32[3,2,128,128]{3,2,1,0:T(8,128)}, f32[3,2,128,128]{3,2,1,0:T(8,128)S(1)}, u32[]{:S(2)}, u32[]{:S(2)}) collective-permute-start(f32[3,2,128,128]{3,2,1,0:T(8,128)} %c_own.1), channel_id=1, source_target_pairs={{0,1},{1,0},{2,3},{3,2},{4,5},{5,4},{6,7},{7,6},{8,9},{9,8},{10,11... | collective-permute-start | bytes 1179656 | tf_op jit(solution)/shard_map/ppermute | solution.py:398
  18.2 11.5 %collective-permute-start.9 = (f32[3,2,128,128]{3,2,1,0:T(8,128)S(1)}, f32[3,2,128,128]{3,2,1,0:T(8,128)S(1)}, u32[]{:S(2)}, u32[]{:S(2)}) collective-permute-start(f32[3,2,128,128]{3,2,1,0:T(8,128)S(1)} %collective-permute-done.8), channel_id=1, source_target_pairs={{0,2},{1,3},{2,0},{3,1},{4,6},{5,7},{6,4},{7,5},{8,10},{9,11},{10,... | collective-permute-start | bytes 1179656 | tf_op jit(solution)/shard_map/ppermute | solution.py:398
  18.3 11.6 %collective-permute-start.6 = (f32[3,2,128,128]{3,2,1,0:T(8,128)}, f32[3,2,128,128]{3,2,1,0:T(8,128)S(1)}, u32[]{:S(2)}, u32[]{:S(2)}) collective-permute-start(f32[3,2,128,128]{3,2,1,0:T(8,128)} %c_own.1), channel_id=1, source_target_pairs={{0,18},{1,19},{2,16},{3,17},{4,22},{5,23},{6,20},{7,21},{8,26},{9,... | collective-permute-start | bytes 1179656 | tf_op jit(solution)/shard_map/ppermute | solution.py:398
  19.4 0.7 copy-start.2
  20.6 1.0 copy-start
  21.7 1.0 copy-start.1
  22.7 9.4 %copy-start.3 = (s32[1,1024]{1,0:T(1,128)S(1)}, s32[1,1024]{1,0:T(1,128)}, u32[]{:S(2)}) copy-start(s32[1,1024]{1,0:T(1,128)} %cells.7) | copy-start | bytes 12292
  24.0 8.1 %collective-permute-start.3 = (f32[4,2,128,128]{3,2,1,0:T(8,128)S(1)}, f32[4,2,128,128]{3,2,1,0:T(8,128)S(1)}, u32[]{:S(2)}, u32[]{:S(2)}) collective-permute-start(f32[4,2,128,128]{3,2,1,0:T(8,128)S(1)} %collective-permute-done.2.p_near), channel_id=1, source_target_pairs={{0,1},{1,0},{2,3},{3,2},{4,5},{5,4},{6,7},{7,6},{8,9},{9,8},{10,11... | collective-permute-start | bytes 1572872 | tf_op jit(solution)/shard_map/ppermute | solution.py:398
  28.4 3.7 %collective-permute-start.5 = (f32[4,2,128,128]{3,2,1,0:T(8,128)S(1)}, f32[4,2,128,128]{3,2,1,0:T(8,128)S(1)}, u32[]{:S(2)}, u32[]{:S(2)}) collective-permute-start(f32[4,2,128,128]{3,2,1,0:T(8,128)S(1)} %collective-permute-done.4.p_far), channel_id=1, source_target_pairs={{0,1},{1,0},{2,3},{3,2},{4,5},{5,4},{6,7},{7,6},{8,9},{9,8},{10,11... | collective-permute-start | bytes 1572872 | tf_op jit(solution)/shard_map/ppermute | solution.py:398
  29.8 1.7 %collective-permute-start.10 = (f32[3,2,128,128]{3,2,1,0:T(8,128)S(1)}, f32[3,2,128,128]{3,2,1,0:T(8,128)S(1)}, u32[]{:S(2)}, u32[]{:S(2)}) collective-permute-start(f32[3,2,128,128]{3,2,1,0:T(8,128)S(1)} %collective-permute-done.9.c_far), channel_id=1, source_target_pairs={{0,1},{1,0},{2,3},{3,2},{4,5},{5,4},{6,7},{7,6},{8,9},{9,8},{10,11... | collective-permute-start | bytes 1179656 | tf_op jit(solution)/shard_map/ppermute | solution.py:398
  29.9 2.1 %collective-permute-start.7 = (f32[3,2,128,128]{3,2,1,0:T(8,128)S(1)}, f32[3,2,128,128]{3,2,1,0:T(8,128)S(1)}, u32[]{:S(2)}, u32[]{:S(2)}) collective-permute-start(f32[3,2,128,128]{3,2,1,0:T(8,128)S(1)} %collective-permute-done.6.c_near), channel_id=1, source_target_pairs={{0,1},{1,0},{2,3},{3,2},{4,5},{5,4},{6,7},{7,6},{8,9},{9,8},{10,11... | collective-permute-start | bytes 1179656 | tf_op jit(solution)/shard_map/ppermute | solution.py:398
  32.1 21.5 %copy-start.4 = (f32[1,4,1024]{2,1,0:T(4,128)S(1)}, f32[1,4,1024]{2,1,0:T(4,128)}, u32[]{:S(2)}) copy-start(f32[1,4,1024]{2,1,0:T(4,128)} %param.6) | copy-start | bytes 49156
  68.9 1.8 %collective-permute-start.11 = (f32[8,6,16,128]{3,2,1,0:T(8,128)S(1)}, f32[8,6,16,128]{3,2,1,0:T(8,128)S(1)}, u32[]{:S(2)}, u32[]{:S(2)}) collective-permute-start(f32[8,6,16,128]{3,2,1,0:T(8,128)S(1)} %get-tuple-element.68), channel_id=1, source_target_pairs={{0,1},{1,0},{2,3},{3,2},{4,5},{5,4},{6,7},{7,6},{8,9},{9,8},{10,11... | collective-permute-start | bytes 1179656 | tf_op jit(solution)/shard_map/ppermute | solution.py:398
  94.1 5.7 %collective-permute-start.12 = (f32[1,6,16,128]{3,2,1,0:T(8,128)S(1)}, f32[1,6,16,128]{3,2,1,0:T(8,128)S(1)}, u32[]{:S(2)}, u32[]{:S(2)}) collective-permute-start(f32[1,6,16,128]{3,2,1,0:T(8,128)S(1)} %bitcast.17), channel_id=1, source_target_pairs={{0,16},{16,0},{1,17},{17,1},{2,18},{18,2},{3,19},{19,3},{4,20},{20... | collective-permute-start | bytes 147464 | tf_op jit(solution)/shard_map/ppermute | solution.py:464
  100.5 16.1 %all-to-all-start.3 = ((f32[8,6,16,128]{3,2,1,0:T(8,128)}), f32[8,6,16,128]{3,2,1,0:T(8,128)S(1)}, u32[]{:S(2)}, u32[]{:S(2)}) async-start(f32[8,6,16,128]{3,2,1,0:T(8,128)} %broadcast_in_dim.13), calls=%async_computation.3 | async-start | bytes 786432 | tf_op jit(solution)/shard_map/all_to_all | solution.py:466
  104.0 1.3 %collective-permute-start.13 = (f32[2,1024]{1,0:T(2,128)S(1)}, f32[2,1024]{1,0:T(2,128)S(1)}, u32[]{:S(2)}, u32[]{:S(2)}) collective-permute-start(f32[2,1024]{1,0:T(2,128)S(1)} %get-tuple-element.69), channel_id=1, source_target_pairs={{0,1},{1,0},{2,3},{3,2},{4,5},{5,4},{6,7},{7,6},{8,9},{9,8},{10,11... | collective-permute-start | bytes 24584 | tf_op jit(solution)/shard_map/ppermute | solution.py:398

commit v10 on v9

--- a/solution.py
+++ b/solution.py
@@ -402,6 +402,7 @@
     p_near = send(fields, routes(sizes, beside))
     c_near = send(conductivity, routes(sizes, around))
     c_next = send(conductivity, along(-1))
+    p_near, c_near = lax.optimization_barrier((p_near, c_near))
     p_far = send(p_near, along(1))
     c_far = send(c_next, routes(sizes, beside))
 
@@ -422,12 +423,14 @@
         [f32(2, KEPT, rows, lanes), four, four, four, four, f32(2, count)],
         [pltpu.VMEM((2 * lanes, 3 * KEPT * rows), BF16)],
     )(fields, p_pair, conductivity, c_pair, receivers, hot_own)
-    ready = p_sample
-    pairs_of = []
-    for x in (p_near, c_near, c_far, p_far):
-        x, token = lax.optimization_barrier((x, ready))
-        pairs_of.append(send(x, swap))
-    p_near_pair, c_near_pair, c_far_pair, p_far_pair = pairs_of
+    def paired(x, ready):
+        x, ready = lax.optimization_barrier((x, ready))
+        return x, send(x, swap)
+
+    p_near, p_near_pair = paired(p_near, p_sample)
+    c_near, c_near_pair = paired(c_near, p_sample)
+    c_far, c_far_pair = paired(c_far, p_sample)
+    p_far, p_far_pair = paired(p_far, (p_near_pair, c_near_pair, c_far_pair))
     kx, ky, kz, dinv, dg, prim, f0, f1, f2, sent = call(
         forward_kernel,
         20,

time: 118 us -> 120 us (1.017)
  starting transfers between devices: 11.5 us -> 14.2 us
    ppermute x13, starting transfers between devices: 7.92 us -> 9.82 us  [send(): return lax.ppermute(x, NAMES, pairs)]
where the time goes in v10:
time: 120 us
  blocking collectives  45.7 us (38%)
  waiting for transfers between devices  38.2 us (32%)
  Pallas kernels  15.9 us (13%)
  starting transfers between devices  14.2 us (12%)
  local copies, waits for them, and re-layouts  4.29 us (4%)
    all_to_all x1, blocking collectives, per_device(): parts = lax.all_to_all(total, 'z', 0, 0, tiled=True)  23.3 us
    ppermute x13, waiting for transfers between devices, send(): return lax.ppermute(x, NAMES, pairs)  22.7 us
    all_to_all x2, blocking collectives, per_device(): got = lax.all_to_all(sent, ('y', 'xl'), 0, 0, tiled=True)  22.5 us
    pallas_call x5, Pallas kernels, run(): pl.pallas_call(kernel, out_shape=tuple((jax.ShapeDtypeStruct(x, kind) for...  15.9 us
    all_to_all x1, waiting for transfers between devices, per_device(): whole = lax.all_to_all(spread, 'z', 0, 0, tiled=True)  10.8 us
    ppermute x13, starting transfers between devices, send(): return lax.ppermute(x, NAMES, pairs)  9.82 us
    ppermute x1, waiting for transfers between devices, per_device(): share = share + lax.ppermute(share, 'xh', [(0, 1), (1, 0)])  4.8 us
    all_to_all x1, starting transfers between devices, per_device(): whole = lax.all_to_all(spread, 'z', 0, 0, tiled=True)  3.45 us
  transfers between devices with their start and end apart: 15, of which 10 were waited for; matrix products, arithmetic and copies ran while one was open for 1% of the time, Pallas kernels for 2%

profile of v10, /device:TPU:4, one launch (start us, length us, event | category | flops | bytes accessed | tf_op | source)
XLA Modules:
  0.0 119.8 jit_solution(9359753229769019255)
XLA Ops:
  0.6 0.1 collective-permute-start
  0.7 1.3 %collective-permute-start.7 = (f32[3,2,128,128]{3,2,1,0:T(8,128)}, f32[3,2,128,128]{3,2,1,0:T(8,128)S(1)}, u32[]{:S(2)}, u32[]{:S(2)}) collective-permute-start(f32[3,2,128,128]{3,2,1,0:T(8,128)} %c_own.1), channel_id=1, source_target_pairs={{2,6},{3,7},{4,0},{5,1},{6,10},{7,11},{8,4},{9,5},{10,14},{11,15},... | collective-permute-start | bytes 1179656 | tf_op jit(solution)/shard_map/ppermute | solution.py:398
  2.0 3.5 %collective-permute-start.2 = (f32[4,2,128,128]{3,2,1,0:T(8,128)}, f32[4,2,128,128]{3,2,1,0:T(8,128)S(1)}, u32[]{:S(2)}, u32[]{:S(2)}) collective-permute-start(f32[4,2,128,128]{3,2,1,0:T(8,128)} %bitcast.12), channel_id=1, source_target_pairs={{0,2},{1,3},{2,0},{3,1},{4,6},{5,7},{6,4},{7,5},{8,10},{9,11},{10,... | collective-permute-start | bytes 1572872 | tf_op jit(solution)/shard_map/ppermute | solution.py:398
  5.5 0.0 collective-permute-start.3
  5.5 0.0 collective-permute-done.p_pair
  5.5 0.0 collective-permute-start.1
  5.5 8.8 %collective-permute-done.7 = f32[3,2,128,128]{3,2,1,0:T(8,128)S(1)} collective-permute-done((f32[3,2,128,128]{3,2,1,0:T(8,128)}, f32[3,2,128,128]{3,2,1,0:T(8,128)S(1)}, u32[]{:S(2)}, u32[]{:S(2)}) %collective-permute-start.7) | collective-permute-done | bytes 393248 | tf_op jit(solution)/shard_map/ppermute | solution.py:398
  14.3 0.4 collective-permute-start.8
  14.7 0.7 copy-done.2
  15.4 0.5 shard_map.59
  16.0 0.7 collective-permute-done.3.c_near
  16.7 1.8 %collective-permute-done.2.p_near = f32[4,2,128,128]{3,2,1,0:T(8,128)S(1)} collective-permute-done((f32[4,2,128,128]{3,2,1,0:T(8,128)}, f32[4,2,128,128]{3,2,1,0:T(8,128)S(1)}, u32[]{:S(2)}, u32[]{:S(2)}) %collective-permute-start.2) | collective-permute-done | bytes 524320 | tf_op jit(solution)/shard_map/ppermute | solution.py:398
  18.4 3.5 %collective-permute-start.5 = (f32[4,2,128,128]{3,2,1,0:T(8,128)S(1)}, f32[4,2,128,128]{3,2,1,0:T(8,128)S(1)}, u32[]{:S(2)}, u32[]{:S(2)}) collective-permute-start(f32[4,2,128,128]{3,2,1,0:T(8,128)S(1)} %collective-permute-done.2.p_near), channel_id=1, source_target_pairs={{0,4},{1,5},{4,8},{5,9},{6,2},{7,3},{8,12},{9,13},{10,6},{11,7},{1... | collective-permute-start | bytes 1572872 | tf_op jit(solution)/shard_map/ppermute | solution.py:398
  21.9 0.0 collective-permute-done.1.c_pair
  21.9 0.0 copy-start
  22.0 1.0 copy-done
  23.0 1.0 copy-done.1
  24.0 1.3 %shard_map.60 = (f32[2,4,128,128]{3,2,1,0:T(8,128)S(1)}, f32[4,128,128]{2,1,0:T(8,128)S(1)}, f32[4,128,128]{2,1,0:T(8,128)S(1)}, f32[4,128,128]{2,1,0:T(8,128)S(...) custom-call(f32[4,2,128,128]{3,2,1,0:T(8,128)S(1)} %bitcast.13, ...), custom_call_target="tpu_custom_call" | custom-call | tf_op jit(solution)/shard_map/pallas_call | solution.py:351
  25.3 0.1 collective-permute-start.4
  25.4 0.5 collective-permute-start.6
  25.9 0.6 collective-permute-done.8.c_far
  26.5 0.0 collective-permute-start.9
  26.5 6.1 %collective-permute-done.5.p_far = f32[4,2,128,128]{3,2,1,0:T(8,128)S(1)} collective-permute-done((f32[4,2,128,128]{3,2,1,0:T(8,128)S(1)}, f32[4,2,128,128]{3,2,1,0:T(8,128)S(1)}, u32[]{:S(2)}, u32[]{:S(2)}) %collective-permute-start.5) | collective-permute-done | bytes 524320 | tf_op jit(solution)/shard_map/ppermute | solution.py:398
  32.5 0.0 collective-permute-done.6.c_near_pair
  32.5 0.0 collective-permute-done.9.c_far_pair
  32.5 0.0 collective-permute-done.4.p_near_pair
  32.5 0.3 collective-permute-start.10
  32.8 1.9 %collective-permute-done.10.p_far_pair = f32[4,2,128,128]{3,2,1,0:T(8,128)S(1)} collective-permute-done((f32[4,2,128,128]{3,2,1,0:T(8,128)S(1)}, f32[4,2,128,128]{3,2,1,0:T(8,128)S(1)}, u32[]{:S(2)}, u32[]{:S(2)}) %collective-permute-start.10) | collective-permute-done | bytes 524320 | tf_op jit(solution)/shard_map/ppermute | solution.py:398
  34.7 0.0 copy-done.3
  34.7 7.4 %shard_map.61 = (f32[12,128,128]{2,1,0:T(8,128)S(1)}, f32[12,128,128]{2,1,0:T(8,128)S(1)}, f32[12,128,128]{2,1,0:T(8,128)S(1)}, f32[12,128,128]{2,1,0:T(8,128)S(...) custom-call(f32[2,4,128,128]{3,2,1,0:T(8,128)S(1)} %get-tuple-elemen, ...), custom_call_target="tpu_custom_call" | custom-call | tf_op jit(solution)/shard_map/pallas_call | solution.py:351
  42.1 13.8 %all_to_all.20.got = f32[8,8,1152]{2,1,0:T(8,128)S(1)} all-to-all(f32[8,8,1152]{2,1,0:T(8,128)S(1)} %get-tuple-element.53), channel_id=1, replica_groups=mesh['z'=8,'xh'=2,'y'=4,'xl'=2,'c'=2] {'y','xl'}, dimensions={0} | all-to-all | bytes 589824 | tf_op jit(solution)/shard_map/all_to_all | solution.py:447
  55.9 0.0 copy-done.4
  55.9 5.4 %shard_map.62 = (f32[2,6,128,128]{3,2,1,0:T(8,128)S(1)}, f32[2,6,128,128]{3,2,1,0:T(8,128)S(1)}, f32[2,6,128,128]{3,2,1,0:T(8,128)S(1)}, f32[2,6,128,128]{3,2,1,...) custom-call(f32[8,8,1152]{2,1,0:T(8,128)S(1)} %all_to_all.20.got, f32[4,1024]{1,0:T(4,128)S(1)} %bitcast.14, ...), custom_call_target="tpu_custom_call" | custom-call | tf_op jit(solution)/shard_map/pallas_call | solution.py:351
  61.4 8.6 %all_to_all.21.got = f32[8,8,128]{2,1,0:T(8,128)S(1)} all-to-all(f32[8,8,128]{2,1,0:T(8,128)S(1)} %get-tuple-element.64), channel_id=1, replica_groups=mesh['z'=8,'xh'=2,'y'=4,'xl'=2,'c'=2] {'y','xl'}, dimensions={0} | all-to-all | bytes 65536 | tf_op jit(solution)/shard_map/all_to_all | solution.py:455
  70.0 1.3 %shard_map.63 = (f32[8,6,16,128]{3,2,1,0:T(8,128)S(1)}, f32[8,6,16,128]{3,2,1,0:T(8,128)S(1)}) custom-call(f32[8,8,128]{2,1,0:T(8,128)S(1)} %all_to_all.21.got, f32[2,6,128,128]{3,2,1,0:T(8,128)S(1)} %get-tuple-element.65.a0, f32[2,6,128,128]{3,2,1,0:T(8,128)S(1)} %get-tuple-element.66.a1, f32[2,6,128,128]{3,2,1,0:T(8,128)S(1)} %get-tuple-element.67.a2, ...), custom_call_target="tpu_custom_call" | custom-call | tf_op jit(solution)/shard_map/pallas_call | solution.py:351
  71.3 0.1 collective-permute-start.11
  71.4 1.7 %collective-permute-done.11 = f32[8,6,16,128]{3,2,1,0:T(8,128)S(1)} collective-permute-done((f32[8,6,16,128]{3,2,1,0:T(8,128)S(1)}, f32[8,6,16,128]{3,2,1,0:T(8,128)S(1)}, u32[]{:S(2)}, u32[]{:S(2)}) %collective-permute-start.11) | collective-permute-done | bytes 393248 | tf_op jit(solution)/shard_map/ppermute | solution.py:398
  73.1 0.1 add.6
  73.2 23.3 %all_to_all.22 = f32[8,6,16,128]{3,2,1,0:T(8,128)S(1)} all-to-all(f32[8,6,16,128]{3,2,1,0:T(8,128)S(1)} %add.6), channel_id=1, replica_groups=mesh['z'=8,'xh'=2,'y'=4,'xl'=2,'c'=2] {'z'}, dimensions={0} | all-to-all | bytes 786432 | tf_op jit(solution)/shard_map/all_to_all | solution.py:464
  96.4 0.9 collective-permute-start.12
  97.3 4.8 %collective-permute-done.12 = f32[1,6,16,128]{3,2,1,0:T(8,128)S(1)} collective-permute-done((f32[1,6,16,128]{3,2,1,0:T(8,128)S(1)}, f32[1,6,16,128]{3,2,1,0:T(8,128)S(1)}, u32[]{:S(2)}, u32[]{:S(2)}) %collective-permute-start.12) | collective-permute-done | bytes 49184 | tf_op jit(solution)/shard_map/ppermute | solution.py:467
  102.1 0.8 broadcast_in_dim.13
  102.9 3.5 %all-to-all-start.3 = ((f32[8,6,16,128]{3,2,1,0:T(8,128)}), f32[8,6,16,128]{3,2,1,0:T(8,128)S(1)}, u32[]{:S(2)}, u32[]{:S(2)}) async-start(f32[8,6,16,128]{3,2,1,0:T(8,128)} %broadcast_in_dim.13), calls=%async_computation.3 | async-start | bytes 786432 | tf_op jit(solution)/shard_map/all_to_all | solution.py:469
  106.4 0.1 collective-permute-start.13
  106.5 1.2 collective-permute-done.13
  107.6 0.6 maximum_select_fusion
  108.3 10.8 %all-to-all-done.3 = f32[8,6,16,128]{3,2,1,0:T(8,128)S(1)} async-done(((f32[8,6,16,128]{3,2,1,0:T(8,128)}), f32[8,6,16,128]{3,2,1,0:T(8,128)S(1)}, u32[]{:S(2)}, u32[]{:S(2)}) %all-to-all-start.3) | async-done | bytes 393248 | tf_op jit(solution)/shard_map/all_to_all | solution.py:469
  119.0 0.8 copy.6
  (6 shorter events, 0.0 us)
Async XLA Ops:
  0.6 4.9 %collective-permute-start = (f32[4,2,128,128]{3,2,1,0:T(8,128)}, f32[4,2,128,128]{3,2,1,0:T(8,128)S(1)}, u32[]{:S(2)}, u32[]{:S(2)}) collective-permute-start(f32[4,2,128,128]{3,2,1,0:T(8,128)} %bitcast.11), channel_id=1, source_target_pairs={{0,1},{1,0},{2,3},{3,2},{4,5},{5,4},{6,7},{7,6},{8,9},{9,8},{10,11... | collective-permute-start | bytes 1572872 | tf_op jit(solution)/shard_map/ppermute | solution.py:398
  0.7 13.6 %collective-permute-start.7 = (f32[3,2,128,128]{3,2,1,0:T(8,128)}, f32[3,2,128,128]{3,2,1,0:T(8,128)S(1)}, u32[]{:S(2)}, u32[]{:S(2)}) collective-permute-start(f32[3,2,128,128]{3,2,1,0:T(8,128)} %c_own.1), channel_id=1, source_target_pairs={{2,6},{3,7},{4,0},{5,1},{6,10},{7,11},{8,4},{9,5},{10,14},{11,15},... | collective-permute-start | bytes 1179656 | tf_op jit(solution)/shard_map/ppermute | solution.py:398
  2.0 16.4 %collective-permute-start.2 = (f32[4,2,128,128]{3,2,1,0:T(8,128)}, f32[4,2,128,128]{3,2,1,0:T(8,128)S(1)}, u32[]{:S(2)}, u32[]{:S(2)}) collective-permute-start(f32[4,2,128,128]{3,2,1,0:T(8,128)} %bitcast.12), channel_id=1, source_target_pairs={{0,2},{1,3},{2,0},{3,1},{4,6},{5,7},{6,4},{7,5},{8,10},{9,11},{10,... | collective-permute-start | bytes 1572872 | tf_op jit(solution)/shard_map/ppermute | solution.py:398
  5.5 11.2 %collective-permute-start.3 = (f32[3,2,128,128]{3,2,1,0:T(8,128)}, f32[3,2,128,128]{3,2,1,0:T(8,128)S(1)}, u32[]{:S(2)}, u32[]{:S(2)}) collective-permute-start(f32[3,2,128,128]{3,2,1,0:T(8,128)} %c_own.1), channel_id=1, source_target_pairs={{0,18},{1,19},{2,16},{3,17},{4,22},{5,23},{6,20},{7,21},{8,26},{9,... | collective-permute-start | bytes 1179656 | tf_op jit(solution)/shard_map/ppermute | solution.py:398
  5.5 16.4 %collective-permute-start.1 = (f32[3,2,128,128]{3,2,1,0:T(8,128)}, f32[3,2,128,128]{3,2,1,0:T(8,128)S(1)}, u32[]{:S(2)}, u32[]{:S(2)}) collective-permute-start(f32[3,2,128,128]{3,2,1,0:T(8,128)} %c_own.1), channel_id=1, source_target_pairs={{0,1},{1,0},{2,3},{3,2},{4,5},{5,4},{6,7},{7,6},{8,9},{9,8},{10,11... | collective-permute-start | bytes 1179656 | tf_op jit(solution)/shard_map/ppermute | solution.py:398
  14.3 12.1 %collective-permute-start.8 = (f32[3,2,128,128]{3,2,1,0:T(8,128)S(1)}, f32[3,2,128,128]{3,2,1,0:T(8,128)S(1)}, u32[]{:S(2)}, u32[]{:S(2)}) collective-permute-start(f32[3,2,128,128]{3,2,1,0:T(8,128)S(1)} %collective-permute-done.7), channel_id=1, source_target_pairs={{0,2},{1,3},{2,0},{3,1},{4,6},{5,7},{6,4},{7,5},{8,10},{9,11},{10,... | collective-permute-start | bytes 1179656 | tf_op jit(solution)/shard_map/ppermute | solution.py:398
  14.7 0.7 copy-start.2
  18.4 14.1 %collective-permute-start.5 = (f32[4,2,128,128]{3,2,1,0:T(8,128)S(1)}, f32[4,2,128,128]{3,2,1,0:T(8,128)S(1)}, u32[]{:S(2)}, u32[]{:S(2)}) collective-permute-start(f32[4,2,128,128]{3,2,1,0:T(8,128)S(1)} %collective-permute-done.2.p_near), channel_id=1, source_target_pairs={{0,4},{1,5},{4,8},{5,9},{6,2},{7,3},{8,12},{9,13},{10,6},{11,7},{1... | collective-permute-start | bytes 1572872 | tf_op jit(solution)/shard_map/ppermute | solution.py:398
  21.9 1.0 copy-start
  23.0 1.0 copy-start.1
  24.0 10.7 %copy-start.3 = (s32[1,1024]{1,0:T(1,128)S(1)}, s32[1,1024]{1,0:T(1,128)}, u32[]{:S(2)}) copy-start(s32[1,1024]{1,0:T(1,128)} %cells.7) | copy-start | bytes 12292
  25.3 7.3 %collective-permute-start.4 = (f32[4,2,128,128]{3,2,1,0:T(8,128)S(1)}, f32[4,2,128,128]{3,2,1,0:T(8,128)S(1)}, u32[]{:S(2)}, u32[]{:S(2)}) collective-permute-start(f32[4,2,128,128]{3,2,1,0:T(8,128)S(1)} %collective-permute-done.2.p_near), channel_id=1, source_target_pairs={{0,1},{1,0},{2,3},{3,2},{4,5},{5,4},{6,7},{7,6},{8,9},{9,8},{10,11... | collective-permute-start | bytes 1572872 | tf_op jit(solution)/shard_map/ppermute | solution.py:398
  25.4 7.2 %collective-permute-start.6 = (f32[3,2,128,128]{3,2,1,0:T(8,128)S(1)}, f32[3,2,128,128]{3,2,1,0:T(8,128)S(1)}, u32[]{:S(2)}, u32[]{:S(2)}) collective-permute-start(f32[3,2,128,128]{3,2,1,0:T(8,128)S(1)} %collective-permute-done.3.c_near), channel_id=1, source_target_pairs={{0,1},{1,0},{2,3},{3,2},{4,5},{5,4},{6,7},{7,6},{8,9},{9,8},{10,11... | collective-permute-start | bytes 1179656 | tf_op jit(solution)/shard_map/ppermute | solution.py:398
  26.5 6.1 %collective-permute-start.9 = (f32[3,2,128,128]{3,2,1,0:T(8,128)S(1)}, f32[3,2,128,128]{3,2,1,0:T(8,128)S(1)}, u32[]{:S(2)}, u32[]{:S(2)}) collective-permute-start(f32[3,2,128,128]{3,2,1,0:T(8,128)S(1)} %collective-permute-done.8.c_far), channel_id=1, source_target_pairs={{0,1},{1,0},{2,3},{3,2},{4,5},{5,4},{6,7},{7,6},{8,9},{9,8},{10,11... | collective-permute-start | bytes 1179656 | tf_op jit(solution)/shard_map/ppermute | solution.py:398
  32.5 2.2 %collective-permute-start.10 = (f32[4,2,128,128]{3,2,1,0:T(8,128)S(1)}, f32[4,2,128,128]{3,2,1,0:T(8,128)S(1)}, u32[]{:S(2)}, u32[]{:S(2)}) collective-permute-start(f32[4,2,128,128]{3,2,1,0:T(8,128)S(1)} %collective-permute-done.5.p_far), channel_id=1, source_target_pairs={{0,1},{1,0},{2,3},{3,2},{4,5},{5,4},{6,7},{7,6},{8,9},{9,8},{10,11... | collective-permute-start | bytes 1572872 | tf_op jit(solution)/shard_map/ppermute | solution.py:398
  34.7 21.2 %copy-start.4 = (f32[1,4,1024]{2,1,0:T(4,128)S(1)}, f32[1,4,1024]{2,1,0:T(4,128)}, u32[]{:S(2)}) copy-start(f32[1,4,1024]{2,1,0:T(4,128)} %param.6) | copy-start | bytes 49156
  71.3 1.8 %collective-permute-start.11 = (f32[8,6,16,128]{3,2,1,0:T(8,128)S(1)}, f32[8,6,16,128]{3,2,1,0:T(8,128)S(1)}, u32[]{:S(2)}, u32[]{:S(2)}) collective-permute-start(f32[8,6,16,128]{3,2,1,0:T(8,128)S(1)} %get-tuple-element.72), channel_id=1, source_target_pairs={{0,1},{1,0},{2,3},{3,2},{4,5},{5,4},{6,7},{7,6},{8,9},{9,8},{10,11... | collective-permute-start | bytes 1179656 | tf_op jit(solution)/shard_map/ppermute | solution.py:398
  96.4 5.7 %collective-permute-start.12 = (f32[1,6,16,128]{3,2,1,0:T(8,128)S(1)}, f32[1,6,16,128]{3,2,1,0:T(8,128)S(1)}, u32[]{:S(2)}, u32[]{:S(2)}) collective-permute-start(f32[1,6,16,128]{3,2,1,0:T(8,128)S(1)} %bitcast.17), channel_id=1, source_target_pairs={{0,16},{16,0},{1,17},{17,1},{2,18},{18,2},{3,19},{19,3},{4,20},{20... | collective-permute-start | bytes 147464 | tf_op jit(solution)/shard_map/ppermute | solution.py:467
  102.9 16.1 %all-to-all-start.3 = ((f32[8,6,16,128]{3,2,1,0:T(8,128)}), f32[8,6,16,128]{3,2,1,0:T(8,128)S(1)}, u32[]{:S(2)}, u32[]{:S(2)}) async-start(f32[8,6,16,128]{3,2,1,0:T(8,128)} %broadcast_in_dim.13), calls=%async_computation.3 | async-start | bytes 786432 | tf_op jit(solution)/shard_map/all_to_all | solution.py:469
  106.4 1.3 %collective-permute-start.13 = (f32[2,1024]{1,0:T(2,128)S(1)}, f32[2,1024]{1,0:T(2,128)S(1)}, u32[]{:S(2)}, u32[]{:S(2)}) collective-permute-start(f32[2,1024]{1,0:T(2,128)S(1)} %get-tuple-element.73), channel_id=1, source_target_pairs={{0,1},{1,0},{2,3},{3,2},{4,5},{5,4},{6,7},{7,6},{8,9},{9,8},{10,11... | collective-permute-start | bytes 24584 | tf_op jit(solution)/shard_map/ppermute | solution.py:398

commit v11 on v10

--- a/solution.py
+++ b/solution.py
@@ -417,20 +417,16 @@
     )(receivers)
     own_c, p_pair = lax.optimization_barrier((conductivity, send(fields, swap)))
     c_pair = send(own_c, swap)
+    p_near_pair, c_near_pair = send(p_near, swap), send(c_near, swap)
+    hot_own, c_near_pair = lax.optimization_barrier((hot_own, c_near_pair))
     p_mid, c_mid, ky_mid, kz_mid, dg_mid, p_sample = call(
         own_kernel,
         8,
         [f32(2, KEPT, rows, lanes), four, four, four, four, f32(2, count)],
         [pltpu.VMEM((2 * lanes, 3 * KEPT * rows), BF16)],
     )(fields, p_pair, conductivity, c_pair, receivers, hot_own)
-    def paired(x, ready):
-        x, ready = lax.optimization_barrier((x, ready))
-        return x, send(x, swap)
-
-    p_near, p_near_pair = paired(p_near, p_sample)
-    c_near, c_near_pair = paired(c_near, p_sample)
-    c_far, c_far_pair = paired(c_far, p_sample)
-    p_far, p_far_pair = paired(p_far, (p_near_pair, c_near_pair, c_far_pair))
+    p_far, ready = lax.optimization_barrier((p_far, p_sample))
+    p_far_pair, c_far_pair = send(p_far, swap), send(c_far, swap)
     kx, ky, kz, dinv, dg, prim, f0, f1, f2, sent = call(
         forward_kernel,
         20,

time: 120 us -> 117 us (0.975)
  waiting for transfers between devices: 38.2 us -> 36.6 us
  starting transfers between devices: 14.2 us -> 12.7 us
    ppermute x13, waiting for transfers between devices: 22.7 us -> 20.7 us  [send(): return lax.ppermute(x, NAMES, pairs)]
where the time goes in v11:
time: 117 us
  blocking collectives  45.8 us (39%)
  waiting for transfers between devices  36.6 us (31%)
  Pallas kernels  15.9 us (14%)
  starting transfers between devices  12.7 us (11%)
  local copies, waits for them, and re-layouts  4.29 us (4%)
    all_to_all x1, blocking collectives, per_device(): parts = lax.all_to_all(total, 'z', 0, 0, tiled=True)  23.3 us
    all_to_all x2, blocking collectives, per_device(): got = lax.all_to_all(sent, ('y', 'xl'), 0, 0, tiled=True)  22.5 us
    ppermute x13, waiting for transfers between devices, send(): return lax.ppermute(x, NAMES, pairs)  20.7 us
    pallas_call x5, Pallas kernels, run(): pl.pallas_call(kernel, out_shape=tuple((jax.ShapeDtypeStruct(x, kind) for...  15.9 us
    all_to_all x1, waiting for transfers between devices, per_device(): whole = lax.all_to_all(spread, 'z', 0, 0, tiled=True)  10.8 us
    ppermute x13, starting transfers between devices, send(): return lax.ppermute(x, NAMES, pairs)  8.65 us
    ppermute x1, waiting for transfers between devices, per_device(): share = share + lax.ppermute(share, 'xh', [(0, 1), (1, 0)])  5.07 us
    all_to_all x1, starting transfers between devices, per_device(): whole = lax.all_to_all(spread, 'z', 0, 0, tiled=True)  3.45 us
  transfers between devices with their start and end apart: 15, of which 10 were waited for; matrix products, arithmetic and copies ran while one was open for 1% of the time, Pallas kernels for 2%

profile of v11, /device:TPU:4, one launch (start us, length us, event | category | flops | bytes accessed | tf_op | source)
XLA Modules:
  0.0 116.7 jit_solution(2905895782097319590)
XLA Ops:
  0.6 1.3 %collective-permute-start.2 = (f32[4,2,128,128]{3,2,1,0:T(8,128)}, f32[4,2,128,128]{3,2,1,0:T(8,128)S(1)}, u32[]{:S(2)}, u32[]{:S(2)}) collective-permute-start(f32[4,2,128,128]{3,2,1,0:T(8,128)} %bitcast.11), channel_id=1, source_target_pairs={{0,2},{1,3},{2,0},{3,1},{4,6},{5,7},{6,4},{7,5},{8,10},{9,11},{10,... | collective-permute-start | bytes 1572872 | tf_op jit(solution)/shard_map/ppermute | solution.py:398
  1.9 0.0 collective-permute-start
  1.9 1.6 %collective-permute-start.3 = (f32[3,2,128,128]{3,2,1,0:T(8,128)}, f32[3,2,128,128]{3,2,1,0:T(8,128)S(1)}, u32[]{:S(2)}, u32[]{:S(2)}) collective-permute-start(f32[3,2,128,128]{3,2,1,0:T(8,128)} %c_own.1), channel_id=1, source_target_pairs={{0,18},{1,19},{2,16},{3,17},{4,22},{5,23},{6,20},{7,21},{8,26},{9,... | collective-permute-start | bytes 1179656 | tf_op jit(solution)/shard_map/ppermute | solution.py:398
  3.5 1.3 %collective-permute-start.8 = (f32[3,2,128,128]{3,2,1,0:T(8,128)}, f32[3,2,128,128]{3,2,1,0:T(8,128)S(1)}, u32[]{:S(2)}, u32[]{:S(2)}) collective-permute-start(f32[3,2,128,128]{3,2,1,0:T(8,128)} %c_own.1), channel_id=1, source_target_pairs={{2,6},{3,7},{4,0},{5,1},{6,10},{7,11},{8,4},{9,5},{10,14},{11,15},... | collective-permute-start | bytes 1179656 | tf_op jit(solution)/shard_map/ppermute | solution.py:398
  4.8 8.8 %collective-permute-done.3.c_near = f32[3,2,128,128]{3,2,1,0:T(8,128)S(1)} collective-permute-done((f32[3,2,128,128]{3,2,1,0:T(8,128)}, f32[3,2,128,128]{3,2,1,0:T(8,128)S(1)}, u32[]{:S(2)}, u32[]{:S(2)}) %collective-permute-start.3) | collective-permute-done | bytes 393248 | tf_op jit(solution)/shard_map/ppermute | solution.py:398
  13.7 0.9 collective-permute-done.2.p_near
  14.6 3.5 %collective-permute-start.6 = (f32[4,2,128,128]{3,2,1,0:T(8,128)S(1)}, f32[4,2,128,128]{3,2,1,0:T(8,128)S(1)}, u32[]{:S(2)}, u32[]{:S(2)}) collective-permute-start(f32[4,2,128,128]{3,2,1,0:T(8,128)S(1)} %collective-permute-done.2.p_near), channel_id=1, source_target_pairs={{0,4},{1,5},{4,8},{5,9},{6,2},{7,3},{8,12},{9,13},{10,6},{11,7},{1... | collective-permute-start | bytes 1572872 | tf_op jit(solution)/shard_map/ppermute | solution.py:398
  18.1 0.1 collective-permute-start.4
  18.2 0.0 collective-permute-done.p_pair
  18.2 0.5 collective-permute-start.1
  18.7 0.0 collective-permute-done.8
  18.7 0.0 collective-permute-start.9
  18.7 0.0 copy-start.2
  18.7 0.7 copy-done.2
  19.4 0.5 shard_map.59
  19.9 0.2 collective-permute-start.5
  20.1 0.0 collective-permute-done.4.c_near_pair
  20.1 0.5 collective-permute-done.1.c_pair
  20.7 1.0 copy-done
  21.7 1.0 copy-done.1
  22.7 1.3 %shard_map.60 = (f32[2,4,128,128]{3,2,1,0:T(8,128)S(1)}, f32[4,128,128]{2,1,0:T(8,128)S(1)}, f32[4,128,128]{2,1,0:T(8,128)S(1)}, f32[4,128,128]{2,1,0:T(8,128)S(...) custom-call(f32[4,2,128,128]{3,2,1,0:T(8,128)S(1)} %bitcast.13, ...), custom_call_target="tpu_custom_call" | custom-call | tf_op jit(solution)/shard_map/pallas_call | solution.py:351
  24.0 4.4 %collective-permute-done.6.p_far = f32[4,2,128,128]{3,2,1,0:T(8,128)S(1)} collective-permute-done((f32[4,2,128,128]{3,2,1,0:T(8,128)S(1)}, f32[4,2,128,128]{3,2,1,0:T(8,128)S(1)}, u32[]{:S(2)}, u32[]{:S(2)}) %collective-permute-start.6) | collective-permute-done | bytes 524320 | tf_op jit(solution)/shard_map/ppermute | solution.py:398
  28.4 0.0 collective-permute-start.7
  28.4 1.5 %collective-permute-done.9.c_far = f32[3,2,128,128]{3,2,1,0:T(8,128)S(1)} collective-permute-done((f32[3,2,128,128]{3,2,1,0:T(8,128)S(1)}, f32[3,2,128,128]{3,2,1,0:T(8,128)S(1)}, u32[]{:S(2)}, u32[]{:S(2)}) %collective-permute-start.9) | collective-permute-done | bytes 393248 | tf_op jit(solution)/shard_map/ppermute | solution.py:398
  29.8 0.0 collective-permute-start.10
  29.8 0.0 collective-permute-done.5.p_near_pair
  29.8 1.7 %collective-permute-done.10.c_far_pair = f32[3,2,128,128]{3,2,1,0:T(8,128)S(1)} collective-permute-done((f32[3,2,128,128]{3,2,1,0:T(8,128)S(1)}, f32[3,2,128,128]{3,2,1,0:T(8,128)S(1)}, u32[]{:S(2)}, u32[]{:S(2)}) %collective-permute-start.10) | collective-permute-done | bytes 393248 | tf_op jit(solution)/shard_map/ppermute | solution.py:398
  31.6 0.0 collective-permute-done.7.p_far_pair
  31.6 0.0 copy-done.3
  31.6 7.4 %shard_map.61 = (f32[12,128,128]{2,1,0:T(8,128)S(1)}, f32[12,128,128]{2,1,0:T(8,128)S(1)}, f32[12,128,128]{2,1,0:T(8,128)S(1)}, f32[12,128,128]{2,1,0:T(8,128)S(...) custom-call(f32[2,4,128,128]{3,2,1,0:T(8,128)S(1)} %get-tuple-elemen, ...), custom_call_target="tpu_custom_call" | custom-call | tf_op jit(solution)/shard_map/pallas_call | solution.py:351
  38.9 13.9 %all_to_all.20.got = f32[8,8,1152]{2,1,0:T(8,128)S(1)} all-to-all(f32[8,8,1152]{2,1,0:T(8,128)S(1)} %get-tuple-element.51), channel_id=1, replica_groups=mesh['z'=8,'xh'=2,'y'=4,'xl'=2,'c'=2] {'y','xl'}, dimensions={0} | all-to-all | bytes 589824 | tf_op jit(solution)/shard_map/all_to_all | solution.py:443
  52.8 0.0 copy-done.4
  52.8 5.4 %shard_map.62 = (f32[2,6,128,128]{3,2,1,0:T(8,128)S(1)}, f32[2,6,128,128]{3,2,1,0:T(8,128)S(1)}, f32[2,6,128,128]{3,2,1,0:T(8,128)S(1)}, f32[2,6,128,128]{3,2,1,...) custom-call(f32[8,8,1152]{2,1,0:T(8,128)S(1)} %all_to_all.20.got, f32[4,1024]{1,0:T(4,128)S(1)} %bitcast.14, ...), custom_call_target="tpu_custom_call" | custom-call | tf_op jit(solution)/shard_map/pallas_call | solution.py:351
  58.3 8.6 %all_to_all.21.got = f32[8,8,128]{2,1,0:T(8,128)S(1)} all-to-all(f32[8,8,128]{2,1,0:T(8,128)S(1)} %get-tuple-element.62), channel_id=1, replica_groups=mesh['z'=8,'xh'=2,'y'=4,'xl'=2,'c'=2] {'y','xl'}, dimensions={0} | all-to-all | bytes 65536 | tf_op jit(solution)/shard_map/all_to_all | solution.py:451
  66.9 1.3 %shard_map.63 = (f32[8,6,16,128]{3,2,1,0:T(8,128)S(1)}, f32[8,6,16,128]{3,2,1,0:T(8,128)S(1)}) custom-call(f32[8,8,128]{2,1,0:T(8,128)S(1)} %all_to_all.21.got, f32[2,6,128,128]{3,2,1,0:T(8,128)S(1)} %get-tuple-element.63.a0, f32[2,6,128,128]{3,2,1,0:T(8,128)S(1)} %get-tuple-element.64.a1, f32[2,6,128,128]{3,2,1,0:T(8,128)S(1)} %get-tuple-element.65.a2, ...), custom_call_target="tpu_custom_call" | custom-call | tf_op jit(solution)/shard_map/pallas_call | solution.py:351
  68.2 0.1 collective-permute-start.11
  68.3 1.7 %collective-permute-done.11 = f32[8,6,16,128]{3,2,1,0:T(8,128)S(1)} collective-permute-done((f32[8,6,16,128]{3,2,1,0:T(8,128)S(1)}, f32[8,6,16,128]{3,2,1,0:T(8,128)S(1)}, u32[]{:S(2)}, u32[]{:S(2)}) %collective-permute-start.11) | collective-permute-done | bytes 393248 | tf_op jit(solution)/shard_map/ppermute | solution.py:398
  70.0 0.1 add.6
  70.0 23.3 %all_to_all.22 = f32[8,6,16,128]{3,2,1,0:T(8,128)S(1)} all-to-all(f32[8,6,16,128]{3,2,1,0:T(8,128)S(1)} %add.6), channel_id=1, replica_groups=mesh['z'=8,'xh'=2,'y'=4,'xl'=2,'c'=2] {'z'}, dimensions={0} | all-to-all | bytes 786432 | tf_op jit(solution)/shard_map/all_to_all | solution.py:460
  93.3 0.6 collective-permute-start.12
  93.9 5.1 %collective-permute-done.12 = f32[1,6,16,128]{3,2,1,0:T(8,128)S(1)} collective-permute-done((f32[1,6,16,128]{3,2,1,0:T(8,128)S(1)}, f32[1,6,16,128]{3,2,1,0:T(8,128)S(1)}, u32[]{:S(2)}, u32[]{:S(2)}) %collective-permute-start.12) | collective-permute-done | bytes 49184 | tf_op jit(solution)/shard_map/ppermute | solution.py:463
  99.0 0.8 broadcast_in_dim.13
  99.8 3.5 %all-to-all-start.3 = ((f32[8,6,16,128]{3,2,1,0:T(8,128)}), f32[8,6,16,128]{3,2,1,0:T(8,128)S(1)}, u32[]{:S(2)}, u32[]{:S(2)}) async-start(f32[8,6,16,128]{3,2,1,0:T(8,128)} %broadcast_in_dim.13), calls=%async_computation.3 | async-start | bytes 786432 | tf_op jit(solution)/shard_map/all_to_all | solution.py:465
  103.3 0.1 collective-permute-start.13
  103.4 1.2 collective-permute-done.13
  104.5 0.6 maximum_select_fusion
  105.1 10.8 %all-to-all-done.3 = f32[8,6,16,128]{3,2,1,0:T(8,128)S(1)} async-done(((f32[8,6,16,128]{3,2,1,0:T(8,128)}), f32[8,6,16,128]{3,2,1,0:T(8,128)S(1)}, u32[]{:S(2)}, u32[]{:S(2)}) %all-to-all-start.3) | async-done | bytes 393248 | tf_op jit(solution)/shard_map/all_to_all | solution.py:465
  115.9 0.8 copy.6
  (6 shorter events, 0.0 us)
Async XLA Ops:
  0.6 14.0 %collective-permute-start.2 = (f32[4,2,128,128]{3,2,1,0:T(8,128)}, f32[4,2,128,128]{3,2,1,0:T(8,128)S(1)}, u32[]{:S(2)}, u32[]{:S(2)}) collective-permute-start(f32[4,2,128,128]{3,2,1,0:T(8,128)} %bitcast.11), channel_id=1, source_target_pairs={{0,2},{1,3},{2,0},{3,1},{4,6},{5,7},{6,4},{7,5},{8,10},{9,11},{10,... | collective-permute-start | bytes 1572872 | tf_op jit(solution)/shard_map/ppermute | solution.py:398
  1.9 16.3 %collective-permute-start = (f32[4,2,128,128]{3,2,1,0:T(8,128)}, f32[4,2,128,128]{3,2,1,0:T(8,128)S(1)}, u32[]{:S(2)}, u32[]{:S(2)}) collective-permute-start(f32[4,2,128,128]{3,2,1,0:T(8,128)} %bitcast.12), channel_id=1, source_target_pairs={{0,1},{1,0},{2,3},{3,2},{4,5},{5,4},{6,7},{7,6},{8,9},{9,8},{10,11... | collective-permute-start | bytes 1572872 | tf_op jit(solution)/shard_map/ppermute | solution.py:398
  1.9 11.7 %collective-permute-start.3 = (f32[3,2,128,128]{3,2,1,0:T(8,128)}, f32[3,2,128,128]{3,2,1,0:T(8,128)S(1)}, u32[]{:S(2)}, u32[]{:S(2)}) collective-permute-start(f32[3,2,128,128]{3,2,1,0:T(8,128)} %c_own.1), channel_id=1, source_target_pairs={{0,18},{1,19},{2,16},{3,17},{4,22},{5,23},{6,20},{7,21},{8,26},{9,... | collective-permute-start | bytes 1179656 | tf_op jit(solution)/shard_map/ppermute | solution.py:398
  3.5 15.2 %collective-permute-start.8 = (f32[3,2,128,128]{3,2,1,0:T(8,128)}, f32[3,2,128,128]{3,2,1,0:T(8,128)S(1)}, u32[]{:S(2)}, u32[]{:S(2)}) collective-permute-start(f32[3,2,128,128]{3,2,1,0:T(8,128)} %c_own.1), channel_id=1, source_target_pairs={{2,6},{3,7},{4,0},{5,1},{6,10},{7,11},{8,4},{9,5},{10,14},{11,15},... | collective-permute-start | bytes 1179656 | tf_op jit(solution)/shard_map/ppermute | solution.py:398
  14.6 13.8 %collective-permute-start.6 = (f32[4,2,128,128]{3,2,1,0:T(8,128)S(1)}, f32[4,2,128,128]{3,2,1,0:T(8,128)S(1)}, u32[]{:S(2)}, u32[]{:S(2)}) collective-permute-start(f32[4,2,128,128]{3,2,1,0:T(8,128)S(1)} %collective-permute-done.2.p_near), channel_id=1, source_target_pairs={{0,4},{1,5},{4,8},{5,9},{6,2},{7,3},{8,12},{9,13},{10,6},{11,7},{1... | collective-permute-start | bytes 1572872 | tf_op jit(solution)/shard_map/ppermute | solution.py:398
  18.1 2.0 %collective-permute-start.4 = (f32[3,2,128,128]{3,2,1,0:T(8,128)S(1)}, f32[3,2,128,128]{3,2,1,0:T(8,128)S(1)}, u32[]{:S(2)}, u32[]{:S(2)}) collective-permute-start(f32[3,2,128,128]{3,2,1,0:T(8,128)S(1)} %collective-permute-done.3.c_near), channel_id=1, source_target_pairs={{0,1},{1,0},{2,3},{3,2},{4,5},{5,4},{6,7},{7,6},{8,9},{9,8},{10,11... | collective-permute-start | bytes 1179656 | tf_op jit(solution)/shard_map/ppermute | solution.py:398
  18.2 2.5 %collective-permute-start.1 = (f32[3,2,128,128]{3,2,1,0:T(8,128)}, f32[3,2,128,128]{3,2,1,0:T(8,128)S(1)}, u32[]{:S(2)}, u32[]{:S(2)}) collective-permute-start(f32[3,2,128,128]{3,2,1,0:T(8,128)} %c_own.1), channel_id=1, source_target_pairs={{0,1},{1,0},{2,3},{3,2},{4,5},{5,4},{6,7},{7,6},{8,9},{9,8},{10,11... | collective-permute-start | bytes 1179656 | tf_op jit(solution)/shard_map/ppermute | solution.py:398
  18.7 11.1 %collective-permute-start.9 = (f32[3,2,128,128]{3,2,1,0:T(8,128)S(1)}, f32[3,2,128,128]{3,2,1,0:T(8,128)S(1)}, u32[]{:S(2)}, u32[]{:S(2)}) collective-permute-start(f32[3,2,128,128]{3,2,1,0:T(8,128)S(1)} %collective-permute-done.8), channel_id=1, source_target_pairs={{0,2},{1,3},{2,0},{3,1},{4,6},{5,7},{6,4},{7,5},{8,10},{9,11},{10,... | collective-permute-start | bytes 1179656 | tf_op jit(solution)/shard_map/ppermute | solution.py:398
  18.7 0.7 copy-start.2
  19.9 9.9 %collective-permute-start.5 = (f32[4,2,128,128]{3,2,1,0:T(8,128)S(1)}, f32[4,2,128,128]{3,2,1,0:T(8,128)S(1)}, u32[]{:S(2)}, u32[]{:S(2)}) collective-permute-start(f32[4,2,128,128]{3,2,1,0:T(8,128)S(1)} %collective-permute-done.2.p_near), channel_id=1, source_target_pairs={{0,1},{1,0},{2,3},{3,2},{4,5},{5,4},{6,7},{7,6},{8,9},{9,8},{10,11... | collective-permute-start | bytes 1572872 | tf_op jit(solution)/shard_map/ppermute | solution.py:398
  20.7 1.0 copy-start
  21.7 1.0 copy-start.1
  22.7 8.8 %copy-start.3 = (s32[1,1024]{1,0:T(1,128)S(1)}, s32[1,1024]{1,0:T(1,128)}, u32[]{:S(2)}) copy-start(s32[1,1024]{1,0:T(1,128)} %cells.7) | copy-start | bytes 12292
  28.4 3.2 %collective-permute-start.7 = (f32[4,2,128,128]{3,2,1,0:T(8,128)S(1)}, f32[4,2,128,128]{3,2,1,0:T(8,128)S(1)}, u32[]{:S(2)}, u32[]{:S(2)}) collective-permute-start(f32[4,2,128,128]{3,2,1,0:T(8,128)S(1)} %collective-permute-done.6.p_far), channel_id=1, source_target_pairs={{0,1},{1,0},{2,3},{3,2},{4,5},{5,4},{6,7},{7,6},{8,9},{9,8},{10,11... | collective-permute-start | bytes 1572872 | tf_op jit(solution)/shard_map/ppermute | solution.py:398
  29.8 1.7 %collective-permute-start.10 = (f32[3,2,128,128]{3,2,1,0:T(8,128)S(1)}, f32[3,2,128,128]{3,2,1,0:T(8,128)S(1)}, u32[]{:S(2)}, u32[]{:S(2)}) collective-permute-start(f32[3,2,128,128]{3,2,1,0:T(8,128)S(1)} %collective-permute-done.9.c_far), channel_id=1, source_target_pairs={{0,1},{1,0},{2,3},{3,2},{4,5},{5,4},{6,7},{7,6},{8,9},{9,8},{10,11... | collective-permute-start | bytes 1179656 | tf_op jit(solution)/shard_map/ppermute | solution.py:398
  31.6 21.3 %copy-start.4 = (f32[1,4,1024]{2,1,0:T(4,128)S(1)}, f32[1,4,1024]{2,1,0:T(4,128)}, u32[]{:S(2)}) copy-start(f32[1,4,1024]{2,1,0:T(4,128)} %param.6) | copy-start | bytes 49156
  68.2 1.8 %collective-permute-start.11 = (f32[8,6,16,128]{3,2,1,0:T(8,128)S(1)}, f32[8,6,16,128]{3,2,1,0:T(8,128)S(1)}, u32[]{:S(2)}, u32[]{:S(2)}) collective-permute-start(f32[8,6,16,128]{3,2,1,0:T(8,128)S(1)} %get-tuple-element.70), channel_id=1, source_target_pairs={{0,1},{1,0},{2,3},{3,2},{4,5},{5,4},{6,7},{7,6},{8,9},{9,8},{10,11... | collective-permute-start | bytes 1179656 | tf_op jit(solution)/shard_map/ppermute | solution.py:398
  93.3 5.7 %collective-permute-start.12 = (f32[1,6,16,128]{3,2,1,0:T(8,128)S(1)}, f32[1,6,16,128]{3,2,1,0:T(8,128)S(1)}, u32[]{:S(2)}, u32[]{:S(2)}) collective-permute-start(f32[1,6,16,128]{3,2,1,0:T(8,128)S(1)} %bitcast.17), channel_id=1, source_target_pairs={{0,16},{16,0},{1,17},{17,1},{2,18},{18,2},{3,19},{19,3},{4,20},{20... | collective-permute-start | bytes 147464 | tf_op jit(solution)/shard_map/ppermute | solution.py:463
  99.8 16.1 %all-to-all-start.3 = ((f32[8,6,16,128]{3,2,1,0:T(8,128)}), f32[8,6,16,128]{3,2,1,0:T(8,128)S(1)}, u32[]{:S(2)}, u32[]{:S(2)}) async-start(f32[8,6,16,128]{3,2,1,0:T(8,128)} %broadcast_in_dim.13), calls=%async_computation.3 | async-start | bytes 786432 | tf_op jit(solution)/shard_map/all_to_all | solution.py:465
  103.3 1.3 %collective-permute-start.13 = (f32[2,1024]{1,0:T(2,128)S(1)}, f32[2,1024]{1,0:T(2,128)S(1)}, u32[]{:S(2)}, u32[]{:S(2)}) collective-permute-start(f32[2,1024]{1,0:T(2,128)S(1)} %get-tuple-element.71), channel_id=1, source_target_pairs={{0,1},{1,0},{2,3},{3,2},{4,5},{5,4},{6,7},{7,6},{8,9},{9,8},{10,11... | collective-permute-start | bytes 24584 | tf_op jit(solution)/shard_map/ppermute | solution.py:398

commit v12 on v11

--- a/solution.py
+++ b/solution.py
@@ -184,20 +184,23 @@
 
 
 def forward_kernel(
-    p_mid, p_near, p_near_pair, p_far, p_far_pair,
+    p_mid, p_near, p_near_b, p_near_pair, p_near_pair_b, p_far, p_far_b, p_far_pair, p_far_pair_b,
     c_mid, c_near, c_near_pair, c_far, c_far_pair, ky_mid, kz_mid, dg_mid, cells, hot_own, p_sample,
     kx, ky, kz, dinv, dg, prim, t0, t1, t2, sent, cond, left, found,
 ):
     block = 2 * lax.axis_index("y") + lax.axis_index("xl")
     core = lax.axis_index("c")
-    here = pl.ds(2 * core, 2)
     prim[:, 4:8] = p_mid[...]
     cond[4:8] = c_mid[...]
     far = 8 * lax.axis_index("xl")
     near = 8 - far
-    for base, first, second in ((near, p_near, p_near_pair), (far, p_far, p_far_pair)):
-        prim[:, pl.ds(base + 2 * core, 2)] = first[here]
-        prim[:, pl.ds(base + 2 - 2 * core, 2)] = second[here]
+    for start, even, odd in (
+        (near + 2 * core, p_near, p_near_b),
+        (near + 2 - 2 * core, p_near_pair, p_near_pair_b),
+        (far + 2 * core, p_far, p_far_b),
+        (far + 2 - 2 * core, p_far_pair, p_far_pair_b),
+    ):
+        prim[:, pl.ds(start, 2)] = jnp.where(core == 0, even[...], odd[...])
     for base, first, second in ((near, c_near, c_near_pair), (far, c_far, c_far_pair)):
         cond[pl.ds(base + 2 * core, 2)] = first[0]
         cond[pl.ds(base + 2 - 2 * core, 2)] = second[0]
@@ -399,11 +402,12 @@
 
     fields = primary[0]
     swap = routes(sizes, lambda h, y, l, c: (h, y, l, 1 - c))
-    p_near = send(fields, routes(sizes, beside))
+    halves = (fields[0:2], fields[2:4])
+    into = [routes(sizes, lambda h, y, l, c, to=to: (h, y, l, to) if c == 1 - to else None) for to in (0, 1)]
+    p_near = [send(x, routes(sizes, beside)) for x in halves]
     c_near = send(conductivity, routes(sizes, around))
     c_next = send(conductivity, along(-1))
-    p_near, c_near = lax.optimization_barrier((p_near, c_near))
-    p_far = send(p_near, along(1))
+    p_far = [send(x, along(1)) for x in p_near]
     c_far = send(c_next, routes(sizes, beside))
 
     rows, lanes = primary.shape[3], primary.shape[4]
@@ -417,7 +421,8 @@
     )(receivers)
     own_c, p_pair = lax.optimization_barrier((conductivity, send(fields, swap)))
     c_pair = send(own_c, swap)
-    p_near_pair, c_near_pair = send(p_near, swap), send(c_near, swap)
+    p_near_pair = [send(x, pairs) for x, pairs in zip(p_near, into)]
+    c_near_pair = send(c_near, swap)
     hot_own, c_near_pair = lax.optimization_barrier((hot_own, c_near_pair))
     p_mid, c_mid, ky_mid, kz_mid, dg_mid, p_sample = call(
         own_kernel,
@@ -425,8 +430,9 @@
         [f32(2, KEPT, rows, lanes), four, four, four, four, f32(2, count)],
         [pltpu.VMEM((2 * lanes, 3 * KEPT * rows), BF16)],
     )(fields, p_pair, conductivity, c_pair, receivers, hot_own)
-    p_far, ready = lax.optimization_barrier((p_far, p_sample))
-    p_far_pair, c_far_pair = send(p_far, swap), send(c_far, swap)
+    p_far[1], ready = lax.optimization_barrier((p_far[1], p_sample))
+    p_far_pair = [send(x, pairs) for x, pairs in zip(p_far, into)]
+    c_far_pair = send(c_far, swap)
     kx, ky, kz, dinv, dg, prim, f0, f1, f2, sent = call(
         forward_kernel,
         20,
@@ -437,7 +443,7 @@
             pltpu.VMEM((6, count), F32),
         ],
     )(
-        p_mid, p_near, p_near_pair, p_far, p_far_pair,
+        p_mid, *p_near, *p_near_pair, *p_far, *p_far_pair,
         c_mid, c_near, c_near_pair, c_far, c_far_pair, ky_mid, kz_mid, dg_mid, receivers, hot_own, p_sample,
     )
     got = lax.all_to_all(sent, ("y", "xl"), 0, 0, tiled=True)

time: 117 us -> 128 us (1.094)
  starting transfers between devices: 12.7 us -> 29.9 us
  waiting for transfers between devices: 36.6 us -> 29.3 us
    ppermute x13 -> x17, starting transfers between devices: 8.65 us -> 24.1 us  [send(): return lax.ppermute(x, NAMES, pairs)]
    ppermute x13 -> x17, waiting for transfers between devices: 20.7 us -> 15.3 us  [send(): return lax.ppermute(x, NAMES, pairs)]
    ppermute x1, starting transfers between devices: 0.61 us -> 2.43 us  [per_device(): share = share + lax.ppermute(share, 'xh', [(0, 1), (1, 0)])]
    ppermute x1, waiting for transfers between devices: 5.07 us -> 3.25 us  [per_device(): share = share + lax.ppermute(share, 'xh', [(0, 1), (1, 0)])]
  transfers between devices with their start and end apart: 15 -> 19, of which waited for: 10 -> 8; matrix products, arithmetic and copies ran while one was open for 1% -> 1% of each run, Pallas kernels for 2% -> 1%
where the time goes in v12:
time: 128 us; the launch traced here: 127 us
  blocking collectives  44.6 us (35%)
  starting transfers between devices  29.9 us (23%)
  waiting for transfers between devices  29.3 us (23%)
  Pallas kernels  15.9 us (12%)
  local copies, waits for them, and re-layouts  5.35 us (4%)
    ppermute x17, starting transfers between devices, send(): return lax.ppermute(x, NAMES, pairs)  24.1 us
    all_to_all x1, blocking collectives, per_device(): parts = lax.all_to_all(total, 'z', 0, 0, tiled=True)  23.2 us
    all_to_all x2, blocking collectives, per_device(): got = lax.all_to_all(sent, ('y', 'xl'), 0, 0, tiled=True)  21.4 us
    pallas_call x5, Pallas kernels, run(): pl.pallas_call(kernel, out_shape=tuple((jax.ShapeDtypeStruct(x, kind) for...  15.9 us
    ppermute x17, waiting for transfers between devices, send(): return lax.ppermute(x, NAMES, pairs)  15.3 us
    all_to_all x1, waiting for transfers between devices, per_device(): whole = lax.all_to_all(spread, 'z', 0, 0, tiled=True)  10.8 us
    all_to_all x1, starting transfers between devices, per_device(): whole = lax.all_to_all(spread, 'z', 0, 0, tiled=True)  3.45 us
    ppermute x1, waiting for transfers between devices, per_device(): share = share + lax.ppermute(share, 'xh', [(0, 1), (1, 0)])  3.25 us
  transfers between devices with their start and end apart: 19, of which 8 were waited for; matrix products, arithmetic and copies ran while one was open for 1% of the time, Pallas kernels for 1%

profile of v12, /device:TPU:4, one launch (start us, length us, event | category | flops | bytes accessed | tf_op | source)
XLA Modules:
  0.0 126.6 jit_solution(8436624199820739098)
XLA Ops:
  0.6 0.1 collective-permute-start
  0.7 1.3 %collective-permute-start.12 = (f32[3,2,128,128]{3,2,1,0:T(8,128)}, f32[3,2,128,128]{3,2,1,0:T(8,128)S(1)}, u32[]{:S(2)}, u32[]{:S(2)}) collective-permute-start(f32[3,2,128,128]{3,2,1,0:T(8,128)} %c_own.1), channel_id=1, source_target_pairs={{2,6},{3,7},{4,0},{5,1},{6,10},{7,11},{8,4},{9,5},{10,14},{11,15},... | collective-permute-start | bytes 1179656 | tf_op jit(solution)/shard_map/ppermute | solution.py:401
  2.0 2.8 %collective-permute-start.2 = (f32[3,2,128,128]{3,2,1,0:T(8,128)}, f32[3,2,128,128]{3,2,1,0:T(8,128)S(1)}, u32[]{:S(2)}, u32[]{:S(2)}) collective-permute-start(f32[3,2,128,128]{3,2,1,0:T(8,128)} %c_own.1), channel_id=1, source_target_pairs={{0,18},{1,19},{2,16},{3,17},{4,22},{5,23},{6,20},{7,21},{8,26},{9,... | collective-permute-start | bytes 1179656 | tf_op jit(solution)/shard_map/ppermute | solution.py:401
  4.9 1.1 slice_bitcast_fusion
  5.9 0.8 collective-permute-start.4
  6.7 1.3 %collective-permute-start.5 = (f32[2,2,128,128]{3,2,1,0:T(8,128)S(1)}, f32[2,2,128,128]{3,2,1,0:T(8,128)S(1)}, u32[]{:S(2)}, u32[]{:S(2)}) collective-permute-start(f32[2,2,128,128]{3,2,1,0:T(8,128)S(1)} %get-tuple-element.68), channel_id=1, source_target_pairs={{0,2},{1,3},{2,0},{3,1},{4,6},{5,7},{6,4},{7,5},{8,10},{9,11},{10,... | collective-permute-start | bytes 786440 | tf_op jit(solution)/shard_map/ppermute | solution.py:401
  8.0 6.3 %collective-permute-done.12 = f32[3,2,128,128]{3,2,1,0:T(8,128)S(1)} collective-permute-done((f32[3,2,128,128]{3,2,1,0:T(8,128)}, f32[3,2,128,128]{3,2,1,0:T(8,128)S(1)}, u32[]{:S(2)}, u32[]{:S(2)}) %collective-permute-start.12) | collective-permute-done | bytes 393248 | tf_op jit(solution)/shard_map/ppermute | solution.py:401
  14.3 0.4 collective-permute-start.13
  14.7 0.0 collective-permute-done.2.c_near
  14.7 0.0 collective-permute-start.3
  14.7 0.0 collective-permute-done.p_pair
  14.8 0.5 collective-permute-start.1
  15.3 0.0 collective-permute-done.4.p_near
  15.3 4.3 %collective-permute-start.8 = (f32[2,2,128,128]{3,2,1,0:T(8,128)S(1)}, f32[2,2,128,128]{3,2,1,0:T(8,128)S(1)}, u32[]{:S(2)}, u32[]{:S(2)}) collective-permute-start(f32[2,2,128,128]{3,2,1,0:T(8,128)S(1)} %collective-permute-done.4.p_near), channel_id=1, source_target_pairs={{0,4},{1,5},{4,8},{5,9},{6,2},{7,3},{8,12},{9,13},{10,6},{11,7},{1... | collective-permute-start | bytes 786440 | tf_op jit(solution)/shard_map/ppermute | solution.py:401
  19.6 1.3 %collective-permute-done.5.p_near_b = f32[2,2,128,128]{3,2,1,0:T(8,128)S(1)} collective-permute-done((f32[2,2,128,128]{3,2,1,0:T(8,128)S(1)}, f32[2,2,128,128]{3,2,1,0:T(8,128)S(1)}, u32[]{:S(2)}, u32[]{:S(2)}) %collective-permute-start.5) | collective-permute-done | bytes 262176 | tf_op jit(solution)/shard_map/ppermute | solution.py:401
  20.8 3.5 %collective-permute-start.9 = (f32[2,2,128,128]{3,2,1,0:T(8,128)S(1)}, f32[2,2,128,128]{3,2,1,0:T(8,128)S(1)}, u32[]{:S(2)}, u32[]{:S(2)}) collective-permute-start(f32[2,2,128,128]{3,2,1,0:T(8,128)S(1)} %collective-permute-done.5.p_near_b), channel_id=1, source_target_pairs={{0,4},{1,5},{4,8},{5,9},{6,2},{7,3},{8,12},{9,13},{10,6},{11,7},{1... | collective-permute-start | bytes 786440 | tf_op jit(solution)/shard_map/ppermute | solution.py:401
  24.3 3.9 %collective-permute-done.13.c_far = f32[3,2,128,128]{3,2,1,0:T(8,128)S(1)} collective-permute-done((f32[3,2,128,128]{3,2,1,0:T(8,128)S(1)}, f32[3,2,128,128]{3,2,1,0:T(8,128)S(1)}, u32[]{:S(2)}, u32[]{:S(2)}) %collective-permute-start.13) | collective-permute-done | bytes 393248 | tf_op jit(solution)/shard_map/ppermute | solution.py:401
  28.2 0.0 collective-permute-start.14
  28.2 0.7 copy-done.2
  28.9 0.5 shard_map.59
  29.4 1.3 %collective-permute-start.6 = (f32[2,2,128,128]{3,2,1,0:T(8,128)S(1)}, f32[2,2,128,128]{3,2,1,0:T(8,128)S(1)}, u32[]{:S(2)}, u32[]{:S(2)}) collective-permute-start(f32[2,2,128,128]{3,2,1,0:T(8,128)S(1)} %collective-permute-done.4.p_near), channel_id=1, source_target_pairs={{1,0},{3,2},{5,4},{7,6},{9,8},{11,10},{13,12},{15,14},{17,16},{19,... | collective-permute-start | bytes 786440 | tf_op jit(solution)/shard_map/ppermute | solution.py:401
  30.7 0.0 collective-permute-done.8.p_far
  30.8 3.1 %collective-permute-start.7 = (f32[2,2,128,128]{3,2,1,0:T(8,128)S(1)}, f32[2,2,128,128]{3,2,1,0:T(8,128)S(1)}, u32[]{:S(2)}, u32[]{:S(2)}) collective-permute-start(f32[2,2,128,128]{3,2,1,0:T(8,128)S(1)} %collective-permute-done.5.p_near_b), channel_id=1, source_target_pairs={{0,1},{2,3},{4,5},{6,7},{8,9},{10,11},{12,13},{14,15},{16,17},{18,... | collective-permute-start | bytes 786440 | tf_op jit(solution)/shard_map/ppermute | solution.py:401
  33.8 1.3 %collective-permute-start.10 = (f32[2,2,128,128]{3,2,1,0:T(8,128)S(1)}, f32[2,2,128,128]{3,2,1,0:T(8,128)S(1)}, u32[]{:S(2)}, u32[]{:S(2)}) collective-permute-start(f32[2,2,128,128]{3,2,1,0:T(8,128)S(1)} %collective-permute-done.8.p_far), channel_id=1, source_target_pairs={{1,0},{3,2},{5,4},{7,6},{9,8},{11,10},{13,12},{15,14},{17,16},{19,... | collective-permute-start | bytes 786440 | tf_op jit(solution)/shard_map/ppermute | solution.py:401
  35.1 0.0 copy-start
  35.1 1.0 copy-done
  36.2 1.0 copy-done.1
  37.2 1.3 %shard_map.60 = (f32[2,4,128,128]{3,2,1,0:T(8,128)S(1)}, f32[4,128,128]{2,1,0:T(8,128)S(1)}, f32[4,128,128]{2,1,0:T(8,128)S(1)}, f32[4,128,128]{2,1,0:T(8,128)S(...) custom-call(f32[4,2,128,128]{3,2,1,0:T(8,128)S(1)} %bitcast.16, ...), custom_call_target="tpu_custom_call" | custom-call | tf_op jit(solution)/shard_map/pallas_call | solution.py:354
  38.5 3.2 %collective-permute-start.11 = (f32[2,2,128,128]{3,2,1,0:T(8,128)S(1)}, f32[2,2,128,128]{3,2,1,0:T(8,128)S(1)}, u32[]{:S(2)}, u32[]{:S(2)}) collective-permute-start(f32[2,2,128,128]{3,2,1,0:T(8,128)S(1)} %collective-permute-done.9.p_far_b), channel_id=1, source_target_pairs={{0,1},{2,3},{4,5},{6,7},{8,9},{10,11},{12,13},{14,15},{16,17},{18,... | collective-permute-start | bytes 786440 | tf_op jit(solution)/shard_map/ppermute | solution.py:401
  41.7 0.9 collective-permute-done.11.p_far_pair_b
  42.7 7.4 %shard_map.61 = (f32[12,128,128]{2,1,0:T(8,128)S(1)}, f32[12,128,128]{2,1,0:T(8,128)S(1)}, f32[12,128,128]{2,1,0:T(8,128)S(1)}, f32[12,128,128]{2,1,0:T(8,128)S(...) custom-call(f32[2,4,128,128]{3,2,1,0:T(8,128)S(1)} %get-tuple-elemen, ...), custom_call_target="tpu_custom_call" | custom-call | tf_op jit(solution)/shard_map/pallas_call | solution.py:354
  50.1 12.7 %all_to_all.20.got = f32[8,8,1152]{2,1,0:T(8,128)S(1)} all-to-all(f32[8,8,1152]{2,1,0:T(8,128)S(1)} %get-tuple-element.47), channel_id=1, replica_groups=mesh['z'=8,'xh'=2,'y'=4,'xl'=2,'c'=2] {'y','xl'}, dimensions={0} | all-to-all | bytes 589824 | tf_op jit(solution)/shard_map/all_to_all | solution.py:449
  62.8 5.4 %shard_map.62 = (f32[2,6,128,128]{3,2,1,0:T(8,128)S(1)}, f32[2,6,128,128]{3,2,1,0:T(8,128)S(1)}, f32[2,6,128,128]{3,2,1,0:T(8,128)S(1)}, f32[2,6,128,128]{3,2,1,...) custom-call(f32[8,8,1152]{2,1,0:T(8,128)S(1)} %all_to_all.20.got, f32[4,1024]{1,0:T(4,128)S(1)} %bitcast.17, ...), custom_call_target="tpu_custom_call" | custom-call | tf_op jit(solution)/shard_map/pallas_call | solution.py:354
  68.3 8.6 %all_to_all.21.got = f32[8,8,128]{2,1,0:T(8,128)S(1)} all-to-all(f32[8,8,128]{2,1,0:T(8,128)S(1)} %get-tuple-element.58), channel_id=1, replica_groups=mesh['z'=8,'xh'=2,'y'=4,'xl'=2,'c'=2] {'y','xl'}, dimensions={0} | all-to-all | bytes 65536 | tf_op jit(solution)/shard_map/all_to_all | solution.py:457
  76.9 1.3 shard_map.63
  78.1 0.1 collective-permute-start.15
  78.2 1.7 %collective-permute-done.15 = f32[8,6,16,128]{3,2,1,0:T(8,128)S(1)} collective-permute-done((f32[8,6,16,128]{3,2,1,0:T(8,128)S(1)}, f32[8,6,16,128]{3,2,1,0:T(8,128)S(1)}, u32[]{:S(2)}, u32[]{:S(2)}) %collective-permute-start.15) | collective-permute-done | bytes 393248 | tf_op jit(solution)/shard_map/ppermute | solution.py:401
  80.0 0.1 add.6
  80.0 23.2 %all_to_all.22 = f32[8,6,16,128]{3,2,1,0:T(8,128)S(1)} all-to-all(f32[8,6,16,128]{3,2,1,0:T(8,128)S(1)} %add.6), channel_id=1, replica_groups=mesh['z'=8,'xh'=2,'y'=4,'xl'=2,'c'=2] {'z'}, dimensions={0} | all-to-all | bytes 786432 | tf_op jit(solution)/shard_map/all_to_all | solution.py:466
  103.3 2.4 %collective-permute-start.16 = (f32[1,6,16,128]{3,2,1,0:T(8,128)S(1)}, f32[1,6,16,128]{3,2,1,0:T(8,128)S(1)}, u32[]{:S(2)}, u32[]{:S(2)}) collective-permute-start(f32[1,6,16,128]{3,2,1,0:T(8,128)S(1)} %bitcast.20), channel_id=1, source_target_pairs={{0,16},{16,0},{1,17},{17,1},{2,18},{18,2},{3,19},{19,3},{4,20},{20... | collective-permute-start | bytes 147464 | tf_op jit(solution)/shard_map/ppermute | solution.py:469
  105.7 3.3 %collective-permute-done.16 = f32[1,6,16,128]{3,2,1,0:T(8,128)S(1)} collective-permute-done((f32[1,6,16,128]{3,2,1,0:T(8,128)S(1)}, f32[1,6,16,128]{3,2,1,0:T(8,128)S(1)}, u32[]{:S(2)}, u32[]{:S(2)}) %collective-permute-start.16) | collective-permute-done | bytes 49184 | tf_op jit(solution)/shard_map/ppermute | solution.py:469
  109.0 0.8 broadcast_in_dim.13
  109.8 3.5 %all-to-all-start.3 = ((f32[8,6,16,128]{3,2,1,0:T(8,128)}), f32[8,6,16,128]{3,2,1,0:T(8,128)S(1)}, u32[]{:S(2)}, u32[]{:S(2)}) async-start(f32[8,6,16,128]{3,2,1,0:T(8,128)} %broadcast_in_dim.13), calls=%async_computation.3 | async-start | bytes 786432 | tf_op jit(solution)/shard_map/all_to_all | solution.py:471
  113.2 0.1 collective-permute-start.17
  113.3 1.2 collective-permute-done.17
  114.5 0.6 maximum_select_fusion
  115.1 10.8 %all-to-all-done.3 = f32[8,6,16,128]{3,2,1,0:T(8,128)S(1)} async-done(((f32[8,6,16,128]{3,2,1,0:T(8,128)}), f32[8,6,16,128]{3,2,1,0:T(8,128)S(1)}, u32[]{:S(2)}, u32[]{:S(2)}) %all-to-all-start.3) | async-done | bytes 393248 | tf_op jit(solution)/shard_map/all_to_all | solution.py:471
  125.9 0.8 copy.6
  (15 shorter events, 0.1 us)
Async XLA Ops:
  0.6 14.1 %collective-permute-start = (f32[4,2,128,128]{3,2,1,0:T(8,128)}, f32[4,2,128,128]{3,2,1,0:T(8,128)S(1)}, u32[]{:S(2)}, u32[]{:S(2)}) collective-permute-start(f32[4,2,128,128]{3,2,1,0:T(8,128)} %bitcast.15), channel_id=1, source_target_pairs={{0,1},{1,0},{2,3},{3,2},{4,5},{5,4},{6,7},{7,6},{8,9},{9,8},{10,11... | collective-permute-start | bytes 1572872 | tf_op jit(solution)/shard_map/ppermute | solution.py:401
  0.7 13.6 %collective-permute-start.12 = (f32[3,2,128,128]{3,2,1,0:T(8,128)}, f32[3,2,128,128]{3,2,1,0:T(8,128)S(1)}, u32[]{:S(2)}, u32[]{:S(2)}) collective-permute-start(f32[3,2,128,128]{3,2,1,0:T(8,128)} %c_own.1), channel_id=1, source_target_pairs={{2,6},{3,7},{4,0},{5,1},{6,10},{7,11},{8,4},{9,5},{10,14},{11,15},... | collective-permute-start | bytes 1179656 | tf_op jit(solution)/shard_map/ppermute | solution.py:401
  2.0 12.7 %collective-permute-start.2 = (f32[3,2,128,128]{3,2,1,0:T(8,128)}, f32[3,2,128,128]{3,2,1,0:T(8,128)S(1)}, u32[]{:S(2)}, u32[]{:S(2)}) collective-permute-start(f32[3,2,128,128]{3,2,1,0:T(8,128)} %c_own.1), channel_id=1, source_target_pairs={{0,18},{1,19},{2,16},{3,17},{4,22},{5,23},{6,20},{7,21},{8,26},{9,... | collective-permute-start | bytes 1179656 | tf_op jit(solution)/shard_map/ppermute | solution.py:401
  5.9 9.3 %collective-permute-start.4 = (f32[2,2,128,128]{3,2,1,0:T(8,128)S(1)}, f32[2,2,128,128]{3,2,1,0:T(8,128)S(1)}, u32[]{:S(2)}, u32[]{:S(2)}) collective-permute-start(f32[2,2,128,128]{3,2,1,0:T(8,128)S(1)} %get-tuple-element.69), channel_id=1, source_target_pairs={{0,2},{1,3},{2,0},{3,1},{4,6},{5,7},{6,4},{7,5},{8,10},{9,11},{10,... | collective-permute-start | bytes 786440 | tf_op jit(solution)/shard_map/ppermute | solution.py:401
  6.7 14.1 %collective-permute-start.5 = (f32[2,2,128,128]{3,2,1,0:T(8,128)S(1)}, f32[2,2,128,128]{3,2,1,0:T(8,128)S(1)}, u32[]{:S(2)}, u32[]{:S(2)}) collective-permute-start(f32[2,2,128,128]{3,2,1,0:T(8,128)S(1)} %get-tuple-element.68), channel_id=1, source_target_pairs={{0,2},{1,3},{2,0},{3,1},{4,6},{5,7},{6,4},{7,5},{8,10},{9,11},{10,... | collective-permute-start | bytes 786440 | tf_op jit(solution)/shard_map/ppermute | solution.py:401
  14.3 13.9 %collective-permute-start.13 = (f32[3,2,128,128]{3,2,1,0:T(8,128)S(1)}, f32[3,2,128,128]{3,2,1,0:T(8,128)S(1)}, u32[]{:S(2)}, u32[]{:S(2)}) collective-permute-start(f32[3,2,128,128]{3,2,1,0:T(8,128)S(1)} %collective-permute-done.12), channel_id=1, source_target_pairs={{0,2},{1,3},{2,0},{3,1},{4,6},{5,7},{6,4},{7,5},{8,10},{9,11},{10,... | collective-permute-start | bytes 1179656 | tf_op jit(solution)/shard_map/ppermute | solution.py:401
  14.7 14.7 %collective-permute-start.3 = (f32[3,2,128,128]{3,2,1,0:T(8,128)S(1)}, f32[3,2,128,128]{3,2,1,0:T(8,128)S(1)}, u32[]{:S(2)}, u32[]{:S(2)}) collective-permute-start(f32[3,2,128,128]{3,2,1,0:T(8,128)S(1)} %collective-permute-done.2.c_near), channel_id=1, source_target_pairs={{0,1},{1,0},{2,3},{3,2},{4,5},{5,4},{6,7},{7,6},{8,9},{9,8},{10,11... | collective-permute-start | bytes 1179656 | tf_op jit(solution)/shard_map/ppermute | solution.py:401
  14.8 19.1 %collective-permute-start.1 = (f32[3,2,128,128]{3,2,1,0:T(8,128)}, f32[3,2,128,128]{3,2,1,0:T(8,128)S(1)}, u32[]{:S(2)}, u32[]{:S(2)}) collective-permute-start(f32[3,2,128,128]{3,2,1,0:T(8,128)} %c_own.1), channel_id=1, source_target_pairs={{0,1},{1,0},{2,3},{3,2},{4,5},{5,4},{6,7},{7,6},{8,9},{9,8},{10,11... | collective-permute-start | bytes 1179656 | tf_op jit(solution)/shard_map/ppermute | solution.py:401
  15.3 15.5 %collective-permute-start.8 = (f32[2,2,128,128]{3,2,1,0:T(8,128)S(1)}, f32[2,2,128,128]{3,2,1,0:T(8,128)S(1)}, u32[]{:S(2)}, u32[]{:S(2)}) collective-permute-start(f32[2,2,128,128]{3,2,1,0:T(8,128)S(1)} %collective-permute-done.4.p_near), channel_id=1, source_target_pairs={{0,4},{1,5},{4,8},{5,9},{6,2},{7,3},{8,12},{9,13},{10,6},{11,7},{1... | collective-permute-start | bytes 786440 | tf_op jit(solution)/shard_map/ppermute | solution.py:401
  20.8 17.6 %collective-permute-start.9 = (f32[2,2,128,128]{3,2,1,0:T(8,128)S(1)}, f32[2,2,128,128]{3,2,1,0:T(8,128)S(1)}, u32[]{:S(2)}, u32[]{:S(2)}) collective-permute-start(f32[2,2,128,128]{3,2,1,0:T(8,128)S(1)} %collective-permute-done.5.p_near_b), channel_id=1, source_target_pairs={{0,4},{1,5},{4,8},{5,9},{6,2},{7,3},{8,12},{9,13},{10,6},{11,7},{1... | collective-permute-start | bytes 786440 | tf_op jit(solution)/shard_map/ppermute | solution.py:401
  28.2 14.5 %collective-permute-start.14 = (f32[3,2,128,128]{3,2,1,0:T(8,128)S(1)}, f32[3,2,128,128]{3,2,1,0:T(8,128)S(1)}, u32[]{:S(2)}, u32[]{:S(2)}) collective-permute-start(f32[3,2,128,128]{3,2,1,0:T(8,128)S(1)} %collective-permute-done.13.c_far), channel_id=1, source_target_pairs={{0,1},{1,0},{2,3},{3,2},{4,5},{5,4},{6,7},{7,6},{8,9},{9,8},{10,11... | collective-permute-start | bytes 1179656 | tf_op jit(solution)/shard_map/ppermute | solution.py:401
  28.2 0.7 copy-start.2
  29.4 12.3 %collective-permute-start.6 = (f32[2,2,128,128]{3,2,1,0:T(8,128)S(1)}, f32[2,2,128,128]{3,2,1,0:T(8,128)S(1)}, u32[]{:S(2)}, u32[]{:S(2)}) collective-permute-start(f32[2,2,128,128]{3,2,1,0:T(8,128)S(1)} %collective-permute-done.4.p_near), channel_id=1, source_target_pairs={{1,0},{3,2},{5,4},{7,6},{9,8},{11,10},{13,12},{15,14},{17,16},{19,... | collective-permute-start | bytes 786440 | tf_op jit(solution)/shard_map/ppermute | solution.py:401
  30.8 11.0 %collective-permute-start.7 = (f32[2,2,128,128]{3,2,1,0:T(8,128)S(1)}, f32[2,2,128,128]{3,2,1,0:T(8,128)S(1)}, u32[]{:S(2)}, u32[]{:S(2)}) collective-permute-start(f32[2,2,128,128]{3,2,1,0:T(8,128)S(1)} %collective-permute-done.5.p_near_b), channel_id=1, source_target_pairs={{0,1},{2,3},{4,5},{6,7},{8,9},{10,11},{12,13},{14,15},{16,17},{18,... | collective-permute-start | bytes 786440 | tf_op jit(solution)/shard_map/ppermute | solution.py:401
  33.8 7.9 %collective-permute-start.10 = (f32[2,2,128,128]{3,2,1,0:T(8,128)S(1)}, f32[2,2,128,128]{3,2,1,0:T(8,128)S(1)}, u32[]{:S(2)}, u32[]{:S(2)}) collective-permute-start(f32[2,2,128,128]{3,2,1,0:T(8,128)S(1)} %collective-permute-done.8.p_far), channel_id=1, source_target_pairs={{1,0},{3,2},{5,4},{7,6},{9,8},{11,10},{13,12},{15,14},{17,16},{19,... | collective-permute-start | bytes 786440 | tf_op jit(solution)/shard_map/ppermute | solution.py:401
  35.1 1.0 copy-start
  36.2 1.0 copy-start.1
  37.2 5.5 %copy-start.3 = (s32[1,1024]{1,0:T(1,128)S(1)}, s32[1,1024]{1,0:T(1,128)}, u32[]{:S(2)}) copy-start(s32[1,1024]{1,0:T(1,128)} %cells.7) | copy-start | bytes 12292
  38.5 4.2 %collective-permute-start.11 = (f32[2,2,128,128]{3,2,1,0:T(8,128)S(1)}, f32[2,2,128,128]{3,2,1,0:T(8,128)S(1)}, u32[]{:S(2)}, u32[]{:S(2)}) collective-permute-start(f32[2,2,128,128]{3,2,1,0:T(8,128)S(1)} %collective-permute-done.9.p_far_b), channel_id=1, source_target_pairs={{0,1},{2,3},{4,5},{6,7},{8,9},{10,11},{12,13},{14,15},{16,17},{18,... | collective-permute-start | bytes 786440 | tf_op jit(solution)/shard_map/ppermute | solution.py:401
  42.7 20.1 %copy-start.4 = (f32[1,4,1024]{2,1,0:T(4,128)S(1)}, f32[1,4,1024]{2,1,0:T(4,128)}, u32[]{:S(2)}) copy-start(f32[1,4,1024]{2,1,0:T(4,128)} %param.6) | copy-start | bytes 49156
  78.1 1.8 %collective-permute-start.15 = (f32[8,6,16,128]{3,2,1,0:T(8,128)S(1)}, f32[8,6,16,128]{3,2,1,0:T(8,128)S(1)}, u32[]{:S(2)}, u32[]{:S(2)}) collective-permute-start(f32[8,6,16,128]{3,2,1,0:T(8,128)S(1)} %get-tuple-element.66), channel_id=1, source_target_pairs={{0,1},{1,0},{2,3},{3,2},{4,5},{5,4},{6,7},{7,6},{8,9},{9,8},{10,11... | collective-permute-start | bytes 1179656 | tf_op jit(solution)/shard_map/ppermute | solution.py:401
  103.3 5.7 %collective-permute-start.16 = (f32[1,6,16,128]{3,2,1,0:T(8,128)S(1)}, f32[1,6,16,128]{3,2,1,0:T(8,128)S(1)}, u32[]{:S(2)}, u32[]{:S(2)}) collective-permute-start(f32[1,6,16,128]{3,2,1,0:T(8,128)S(1)} %bitcast.20), channel_id=1, source_target_pairs={{0,16},{16,0},{1,17},{17,1},{2,18},{18,2},{3,19},{19,3},{4,20},{20... | collective-permute-start | bytes 147464 | tf_op jit(solution)/shard_map/ppermute | solution.py:469
  109.8 16.1 %all-to-all-start.3 = ((f32[8,6,16,128]{3,2,1,0:T(8,128)}), f32[8,6,16,128]{3,2,1,0:T(8,128)S(1)}, u32[]{:S(2)}, u32[]{:S(2)}) async-start(f32[8,6,16,128]{3,2,1,0:T(8,128)} %broadcast_in_dim.13), calls=%async_computation.3 | async-start | bytes 786432 | tf_op jit(solution)/shard_map/all_to_all | solution.py:471
  113.2 1.3 collective-permute-start.17

commit v13 on v11

--- a/solution.py
+++ b/solution.py
@@ -418,7 +418,7 @@
     own_c, p_pair = lax.optimization_barrier((conductivity, send(fields, swap)))
     c_pair = send(own_c, swap)
     p_near_pair, c_near_pair = send(p_near, swap), send(c_near, swap)
-    hot_own, c_near_pair = lax.optimization_barrier((hot_own, c_near_pair))
+    hot_own, c_near_pair, p_near_pair = lax.optimization_barrier((hot_own, c_near_pair, p_near_pair))
     p_mid, c_mid, ky_mid, kz_mid, dg_mid, p_sample = call(
         own_kernel,
         8,

time: 117 us -> 118 us (level)
  transfers between devices with their start and end apart: 15 -> 15, of which waited for: 10 -> 9; matrix products, arithmetic and copies ran while one was open for 1% -> 1% of each run, Pallas kernels for 2% -> 2%
where the time goes in v13:
time: 118 us
  blocking collectives  45.8 us (39%)
  waiting for transfers between devices  36.8 us (31%)
  Pallas kernels  15.9 us (13%)
  starting transfers between devices  13.3 us (11%)
  local copies, waits for them, and re-layouts  4.29 us (4%)
    all_to_all x1, blocking collectives, per_device(): parts = lax.all_to_all(total, 'z', 0, 0, tiled=True)  23.2 us
    all_to_all x2, blocking collectives, per_device(): got = lax.all_to_all(sent, ('y', 'xl'), 0, 0, tiled=True)  22.6 us
    ppermute x13, waiting for transfers between devices, send(): return lax.ppermute(x, NAMES, pairs)  21.3 us
    pallas_call x5, Pallas kernels, run(): pl.pallas_call(kernel, out_shape=tuple((jax.ShapeDtypeStruct(x, kind) for...  15.9 us
    all_to_all x1, waiting for transfers between devices, per_device(): whole = lax.all_to_all(spread, 'z', 0, 0, tiled=True)  10.8 us
    ppermute x13, starting transfers between devices, send(): return lax.ppermute(x, NAMES, pairs)  8.93 us
    ppermute x1, waiting for transfers between devices, per_device(): share = share + lax.ppermute(share, 'xh', [(0, 1), (1, 0)])  4.79 us
    all_to_all x1, starting transfers between devices, per_device(): whole = lax.all_to_all(spread, 'z', 0, 0, tiled=True)  3.45 us
  transfers between devices with their start and end apart: 15, of which 9 were waited for; matrix products, arithmetic and copies ran while one was open for 1% of the time, Pallas kernels for 2%

profile of v13, /device:TPU:4, one launch (start us, length us, event | category | flops | bytes accessed | tf_op | source)
XLA Modules:
  0.0 117.5 jit_solution(14202589214344768287)
XLA Ops:
  0.6 1.3 %collective-permute-start.2 = (f32[4,2,128,128]{3,2,1,0:T(8,128)}, f32[4,2,128,128]{3,2,1,0:T(8,128)S(1)}, u32[]{:S(2)}, u32[]{:S(2)}) collective-permute-start(f32[4,2,128,128]{3,2,1,0:T(8,128)} %bitcast.11), channel_id=1, source_target_pairs={{0,2},{1,3},{2,0},{3,1},{4,6},{5,7},{6,4},{7,5},{8,10},{9,11},{10,... | collective-permute-start | bytes 1572872 | tf_op jit(solution)/shard_map/ppermute | solution.py:398
  1.9 1.6 %collective-permute-start.3 = (f32[3,2,128,128]{3,2,1,0:T(8,128)}, f32[3,2,128,128]{3,2,1,0:T(8,128)S(1)}, u32[]{:S(2)}, u32[]{:S(2)}) collective-permute-start(f32[3,2,128,128]{3,2,1,0:T(8,128)} %c_own.1), channel_id=1, source_target_pairs={{0,18},{1,19},{2,16},{3,17},{4,22},{5,23},{6,20},{7,21},{8,26},{9,... | collective-permute-start | bytes 1179656 | tf_op jit(solution)/shard_map/ppermute | solution.py:398
  3.5 0.0 collective-permute-start
  3.5 1.3 %collective-permute-start.8 = (f32[3,2,128,128]{3,2,1,0:T(8,128)}, f32[3,2,128,128]{3,2,1,0:T(8,128)S(1)}, u32[]{:S(2)}, u32[]{:S(2)}) collective-permute-start(f32[3,2,128,128]{3,2,1,0:T(8,128)} %c_own.1), channel_id=1, source_target_pairs={{2,6},{3,7},{4,0},{5,1},{6,10},{7,11},{8,4},{9,5},{10,14},{11,15},... | collective-permute-start | bytes 1179656 | tf_op jit(solution)/shard_map/ppermute | solution.py:398
  4.8 7.9 %collective-permute-done.3.c_near = f32[3,2,128,128]{3,2,1,0:T(8,128)S(1)} collective-permute-done((f32[3,2,128,128]{3,2,1,0:T(8,128)}, f32[3,2,128,128]{3,2,1,0:T(8,128)S(1)}, u32[]{:S(2)}, u32[]{:S(2)}) %collective-permute-start.3) | collective-permute-done | bytes 393248 | tf_op jit(solution)/shard_map/ppermute | solution.py:398
  12.7 1.9 %collective-permute-done.2.p_near = f32[4,2,128,128]{3,2,1,0:T(8,128)S(1)} collective-permute-done((f32[4,2,128,128]{3,2,1,0:T(8,128)}, f32[4,2,128,128]{3,2,1,0:T(8,128)S(1)}, u32[]{:S(2)}, u32[]{:S(2)}) %collective-permute-start.2) | collective-permute-done | bytes 524320 | tf_op jit(solution)/shard_map/ppermute | solution.py:398
  14.6 0.0 collective-permute-start.5
  14.6 3.5 %collective-permute-start.6 = (f32[4,2,128,128]{3,2,1,0:T(8,128)S(1)}, f32[4,2,128,128]{3,2,1,0:T(8,128)S(1)}, u32[]{:S(2)}, u32[]{:S(2)}) collective-permute-start(f32[4,2,128,128]{3,2,1,0:T(8,128)S(1)} %collective-permute-done.2.p_near), channel_id=1, source_target_pairs={{0,4},{1,5},{4,8},{5,9},{6,2},{7,3},{8,12},{9,13},{10,6},{11,7},{1... | collective-permute-start | bytes 1572872 | tf_op jit(solution)/shard_map/ppermute | solution.py:398
  18.1 0.3 collective-permute-start.4
  18.4 0.0 collective-permute-done.p_pair
  18.4 0.3 collective-permute-start.1
  18.7 0.0 collective-permute-done.8
  18.7 0.0 collective-permute-start.9
  18.7 0.0 copy-start.2
  18.7 0.7 copy-done.2
  19.4 0.5 shard_map.59
  19.9 0.0 collective-permute-done.4.c_near_pair
  20.0 0.0 collective-permute-done.5.p_near_pair
  20.0 0.7 collective-permute-done.1.c_pair
  20.7 1.0 copy-done
  21.7 1.0 copy-done.1
  22.7 1.3 %shard_map.60 = (f32[2,4,128,128]{3,2,1,0:T(8,128)S(1)}, f32[4,128,128]{2,1,0:T(8,128)S(1)}, f32[4,128,128]{2,1,0:T(8,128)S(1)}, f32[4,128,128]{2,1,0:T(8,128)S(...) custom-call(f32[4,2,128,128]{3,2,1,0:T(8,128)S(1)} %bitcast.13, ...), custom_call_target="tpu_custom_call" | custom-call | tf_op jit(solution)/shard_map/pallas_call | solution.py:351
  24.0 5.9 %collective-permute-done.6.p_far = f32[4,2,128,128]{3,2,1,0:T(8,128)S(1)} collective-permute-done((f32[4,2,128,128]{3,2,1,0:T(8,128)S(1)}, f32[4,2,128,128]{3,2,1,0:T(8,128)S(1)}, u32[]{:S(2)}, u32[]{:S(2)}) %collective-permute-start.6) | collective-permute-done | bytes 524320 | tf_op jit(solution)/shard_map/ppermute | solution.py:398
  29.9 0.0 collective-permute-start.7
  29.9 0.0 collective-permute-done.9.c_far
  30.0 0.5 collective-permute-start.10
  30.4 2.0 %collective-permute-done.10.c_far_pair = f32[3,2,128,128]{3,2,1,0:T(8,128)S(1)} collective-permute-done((f32[3,2,128,128]{3,2,1,0:T(8,128)S(1)}, f32[3,2,128,128]{3,2,1,0:T(8,128)S(1)}, u32[]{:S(2)}, u32[]{:S(2)}) %collective-permute-start.10) | collective-permute-done | bytes 393248 | tf_op jit(solution)/shard_map/ppermute | solution.py:398
  32.4 0.0 collective-permute-done.7.p_far_pair
  32.4 0.0 copy-done.3
  32.4 7.4 %shard_map.61 = (f32[12,128,128]{2,1,0:T(8,128)S(1)}, f32[12,128,128]{2,1,0:T(8,128)S(1)}, f32[12,128,128]{2,1,0:T(8,128)S(1)}, f32[12,128,128]{2,1,0:T(8,128)S(...) custom-call(f32[2,4,128,128]{3,2,1,0:T(8,128)S(1)} %get-tuple-elemen, ...), custom_call_target="tpu_custom_call" | custom-call | tf_op jit(solution)/shard_map/pallas_call | solution.py:351
  39.8 13.9 %all_to_all.20.got = f32[8,8,1152]{2,1,0:T(8,128)S(1)} all-to-all(f32[8,8,1152]{2,1,0:T(8,128)S(1)} %get-tuple-element.53), channel_id=1, replica_groups=mesh['z'=8,'xh'=2,'y'=4,'xl'=2,'c'=2] {'y','xl'}, dimensions={0} | all-to-all | bytes 589824 | tf_op jit(solution)/shard_map/all_to_all | solution.py:443
  53.7 0.0 copy-done.4
  53.7 5.4 %shard_map.62 = (f32[2,6,128,128]{3,2,1,0:T(8,128)S(1)}, f32[2,6,128,128]{3,2,1,0:T(8,128)S(1)}, f32[2,6,128,128]{3,2,1,0:T(8,128)S(1)}, f32[2,6,128,128]{3,2,1,...) custom-call(f32[8,8,1152]{2,1,0:T(8,128)S(1)} %all_to_all.20.got, f32[4,1024]{1,0:T(4,128)S(1)} %bitcast.14, ...), custom_call_target="tpu_custom_call" | custom-call | tf_op jit(solution)/shard_map/pallas_call | solution.py:351
  59.2 8.6 %all_to_all.21.got = f32[8,8,128]{2,1,0:T(8,128)S(1)} all-to-all(f32[8,8,128]{2,1,0:T(8,128)S(1)} %get-tuple-element.64), channel_id=1, replica_groups=mesh['z'=8,'xh'=2,'y'=4,'xl'=2,'c'=2] {'y','xl'}, dimensions={0} | all-to-all | bytes 65536 | tf_op jit(solution)/shard_map/all_to_all | solution.py:451
  67.8 1.3 %shard_map.63 = (f32[8,6,16,128]{3,2,1,0:T(8,128)S(1)}, f32[8,6,16,128]{3,2,1,0:T(8,128)S(1)}) custom-call(f32[8,8,128]{2,1,0:T(8,128)S(1)} %all_to_all.21.got, f32[2,6,128,128]{3,2,1,0:T(8,128)S(1)} %get-tuple-element.65.a0, f32[2,6,128,128]{3,2,1,0:T(8,128)S(1)} %get-tuple-element.66.a1, f32[2,6,128,128]{3,2,1,0:T(8,128)S(1)} %get-tuple-element.67.a2, ...), custom_call_target="tpu_custom_call" | custom-call | tf_op jit(solution)/shard_map/pallas_call | solution.py:351
  69.0 0.1 collective-permute-start.11
  69.1 1.7 %collective-permute-done.11 = f32[8,6,16,128]{3,2,1,0:T(8,128)S(1)} collective-permute-done((f32[8,6,16,128]{3,2,1,0:T(8,128)S(1)}, f32[8,6,16,128]{3,2,1,0:T(8,128)S(1)}, u32[]{:S(2)}, u32[]{:S(2)}) %collective-permute-start.11) | collective-permute-done | bytes 393248 | tf_op jit(solution)/shard_map/ppermute | solution.py:398
  70.9 0.1 add.6
  70.9 23.2 %all_to_all.22 = f32[8,6,16,128]{3,2,1,0:T(8,128)S(1)} all-to-all(f32[8,6,16,128]{3,2,1,0:T(8,128)S(1)} %add.6), channel_id=1, replica_groups=mesh['z'=8,'xh'=2,'y'=4,'xl'=2,'c'=2] {'z'}, dimensions={0} | all-to-all | bytes 786432 | tf_op jit(solution)/shard_map/all_to_all | solution.py:460
  94.2 0.9 collective-permute-start.12
  95.1 4.8 %collective-permute-done.12 = f32[1,6,16,128]{3,2,1,0:T(8,128)S(1)} collective-permute-done((f32[1,6,16,128]{3,2,1,0:T(8,128)S(1)}, f32[1,6,16,128]{3,2,1,0:T(8,128)S(1)}, u32[]{:S(2)}, u32[]{:S(2)}) %collective-permute-start.12) | collective-permute-done | bytes 49184 | tf_op jit(solution)/shard_map/ppermute | solution.py:463
  99.9 0.8 broadcast_in_dim.13
  100.7 3.5 %all-to-all-start.3 = ((f32[8,6,16,128]{3,2,1,0:T(8,128)}), f32[8,6,16,128]{3,2,1,0:T(8,128)S(1)}, u32[]{:S(2)}, u32[]{:S(2)}) async-start(f32[8,6,16,128]{3,2,1,0:T(8,128)} %broadcast_in_dim.13), calls=%async_computation.3 | async-start | bytes 786432 | tf_op jit(solution)/shard_map/all_to_all | solution.py:465
  104.1 0.1 collective-permute-start.13
  104.2 1.2 collective-permute-done.13
  105.4 0.6 maximum_select_fusion
  106.0 10.8 %all-to-all-done.3 = f32[8,6,16,128]{3,2,1,0:T(8,128)S(1)} async-done(((f32[8,6,16,128]{3,2,1,0:T(8,128)}), f32[8,6,16,128]{3,2,1,0:T(8,128)S(1)}, u32[]{:S(2)}, u32[]{:S(2)}) %all-to-all-start.3) | async-done | bytes 393248 | tf_op jit(solution)/shard_map/all_to_all | solution.py:465
  116.8 0.8 copy.6
  (6 shorter events, 0.0 us)
Async XLA Ops:
  0.6 14.0 %collective-permute-start.2 = (f32[4,2,128,128]{3,2,1,0:T(8,128)}, f32[4,2,128,128]{3,2,1,0:T(8,128)S(1)}, u32[]{:S(2)}, u32[]{:S(2)}) collective-permute-start(f32[4,2,128,128]{3,2,1,0:T(8,128)} %bitcast.11), channel_id=1, source_target_pairs={{0,2},{1,3},{2,0},{3,1},{4,6},{5,7},{6,4},{7,5},{8,10},{9,11},{10,... | collective-permute-start | bytes 1572872 | tf_op jit(solution)/shard_map/ppermute | solution.py:398
  1.9 10.8 %collective-permute-start.3 = (f32[3,2,128,128]{3,2,1,0:T(8,128)}, f32[3,2,128,128]{3,2,1,0:T(8,128)S(1)}, u32[]{:S(2)}, u32[]{:S(2)}) collective-permute-start(f32[3,2,128,128]{3,2,1,0:T(8,128)} %c_own.1), channel_id=1, source_target_pairs={{0,18},{1,19},{2,16},{3,17},{4,22},{5,23},{6,20},{7,21},{8,26},{9,... | collective-permute-start | bytes 1179656 | tf_op jit(solution)/shard_map/ppermute | solution.py:398
  3.5 14.9 %collective-permute-start = (f32[4,2,128,128]{3,2,1,0:T(8,128)}, f32[4,2,128,128]{3,2,1,0:T(8,128)S(1)}, u32[]{:S(2)}, u32[]{:S(2)}) collective-permute-start(f32[4,2,128,128]{3,2,1,0:T(8,128)} %bitcast.12), channel_id=1, source_target_pairs={{0,1},{1,0},{2,3},{3,2},{4,5},{5,4},{6,7},{7,6},{8,9},{9,8},{10,11... | collective-permute-start | bytes 1572872 | tf_op jit(solution)/shard_map/ppermute | solution.py:398
  3.5 15.2 %collective-permute-start.8 = (f32[3,2,128,128]{3,2,1,0:T(8,128)}, f32[3,2,128,128]{3,2,1,0:T(8,128)S(1)}, u32[]{:S(2)}, u32[]{:S(2)}) collective-permute-start(f32[3,2,128,128]{3,2,1,0:T(8,128)} %c_own.1), channel_id=1, source_target_pairs={{2,6},{3,7},{4,0},{5,1},{6,10},{7,11},{8,4},{9,5},{10,14},{11,15},... | collective-permute-start | bytes 1179656 | tf_op jit(solution)/shard_map/ppermute | solution.py:398
  14.6 5.4 %collective-permute-start.5 = (f32[4,2,128,128]{3,2,1,0:T(8,128)S(1)}, f32[4,2,128,128]{3,2,1,0:T(8,128)S(1)}, u32[]{:S(2)}, u32[]{:S(2)}) collective-permute-start(f32[4,2,128,128]{3,2,1,0:T(8,128)S(1)} %collective-permute-done.2.p_near), channel_id=1, source_target_pairs={{0,1},{1,0},{2,3},{3,2},{4,5},{5,4},{6,7},{7,6},{8,9},{9,8},{10,11... | collective-permute-start | bytes 1572872 | tf_op jit(solution)/shard_map/ppermute | solution.py:398
  14.6 15.3 %collective-permute-start.6 = (f32[4,2,128,128]{3,2,1,0:T(8,128)S(1)}, f32[4,2,128,128]{3,2,1,0:T(8,128)S(1)}, u32[]{:S(2)}, u32[]{:S(2)}) collective-permute-start(f32[4,2,128,128]{3,2,1,0:T(8,128)S(1)} %collective-permute-done.2.p_near), channel_id=1, source_target_pairs={{0,4},{1,5},{4,8},{5,9},{6,2},{7,3},{8,12},{9,13},{10,6},{11,7},{1... | collective-permute-start | bytes 1572872 | tf_op jit(solution)/shard_map/ppermute | solution.py:398
  18.1 1.8 %collective-permute-start.4 = (f32[3,2,128,128]{3,2,1,0:T(8,128)S(1)}, f32[3,2,128,128]{3,2,1,0:T(8,128)S(1)}, u32[]{:S(2)}, u32[]{:S(2)}) collective-permute-start(f32[3,2,128,128]{3,2,1,0:T(8,128)S(1)} %collective-permute-done.3.c_near), channel_id=1, source_target_pairs={{0,1},{1,0},{2,3},{3,2},{4,5},{5,4},{6,7},{7,6},{8,9},{9,8},{10,11... | collective-permute-start | bytes 1179656 | tf_op jit(solution)/shard_map/ppermute | solution.py:398
  18.4 2.3 %collective-permute-start.1 = (f32[3,2,128,128]{3,2,1,0:T(8,128)}, f32[3,2,128,128]{3,2,1,0:T(8,128)S(1)}, u32[]{:S(2)}, u32[]{:S(2)}) collective-permute-start(f32[3,2,128,128]{3,2,1,0:T(8,128)} %c_own.1), channel_id=1, source_target_pairs={{0,1},{1,0},{2,3},{3,2},{4,5},{5,4},{6,7},{7,6},{8,9},{9,8},{10,11... | collective-permute-start | bytes 1179656 | tf_op jit(solution)/shard_map/ppermute | solution.py:398
  18.7 11.2 %collective-permute-start.9 = (f32[3,2,128,128]{3,2,1,0:T(8,128)S(1)}, f32[3,2,128,128]{3,2,1,0:T(8,128)S(1)}, u32[]{:S(2)}, u32[]{:S(2)}) collective-permute-start(f32[3,2,128,128]{3,2,1,0:T(8,128)S(1)} %collective-permute-done.8), channel_id=1, source_target_pairs={{0,2},{1,3},{2,0},{3,1},{4,6},{5,7},{6,4},{7,5},{8,10},{9,11},{10,... | collective-permute-start | bytes 1179656 | tf_op jit(solution)/shard_map/ppermute | solution.py:398
  18.7 0.7 copy-start.2
  20.7 1.0 copy-start
  21.7 1.0 copy-start.1
  22.7 9.7 %copy-start.3 = (s32[1,1024]{1,0:T(1,128)S(1)}, s32[1,1024]{1,0:T(1,128)}, u32[]{:S(2)}) copy-start(s32[1,1024]{1,0:T(1,128)} %cells.7) | copy-start | bytes 12292
  29.9 2.5 %collective-permute-start.7 = (f32[4,2,128,128]{3,2,1,0:T(8,128)S(1)}, f32[4,2,128,128]{3,2,1,0:T(8,128)S(1)}, u32[]{:S(2)}, u32[]{:S(2)}) collective-permute-start(f32[4,2,128,128]{3,2,1,0:T(8,128)S(1)} %collective-permute-done.6.p_far), channel_id=1, source_target_pairs={{0,1},{1,0},{2,3},{3,2},{4,5},{5,4},{6,7},{7,6},{8,9},{9,8},{10,11... | collective-permute-start | bytes 1572872 | tf_op jit(solution)/shard_map/ppermute | solution.py:398
  30.0 2.4 %collective-permute-start.10 = (f32[3,2,128,128]{3,2,1,0:T(8,128)S(1)}, f32[3,2,128,128]{3,2,1,0:T(8,128)S(1)}, u32[]{:S(2)}, u32[]{:S(2)}) collective-permute-start(f32[3,2,128,128]{3,2,1,0:T(8,128)S(1)} %collective-permute-done.9.c_far), channel_id=1, source_target_pairs={{0,1},{1,0},{2,3},{3,2},{4,5},{5,4},{6,7},{7,6},{8,9},{9,8},{10,11... | collective-permute-start | bytes 1179656 | tf_op jit(solution)/shard_map/ppermute | solution.py:398
  32.4 21.3 %copy-start.4 = (f32[1,4,1024]{2,1,0:T(4,128)S(1)}, f32[1,4,1024]{2,1,0:T(4,128)}, u32[]{:S(2)}) copy-start(f32[1,4,1024]{2,1,0:T(4,128)} %param.6) | copy-start | bytes 49156
  69.0 1.8 %collective-permute-start.11 = (f32[8,6,16,128]{3,2,1,0:T(8,128)S(1)}, f32[8,6,16,128]{3,2,1,0:T(8,128)S(1)}, u32[]{:S(2)}, u32[]{:S(2)}) collective-permute-start(f32[8,6,16,128]{3,2,1,0:T(8,128)S(1)} %get-tuple-element.72), channel_id=1, source_target_pairs={{0,1},{1,0},{2,3},{3,2},{4,5},{5,4},{6,7},{7,6},{8,9},{9,8},{10,11... | collective-permute-start | bytes 1179656 | tf_op jit(solution)/shard_map/ppermute | solution.py:398
  94.2 5.7 %collective-permute-start.12 = (f32[1,6,16,128]{3,2,1,0:T(8,128)S(1)}, f32[1,6,16,128]{3,2,1,0:T(8,128)S(1)}, u32[]{:S(2)}, u32[]{:S(2)}) collective-permute-start(f32[1,6,16,128]{3,2,1,0:T(8,128)S(1)} %bitcast.17), channel_id=1, source_target_pairs={{0,16},{16,0},{1,17},{17,1},{2,18},{18,2},{3,19},{19,3},{4,20},{20... | collective-permute-start | bytes 147464 | tf_op jit(solution)/shard_map/ppermute | solution.py:463
  100.7 16.1 %all-to-all-start.3 = ((f32[8,6,16,128]{3,2,1,0:T(8,128)}), f32[8,6,16,128]{3,2,1,0:T(8,128)S(1)}, u32[]{:S(2)}, u32[]{:S(2)}) async-start(f32[8,6,16,128]{3,2,1,0:T(8,128)} %broadcast_in_dim.13), calls=%async_computation.3 | async-start | bytes 786432 | tf_op jit(solution)/shard_map/all_to_all | solution.py:465
  104.1 1.3 %collective-permute-start.13 = (f32[2,1024]{1,0:T(2,128)S(1)}, f32[2,1024]{1,0:T(2,128)S(1)}, u32[]{:S(2)}, u32[]{:S(2)}) collective-permute-start(f32[2,1024]{1,0:T(2,128)S(1)} %get-tuple-element.73), channel_id=1, source_target_pairs={{0,1},{1,0},{2,3},{3,2},{4,5},{5,4},{6,7},{7,6},{8,9},{9,8},{10,11... | collective-permute-start | bytes 24584 | tf_op jit(solution)/shard_map/ppermute | solution.py:398
